TPU v7x, 32 devices: a whole 2x2x4 slice. The times are simulated.
32 devices in a mesh: batch: 8 (over z, y), fsdp: 4 (over x, core).
Axes of the slice: x: 2, y: 2, z: 4, core: 2. Of those that a mesh axis runs over, the one named last changes fastest.
Arguments:
- incoming_hidden_matrix: bfloat16 [32, 1024, 768], P(('batch', 'fsdp')), may hold values from -6 to 6
- sequence_membership: int32 [32, 1024], P(('batch', 'fsdp')), may hold values from 0 to 7, never falling along the last dimension, each value on 1 to 512 neighbouring positions
- matching_passages: int32 [32, 4], P(('batch', 'fsdp')), may hold values from 0 to 127
- softness_scale: float32 [], replicated, may hold values from 0.03 to 0.06
- combined_projection_matrix: bfloat16 [768, 2304], P('fsdp'), may hold values from -0.21875 to 0.21875
- mixer_projection_matrix: bfloat16 [768, 768], P('fsdp'), may hold values from -0.625 to 0.625
- widening_matrix: bfloat16 [768, 3072], P('fsdp'), may hold values from -0.21875 to 0.21875
- gating_matrix: bfloat16 [768, 3072], P('fsdp'), may hold values from -0.21875 to 0.21875
- narrowing_matrix: bfloat16 [3072, 768], P('fsdp'), may hold values from -0.109375 to 0.109375
- mixer_scaling_factor: bfloat16 [768], P('fsdp'), may hold values from 0.5 to 1.5
- mixer_scaling_offset: bfloat16 [768], P('fsdp'), may hold values from -0.59765625 to 0.59765625
- perceptron_scaling_factor: bfloat16 [768], P('fsdp'), may hold values from 0.5 to 1.5
- perceptron_scaling_offset: bfloat16 [768], P('fsdp'), may hold values from -0.59765625 to 0.59765625
Outputs:
- query_loss: float32 [32, 4], P(('batch', 'fsdp'))
- grad_input: float32 [32, 1024, 768], P(('batch', 'fsdp'))
- grad_w_qkv: float32 [768, 2304], P('fsdp')
- grad_w_out: float32 [768, 768], P('fsdp')
- grad_w_up: float32 [768, 3072], P('fsdp')
- grad_w_gate: float32 [768, 3072], P('fsdp')
- grad_w_down: float32 [3072, 768], P('fsdp')
- grad_gain_attn: float32 [768], P('fsdp')
- grad_bias_attn: float32 [768], P('fsdp')
- grad_gain_ffn: float32 [768], P('fsdp')
- grad_bias_ffn: float32 [768], P('fsdp')
Inputs may be any that keep to these rules, and one draw needn't show every extreme that they name: `sequence_membership`: along each row the numbers never fall; every number appears in every row, on 1 to 512 tokens, and one segment of each row has exactly 512 tokens.
All inputs are finite; a program needn't handle non-finite values.
Results may differ from a plain program's by a relative error of at most 0.013.
Values may be sent and summed in bfloat16 or wider, within the bound.
No kernel may reach another device: no remote copies, remote signals or barrier semaphores. Data moves between devices by JAX's collectives and lax.ppermute only.
A program may use at most 256 MiB of HBM per device.

v0:
```python
import math

import jax
import jax.numpy as jnp
from jax import lax
from jax.sharding import PartitionSpec as P

HEADS = 12
QSEG = 4
SEGS = 8


EPSILON = 1e-06
HIGHEST = lax.Precision.HIGHEST


def layer_norm(value_in, gain_vec, offset_vec):
    center = value_in - jnp.mean(value_in, axis=-1, keepdims=True)
    spread = jnp.mean(center * center, axis=-1, keepdims=True)
    return center * lax.rsqrt(spread + EPSILON) * gain_vec + offset_vec


def swiglu(gate_proj, up_proj):
    return jax.nn.silu(gate_proj) * up_proj


def matmul_low(left_op, right_op):
    return jnp.dot(left_op, right_op, preferred_element_type=jnp.float32)


def matmul_t(left_op, right_op):
    return lax.dot_general(
        left_op, right_op, (((0,), (0,)), ((), ())), preferred_element_type=jnp.float32
    )


def multiply_by_flipped_second(left_op, right_op):
    return lax.dot_general(
        left_op, right_op, (((1,), (1,)), ((), ())), preferred_element_type=jnp.float32
    )


def rotary_tables(segment_row, head_dim, seg_count):
    row_len = segment_row.shape[0]
    seg_marks = (segment_row[:, None] == jnp.arange(seg_count, dtype=jnp.int32)[None, :]).astype(
        jnp.int32
    )
    seg_sizes = jnp.sum(seg_marks, axis=0)
    firsts = jnp.cumsum(seg_sizes) - seg_sizes
    positions = jnp.arange(row_len, dtype=jnp.int32) - jnp.sum(seg_marks * firsts[None, :], axis=1)
    inverse = 1000.0 ** (-(jnp.arange(head_dim // 2, dtype=jnp.float32) * 2.0) / head_dim)
    angles = positions.astype(jnp.float32)[:, None] * inverse[None, :]
    return (jnp.cos(angles), jnp.sin(angles))


def rotate(tensor, cosine, sine_tab):
    middle = tensor.shape[-1] // 2
    first_part = tensor[..., :middle]
    second_part = tensor[..., middle:]
    cos_b = cosine[:, None, :]
    sin_b = sine_tab[:, None, :]
    return jnp.concatenate(
        [first_part * cos_b - second_part * sin_b, second_part * cos_b + first_part * sin_b],
        axis=-1,
    )


def rotate_back(tensor, cosine, sine_tab):
    middle = tensor.shape[-1] // 2
    first_part = tensor[..., :middle]
    second_part = tensor[..., middle:]
    cos_b = cosine[:, None, :]
    sin_b = sine_tab[:, None, :]
    return jnp.concatenate(
        [first_part * cos_b + second_part * sin_b, second_part * cos_b - first_part * sin_b],
        axis=-1,
    )


def pool_embed(hidden_two, seg_marks):
    pooled = lax.dot_general(
        seg_marks,
        hidden_two,
        (((0,), (0,)), ((), ())),
        precision=HIGHEST,
        preferred_element_type=jnp.float32,
    )
    pooled = pooled / jnp.sum(seg_marks, axis=0)[:, None]
    return pooled * lax.rsqrt(jnp.sum(pooled * pooled, axis=-1, keepdims=True) + EPSILON)


def block_scores(q_block, seg_block, keys_all, segment_row, scale_factor):
    scores = (
        jnp.einsum("qhd,khd->hqk", q_block, keys_all, preferred_element_type=jnp.float32)
        * scale_factor
    )
    same_seg = seg_block[:, None] == segment_row[None, :]
    return jnp.where(same_seg[None], scores, -1e30)


def attend_forward(queries, keys_all, values, segment_row, scale_factor):
    row_len, head_count, head_dim = queries.shape
    block_rows = min(512, row_len)
    block_count = row_len // block_rows
    q_blocks = queries.reshape(block_count, block_rows, head_count, head_dim)
    s_blocks = segment_row.reshape(block_count, block_rows)

    def one_block(block_in):
        scores = block_scores(block_in[0], block_in[1], keys_all, segment_row, scale_factor)
        row_peak = jnp.max(scores, axis=-1, keepdims=True)
        exp_scores = jnp.exp(scores - row_peak)
        exp_total = jnp.sum(exp_scores, axis=-1, keepdims=True)
        attn_probs = (exp_scores / exp_total).astype(jnp.bfloat16)
        out_block = jnp.einsum(
            "hqk,khd->qhd", attn_probs, values, preferred_element_type=jnp.float32
        )
        return (out_block, (row_peak + jnp.log(exp_total))[..., 0])

    out_blocks, log_sums = lax.map(one_block, (q_blocks, s_blocks))
    return (out_blocks.reshape(row_len, head_count * head_dim), log_sums)


def attend_backward(queries, keys_all, values, segment_row, log_sums, grad_attended, scale_factor):
    row_len, head_count, head_dim = queries.shape
    block_rows = min(512, row_len)
    block_count = row_len // block_rows
    q_blocks = queries.reshape(block_count, block_rows, head_count, head_dim)
    s_blocks = segment_row.reshape(block_count, block_rows)
    g_blocks = grad_attended.reshape(block_count, block_rows, head_count, head_dim)

    def one_block(running, pieces):
        grad_keys, grad_values = running
        q_block, seg_block, lse_block, g_block = pieces
        scores = block_scores(q_block, seg_block, keys_all, segment_row, scale_factor)
        attn_probs = jnp.exp(scores - lse_block[..., None])
        grad_probs = jnp.einsum("qhd,khd->hqk", g_block, values, preferred_element_type=jnp.float32)
        inner_sum = jnp.sum(attn_probs * grad_probs, axis=-1, keepdims=True)
        grad_scores = (attn_probs * (grad_probs - inner_sum)).astype(jnp.bfloat16)
        grad_q = (
            jnp.einsum("hqk,khd->qhd", grad_scores, keys_all, preferred_element_type=jnp.float32)
            * scale_factor
        )
        grad_keys = (
            grad_keys
            + jnp.einsum("hqk,qhd->khd", grad_scores, q_block, preferred_element_type=jnp.float32)
            * scale_factor
        )
        grad_values = grad_values + jnp.einsum(
            "hqk,qhd->khd",
            attn_probs.astype(jnp.bfloat16),
            g_block,
            preferred_element_type=jnp.float32,
        )
        return ((grad_keys, grad_values), grad_q)

    zero_kv = jnp.zeros((row_len, head_count, head_dim), jnp.float32)
    (grad_keys, grad_values), grad_q = lax.scan(
        one_block, (zero_kv, zero_kv), (q_blocks, s_blocks, log_sums, g_blocks)
    )
    return (grad_q.reshape(row_len, head_count, head_dim), grad_keys, grad_values)


def per_device(
    incoming_hidden_matrix,
    sequence_membership,
    matching_passages,
    softness_scale,
    combined_projection_matrix,
    mixer_projection_matrix,
    widening_matrix,
    gating_matrix,
    narrowing_matrix,
    mixer_scaling_factor,
    mixer_scaling_offset,
    perceptron_scaling_factor,
    perceptron_scaling_offset,
):
    full_qkv, full_out, full_up, full_gate, full_down, full_ga, full_ba, full_gf, full_bf = (
        lax.all_gather(combined_projection_matrix, "fsdp", axis=0, tiled=True),
        lax.all_gather(mixer_projection_matrix, "fsdp", axis=0, tiled=True),
        lax.all_gather(widening_matrix, "fsdp", axis=0, tiled=True),
        lax.all_gather(gating_matrix, "fsdp", axis=0, tiled=True),
        lax.all_gather(narrowing_matrix, "fsdp", axis=0, tiled=True),
        lax.all_gather(mixer_scaling_factor, "fsdp", axis=0, tiled=True),
        lax.all_gather(mixer_scaling_offset, "fsdp", axis=0, tiled=True),
        lax.all_gather(perceptron_scaling_factor, "fsdp", axis=0, tiled=True),
        lax.all_gather(perceptron_scaling_offset, "fsdp", axis=0, tiled=True),
    )
    tokens = incoming_hidden_matrix[0]
    tokens_f = tokens.astype(jnp.float32)
    segment_row = sequence_membership[0]
    target_row = matching_passages[0]
    row_len = tokens.shape[0]
    model_width = tokens.shape[1]
    head_count = HEADS
    head_dim = model_width // head_count
    scale_factor = 1.0 / math.sqrt(head_dim)
    cosine, sine_tab = rotary_tables(segment_row, head_dim, SEGS)
    joined = matmul_low(tokens, full_qkv).reshape(row_len, 3, head_count, head_dim)
    queries = rotate(joined[:, 0], cosine, sine_tab).astype(jnp.bfloat16)
    keys_all = rotate(joined[:, 1], cosine, sine_tab).astype(jnp.bfloat16)
    values = joined[:, 2].astype(jnp.bfloat16)
    attended, log_sums = attend_forward(queries, keys_all, values, segment_row, scale_factor)
    att_low = attended.astype(jnp.bfloat16)
    branch = matmul_low(att_low, full_out)
    hidden_one, ln_one_back = jax.vjp(
        layer_norm, tokens_f + branch, full_ga.astype(jnp.float32), full_ba.astype(jnp.float32)
    )
    hidden_low = hidden_one.astype(jnp.bfloat16)
    up_proj = matmul_low(hidden_low, full_up)
    gate_proj = matmul_low(hidden_low, full_gate)
    product, act_back = jax.vjp(swiglu, gate_proj, up_proj)
    prod_low = product.astype(jnp.bfloat16)
    ffn_out = matmul_low(prod_low, full_down)
    hidden_two, ln_two_back = jax.vjp(
        layer_norm, hidden_one + ffn_out, full_gf.astype(jnp.float32), full_bf.astype(jnp.float32)
    )
    seg_marks = (segment_row[:, None] == jnp.arange(SEGS, dtype=jnp.int32)[None, :]).astype(
        jnp.float32
    )
    normed, pool_back = jax.vjp(lambda hidden: pool_embed(hidden, seg_marks), hidden_two)
    embed_low = normed.astype(jnp.bfloat16)
    question_embedding_rows = embed_low[:QSEG]
    passage_embedding_rows = embed_low[QSEG:]
    passage_portion = lax.all_gather(passage_embedding_rows, ("batch", "fsdp"), axis=0, tiled=True)
    row_peak = jnp.full((QSEG,), -1e30, jnp.float32)
    pairwise_match_scores = (
        multiply_by_flipped_second(question_embedding_rows, passage_portion) / softness_scale
    )
    columns = jnp.arange(passage_portion.shape[0], dtype=jnp.int32)
    target_flag = target_row[:, None] == columns[None, :]
    chosen = jnp.sum(jnp.where(target_flag, pairwise_match_scores, 0.0), axis=1)
    new_peak = jnp.maximum(row_peak, jnp.max(pairwise_match_scores, axis=1))
    row_mass = jnp.sum(jnp.exp(pairwise_match_scores - new_peak[:, None]), axis=1)
    row_peak, row_mass, chosen = (new_peak, row_mass, chosen)
    log_partition_sum = row_peak + jnp.log(row_mass)
    query_loss = (log_partition_sum - chosen)[None, :]
    query_f = question_embedding_rows.astype(jnp.float32)
    passage_portion = lax.all_gather(passage_embedding_rows, ("batch", "fsdp"), axis=0, tiled=True)
    pairwise_match_scores = (
        multiply_by_flipped_second(question_embedding_rows, passage_portion) / softness_scale
    )
    columns = jnp.arange(passage_portion.shape[0], dtype=jnp.int32)
    target_flag = (target_row[:, None] == columns[None, :]).astype(jnp.float32)
    current_weight = (
        jnp.exp(pairwise_match_scores - log_partition_sum[:, None]) - target_flag
    ) / softness_scale
    grad_query = jnp.dot(current_weight, passage_portion.astype(jnp.float32), precision=HIGHEST)
    grad_query, grad_table = (grad_query, current_weight)
    grad_doc = lax.psum_scatter(
        lax.dot_general(
            grad_table,
            query_f,
            (((0,), (0,)), ((), ())),
            precision=HIGHEST,
            preferred_element_type=jnp.float32,
        ),
        ("batch", "fsdp"),
        scatter_dimension=0,
        tiled=True,
    )
    (grad_hidden_two,) = pool_back(jnp.concatenate([grad_query, grad_doc], axis=0))
    grad_sum_two, grad_gf, grad_bf = ln_two_back(grad_hidden_two)
    grad_ffn_low = grad_sum_two.astype(jnp.bfloat16)
    back_qkv, back_out, back_up, back_gate, back_down = (
        lax.all_gather(combined_projection_matrix, "fsdp", axis=0, tiled=True),
        lax.all_gather(mixer_projection_matrix, "fsdp", axis=0, tiled=True),
        lax.all_gather(widening_matrix, "fsdp", axis=0, tiled=True),
        lax.all_gather(gating_matrix, "fsdp", axis=0, tiled=True),
        lax.all_gather(narrowing_matrix, "fsdp", axis=0, tiled=True),
    )
    grad_wdown = matmul_t(prod_low, grad_ffn_low)
    grad_product = multiply_by_flipped_second(grad_ffn_low, back_down)
    grad_gate_f, grad_up_f = act_back(grad_product)
    grad_gate_low = grad_gate_f.astype(jnp.bfloat16)
    grad_up_low = grad_up_f.astype(jnp.bfloat16)
    grad_wup = matmul_t(hidden_low, grad_up_low)
    grad_wgate = matmul_t(hidden_low, grad_gate_low)
    grad_hidden_one = (
        grad_sum_two
        + multiply_by_flipped_second(grad_up_low, back_up)
        + multiply_by_flipped_second(grad_gate_low, back_gate)
    )
    grad_sum_one, grad_ga, grad_ba = ln_one_back(grad_hidden_one)
    grad_branch = grad_sum_one.astype(jnp.bfloat16)
    grad_wout = matmul_t(att_low, grad_branch)
    grad_attended = (
        multiply_by_flipped_second(grad_branch, back_out)
        .astype(jnp.bfloat16)
        .reshape(row_len, head_count, head_dim)
    )
    grad_q_rot, grad_k_rot, grad_values = attend_backward(
        queries, keys_all, values, segment_row, log_sums, grad_attended, scale_factor
    )
    grad_joined = jnp.stack(
        [
            rotate_back(grad_q_rot, cosine, sine_tab),
            rotate_back(grad_k_rot, cosine, sine_tab),
            grad_values,
        ],
        axis=1,
    )
    grad_joined = grad_joined.reshape(row_len, 3 * model_width).astype(jnp.bfloat16)
    grad_wqkv = matmul_t(tokens, grad_joined)
    grad_tokens = grad_sum_one + multiply_by_flipped_second(grad_joined, back_qkv)
    part_qkv, part_out, part_up, part_gate, part_down, part_ga, part_ba, part_gf, part_bf = (
        lax.psum_scatter(
            grad_wqkv.astype(jnp.bfloat16), "fsdp", scatter_dimension=0, tiled=True
        ).astype(jnp.float32),
        lax.psum_scatter(
            grad_wout.astype(jnp.bfloat16), "fsdp", scatter_dimension=0, tiled=True
        ).astype(jnp.float32),
        lax.psum_scatter(
            grad_wup.astype(jnp.bfloat16), "fsdp", scatter_dimension=0, tiled=True
        ).astype(jnp.float32),
        lax.psum_scatter(
            grad_wgate.astype(jnp.bfloat16), "fsdp", scatter_dimension=0, tiled=True
        ).astype(jnp.float32),
        lax.psum_scatter(
            grad_wdown.astype(jnp.bfloat16), "fsdp", scatter_dimension=0, tiled=True
        ).astype(jnp.float32),
        lax.psum_scatter(
            grad_ga.astype(jnp.bfloat16), "fsdp", scatter_dimension=0, tiled=True
        ).astype(jnp.float32),
        lax.psum_scatter(
            grad_ba.astype(jnp.bfloat16), "fsdp", scatter_dimension=0, tiled=True
        ).astype(jnp.float32),
        lax.psum_scatter(
            grad_gf.astype(jnp.bfloat16), "fsdp", scatter_dimension=0, tiled=True
        ).astype(jnp.float32),
        lax.psum_scatter(
            grad_bf.astype(jnp.bfloat16), "fsdp", scatter_dimension=0, tiled=True
        ).astype(jnp.float32),
    )
    sum_qkv, sum_out, sum_up, sum_gate, sum_down, sum_ga, sum_ba, sum_gf, sum_bf = lax.psum(
        (part_qkv, part_out, part_up, part_gate, part_down, part_ga, part_ba, part_gf, part_bf),
        "batch",
    )
    return (
        query_loss,
        grad_tokens[None],
        sum_qkv,
        sum_out,
        sum_up,
        sum_gate,
        sum_down,
        sum_ga,
        sum_ba,
        sum_gf,
        sum_bf,
    )


def solution(mesh):
    return jax.shard_map(
        per_device,
        mesh=mesh,
        in_specs=(
            P(("batch", "fsdp"), None, None),
            P(("batch", "fsdp"), None),
            P(("batch", "fsdp"), None),
            P(),
            P("fsdp", None),
            P("fsdp", None),
            P("fsdp", None),
            P("fsdp", None),
            P("fsdp", None),
            P("fsdp"),
            P("fsdp"),
            P("fsdp"),
            P("fsdp"),
        ),
        out_specs=(
            P(("batch", "fsdp"), None),
            P(("batch", "fsdp"), None, None),
            P("fsdp", None),
            P("fsdp", None),
            P("fsdp", None),
            P("fsdp", None),
            P("fsdp", None),
            P("fsdp"),
            P("fsdp"),
            P("fsdp"),
            P("fsdp"),
        ),
        check_vma=False,
    )
```

profile of v0, /device:TPU:0, one launch (start us, length us, event | category | flops | bytes accessed | tf_op | source)
XLA Modules:
  0.0 1269.4 jit_solution(9940979249125146166)
XLA Ops:
  14.6 8.5 all-reduce.11
  29.5 13.7 %all-gather.7.cloned.1.call-done = bf16[768,2304]{1,0:T(8,128)(2,1)} async-done(((bf16[192,2304]{1,0:T(8,128)(2,1)}), bf16[768,2304]{1,0:T(8,128)(2,1)}) %all-gather.7.cloned.1.call-update) | async-done | bytes 3538960 | tf_op jit(solution)/shard_map/all_gather | solution.py:179
  43.2 4.5 copy.71
  47.8 5.5 fusion.45
  59.1 76.6 %while.27 = (s32[]{:T(128)}, bf16[2,512,12,64]{1,3,2,0:T(8,128)(2,1)S(1)}, f32[2,12,512]{2,1,0:T(8,128)S(1)}, s32[2,512]{1,0:T(2,128)S(1)}, s32[1,1024]{1,0:T(1,...) while((s32[]{:T(128)}, ...), condition=%wide.region_6.7_spmd, body=%wide.region_3.6_spmd.sunk | while | flops 1686628352 | bytes 184010896 | solution.py:119
  59.7 12.5 fusion.130
  72.1 13.0 %fusion.131 = f32[12,512]{1,0:T(8,128)S(1)} fusion(f32[12,512,1024]{2,1,0:T(8,128)} %get-tuple-element.462, f32[12,512]{1,0:T(8,128)S(1)} %get-tuple-element.463, pred[512,1024]{1,0:T(8,128)(4,1)S(1)} %broadcast_compare_fusion.4), kind=kLoop, calls=%fused_computation.4.clone.1 | loop fusion | flops 25159680 | bytes 25739264 | tf_op jit(solution)/shard_map/while/body/eval_jaxpr/reduce_sum | solution.py:112
  85.2 3.2 copy-done
  88.4 9.0 bitcast_dynamic-update-slice_fusion.6
  97.8 12.4 fusion.130
  110.2 13.2 %fusion.131 = f32[12,512]{1,0:T(8,128)S(1)} fusion(f32[12,512,1024]{2,1,0:T(8,128)} %get-tuple-element.462, f32[12,512]{1,0:T(8,128)S(1)} %get-tuple-element.463, pred[512,1024]{1,0:T(8,128)(4,1)S(1)} %broadcast_compare_fusion.4), kind=kLoop, calls=%fused_computation.4.clone.1 | loop fusion | flops 25159680 | bytes 25739264 | tf_op jit(solution)/shard_map/while/body/eval_jaxpr/reduce_sum | solution.py:112
  123.3 3.3 copy-done
  126.6 9.0 bitcast_dynamic-update-slice_fusion.6
  137.8 3.9 fusion.75
  143.9 10.8 fusion.79
  154.7 15.0 %multiply_convert_fusion.2 = (bf16[1024,3072]{1,0:T(8,128)(2,1)}, f32[1024,3072]{1,0:T(8,128)}) fusion(f32[1024,3072]{1,0:T(8,128)} %fusion.79, bf16[1024,768]{0,1:T(8,128)(2,1)S(1)} %fusion.41, bf16[768,3072]{1,0:T(8,128)(2,1)} %all-gather.13.cloned.1.call-done), kind=kOutput, calls=%fused_computation.49 | convolution fusion | flops 4850712576 | bytes 37748736 | tf_op jit(solution)/shard_map/dot_general | solution.py:28
  169.7 9.4 all-gather.15.cloned.1.call-done
  179.2 9.4 fusion.76
  189.3 2.1 multiply_reduce_fusion.8
  191.5 41.1 %all-gather = bf16[32,4,768]{2,1,0:T(4,128)(2,1)S(1)} all-gather(bf16[1,4,768]{2,1,0:T(4,128)(2,1)S(1)} %slice_bitcast_fusion.2), channel_id=1, replica_groups=mesh['batch'=8,'fsdp'=4] {'batch','fsdp'}, dimensions={0}, use_global_device_ids=true | all-gather | bytes 202752 | tf_op jit(solution)/shard_map/all_gather | solution.py:225
  235.4 123.3 %all-reduce.15.cloned.1.call-done = f32[128,768]{1,0:T(8,128)} async-done(((f32[128,768]{1,0:T(8,128)}), f32[128,768]{1,0:T(8,128)}) %all-reduce.15.cloned.1.call-update) | async-done | bytes 393232
  359.5 3.7 fusion.78
  363.2 3.6 copy.76
  366.8 4.5 multiply_reduce_fusion.1
  371.5 2.5 fusion.73
  374.0 20.5 %fusion.33 = (bf16[1024,3072]{1,0:T(8,128)(2,1)}, bf16[1024,3072]{1,0:T(8,128)(2,1)}) fusion(f32[1024,3072]{1,0:T(8,128)} %fusion.79, f32[1024,3072]{1,0:T(8,128)} %get-tuple-element.337, bf16[3072,768]{1,0:T(8,128)(2,1)} %all-gather.15.cloned.1.call-done, f32[1024,768]{0,1:T(8,128)} %get-tuple-element.307, f32[1024]{0:T(1024)S(1)} %negate_multiply_fusion.1), kind=kOutput, calls=%fused_computation.47 | convolution fusion | flops 4877451264 | bytes 45617152 | tf_op jit(solution)/shard_map/dot_general | solution.py:38
  394.5 8.7 fusion.80
  403.3 8.9 multiply_reduce_fusion.2
  414.6 2.5 convolution_convert_fusion.5
  417.2 4.5 convolution_convert_fusion.4
  423.4 2.4 reshape_reshape.3
  425.8 2.9 copy.80
  428.7 229.3 %while.28 = (s32[]{:T(128)}, f32[1024,12,64]{0,2,1:T(8,128)}, f32[1024,12,64]{0,2,1:T(8,128)}, f32[2,512,12,64]{1,0,3,2:T(2,128)}, bf16[2,512,12,64]{1,3,2,0:T(8...) while((s32[]{:T(128)}, f32[1024,12,64]{0,2,1:T(8,128)}, ...), condition=%wide.region_24.25_spmd.clone, body=%wide.region_22.24_spmd.clone.sunk | while | flops 4125747200 | bytes 231925968 | solution.py:157
  429.5 11.6 fusion.141
  441.0 13.5 %bitcast_add_fusion.5 = f32[1024,12,64]{0,2,1:T(8,128)} fusion(f32[1024,12,64]{0,2,1:T(8,128)} %get-tuple-element.519, f32[12,512,1024]{2,1,0:T(8,128)} %fusion.141, f32[12,512]{1,0:T(8,128)S(1)} %dynamic-slice_bitcast_fusion.2, pred[512,1024]{1,0:T(8,128)(4,1)S(1)} %broadcast_compare_fusion.5, pred[]{:T(512)S(6)} %compare.3, ...), kind=kOutput, calls=%fused_computation.22.clone.1 | convolution fusion | flops 832045056 | bytes 32800772 | tf_op jit(solution)/shard_map/while/body/eval_jaxpr/hqk,qhd->khd/dot_general | solution.py:148
  454.5 18.0 %multiply_reduce_fusion.10 = (f32[12,512]{1,0:T(8,128)S(1)}, f32[12,512,1024]{2,1,0:T(8,128)}) fusion(f32[12,512,1024]{2,1,0:T(8,128)} %fusion.141, f32[12,512]{1,0:T(8,128)S(1)} %dynamic-slice_bitcast_fusion.2, pred[512,1024]{1,0:T(8,128)(4,1)S(1)} %broadcast_compare_fusion.5, bf16[1024,12,64]{0,2,1:T(8,128)(2,1)} %get-tuple-element.540, ...), kind=kOutput, calls=%fused_computation.17.clone.1 | convolution fusion | flops 836757504 | bytes 53264388 | tf_op jit(solution)/shard_map/while/body/eval_jaxpr/qhd,khd->hqk/dot_general | solution.py:136
  472.6 21.2 %multiply_convert_fusion.5 = bf16[12,512,1024]{2,1,0:T(8,128)(2,1)} fusion(f32[12,512,1024]{2,1,0:T(8,128)} %get-tuple-element.475, f32[12,512,1024]{2,1,0:T(8,128)} %fusion.141, f32[12,512]{1,0:T(8,128)S(1)} %get-tuple-element.476, f32[12,512]{1,0:T(8,128)S(1)} %dynamic-slice_bitcast_fusion.2, pred[512,1024]{1,0:T(8,128)(4,1)S(1)} %broadcast_compare_fusion.5), kind=kLoop, calls=%fused_computation.16.clone.1 | loop fusion | flops 37748736 | bytes 63488000 | tf_op jit(solution)/shard_map/while/body/eval_jaxpr/convert_element_type | solution.py:138
  493.8 9.6 multiply_bitcast_fusion.2
  503.4 8.9 bitcast_add_fusion.4
  513.9 28.7 %dynamic_update_slice.19 = f32[2,512,12,64]{1,0,3,2:T(2,128)} dynamic-update-slice(f32[2,512,12,64]{1,0,3,2:T(2,128)} %get-tuple-element.520, f32[1,512,12,64]{1,0,3,2:T(1,128)S(1)} %copy.120, s32[]{:T(128)S(6)} %copy.143, s32[]{:T(128)} %constant.70.clone.1..sunk, s32[]{:T(128)} %constant.70.clone.1..sunk, s32[]{:T(128)} %constant.70.clone.1..sunk) | dynamic-update-slice | bytes 3145732 | tf_op jit(solution)/shard_map/while/body/jit(dynamic_update_index_in_dim)/dynamic_update_slice | solution.py:119
  543.0 11.5 fusion.141
  554.4 14.4 %bitcast_add_fusion.5 = f32[1024,12,64]{0,2,1:T(8,128)} fusion(f32[1024,12,64]{0,2,1:T(8,128)} %get-tuple-element.519, f32[12,512,1024]{2,1,0:T(8,128)} %fusion.141, f32[12,512]{1,0:T(8,128)S(1)} %dynamic-slice_bitcast_fusion.2, pred[512,1024]{1,0:T(8,128)(4,1)S(1)} %broadcast_compare_fusion.5, pred[]{:T(512)S(6)} %compare.3, ...), kind=kOutput, calls=%fused_computation.22.clone.1 | convolution fusion | flops 832045056 | bytes 32800772 | tf_op jit(solution)/shard_map/while/body/eval_jaxpr/hqk,qhd->khd/dot_general | solution.py:148
  568.8 18.0 %multiply_reduce_fusion.10 = (f32[12,512]{1,0:T(8,128)S(1)}, f32[12,512,1024]{2,1,0:T(8,128)}) fusion(f32[12,512,1024]{2,1,0:T(8,128)} %fusion.141, f32[12,512]{1,0:T(8,128)S(1)} %dynamic-slice_bitcast_fusion.2, pred[512,1024]{1,0:T(8,128)(4,1)S(1)} %broadcast_compare_fusion.5, bf16[1024,12,64]{0,2,1:T(8,128)(2,1)} %get-tuple-element.540, ...), kind=kOutput, calls=%fused_computation.17.clone.1 | convolution fusion | flops 836757504 | bytes 53264388 | tf_op jit(solution)/shard_map/while/body/eval_jaxpr/qhd,khd->hqk/dot_general | solution.py:136
  586.9 21.2 %multiply_convert_fusion.5 = bf16[12,512,1024]{2,1,0:T(8,128)(2,1)} fusion(f32[12,512,1024]{2,1,0:T(8,128)} %get-tuple-element.475, f32[12,512,1024]{2,1,0:T(8,128)} %fusion.141, f32[12,512]{1,0:T(8,128)S(1)} %get-tuple-element.476, f32[12,512]{1,0:T(8,128)S(1)} %dynamic-slice_bitcast_fusion.2, pred[512,1024]{1,0:T(8,128)(4,1)S(1)} %broadcast_compare_fusion.5), kind=kLoop, calls=%fused_computation.16.clone.1 | loop fusion | flops 37748736 | bytes 63488000 | tf_op jit(solution)/shard_map/while/body/eval_jaxpr/convert_element_type | solution.py:138
  608.1 9.6 multiply_bitcast_fusion.2
  617.7 9.8 bitcast_add_fusion.4
  629.1 28.7 %dynamic_update_slice.19 = f32[2,512,12,64]{1,0,3,2:T(2,128)} dynamic-update-slice(f32[2,512,12,64]{1,0,3,2:T(2,128)} %get-tuple-element.520, f32[1,512,12,64]{1,0,3,2:T(1,128)S(1)} %copy.120, s32[]{:T(128)S(6)} %copy.143, s32[]{:T(128)} %constant.70.clone.1..sunk, s32[]{:T(128)} %constant.70.clone.1..sunk, s32[]{:T(128)} %constant.70.clone.1..sunk) | dynamic-update-slice | bytes 3145732 | tf_op jit(solution)/shard_map/while/body/jit(dynamic_update_index_in_dim)/dynamic_update_slice | solution.py:119
  658.0 5.8 reshape.343
  663.7 2.9 multiply_add_fusion.2
  667.0 2.3 maximum_convert_fusion
  669.3 2.2 copy-done.11
  671.6 4.0 fusion.35
  675.6 4.0 copy.93
  681.0 9.4 convolution_convert_fusion.2
  690.5 9.5 convolution_convert_fusion.1
  700.0 1.8 copy-done.14
  701.9 10.1 convolution_convert_fusion
  713.9 8.1 add_bitcast_fusion
  722.1 3.5 copy.84
  725.6 5.9 all-reduce.10
  733.3 36.6 %reduce-scatter.10.cloned.1.call-done = bf16[192,3072]{1,0:T(8,128)(2,1)} async-done(((bf16[768,3072]{1,0:T(8,128)(2,1)}), bf16[192,3072]{1,0:T(8,128)(2,1)}) %reduce-scatter.10.cloned.1.call-update) | async-done | bytes 1179664 | tf_op jit(solution)/shard_map/reduce_scatter | solution.py:313
  769.9 50.2 %reduce-scatter.12.cloned.1.call-done = bf16[192,3072]{1,0:T(8,128)(2,1)} async-done(((bf16[768,3072]{1,0:T(8,128)(2,1)}), bf16[192,3072]{1,0:T(8,128)(2,1)}) %reduce-scatter.12.cloned.1.call-update) | async-done | bytes 1179664 | tf_op jit(solution)/shard_map/reduce_scatter | solution.py:316
  820.1 50.6 %reduce-scatter.14.cloned.1.call-done = bf16[768,768]{1,0:T(8,128)(2,1)} async-done(((bf16[3072,768]{1,0:T(8,128)(2,1)}), bf16[768,768]{1,0:T(8,128)(2,1)}) %reduce-scatter.14.cloned.1.call-update) | async-done | bytes 1179664 | tf_op jit(solution)/shard_map/reduce_scatter | solution.py:319
  870.7 390.1 %all-reduce.16 = (f32[192,2304]{0,1:T(8,128)S(1)}, f32[192,768]{1,0:T(8,128)}, f32[192,3072]{1,0:T(8,128)}, f32[192,3072]{1,0:T(8,128)}, f32[768,768]{1,0:T(8,12...) all-reduce(bf16[192,2304]{0,1:T(8,128)(2,1)S(1)} %copy.94, ...), channel_id=1, replica_groups=mesh['batch'=8,'fsdp'=4] {'batch'}, use_global_device_ids=true, to_apply=%region_26.27 | all-reduce | flops 2360064 | bytes 14161920 | tf_op jit(solution)/shard_map/psum | solution.py:335
  (208 shorter events, 42.6 us)
Async XLA Ops:
  7.2 5.2 copy-start.39
  7.2 3.5 copy-start.25
  7.2 6.4 copy-start.43
  7.2 6.6 copy-start.44
  7.2 6.9 copy-start.45
  7.2 7.1 copy-start.46
  7.2 19.4 %copy-start.16 = (bf16[1,1024,768]{2,1,0:T(8,128)(2,1)S(1)}, bf16[1,1024,768]{2,1,0:T(8,128)(2,1)}, u32[]{:S(2)}) copy-start(bf16[1,1024,768]{2,1,0:T(8,128)(2,1)} %param.17) | copy-start | bytes 4718596
  7.3 36.0 %all-gather.7.cloned.1.call-start = ((), (), s32[]{:S(2)}) async-start(), calls=%async_computation.5 | async-start | bytes 4423680 | tf_op jit(solution)/shard_map/all_gather | solution.py:179
  8.0 129.8 %all-gather.9.cloned.1.call-start = ((), (), s32[]{:S(2)}) async-start(), calls=%async_computation.6 | async-start | bytes 1474560 | tf_op jit(solution)/shard_map/all_gather | solution.py:180
  8.7 135.2 %all-gather.11.cloned.1.call-start = ((), (), s32[]{:S(2)}) async-start(), calls=%async_computation.7 | async-start | bytes 5898240 | tf_op jit(solution)/shard_map/all_gather | solution.py:182
  9.5 145.3 %all-gather.13.cloned.1.call-start = ((), (), s32[]{:S(2)}) async-start(), calls=%async_computation.8 | async-start | bytes 5898240 | tf_op jit(solution)/shard_map/all_gather | solution.py:181
  10.0 169.1 %all-gather.15.cloned.1.call-start = ((), (), s32[]{:S(2)}) async-start(), calls=%async_computation.9 | async-start | bytes 5898240 | tf_op jit(solution)/shard_map/all_gather | solution.py:183
  10.6 348.0 %all-reduce.15.cloned.1.call-start = ((), (), s32[]{:S(2)}) async-start(), calls=%async_computation.15 | async-start | bytes 786432
  54.7 1.1 copy-start.21
  54.7 1.1 copy-start.23
  57.0 2.1 copy-start.20
  57.0 2.1 copy-start.26
  72.1 16.3 %copy-start = (f32[12,512,1024]{2,1,0:T(8,128)S(1)}, f32[12,512,1024]{2,1,0:T(8,128)}, u32[]{:S(2)}) copy-start(f32[12,512,1024]{2,1,0:T(8,128)} %get-tuple-element.462) | copy-start | bytes 75497472 | tf_op jit(solution)/shard_map/while
  110.2 16.4 %copy-start = (f32[12,512,1024]{2,1,0:T(8,128)S(1)}, f32[12,512,1024]{2,1,0:T(8,128)}, u32[]{:S(2)}) copy-start(f32[12,512,1024]{2,1,0:T(8,128)} %get-tuple-element.462) | copy-start | bytes 75497472 | tf_op jit(solution)/shard_map/while
  137.7 4.0 copy-start.18
  141.7 1.7 copy-start.5
  141.7 1.7 copy-start.28
  141.7 1.6 copy-start.29
  143.9 10.9 copy-start.9
  188.5 2.8 copy-start.3
  188.5 0.7 copy-start.27
  188.6 0.7 copy-start.30
  188.6 0.7 copy-start.33
  188.6 44.3 %copy-start.38 = (s32[1,4]{1,0:T(1,128)S(1)}, s32[1,4]{1,0:T(1,128)}, u32[]{:S(2)}) copy-start(s32[1,4]{1,0:T(1,128)} %param.19) | copy-start | bytes 52
  234.9 496.8 %reduce-scatter.8.cloned.1.call-start = ((), (), s32[]{:S(2)}) async-start(), calls=%async_computation.10 | async-start | bytes 1474560 | tf_op jit(solution)/shard_map/reduce_scatter | solution.py:310
  366.8 4.5 copy-start.4
  366.8 4.7 copy-start.7
  374.0 29.3 %copy-start.34 = (f32[1024]{0:T(1024)}, f32[1024]{0:T(1024)S(1)}, u32[]{:S(2)}) copy-start(f32[1024]{0:T(1024)S(1)} %negate_multiply_fusion.1) | copy-start | bytes 12292
  394.5 8.8 copy-start.6
  394.5 8.8 copy-start.13
  394.5 8.8 copy-start.47
  412.2 2.5 copy-start.19
  413.0 1.7 copy-start.15
  413.0 4.2 copy-start.36
  414.6 2.6 copy-start.42
  417.1 314.6 %reduce-scatter.16.cloned.1.call-start = ((), (), s32[]{:S(2)}) async-start(), calls=%async_computation.14 | async-start | bytes 4423680
  429.5 11.6 copy-start.8
  503.4 8.9 copy-start.2
  543.0 11.5 copy-start.8
  617.7 9.8 copy-start.2
  657.9 5.8 copy-start.1
  657.9 5.8 copy-start.22
  658.0 5.8 copy-start.24
  667.0 4.5 copy-start.17
  669.3 2.2 copy-start.11
  679.6 1.4 copy-start.10
  679.6 90.3 %reduce-scatter.10.cloned.1.call-start = ((), (), s32[]{:S(2)}) async-start(), calls=%async_computation.11 | async-start | bytes 5898240 | tf_op jit(solution)/shard_map/reduce_scatter | solution.py:313
  690.4 129.7 %reduce-scatter.12.cloned.1.call-start = ((), (), s32[]{:S(2)}) async-start(), calls=%async_computation.12 | async-start | bytes 5898240 | tf_op jit(solution)/shard_map/reduce_scatter | solution.py:316
  700.0 1.9 copy-start.14
  700.0 1.9 copy-start.35
  700.0 170.8 %reduce-scatter.14.cloned.1.call-start = ((), (), s32[]{:S(2)}) async-start(), calls=%async_computation.13 | async-start | bytes 5898240 | tf_op jit(solution)/shard_map/reduce_scatter | solution.py:319
  711.9 2.0 copy-start.12
  711.9 2.0 copy-start.37
  722.0 3.6 copy-start.31
  722.0 3.6 copy-start.32
  722.1 3.6 copy-start.40
  722.1 3.6 copy-start.41
Sparse Core Ops, SparseCore 0:
  9.6 33.5 all-gather.6
  44.8 17.4 all-gather.8
  63.9 37.4 all-gather.10
  102.8 37.4 all-gather.12
  141.7 37.4 all-gather.14
  235.0 123.5 all-reduce.14
  417.3 24.6 reduce-scatter.7
  679.7 39.5 reduce-scatter.15
  722.0 47.8 reduce-scatter.9
  772.3 47.8 reduce-scatter.11
  822.8 47.8 reduce-scatter.13
where the time goes:
time: 1280 us; the launch traced here: 1270 us
  blocking collectives  446 us (35%)
  matrix products  306 us (24%)
  waiting for transfers between devices  287 us (22%)
  local copies, waits for them, and re-layouts  120 us (9%)
  other arithmetic  92.4 us (7%)
  between operations  16.9 us (1%)
    psum x1, blocking collectives, per_device(): lax.psum((part_qkv, part_out, part_up, part_gate, part_down, part_ga, par...  390 us
    unnamed x13, waiting for transfers between devices  126 us
    dynamic_update_slice x4, local copies, waits for them, and re-layouts, attend_forward(): out_blocks, log_sums = lax.map(one_block, (q_blocks, s_blocks))  60.6 us
    dot_general x6, matrix products, multiply_by_flipped_second(): lax.dot_general(left_op, right_op, (((1,), (1,)), ((), ())), preferred_el...  51.1 us
    reduce_scatter x1, waiting for transfers between devices, per_device(): lax.psum_scatter(grad_wdown.astype(jnp.bfloat16), 'fsdp', scatter_dimensi...  50.6 us
    reduce_scatter x1, waiting for transfers between devices, per_device(): lax.psum_scatter(grad_wgate.astype(jnp.bfloat16), 'fsdp', scatter_dimensi...  50.2 us
    dot_general x4, matrix products, block_scores(): jnp.einsum('qhd,khd->hqk', q_block, keys_all, preferred_element_type=jnp....  47.8 us
    dot_general x5, matrix products, matmul_low(): return jnp.dot(left_op, right_op, preferred_element_type=jnp.float32)  44.6 us
  transfers between devices with their start and end apart: 11, of which 6 were waited for; matrix products, arithmetic and copies ran while one was open for 34% of the time, Pallas kernels for 0%

commit v1 on v0

v1 whole, which is shorter than its diff:
```python
import functools
import math

import jax
import jax.numpy as jnp
from jax import lax
from jax.experimental import pallas as pl
from jax.experimental.pallas import tpu as pltpu
from jax.sharding import PartitionSpec as P

HEADS = 12
HD = 64
QSEG = 4
SEGS = 8
EPSILON = 1e-06
NEG = -1e30
LANE = 128
BLOCK = 256
PAIRS = HEADS // 2
PART = 384
SMALL = 16
MIB = 2**20

bf16 = jnp.bfloat16
f32 = jnp.float32


def dot(left, right, left_dim, right_dim):
    return lax.dot_general(
        left, right, (((left_dim,), (right_dim,)), ((), ())), preferred_element_type=f32
    )


def split_three(value):
    high = value.astype(bf16)
    rest = value - high.astype(f32)
    middle = rest.astype(bf16)
    low = (rest - middle.astype(f32)).astype(bf16)
    return high, middle, low


def params(limit=60):
    return dict(
        compiler_params=pltpu.CompilerParams(vmem_limit_bytes=limit * MIB),
        cost_estimate=pl.CostEstimate(flops=1, bytes_accessed=1, transcendentals=0),
    )


def shape(dims, dtype):
    return jax.ShapeDtypeStruct(dims, dtype)


ANY = pl.BlockSpec(memory_space=pl.ANY)


def whole(dims):
    return pl.BlockSpec(dims, lambda *_: (0,) * len(dims))


def swap_halves(tile):
    lane = lax.broadcasted_iota(jnp.int32, (1, LANE), 1)
    in_first = (lane & 63) < 32
    return jnp.where(in_first, pltpu.roll(tile, 96, 1), pltpu.roll(tile, 32, 1))


def norm_parts(value):
    center = value - jnp.mean(value, axis=1, keepdims=True)
    spread = jnp.mean(center * center, axis=1, keepdims=True)
    inv = lax.rsqrt(spread + EPSILON)
    return center * inv, inv


def norm_back(scaled, xhat, inv):
    mean_one = jnp.mean(scaled, axis=1, keepdims=True)
    mean_two = jnp.mean(scaled * xhat, axis=1, keepdims=True)
    return inv * (scaled - mean_one - xhat * mean_two)


def piece_copies(row_of, pieces, scratch, sems):
    return [
        pltpu.make_async_copy(
            piece, scratch.at[pl.ds(pl.multiple_of(row_of(k), 32), piece.shape[0])], sems.at[k]
        )
        for k, piece in enumerate(pieces)
    ]


def store_turned(ref, value, own, columns=slice(None)):
    rows = ref.shape[0] // 4
    turned = value.T
    for shard in range(4):
        at = pl.ds(pl.multiple_of((shard ^ own) * rows, 64), rows)
        ref[at, columns] = turned[shard * rows : (shard + 1) * rows]


def qkv_kernel(rows_ref, x_ref, cos_ref, sin_ref, *refs):
    pieces = refs[:4]
    out_ref, xt_ref, weight, sems = refs[4:]
    step = pl.program_id(0)
    width = x_ref.shape[1]

    @pl.when(step == 0)
    def _():
        copies = piece_copies(lambda k: rows_ref[k], pieces, weight, sems)
        for copy in copies:
            copy.start()
        store_turned(xt_ref, x_ref[...], rows_ref[6])
        for copy in copies:
            copy.wait()

    joined = dot(x_ref[...], weight[:, pl.ds(pl.multiple_of(step * width, LANE), width)], 1, 0)

    @pl.when(step < 2)
    def _():
        scale = jnp.where(step == 0, 1.0 / math.sqrt(HD), 1.0)
        cos, sin = cos_ref[...] * scale, sin_ref[...] * scale
        for t in range(width // LANE):
            tile = joined[:, t * LANE : (t + 1) * LANE]
            out_ref[:, t * LANE : (t + 1) * LANE] = (tile * cos + swap_halves(tile) * sin).astype(bf16)

    @pl.when(step == 2)
    def _():
        out_ref[...] = joined.astype(bf16)


def key_range(first, count, total):
    blocks = (count + 1) >> 1
    first = jnp.minimum(first, total // LANE - 2 * blocks)
    return pl.multiple_of(first * LANE, LANE), blocks


def attend_kernel(lo_ref, n_ref, q_ref, k_ref, v_ref, mq_ref, mk_ref, o_ref, lse_ref):
    step = pl.program_id(0)
    lo, count = key_range(lo_ref[step], n_ref[step], k_ref.shape[0])
    first = lax.broadcasted_iota(jnp.int32, (1, LANE), 1) < HD
    zero = jnp.zeros((), bf16)
    mask_q = mq_ref[...]

    def run(width):
        keys = pl.ds(lo, width)
        mask_k = mk_ref[keys, :]

        def pair(p, _):
            cols = pl.ds(pl.multiple_of(p * LANE, LANE), LANE)
            q_pair, k_pair, v_pair = q_ref[:, cols], k_ref[keys, cols], v_ref[keys, cols]
            k_ext = jnp.concatenate([k_pair, mask_k], axis=1)
            outs, sums = [], []
            for h in range(2):
                q_one = jnp.where(first if h == 0 else ~first, q_pair, zero)
                scores = dot(jnp.concatenate([q_one, mask_q], axis=1), k_ext, 1, 1)
                peak = jnp.max(scores, axis=1, keepdims=True)
                weight = jnp.exp(scores - peak)
                total = jnp.sum(weight, axis=1, keepdims=True)
                outs.append(dot(weight.astype(bf16), v_pair, 1, 0) * (1.0 / total))
                sums.append(peak + jnp.log(total))
            o_ref[:, cols] = jnp.where(first, outs[0], outs[1]).astype(bf16)
            turned = jnp.where(first, sums[0], sums[1]).T
            lse_ref[p, 0:1, :] = turned[0:1]
            lse_ref[p, 1:2, :] = turned[HD : HD + 1]
            return 0

        lax.fori_loop(0, PAIRS // 2, pair, 0, unroll=True)

    for n in range(1, k_ref.shape[0] // BLOCK + 1):
        pl.when(count == n)(functools.partial(run, n * BLOCK))


def attend_back_kernel(
    lo_ref, n_ref, q_ref, k_ref, v_ref, do_ref, lse_ref, dl_ref, mq_ref, mk_ref, cos_ref, sin_ref, cosb_ref, sinb_ref,
    gq_ref, gk_ref, gv_ref, dq_acc,
):
    step = pl.program_id(0)

    @pl.when(step == 0)
    def _():
        dq_acc[...] = jnp.zeros_like(dq_acc)

    lo, count = key_range(lo_ref[step], n_ref[step], q_ref.shape[0])
    first = lax.broadcasted_iota(jnp.int32, (1, LANE), 1) < HD
    zero = jnp.zeros((), bf16)
    mask_k = mk_ref[...]
    cosb, sinb = cosb_ref[...], sinb_ref[...]

    def run(width):
        queries = pl.ds(lo, width)
        mask_q = mq_ref[queries, :]

        def pair(p, _):
            cols = pl.ds(pl.multiple_of(p * LANE, LANE), LANE)
            k_pair, v_pair = k_ref[:, cols], v_ref[:, cols]
            q_pair, do_pair = q_ref[queries, cols], do_ref[queries, cols]
            q_ext = jnp.concatenate([q_pair, mask_q], axis=1)
            k_turned = k_pair.T
            dk, dv = [], []
            for h in range(2):
                mine = first if h == 0 else ~first
                k_one, v_one = jnp.where(mine, k_pair, zero), jnp.where(mine, v_pair, zero)
                scores = dot(jnp.concatenate([k_one, mask_k], axis=1), q_ext, 1, 1)
                probs = jnp.exp(scores - lse_ref[p, h : h + 1, queries])
                dprobs = dot(v_one, do_pair, 1, 1)
                dscores = (probs * (dprobs - dl_ref[p, h : h + 1, queries])).astype(bf16)
                dv.append(dot(probs.astype(bf16), do_pair, 1, 0))
                dk.append(dot(dscores, q_pair, 1, 0))
                rows = pl.ds(pl.multiple_of(p * LANE + h * HD, HD), HD)
                dq_acc[rows, queries] += dot(k_turned[h * HD : (h + 1) * HD], dscores, 1, 0)
            gv_ref[:, cols] = jnp.where(first, dv[0], dv[1]).astype(bf16)
            grad = jnp.where(first, dk[0], dk[1])
            gk_ref[:, cols] = (grad * cosb - swap_halves(grad) * sinb).astype(bf16)
            return 0

        lax.fori_loop(0, PAIRS // 2, pair, 0, unroll=True)

    for n in range(1, q_ref.shape[0] // BLOCK + 1):
        pl.when(count == n)(functools.partial(run, n * BLOCK))

    @pl.when(step == pl.num_programs(0) - 1)
    def _():
        cos, sin = cos_ref[...], sin_ref[...]
        for p in range(PAIRS // 2):
            grad = dq_acc[p * LANE : (p + 1) * LANE, :].T * (1.0 / math.sqrt(HD))
            gq_ref[:, p * LANE : (p + 1) * LANE] = (grad * cos - swap_halves(grad) * sin).astype(bf16)


def mixer_kernel(rows_ref, att0_ref, att1_ref, x_ref, vec_ref, *refs):
    pieces = refs[:6]
    xhat_ref, inv_ref, low_ref, lowt_ref, full_ref, weight, sems, out_sem = refs[7:]
    step = pl.program_id(0)
    out_copy = pltpu.make_async_copy(weight, full_ref, out_sem)

    @pl.when(step == 0)
    def _():
        copies = piece_copies(lambda k: rows_ref[k], pieces, weight, sems)
        for copy in copies:
            copy.start()
        for copy in copies:
            copy.wait()
        out_copy.start()

    branch = dot(att0_ref[...], weight[0:PART, :], 1, 0) + dot(att1_ref[...], weight[PART:, :], 1, 0)
    xhat, inv = norm_parts(x_ref[...].astype(f32) + branch)
    low = (xhat * vec_ref[0:1] + vec_ref[1:2]).astype(bf16)
    xhat_ref[...] = xhat
    inv_ref[...] = jnp.broadcast_to(inv, inv_ref.shape)
    low_ref[...] = low
    store_turned(lowt_ref, low, rows_ref[6])

    @pl.when(step == pl.num_programs(0) - 1)
    def _():
        out_copy.wait()


def ffn_kernel(rows_ref, low_ref, xhat_ref, vec_ref, mark_ref, cnt_ref, *refs):
    up_pieces, gate_pieces, down_pieces = refs[0:6], refs[6:12], refs[12:18]
    up_fac_ref, gate_fac_ref, prod_ref, xhat2_ref, inv2_ref, pool_ref, emb_ref = refs[18:25]
    full_up, full_gate, full_down = refs[25:28]
    w_up, w_gate, w_down, sems, down_sems, out_sems, pooled, total = refs[28:]
    step = pl.program_id(0)
    own = rows_ref[6]
    tokens, width = low_ref.shape
    wide = prod_ref.shape[1]
    steps = 4

    def in_copies(rel):
        cols = pl.ds(pl.multiple_of((own ^ rel) * wide, LANE), wide)
        copies = []
        for which, (pieces, scratch) in enumerate(((up_pieces, w_up), (gate_pieces, w_gate))):
            for k, piece in enumerate(pieces):
                rows = pl.ds(pl.multiple_of(rows_ref[k], 32), piece.shape[0])
                copies.append(
                    pltpu.make_async_copy(piece.at[:, cols], scratch.at[rel, rows], sems.at[rel * 12 + which * 6 + k])
                )
        for k in ((0,), (1,), (2, 3), (4, 5))[rel]:
            piece = down_pieces[k]
            start = 0 if k < 2 else pl.multiple_of(rows_ref[7 + (k & 1)], 32)
            copies.append(
                pltpu.make_async_copy(piece, w_down.at[rel, pl.ds(start, piece.shape[0])], down_sems.at[k])
            )
        return copies

    def out_copies(rel):
        cols = pl.ds(pl.multiple_of((own ^ rel) * wide, LANE), wide)
        return [
            pltpu.make_async_copy(w_up.at[rel], full_up.at[:, cols], out_sems.at[rel * 3]),
            pltpu.make_async_copy(w_gate.at[rel], full_gate.at[:, cols], out_sems.at[rel * 3 + 1]),
            pltpu.make_async_copy(w_down.at[rel], full_down.at[cols], out_sems.at[rel * 3 + 2]),
        ]

    @pl.when(step == 0)
    def _():
        for rel in range(2):
            for copy in in_copies(rel):
                copy.start()
        pooled[...] = jnp.zeros_like(pooled)

    for rel in range(steps):

        @pl.when(step == rel)
        def _(rel=rel):
            for copy in in_copies(rel):
                copy.wait()
            for copy in out_copies(rel):
                copy.start()
            if 0 < rel < steps - 1:
                for copy in in_copies(rel + 1):
                    copy.start()

    rows_at = 512

    def rows_block(i, _):
        rows = pl.ds(pl.multiple_of(i * rows_at, rows_at), rows_at)
        low = low_ref[rows, :]
        up = dot(low, w_up[step], 1, 0)
        gate = dot(low, w_gate[step], 1, 0)
        sig = 0.5 * jnp.tanh(0.5 * gate) + 0.5
        act = gate * sig
        up_fac_ref[rows, :] = act.astype(bf16)
        gate_fac_ref[rows, :] = (up * (sig + act * (1.0 - sig))).astype(bf16)
        prod = (act * up).astype(bf16)
        prod_ref[rows, :] = prod
        ffn = dot(prod, w_down[step], 1, 0)

        total[rows, :] = jnp.where(step == 0, ffn, total[rows, :] + ffn)
        return 0

    lax.fori_loop(0, tokens // rows_at, rows_block, 0, unroll=True)

    @pl.when(step == steps - 1)
    def _():
        def norm_block(i, _):
            rows = pl.ds(pl.multiple_of(i * BLOCK, BLOCK), BLOCK)
            xhat, inv = norm_parts(xhat_ref[rows, :] * vec_ref[0:1] + vec_ref[1:2] + total[rows, :])
            xhat2_ref[rows, :] = xhat
            inv2_ref[rows, :] = jnp.broadcast_to(inv, (BLOCK, LANE))
            marks = mark_ref[:, rows]
            part = jnp.zeros(pooled.shape, f32)
            for piece in split_three(xhat):
                part += dot(marks, piece, 1, 0)
            pooled[...] += part
            return 0

        lax.fori_loop(0, tokens // BLOCK, norm_block, 0)
        mean_xhat = pooled[0:SEGS] / cnt_ref[:, 0:1]
        pool = mean_xhat * vec_ref[2:3] + vec_ref[3:4]
        inv_len = lax.rsqrt(jnp.sum(pool * pool, axis=1, keepdims=True) + EPSILON)
        pool_ref[0:SEGS] = mean_xhat
        pool_ref[SEGS:] = pool
        emb_ref[...] = (pool * inv_len).astype(bf16)
        for rel in range(steps):
            for copy in out_copies(rel):
                copy.wait()


def loss_kernel(soft_ref, blk_ref, all_ref, ids_ref, pool_ref, cnt_ref, loss_ref, rows_ref, small_ref, acc):
    step = pl.program_id(0)
    soft = soft_ref[0]
    width = acc.shape[1]
    block, everyone = blk_ref[:, 0:width], all_ref[:, 0:width]
    target = blk_ref[:, width : width + LANE].astype(f32)
    target = target[:, 0:1] * 32.0 + target[:, 1:2]
    row = lax.broadcasted_iota(jnp.int32, (block.shape[0], 1), 0)
    asks = (row & (SEGS - 1)) < QSEG
    ids = ids_ref[0:1, :]
    logits = jnp.where(ids >= 0, dot(block, everyone, 1, 1) / soft, NEG)
    hit = asks & (target == ids)
    peak = jnp.max(logits, axis=1, keepdims=True)
    lse = peak + jnp.log(jnp.sum(jnp.exp(logits - peak), axis=1, keepdims=True))
    grad = (jnp.exp(logits - lse) - jnp.where(hit, 1.0, 0.0)) / soft
    grad = jnp.where(asks, grad, 0.0)
    turned = grad[:, 0:LANE].T[0:SEGS]
    part = jnp.zeros(acc.shape, f32)
    for piece in split_three(turned):
        part += dot(piece, block, 1, 0)

    @pl.when(step == 0)
    def _():
        own = part
        for piece in split_three(grad[0:SEGS]):
            own += dot(piece, everyone, 1, 0)
        acc[...] = own
        chosen = jnp.sum(jnp.where(hit, logits, 0.0), axis=1, keepdims=True)
        loss_ref[...] = jnp.broadcast_to((lse - chosen)[0:SEGS], loss_ref.shape)

    @pl.when(step > 0)
    def _():
        acc[...] += part

    @pl.when(step == pl.num_programs(0) - 1)
    def _():
        g = acc[...]
        mean_xhat, pool = pool_ref[0:SEGS], pool_ref[SEGS:]
        inv_len = lax.rsqrt(jnp.sum(pool * pool, axis=1, keepdims=True) + EPSILON)
        back = inv_len * g - inv_len * inv_len * inv_len * pool * jnp.sum(pool * g, axis=1, keepdims=True)
        rows_ref[...] = jnp.zeros_like(rows_ref)
        rows_ref[0:SEGS] = back / cnt_ref[:, 0:1]
        small_ref[...] = jnp.zeros_like(small_ref)
        small_ref[0:1] = jnp.sum(back * mean_xhat, axis=0, keepdims=True)
        small_ref[1:2] = jnp.sum(back, axis=0, keepdims=True)


def norm_two_back_kernel(mq_ref, rows_ref, xhat_ref, inv_ref, vec_ref, sum_ref, low_ref, lowt_ref):
    marks = mq_ref[...]
    scaled = jnp.zeros(xhat_ref.shape, f32)
    for piece in split_three(rows_ref[...] * vec_ref[2:3]):
        scaled += dot(marks, piece, 1, 0)
    grad = norm_back(scaled, xhat_ref[...], inv_ref[:, 0:1])
    sum_ref[...] = grad
    low = grad.astype(bf16)
    low_ref[...] = low
    lowt_ref[...] = low.T


def ffn_back_kernel(
    g, groups, info_ref, prod_any, up_fac_any, gate_fac_any, low_any, lowt_any, hidt_any, wu_any, wg_any, wd_any, hid_any,
    *refs,
):
    out_any, keep_any, send_any = refs[-18:-15]
    prod, up_fac, gate_fac, low, lowt, hidt, wu, wg, wd, hid, keep, send, total, sems, out_sems = refs[-15:]
    own = info_ref[4]
    rows = keep.shape[3]
    targets = [(keep, 0), (send, 0), (keep, 1), (send, 1)]

    def strip(index):
        if isinstance(index, int):
            return pl.ds((index * groups + g) * BLOCK, BLOCK)
        return pl.ds(pl.multiple_of((index * groups + g) * BLOCK, BLOCK), BLOCK)

    def blocks(source, to, first, relative=False, by_rows=False):
        copies = []
        for k in range(4):
            here, there = strip(info_ref[k] if relative else k), pl.ds(k * BLOCK, BLOCK)
            if by_rows:
                copy = pltpu.make_async_copy(source.at[here], to.at[there], sems.at[first + k])
            else:
                copy = pltpu.make_async_copy(source.at[:, here], to.at[:, there], sems.at[first + k])
            copies.append(copy)
        return copies

    def one(source, to, first):
        return [pltpu.make_async_copy(source, to, sems.at[first])]

    loads = dict(
        low=one(low_any, low, 0),
        wd=blocks(wd_any, wd, 4, by_rows=True),
        up_fac=blocks(up_fac_any, up_fac, 8),
        hidt=one(hidt_any, hidt, 1),
        gate_fac=blocks(gate_fac_any, gate_fac, 12),
        lowt=one(lowt_any, lowt, 2),
        prod=blocks(prod_any, prod, 16, relative=True),
        wu=blocks(wu_any, wu, 20),
        wg=blocks(wg_any, wg, 24),
        hid=one(hid_any, hid, 3),
    )
    for copies in loads.values():
        for copy in copies:
            copy.start()

    def arrive(*names):
        for name in names:
            for copy in loads[name]:
                copy.wait()

    def store(rel, tile, value):
        ref, across = targets[rel]
        away = (tile // 3) ^ own
        ref[across, away & 1, away >> 1, :, tile % 3 * LANE : (tile % 3 + 1) * LANE] = value.astype(bf16)

    def store_columns(kind, value):
        for rel in range(4):
            for t in range(8):
                store(rel, kind * 8 + t, value[rel * rows : (rel + 1) * rows, t * LANE : (t + 1) * LANE])

    arrive("low", "wd", "up_fac")
    dprod = dot(low[...], wd[...], 1, 1)
    dup = (dprod * up_fac[...].astype(f32)).astype(bf16)
    arrive("gate_fac")
    dgate = (dprod * gate_fac[...].astype(f32)).astype(bf16)
    arrive("hidt")
    store_columns(0, dot(hidt[...], dup, 1, 0))
    store_columns(1, dot(hidt[...], dgate, 1, 0))
    arrive("lowt", "prod")
    down = dot(lowt[...], prod[...], 1, 0)
    for rel in range(4):
        for k in range(4):
            for t in range(2):
                at = rel * BLOCK + t * LANE
                store(rel, 16 + 2 * k + t, down[k * rows : (k + 1) * rows, at : at + LANE])
    outs = [
        pltpu.make_async_copy(send, send_any, out_sems.at[0]),
        pltpu.make_async_copy(keep, keep_any, out_sems.at[1]),
        pltpu.make_async_copy(total, out_any, out_sems.at[2]),
    ]
    outs[0].start()
    outs[1].start()
    arrive("wu", "wg", "hid")
    total[...] = hid[...] + dot(dup, wu[...], 1, 1) + dot(dgate, wg[...], 1, 1)
    outs[2].start()
    for copy in outs:
        copy.wait()


def mixer_back_kernel(info_ref, grad_ref, xhat_ref, inv_ref, vec_ref, att0_ref, att1_ref, w_ref, heads_ref, *refs):
    sum_ref, low_ref, datt_ref, dl_ref, attt_ref, small_ref = refs[-6:]
    step = pl.program_id(0)
    grad, xhat = grad_ref[...], xhat_ref[...]
    out = norm_back(grad * vec_ref[0:1], xhat, inv_ref[:, 0:1])
    sum_ref[...] = out
    low = out.astype(bf16)
    low_ref[...] = low
    datt = dot(low, w_ref[...], 1, 1).astype(bf16)
    datt_ref[...] = datt
    att = jnp.concatenate([att0_ref[...], att1_ref[...]], axis=1)
    store_turned(attt_ref, att, info_ref[0])
    inner = datt.astype(f32) * att.astype(f32)
    heads = heads_ref[...]
    rows = jnp.zeros((heads.shape[0], inner.shape[0]), f32)
    for piece in split_three(inner)[:2]:
        rows += dot(heads, piece, 1, 1)
    for p in range(PAIRS):
        dl_ref[p] = rows[p * 8 : (p + 1) * 8]

    @pl.when(step == 0)
    def _():
        small_ref[...] = jnp.zeros_like(small_ref)

    small_ref[0:1] += jnp.sum(grad * xhat, axis=0, keepdims=True)
    small_ref[1:2] += jnp.sum(grad, axis=0, keepdims=True)


def qkv_back_kernel(extra, info_ref, xt_ref, attt_ref, gq_ref, gk_ref, gv_ref, gb_ref, small_ref, *refs):
    keep_ref, send_ref = refs[-2:]
    step = pl.program_id(0)
    half = keep_ref.shape[3] - extra
    own_y = info_ref[4] & 1
    targets = [(keep_ref, 0), (send_ref, 0), (keep_ref, 1), (send_ref, 1)]

    def run(left_ref, right_ref):
        value = dot(left_ref[...], right_ref[...], 1, 0).astype(bf16)
        for rel, (ref, across) in enumerate(targets):
            for y in range(2):
                at = (2 * rel + y) * half
                ref[across, y ^ own_y, 0, 0:half, :] = value[at : at + half]
                if extra:
                    ref[across, y ^ own_y, 0, half:, :] = small_ref[info_ref[rel], y].astype(bf16)

    for which, right_ref in enumerate((gq_ref, gk_ref, gv_ref, gb_ref)):
        pl.when(step == which)(functools.partial(run, xt_ref if which < 3 else attt_ref, right_ref))


BIT = dict(y=0, z0=1, z1=2)


def copy_part(order, own, part, pair, write):
    away = part ^ own
    one, two, three = [(away >> BIT[axis]) & 1 for axis in order if axis != "x"]
    for which in range(2):

        @pl.when(one == which)
        def _(which=which):
            write(pair[which][two * 2 + three].astype(f32))


def ffn_out_kernel(orders, info_ref, *refs):
    groups = (len(refs) - 3) // 2
    up_ref, gate_ref, down_ref = refs[-3:]
    own = info_ref[4]
    rows = up_ref.shape[0]
    for g in range(groups):
        for part in range(8):

            def write(value, g=g, part=part):
                for t in range(3):
                    tile = part * 3 + t
                    block = value[:, t * LANE : (t + 1) * LANE]
                    kind, within = tile // 8, tile % 8
                    if kind < 2:
                        at = ((within // 2) * groups + g) * BLOCK + (within % 2) * LANE
                        (up_ref, gate_ref)[kind][:, at : at + LANE] = block
                    else:
                        at = g * BLOCK + (within % 2) * LANE
                        col = (within // 2) * rows
                        down_ref[at : at + LANE, col : col + rows] = block.T

            copy_part(orders[g], own, part, refs[2 * g : 2 * g + 2], write)


def qkv_out_kernel(orders, info_ref, *refs):
    qkv_ref, out_ref, small_ref = refs[-3:]
    own = info_ref[4]
    half = qkv_ref.shape[0] // 2
    width = out_ref.shape[1]
    for h in range(2):
        for part in range(8):

            def write(value, h=h, part=part):
                y, c = part & 1, part >> 1
                rows = slice(y * half, (y + 1) * half)
                if c < 3:
                    at = c * width + h * PART
                    qkv_ref[rows, at : at + PART] = value[0:half]
                else:
                    out_ref[rows, h * PART : (h + 1) * PART] = value[0:half]
                if h == 0 and c == 0:
                    small_ref[y * 8 : y * 8 + 8] = value[half : half + 8]

            copy_part(orders[h], own, part, refs[2 * h : 2 * h + 2], write)


def input_back_kernel(rows_ref, gq0, gk0, gv0, gq1, gk1, gv1, sum_ref, *refs):
    pieces = refs[:4]
    out_ref, weight, sems = refs[-3:]
    width = sum_ref.shape[1]

    @pl.when(pl.program_id(0) == 0)
    def _():
        copies = piece_copies(lambda k: rows_ref[k], pieces, weight, sems)
        for copy in copies:
            copy.start()
        for copy in copies:
            copy.wait()

    total = sum_ref[...]
    for half, parts in enumerate(((gq0, gk0, gv0), (gq1, gk1, gv1))):
        for part, ref in enumerate(parts):
            at = part * width + half * PART
            total += dot(ref[...], weight[:, at : at + PART], 1, 1)
    out_ref[...] = total


def xor_permute(value, axis, size, bits):
    return lax.ppermute(value, axis, [(i, i ^ bits) for i in range(size)])


def drop_last(kernel, count, inputs, *refs):
    return kernel(*refs[:inputs], *refs[inputs + count :])


def gather_relative(value, axis, size):
    if size <= 8:
        return jnp.stack([value] + [xor_permute(value, axis, size, k) for k in range(1, size)])
    everyone = lax.all_gather(value, axis, axis=0)
    return jnp.take(everyone, jnp.arange(size) ^ lax.axis_index(axis), axis=0)


def absolute(stacked, own, bits):
    count = stacked.shape[0]
    for bit in range(bits):
        step = 1 << bit
        view = stacked.reshape((count // (2 * step), 2, step) + stacked.shape[1:])
        view = jnp.where((own >> bit) & 1 == 1, view[:, ::-1], view)
        stacked = view.reshape(stacked.shape)
    return stacked


def per_device(
    sizes,
    incoming_hidden_matrix,
    sequence_membership,
    matching_passages,
    softness_scale,
    combined_projection_matrix,
    mixer_projection_matrix,
    widening_matrix,
    gating_matrix,
    narrowing_matrix,
    mixer_scaling_factor,
    mixer_scaling_offset,
    perceptron_scaling_factor,
    perceptron_scaling_offset,
):
    nb, nf = sizes
    b, f = lax.axis_index("batch"), lax.axis_index("fsdp")
    x = incoming_hidden_matrix[0]
    segment = sequence_membership[0]
    T, D = x.shape
    FF = widening_matrix.shape[1]
    R = D // nf
    nblk = T // BLOCK
    y_bit = b & 1

    def tie(value, *others):
        return lax.optimization_barrier((value,) + others)[0]

    def halves_across(own):
        rows = own.shape[0]
        return xor_permute(lax.dynamic_slice_in_dim(own, y_bit * (rows // 2), rows // 2, 0), "fsdp", nf, 2)

    def gather_rest(own, mine, *others):
        mine = tie(mine, *others)
        other = xor_permute(mine, "batch", nb, 1)
        return (
            own,
            xor_permute(tie(own, *others), "fsdp", nf, 1),
            mine,
            other,
            xor_permute(mine, "fsdp", nf, 1),
            xor_permute(other, "fsdp", nf, 1),
        )

    def piece_rows(rows, share):
        half = rows // 2
        y = y_bit if share else 0 * y_bit
        two, three = (f ^ 2) * rows, (f ^ 3) * rows
        halves = [y * half, (1 - y) * half]
        starts = [f * rows, (f ^ 1) * rows, two + halves[0], two + halves[1], three + halves[0], three + halves[1]]
        down = [y * (FF // nf // 2), (1 - y) * (FF // nf // 2)]
        return jnp.stack(starts + [f] + down).astype(jnp.int32)

    rows = combined_projection_matrix.shape[0]
    beyond = xor_permute(combined_projection_matrix, "fsdp", nf, 2)
    beside = xor_permute(combined_projection_matrix, "fsdp", nf, 1)
    far = xor_permute(beyond, "fsdp", nf, 1)
    qkv_pieces = (combined_projection_matrix, beside, beyond, far)
    later = lax.optimization_barrier(
        (beyond, mixer_projection_matrix, widening_matrix, gating_matrix, narrowing_matrix)
    )[1:]
    up_half, out_half, gate_half, down_half = [halves_across(later[k]) for k in (1, 0, 2, 3)]
    vectors = jnp.stack(
        [mixer_scaling_factor, mixer_scaling_offset, perceptron_scaling_factor, perceptron_scaling_offset]
    )

    marks = (segment[:, None] == jnp.arange(SEGS, dtype=jnp.int32)[None, :]).astype(jnp.int32)
    counts = jnp.sum(marks, axis=0)
    ends = jnp.cumsum(counts)
    firsts = ends - counts
    start_of = jnp.sum(marks * firsts[None, :], axis=1)
    end_of = jnp.sum(marks * ends[None, :], axis=1)
    positions = jnp.arange(T, dtype=jnp.int32) - start_of
    inverse = 1000.0 ** (-(jnp.arange(HD // 2, dtype=f32) * 2.0) / HD)
    angles = positions.astype(f32)[:, None] * inverse[None, :]
    cosine, sine = jnp.cos(angles), jnp.sin(angles)
    cosine = jnp.concatenate([cosine] * 4, axis=1)
    sine = jnp.concatenate([-sine, sine, -sine, sine], axis=1)
    same = segment[:, None] == jnp.arange(LANE, dtype=jnp.int32)[None, :]
    mask_q = same.astype(bf16)
    mask_k = jnp.where(same | (jnp.arange(LANE)[None, :] >= SEGS), 0.0, NEG).astype(bf16)
    mark_rows = (jnp.arange(16, dtype=jnp.int32)[:, None] == segment[None, :]).astype(bf16)
    lo = (start_of.reshape(nblk, BLOCK)[:, 0] // LANE).astype(jnp.int32)
    hi = ((end_of.reshape(nblk, BLOCK)[:, -1] + LANE - 1) // LANE).astype(jnp.int32)
    spans = hi - lo
    count_rows = jnp.broadcast_to(counts.astype(f32)[:, None], (SEGS, LANE))

    def rowblk(width, rows=BLOCK):
        return pl.BlockSpec((rows, width), lambda i, *_: (i, 0))

    def colblk(height, cols=BLOCK):
        return pl.BlockSpec((height, cols), lambda i, *_: (0, i))

    whole_rows = jnp.stack([f * R, (f ^ 1) * R, (f ^ 2) * R, (f ^ 3) * R, f, f, f]).astype(jnp.int32)
    qkv, x_turned = pl.pallas_call(
        qkv_kernel,
        grid_spec=pltpu.PrefetchScalarGridSpec(
            num_scalar_prefetch=1,
            grid=(3,),
            in_specs=[whole((T, D)), whole((T, LANE)), whole((T, LANE))] + [ANY] * 4,
            out_specs=[pl.BlockSpec((T, D), lambda i, *_: (0, i)), whole((D, T))],
            scratch_shapes=[pltpu.VMEM((D, 3 * D), bf16), pltpu.SemaphoreType.DMA((4,))],
        ),
        out_shape=[shape((T, 3 * D), bf16), shape((D, T), bf16)],
        **params(),
    )(whole_rows, x, cosine, sine, *qkv_pieces)

    vectors = absolute(gather_relative(tie(vectors, qkv), "fsdp", nf), f, 2)
    vectors = vectors.transpose(1, 0, 2).reshape(4, D).astype(f32)

    def attend(h, *after):
        def keys(part):
            return pl.BlockSpec((T, PART), lambda i, *_: (0, 2 * part + h))

        return pl.pallas_call(
            functools.partial(drop_last, attend_kernel, len(after), 7),
            grid_spec=pltpu.PrefetchScalarGridSpec(
                num_scalar_prefetch=2,
                grid=(nblk,),
                in_specs=[
                    pl.BlockSpec((BLOCK, PART), lambda i, *_: (i, h)),
                    keys(1),
                    keys(2),
                    rowblk(LANE),
                    whole((T, LANE)),
                ]
                + [ANY] * len(after),
                out_specs=[rowblk(PART), pl.BlockSpec((PAIRS // 2, 8, BLOCK), lambda i, *_: (0, 0, i))],
            ),
            out_shape=[shape((T, PART), bf16), shape((PAIRS // 2, 8, T), f32)],
            **params(),
        )(lo, spans, qkv, qkv, qkv, mask_q, mask_k, *after)

    up_pieces = gather_rest(widening_matrix, up_half, qkv)
    attended0, lse0 = attend(0, up_pieces[2])
    out_pieces = gather_rest(mixer_projection_matrix, out_half, attended0)
    gate_pieces = gather_rest(gating_matrix, gate_half, attended0)
    attended1, lse1 = attend(1, gate_pieces[2], out_pieces[2])
    down_pieces = gather_rest(narrowing_matrix, down_half, attended1)

    shared_rows = piece_rows(R, True)
    xhat1, inv1, low1, low1_turned, full_out = pl.pallas_call(
        mixer_kernel,
        grid_spec=pltpu.PrefetchScalarGridSpec(
            num_scalar_prefetch=1,
            grid=(nblk,),
            in_specs=[rowblk(PART), rowblk(PART), rowblk(D), whole((4, D))] + [ANY] * 7,
            out_specs=[rowblk(D), rowblk(LANE), rowblk(D), colblk(D), ANY],
            scratch_shapes=[pltpu.VMEM((D, D), bf16), pltpu.SemaphoreType.DMA((6,)), pltpu.SemaphoreType.DMA],
        ),
        out_shape=[shape((T, D), f32), shape((T, LANE), f32), shape((T, D), bf16), shape((D, T), bf16), shape((D, D), bf16)],
        **params(),
    )(shared_rows, attended0, attended1, x, vectors, *out_pieces, down_pieces[2])

    W = FF // nf
    up_fac, gate_fac, prod, xhat2, inv2, pool, embed, full_up, full_gate, full_down = pl.pallas_call(
        ffn_kernel,
        grid_spec=pltpu.PrefetchScalarGridSpec(
            num_scalar_prefetch=1,
            grid=(nf,),
            in_specs=[whole((T, D)), whole((T, D)), whole((4, D)), whole((16, T)), whole((SEGS, LANE))] + [ANY] * 18,
            out_specs=[pl.BlockSpec((T, W), lambda i, rows: (0, rows[6] ^ i))] * 3
            + [whole((T, D)), whole((T, LANE)), whole((2 * SEGS, D)), whole((SEGS, D))]
            + [ANY] * 3,
            scratch_shapes=[
                pltpu.VMEM((nf, D, W), bf16),
                pltpu.VMEM((nf, D, W), bf16),
                pltpu.VMEM((nf, W, D), bf16),
                pltpu.SemaphoreType.DMA((nf * 12,)),
                pltpu.SemaphoreType.DMA((6,)),
                pltpu.SemaphoreType.DMA((nf * 3,)),
                pltpu.VMEM((16, D), f32),
                pltpu.VMEM((T, D), f32),
            ],
        ),
        out_shape=[shape((T, FF), bf16)] * 3
        + [shape((T, D), f32), shape((T, LANE), f32), shape((2 * SEGS, D), f32), shape((SEGS, D), bf16)]
        + [shape((D, FF), bf16), shape((D, FF), bf16), shape((FF, D), bf16)],
        **params(),
    )(shared_rows, low1, xhat1, vectors, mark_rows, count_rows, *up_pieces, *gate_pieces, *down_pieces)

    ranks = nb * nf
    total_rows = ranks * SEGS
    target = jnp.concatenate([matching_passages[0], jnp.zeros((SEGS - QSEG,), jnp.int32)])
    digits = jnp.pad(jnp.stack([target >> 5, target & 31], axis=1), ((0, 0), (0, LANE - 2))).astype(bf16)
    sent = jnp.concatenate([embed, digits], axis=1)
    everyone = gather_relative(sent, "fsdp", nf)
    if nb == 8:
        everyone = jnp.concatenate([everyone, xor_permute(everyone, "batch", nb, 1)])
        everyone = jnp.stack([everyone] + [xor_permute(everyone, "batch", nb, 2 * z) for z in range(1, 4)])
    else:
        everyone = gather_relative(everyone, "batch", nb)
    everyone = everyone.reshape(total_rows, D + LANE)
    rank_of = ((jnp.arange(nb)[:, None] ^ b) * nf + (jnp.arange(nf)[None, :] ^ f)).reshape(ranks, 1)
    place_of = jnp.arange(SEGS)[None, :]
    doc_ids = jnp.where(place_of >= QSEG, rank_of * (SEGS - QSEG) + place_of - QSEG, -1).reshape(1, total_rows)
    doc_ids = jnp.broadcast_to(doc_ids, (8, total_rows)).astype(f32)
    loss_rows, grad_rows, small_two = pl.pallas_call(
        loss_kernel,
        grid=(total_rows // BLOCK,),
        in_specs=[
            pl.BlockSpec(memory_space=pltpu.SMEM),
            rowblk(D + LANE),
            whole((total_rows, D + LANE)),
            whole((8, total_rows)),
            whole((2 * SEGS, D)),
            whole((SEGS, LANE)),
        ],
        out_specs=[whole((SEGS, LANE)), whole((LANE, D)), whole((8, D))],
        out_shape=[shape((SEGS, LANE), f32), shape((LANE, D), f32), shape((8, D), f32)],
        scratch_shapes=[pltpu.VMEM((SEGS, D), f32)],
        **params(),
    )(softness_scale.reshape(1), everyone, everyone, doc_ids, pool, count_rows)
    query_loss = loss_rows[:QSEG, 0].reshape(1, QSEG)

    sum_two, grad_low, grad_low_turned = pl.pallas_call(
        norm_two_back_kernel,
        grid=(nblk,),
        in_specs=[rowblk(LANE), whole((LANE, D)), rowblk(D), rowblk(LANE), whole((4, D))],
        out_specs=[rowblk(D), rowblk(D), colblk(D)],
        out_shape=[shape((T, D), f32), shape((T, D), bf16), shape((D, T), bf16)],
        **params(),
    )(mask_q, grad_rows, xhat2, inv2, vectors)

    def add(*terms):
        return sum([term.astype(f32) for term in terms]).astype(bf16)

    def across(value, axis):
        if axis == "x":
            return xor_permute(value, "fsdp", nf, 2)
        return xor_permute(value, "batch", nb, 1 << BIT[axis])

    class Reduce:
        def __init__(self, keep, send, *order):
            if nb != 8:
                order = ("x", "y", "z0", "z1")
            self.order, self.axes, self.stage = order, ["x", "y", "z1", "z0"], 0
            view = (2, 2, 2, 2) + keep.shape[-2:]
            self.terms = [keep.reshape(view), xor_permute(send, "fsdp", nf, 1).reshape(view)]

        def step(self, *after):
            self.stage += 1
            if nb != 8 and self.stage > 1:
                if self.stage == 2:
                    total = lax.psum(sum([term.astype(f32) for term in self.terms]), "batch").astype(bf16)
                    total = total.swapaxes(1, 2)
                    self.parts = [total[k].reshape((4,) + total.shape[-2:]) for k in range(2)]
                    self.out = self.parts[0]
                return
            self.terms[-1] = tie(self.terms[-1], *after)
            if self.stage <= 4:
                axis = self.order[self.stage - 1]
                at = self.axes.index(axis)
                self.axes.pop(at)
                self.out = add(*[lax.index_in_dim(term, 1, at, keepdims=False) for term in self.terms])
                self.terms = [lax.index_in_dim(term, 0, at, keepdims=False) for term in self.terms]
                self.terms.append(across(self.out, axis))
                return
            axis = [axis for axis in self.order if axis != "x"][7 - self.stage]
            if self.stage == 5:
                self.out = add(*self.terms)[None]
            else:
                self.out = jnp.concatenate(self.terms, axis=0)
            self.terms = [self.out, across(self.out, axis)]
            self.parts = self.terms

    own_part = b if nb == 8 else 0
    info = jnp.stack([f, f ^ 1, f ^ 2, f ^ 3, own_part + 0 * f]).astype(jnp.int32)
    groups = W // BLOCK

    def ffn_back(g, grad_hidden, *after):
        wide = nf * BLOCK
        parts = (2, 2, 4, R, PART)
        return pl.pallas_call(
            functools.partial(ffn_back_kernel, g, groups),
            grid_spec=pltpu.PrefetchScalarGridSpec(
                num_scalar_prefetch=1,
                grid=(1,),
                in_specs=[ANY] * (10 + len(after)),
                out_specs=[ANY] * 3,
                scratch_shapes=[pltpu.VMEM((T, wide), bf16)] * 3
                + [pltpu.VMEM((T, D), bf16), pltpu.VMEM((D, T), bf16), pltpu.VMEM((D, T), bf16)]
                + [pltpu.VMEM((D, wide), bf16)] * 2
                + [pltpu.VMEM((wide, D), bf16), pltpu.VMEM((T, D), f32)]
                + [pltpu.VMEM(parts, bf16)] * 2
                + [pltpu.VMEM((T, D), f32), pltpu.SemaphoreType.DMA((28,)), pltpu.SemaphoreType.DMA((3,))],
            ),
            out_shape=[shape((T, D), f32)] + [shape(parts, bf16)] * 2,
            **params(),
        )(
            info, prod, up_fac, gate_fac, grad_low, grad_low_turned, low1_turned, full_up, full_gate, full_down,
            grad_hidden, *after,
        )

    grad_hidden, keep, send = ffn_back(0, sum_two)
    r0 = Reduce(keep, send, "x", "z0", "y", "z1")
    grad_hidden, keep, send = ffn_back(1, grad_hidden)
    r1 = Reduce(keep, send, "y", "x", "z0", "z1")
    r0.step(grad_hidden)
    grad_hidden, keep, send = ffn_back(2, grad_hidden, r0.out)
    r2 = Reduce(keep, send, "x", "y", "z0", "z1")
    r1.step(grad_hidden)

    heads = (
        (jnp.arange(PAIRS * 8)[:, None] // 8 * 2 + jnp.arange(PAIRS * 8)[:, None] % 8 == jnp.arange(D)[None, :] // HD)
        & (jnp.arange(PAIRS * 8)[:, None] % 8 < 2)
    ).astype(bf16)
    sum_one, grad_branch, grad_att, delta, att_turned, small_one = pl.pallas_call(
        mixer_back_kernel,
        grid_spec=pltpu.PrefetchScalarGridSpec(
            num_scalar_prefetch=1,
            grid=(nblk,),
            in_specs=[
                rowblk(D),
                rowblk(D),
                rowblk(LANE),
                whole((4, D)),
                rowblk(PART),
                rowblk(PART),
                whole((D, D)),
                whole((PAIRS * 8, D)),
                ANY,
            ],
            out_specs=[
                rowblk(D),
                rowblk(D),
                rowblk(D),
                pl.BlockSpec((PAIRS, 8, BLOCK), lambda i, *_: (0, 0, i)),
                colblk(D),
                whole((8, D)),
            ],
        ),
        out_shape=[
            shape((T, D), f32),
            shape((T, D), bf16),
            shape((T, D), bf16),
            shape((PAIRS, 8, T), f32),
            shape((D, T), bf16),
            shape((8, D), f32),
        ],
        **params(),
    )(info, grad_hidden, xhat1, inv1, vectors, attended0, attended1, full_out, heads, r1.out)
    r2.step(grad_branch)
    r0.step(grad_branch)

    def attend_back(h, *after):
        def cols(part, rows=None):
            at = 2 * part + h
            return pl.BlockSpec((rows or T, PART), (lambda i, *_: (i, at)) if rows else (lambda i, *_: (0, at)))

        kernel = functools.partial(drop_last, attend_back_kernel, len(after), 14)
        return pl.pallas_call(
            kernel,
            grid_spec=pltpu.PrefetchScalarGridSpec(
                num_scalar_prefetch=2,
                grid=(nblk,),
                in_specs=[
                    cols(0),
                    cols(1, BLOCK),
                    cols(2, BLOCK),
                    cols(0),
                    whole((PAIRS // 2, 8, T)),
                    pl.BlockSpec((PAIRS // 2, 8, T), lambda i, *_: (h, 0, 0)),
                    whole((T, LANE)),
                    rowblk(LANE),
                    whole((T, LANE)),
                    whole((T, LANE)),
                    rowblk(LANE),
                    rowblk(LANE),
                ]
                + [ANY] * len(after),
                out_specs=[whole((T, PART)), rowblk(PART), rowblk(PART)],
                scratch_shapes=[pltpu.VMEM((PART, T), f32)],
            ),
            out_shape=[shape((T, PART), bf16)] * 3,
            **params(),
        )(lo, spans, qkv, qkv, qkv, grad_att, (lse0, lse1)[h], delta, mask_q, mask_k, cosine, sine, cosine, sine, *after)

    small = jnp.stack([small_one[0], small_one[1], small_two[0], small_two[1]]).reshape(4, nf, R)
    small = small.transpose(1, 0, 2).reshape(nf, 2, 1, 2 * R)
    small = jnp.pad(small, ((0, 0), (0, 0), (0, SMALL - 1), (0, 0)))

    def qkv_back(h, grads, extra, *after):
        dims = (2, 2, 4, R // 2 + extra, PART)
        parts = pl.BlockSpec(dims[:2] + (1,) + dims[3:], lambda c, info: (0, 0, c ^ (info[4] >> 1), 0, 0))
        return pl.pallas_call(
            functools.partial(qkv_back_kernel, extra),
            grid_spec=pltpu.PrefetchScalarGridSpec(
                num_scalar_prefetch=1,
                grid=(4,),
                in_specs=[whole((D, T)), whole((D, T))]
                + [whole((T, PART))] * 3
                + [pl.BlockSpec((T, PART), lambda c, *_: (0, h)), whole((nf, 2, SMALL, PART))]
                + [ANY] * len(after),
                out_specs=[parts, parts],
            ),
            out_shape=[shape(dims, bf16)] * 2,
            **params(),
        )(info, x_turned, att_turned, *grads, grad_branch, small, *after)

    grads0 = attend_back(0, r2.out, r0.out)
    r0.step(grads0[0])
    r1.step(grads0[0])
    keep, send = qkv_back(0, grads0, SMALL, r0.out, r1.out)
    r3 = Reduce(keep, send, "x", "z0", "y", "z1")
    r0.step(keep)
    r2.step(keep)
    grads1 = attend_back(1, r0.out, r2.out)
    r3.step(grads1[0])
    r0.step(grads1[0])
    r1.step(grads1[0])
    r2.step(grads1[0])
    keep, send = qkv_back(1, grads1, 0, r3.out, r0.out, r1.out, r2.out)
    r4 = Reduce(keep, send, "x", "y", "z0", "z1")
    r0.step(keep)
    r1.step(keep)
    r2.step(keep)
    r4.step(r0.out, r1.out, r2.out)

    grad_input = pl.pallas_call(
        input_back_kernel,
        grid_spec=pltpu.PrefetchScalarGridSpec(
            num_scalar_prefetch=1,
            grid=(nblk,),
            in_specs=[rowblk(PART)] * 6 + [rowblk(D)] + [ANY] * 5,
            out_specs=rowblk(D),
            scratch_shapes=[pltpu.VMEM((D, 3 * D), bf16), pltpu.SemaphoreType.DMA((4,))],
        ),
        out_shape=shape((T, D), f32),
        **params(),
    )(whole_rows, *grads0, *grads1, sum_one, *qkv_pieces, r4.out)

    def together(groups, *after):
        for group in groups:
            group.step(*after)
        return [group.out for group in groups]

    last = together([r3, r0, r1, r2], grad_input)
    last = together([r4, r3, r1, r2], *last)
    last = together([r4, r3, r1, r2], *last)
    last = together([r4, r3], *last)
    sum_up, sum_gate, sum_down = pl.pallas_call(
        functools.partial(ffn_out_kernel, (r0.order, r1.order, r2.order)),
        grid_spec=pltpu.PrefetchScalarGridSpec(
            num_scalar_prefetch=1,
            grid=(1,),
            in_specs=[whole((4, R, PART))] * (2 * groups),
            out_specs=[whole((R, FF)), whole((R, FF)), whole((W, D))],
        ),
        out_shape=[shape((R, FF), f32), shape((R, FF), f32), shape((W, D), f32)],
        **params(),
    )(info, *r0.parts, *r1.parts, *r2.parts)
    last = together([r4, r3], *last)
    last = together([r4, r3], sum_up, *last)
    last = together([r4], *last)
    sum_qkv, sum_out, sum_small = pl.pallas_call(
        functools.partial(qkv_out_kernel, (r3.order, r4.order)),
        grid_spec=pltpu.PrefetchScalarGridSpec(
            num_scalar_prefetch=1,
            grid=(1,),
            in_specs=[whole((4, R // 2 + SMALL, PART))] * 2 + [whole((4, R // 2, PART))] * 2,
            out_specs=[whole((R, 3 * D)), whole((R, D)), whole((16, PART))],
        ),
        out_shape=[shape((R, 3 * D), f32), shape((R, D), f32), shape((16, PART), f32)],
        **params(),
    )(info, *r3.parts, *r4.parts)
    return (
        query_loss,
        grad_input[None],
        sum_qkv,
        sum_out,
        sum_up,
        sum_gate,
        sum_down,
        sum_small[0, :R],
        sum_small[0, R : 2 * R],
        sum_small[8, :R],
        sum_small[8, R : 2 * R],
    )


def solution(mesh):
    sizes = (mesh.shape["batch"], mesh.shape["fsdp"])
    return jax.shard_map(
        functools.partial(per_device, sizes),
        mesh=mesh,
        in_specs=(
            P(("batch", "fsdp"), None, None),
            P(("batch", "fsdp"), None),
            P(("batch", "fsdp"), None),
            P(),
            P("fsdp", None),
            P("fsdp", None),
            P("fsdp", None),
            P("fsdp", None),
            P("fsdp", None),
            P("fsdp"),
            P("fsdp"),
            P("fsdp"),
            P("fsdp"),
        ),
        out_specs=(
            P(("batch", "fsdp"), None),
            P(("batch", "fsdp"), None, None),
            P("fsdp", None),
            P("fsdp", None),
            P("fsdp", None),
            P("fsdp", None),
            P("fsdp", None),
            P("fsdp"),
            P("fsdp"),
            P("fsdp"),
            P("fsdp"),
        ),
        check_vma=False,
    )
```

time: 1280 us -> 534 us (0.42)
  blocking collectives: 446 us -> 0 us
  matrix products: 306 us -> 0 us
  Pallas kernels: 0 us -> 237 us
  waiting for transfers between devices: 287 us -> 115 us
  local copies, waits for them, and re-layouts: 120 us -> 48.2 us
  starting transfers between devices: 0.61 us -> 67.7 us
  other arithmetic: 92.4 us -> 56.1 us
  between operations: 16.9 us -> 2.52 us
    psum x1 -> x0, blocking collectives: 390 us -> none  [per_device(): lax.psum((part_qkv, part_out, part_up, part_gate, part_down, part_ga, par...]
    dot_general x34 -> x0, matrix products: 306 us -> none  [the longest x6 51.1 us: multiply_by_flipped_second(): lax.dot_general(left_op, right_op, (((1,), (1,)), ((), ())), preferred_el...]
    pallas_call x0 -> x18, Pallas kernels: none -> 237 us  [the longest x3 57 us: ffn_back(): pl.pallas_call(functools.partial(ffn_back_kernel, g, groups), grid_spec=p...]
    reduce_scatter x4 -> x0, waiting for transfers between devices: 137 us -> none  [the longest x1 50.6 us: per_device(): lax.psum_scatter(grad_wdown.astype(jnp.bfloat16), 'fsdp', scatter_dimensi...]
    unnamed x13 -> x0, waiting for transfers between devices: 126 us -> none
    ppermute x0 -> x73, waiting for transfers between devices: none -> 115 us  [xor_permute(): return lax.ppermute(value, axis, [(i, i ^ bits) for i in range(size)])]
    ppermute x0 -> x73, starting transfers between devices: none -> 67.7 us  [xor_permute(): return lax.ppermute(value, axis, [(i, i ^ bits) for i in range(size)])]
    dynamic_update_slice x4 -> x0, local copies, waits for them, and re-layouts: 60.6 us -> none  [attend_forward(): out_blocks, log_sums = lax.map(one_block, (q_blocks, s_blocks))]
  transfers between devices with their start and end apart: 11 -> 73, of which waited for: 6 -> 25; matrix products, arithmetic and copies ran while one was open for 34% -> 18% of each run, Pallas kernels for 0% -> 31%
where the time goes in v1:
time: 534 us; the launch traced here: 526 us
  Pallas kernels  237 us (44%)
  waiting for transfers between devices  115 us (22%)
  starting transfers between devices  67.7 us (13%)
  other arithmetic  56.1 us (11%)
  local copies, waits for them, and re-layouts  48.2 us (9%)
    ppermute x73, waiting for transfers between devices, xor_permute(): return lax.ppermute(value, axis, [(i, i ^ bits) for i in range(size)])  115 us
    ppermute x73, starting transfers between devices, xor_permute(): return lax.ppermute(value, axis, [(i, i ^ bits) for i in range(size)])  67.7 us
    pallas_call x3, Pallas kernels, ffn_back(): pl.pallas_call(functools.partial(ffn_back_kernel, g, groups), grid_spec=p...  57 us
    pallas_call x2, Pallas kernels, attend_back(): pl.pallas_call(kernel, grid_spec=pltpu.PrefetchScalarGridSpec(num_scalar_...  37.3 us
    pallas_call x1, Pallas kernels, per_device(): pl.pallas_call(ffn_kernel, grid_spec=pltpu.PrefetchScalarGridSpec(num_sca...  30.8 us
    pallas_call x2, Pallas kernels, attend(): pl.pallas_call(functools.partial(drop_last, attend_kernel, len(after), 7)...  27.9 us
    convert_element_type x17, other arithmetic, add(): return sum([term.astype(f32) for term in terms]).astype(bf16)  23.5 us
    pallas_call x2, Pallas kernels, qkv_back(): pl.pallas_call(functools.partial(qkv_back_kernel, extra), grid_spec=pltpu...  17.1 us
  transfers between devices with their start and end apart: 73, of which 25 were waited for; matrix products, arithmetic and copies ran while one was open for 18% of the time, Pallas kernels for 31%

profile of v1, /device:TPU:0, one launch (start us, length us, event | category | flops | bytes accessed | tf_op | source)
XLA Modules:
  0.0 526.2 jit_solution(51430090506415982)
XLA Ops:
  0.6 3.0 collective-permute-start.1
  9.5 3.1 fusion.29
  12.6 10.9 %collective-permute-done.1.refs_2_ = bf16[192,2304]{1,0:T(8,128)(2,1)S(1)} collective-permute-done((bf16[192,2304]{1,0:T(8,128)(2,1)}, bf16[192,2304]{1,0:T(8,128)(2,1)S(1)}, u32[]{:S(2)}, u32[]{:S(2)}) %collective-permute-start.1) | collective-permute-done | bytes 884768 | tf_op jit(solution)/shard_map/ppermute | solution.py:630
  32.5 4.4 pad_maximum_fusion.3
  37.9 13.9 %shard_map.212 = (bf16[1024,2304]{1,0:T(8,128)(2,1)}, bf16[768,1024]{1,0:T(8,128)(2,1)}) custom-call(s32[7]{0:T(128)} %stack.148.rows_ref, bf16[1024,768]{1,0:T(8,128)(2,1)} %bitcast.266, f32[1024,128]{1,0:T(8,128)} %get-tuple-element.250.cos_ref.refs_10_.refs_12_, f32[1024,128]{1,0:T(8,128)} %get-tuple-element.251.sin_ref.refs_11_.refs_13_, ...), custom_call_target="tpu_custom_call" | custom-call | flops 1 | bytes 1 | tf_op jit(solution)/shard_map/pallas_call | solution.py:749
  52.7 14.0 %shard_map.213 = (bf16[1024,384]{1,0:T(8,128)(2,1)}, f32[3,8,1024]{2,1,0:T(8,128)}) custom-call(s32[4]{0:T(128)} %get-tuple-element.226.refs_0_, s32[4]{0:T(128)} %get-tuple-element.225.refs_1_, bf16[1024,2304]{1,0:T(8,128)(2,1)} %get-tuple-element.117.refs_2_.refs_3_.refs_4_, bf16[1024,2304]{1,0:T(8,128)(2,1)} %get-tuple-element.117.refs_2_.refs_3_.refs_4_, ...), custom_call_target="tpu_custom_call" | custom-call | flops 1 | bytes 1 | tf_op jit(solution)/shard_map/pallas_call | solution.py:769
  68.0 4.8 collective-permute-done.10.refs_3_
  78.8 13.9 %shard_map.214 = (bf16[1024,384]{1,0:T(8,128)(2,1)}, f32[3,8,1024]{2,1,0:T(8,128)}) custom-call(s32[4]{0:T(128)} %get-tuple-element.226.refs_0_, s32[4]{0:T(128)} %get-tuple-element.225.refs_1_, bf16[1024,2304]{1,0:T(8,128)(2,1)} %get-tuple-element.117.refs_2_.refs_3_.refs_4_, bf16[1024,2304]{1,0:T(8,128)(2,1)} %get-tuple-element.117.refs_2_.refs_3_.refs_4_, ...), custom_call_target="tpu_custom_call" | custom-call | flops 1 | bytes 1 | tf_op jit(solution)/shard_map/pallas_call | solution.py:769
  96.7 13.1 %collective-permute-done.19.refs_9_ = bf16[96,3072]{1,0:T(8,128)(2,1)S(1)} collective-permute-done((bf16[96,3072]{1,0:T(8,128)(2,1)}, bf16[96,3072]{1,0:T(8,128)(2,1)S(1)}, u32[]{:S(2)}, u32[]{:S(2)}) %collective-permute-start.19) | collective-permute-done | bytes 589856 | tf_op jit(solution)/shard_map/ppermute | solution.py:630
  115.6 6.0 %collective-permute-done.23.refs_15_ = bf16[384,768]{1,0:T(8,128)(2,1)} collective-permute-done((bf16[384,768]{1,0:T(8,128)(2,1)}, bf16[384,768]{1,0:T(8,128)(2,1)}, u32[]{:S(2)}, u32[]{:S(2)}) %collective-permute-start.23) | collective-permute-done | bytes 589856 | tf_op jit(solution)/shard_map/ppermute | solution.py:630
  123.6 9.1 %shard_map.215 = (f32[1024,768]{1,0:T(8,128)}, f32[1024,128]{1,0:T(8,128)}, bf16[1024,768]{1,0:T(8,128)(2,1)}, bf16[768,1024]{1,0:T(8,128)(2,1)}, bf16[768,768]{1,0:T(8,128)(2,1)}) custom-call(s32[9]{0:T(128)} %stack.145.rows_ref, bf16[1024,384]{1,0:T(8,128)(2,1)} %get-tuple-element.120.att0_ref, bf16[1024,384]{1,0:T(8,128)(2,1)} %get-tuple-element.125.att1_ref, ...), custom_call_target="tpu_custom_call" | custom-call | flops 1 | bytes 1 | tf_op jit(solution)/shard_map/pallas_call | solution.py:796
  133.4 30.8 %shard_map.216 = (bf16[1024,3072]{1,0:T(8,128)(2,1)}, bf16[1024,3072]{1,0:T(8,128)(2,1)}, bf16[1024,3072]{1,0:T(8,128)(2,1)}, f32[1024,768]{1,0:T(8,128)}, f32[1...) custom-call(s32[9]{0:T(128)} %stack.145.rows_ref, ...), custom_call_target="tpu_custom_call" | custom-call | flops 1 | bytes 1 | tf_op jit(solution)/shard_map/pallas_call | solution.py:810
  170.1 2.8 collective-permute-done.29
  173.0 4.8 collective-permute-start.32
  179.2 2.6 collective-permute-done.32
  181.7 4.7 collective-permute-done.31
  187.9 3.1 shard_map.217
  191.1 6.9 %shard_map.218 = (f32[1024,768]{1,0:T(8,128)}, bf16[1024,768]{1,0:T(8,128)(2,1)}, bf16[768,1024]{1,0:T(8,128)(2,1)}) custom-call(bf16[1024,128]{1,0:T(8,128)(2,1)} %fusion.12.refs_5_.mq_ref.refs_8_, f32[128,768]{1,0:T(8,128)} %get-tuple-element.141.rows_ref, f32[1024,768]{1,0:T(8,128)} %get-tuple-element.142.xhat_ref, ...), custom_call_target="tpu_custom_call" | custom-call | flops 1 | bytes 1 | tf_op jit(solution)/shard_map/pallas_call | solution.py:870
  198.0 18.8 %shard_map.219 = (f32[1024,768]{1,0:T(8,128)}, bf16[2,2,4,192,384]{4,3,2,1,0:T(8,128)(2,1)}, bf16[2,2,4,192,384]{4,3,2,1,0:T(8,128)(2,1)}) custom-call(s32[5]{0:T(128)} %stack.176.info_ref, bf16[1024,3072]{1,0:T(8,128)(2,1)} %get-tuple-element.138.prod_any, bf16[1024,3072]{1,0:T(8,128)(2,1)} %get-tuple-element.139.up_fac_any, ...), custom_call_target="tpu_custom_call" | custom-call | flops 1 | bytes 1 | tf_op jit(solution)/shard_map/pallas_call | solution.py:928
  216.9 19.0 %shard_map.220 = (f32[1024,768]{1,0:T(8,128)}, bf16[2,2,4,192,384]{4,3,2,1,0:T(8,128)(2,1)}, bf16[2,2,4,192,384]{4,3,2,1,0:T(8,128)(2,1)}) custom-call(s32[5]{0:T(128)} %stack.176.info_ref, bf16[1024,3072]{1,0:T(8,128)(2,1)} %get-tuple-element.138.prod_any, bf16[1024,3072]{1,0:T(8,128)(2,1)} %get-tuple-element.139.up_fac_any, ...), custom_call_target="tpu_custom_call" | custom-call | flops 1 | bytes 1 | tf_op jit(solution)/shard_map/pallas_call | solution.py:928
  236.4 2.9 fusion.52
  241.1 2.4 copy.97.refs_0_
  243.5 19.2 %shard_map.221 = (f32[1024,768]{1,0:T(8,128)}, bf16[2,2,4,192,384]{4,3,2,1,0:T(8,128)(2,1)}, bf16[2,2,4,192,384]{4,3,2,1,0:T(8,128)(2,1)}) custom-call(s32[5]{0:T(128)} %stack.176.info_ref, bf16[1024,3072]{1,0:T(8,128)(2,1)} %get-tuple-element.138.prod_any, bf16[1024,3072]{1,0:T(8,128)(2,1)} %get-tuple-element.139.up_fac_any, ...), custom_call_target="tpu_custom_call" | custom-call | flops 1 | bytes 1 | tf_op jit(solution)/shard_map/pallas_call | solution.py:928
  262.8 2.4 collective-permute-start.36
  266.6 1.9 slice_bitcast_fusion.4
  268.6 2.1 copy.99
  272.3 10.6 %shard_map.222 = (f32[1024,768]{1,0:T(8,128)}, bf16[1024,768]{1,0:T(8,128)(2,1)}, bf16[1024,768]{1,0:T(8,128)(2,1)}, f32[6,8,1024]{2,1,0:T(8,128)}, bf16[768,1024]{1,0:T(8,128)(2,1)}, /*index=5*/f32[8,768]{1,0:T(8,128)}) custom-call(s32[5]{0:T(128)} %stack.176.info_ref, f32[1024,768]{1,0:T(8,128)} %get-tuple-element.156.grad_ref, ...), custom_call_target="tpu_custom_call" | custom-call | flops 1 | bytes 1 | tf_op jit(solution)/shard_map/pallas_call | solution.py:962
  286.1 6.0 %collective-permute-done.36 = bf16[2,2,2,192,384]{4,3,1,2,0:T(8,128)(2,1)} collective-permute-done((bf16[2,2,2,192,384]{4,3,1,2,0:T(8,128)(2,1)}, bf16[2,2,2,192,384]{4,3,1,2,0:T(8,128)(2,1)}, u32[]{:S(2)}, u32[]{:S(2)}) %collective-permute-start.36) | collective-permute-done | bytes 1179680 | tf_op jit(solution)/shard_map/ppermute | solution.py:630
  292.1 2.1 fusion.8.refs_15_
  299.1 2.4 fusion.51
  301.5 2.6 fusion.refs_14_
  305.8 18.9 %shard_map.223 = (bf16[1024,384]{1,0:T(8,128)(2,1)}, bf16[1024,384]{1,0:T(8,128)(2,1)}, bf16[1024,384]{1,0:T(8,128)(2,1)}) custom-call(s32[4]{0:T(128)} %get-tuple-element.226.refs_0_, s32[4]{0:T(128)} %get-tuple-element.225.refs_1_, bf16[1024,2304]{1,0:T(8,128)(2,1)} %get-tuple-element.117.refs_2_.refs_3_.refs_4_, ...), custom_call_target="tpu_custom_call" | custom-call | flops 1 | bytes 1 | tf_op jit(solution)/shard_map/pallas_call | solution.py:1006
  324.7 2.1 fusion.10.refs_0_
  326.8 1.9 slice_bitcast_fusion.7
  330.3 2.2 slice_bitcast_fusion.8
  332.7 8.5 %shard_map.224 = (bf16[2,2,4,112,384]{4,3,2,1,0:T(8,128)(2,1)}, bf16[2,2,4,112,384]{4,3,2,1,0:T(8,128)(2,1)}) custom-call(s32[5]{0:T(128)} %stack.176.info_ref, bf16[768,1024]{1,0:T(8,128)(2,1)} %get-tuple-element.175.xt_ref, bf16[768,1024]{1,0:T(8,128)(2,1)} %get-tuple-element.176.attt_ref, bf16[1024,384]{1,0:T(8,128)(2,1)} %get-tuple-element.170.gq_ref.gq0, ...), custom_call_target="tpu_custom_call" | custom-call | flops 1 | bytes 1 | tf_op jit(solution)/shard_map/pallas_call | solution.py:1040
  344.5 2.0 collective-permute-start.42
  348.1 2.1 collective-permute-start.44
  350.2 18.4 %shard_map.225 = (bf16[1024,384]{1,0:T(8,128)(2,1)}, bf16[1024,384]{1,0:T(8,128)(2,1)}, bf16[1024,384]{1,0:T(8,128)(2,1)}) custom-call(s32[4]{0:T(128)} %get-tuple-element.226.refs_0_, s32[4]{0:T(128)} %get-tuple-element.225.refs_1_, bf16[1024,2304]{1,0:T(8,128)(2,1)} %get-tuple-element.117.refs_2_.refs_3_.refs_4_, ...), custom_call_target="tpu_custom_call" | custom-call | flops 1 | bytes 1 | tf_op jit(solution)/shard_map/pallas_call | solution.py:1006
  369.9 2.2 fusion.31.refs_1_
  374.0 2.2 fusion.2.refs_0_
  378.0 8.6 %shard_map.226 = (bf16[2,2,4,96,384]{4,3,2,1,0:T(8,128)(2,1)}, bf16[2,2,4,96,384]{4,3,2,1,0:T(8,128)(2,1)}) custom-call(s32[5]{0:T(128)} %stack.176.info_ref, bf16[768,1024]{1,0:T(8,128)(2,1)} %get-tuple-element.175.xt_ref, bf16[768,1024]{1,0:T(8,128)(2,1)} %get-tuple-element.176.attt_ref, bf16[1024,384]{1,0:T(8,128)(2,1)} %get-tuple-element.183.gq_ref.gq1, ...), custom_call_target="tpu_custom_call" | custom-call | flops 1 | bytes 1 | tf_op jit(solution)/shard_map/pallas_call | solution.py:1040
  388.4 2.8 collective-permute-start.46
  395.5 5.4 %collective-permute-done.47 = bf16[2,192,384]{2,1,0:T(8,128)(2,1)S(1)} collective-permute-done((bf16[2,192,384]{2,1,0:T(8,128)(2,1)}, bf16[2,192,384]{2,1,0:T(8,128)(2,1)S(1)}, u32[]{:S(2)}, u32[]{:S(2)}) %collective-permute-start.47) | collective-permute-done | bytes 294944 | tf_op jit(solution)/shard_map/ppermute | solution.py:630
  400.9 1.9 fusion.22
  406.4 2.1 collective-permute-done.48
  408.5 1.9 fusion.21
  413.4 11.4 %shard_map.227 = f32[1024,768]{1,0:T(8,128)} custom-call(s32[7]{0:T(128)} %stack.148.rows_ref, bf16[1024,384]{1,0:T(8,128)(2,1)} %get-tuple-element.170.gq_ref.gq0, bf16[1024,384]{1,0:T(8,128)(2,1)} %get-tuple-element.171.gk_ref.gk0, bf16[1024,384]{1,0:T(8,128)(2,1)} %get-tuple-element.172.gv_ref.gv0, bf16[1024,384]{1,0:T(8,128)(2,1)} %get-tuple-element.183.gq_ref.gq1, ...), custom_call_target="tpu_custom_call" | custom-call | flops 1 | bytes 1 | tf_op jit(solution)/shard_map/pallas_call | solution.py:1074
  427.6 2.7 collective-permute-start.56
  431.8 2.2 collective-permute-start.50
  435.1 8.0 %collective-permute-done.57 = bf16[1,192,384]{2,1,0:T(8,128)(2,1)S(1)} collective-permute-done((bf16[1,192,384]{2,1,0:T(8,128)(2,1)S(1)}, bf16[1,192,384]{2,1,0:T(8,128)(2,1)S(1)}, u32[]{:S(2)}, u32[]{:S(2)}) %collective-permute-start.57) | collective-permute-done | bytes 147488 | tf_op jit(solution)/shard_map/ppermute | solution.py:630
  443.2 2.1 collective-permute-start.60
  445.3 2.5 collective-permute-done.50
  452.1 14.7 %collective-permute-done.61 = bf16[2,192,384]{2,1,0:T(8,128)(2,1)S(1)} collective-permute-done((bf16[2,192,384]{2,1,0:T(8,128)(2,1)S(1)}, bf16[2,192,384]{2,1,0:T(8,128)(2,1)S(1)}, u32[]{:S(2)}, u32[]{:S(2)}) %collective-permute-start.61) | collective-permute-done | bytes 294944 | tf_op jit(solution)/shard_map/ppermute | solution.py:630
  466.8 4.0 collective-permute-done.60
  479.5 2.2 collective-permute-done.63
  481.8 2.6 collective-permute-start.68
  485.4 3.3 collective-permute-done.68
  491.6 8.7 %collective-permute-done.67.refs_5_ = bf16[4,192,384]{2,1,0:T(8,128)(2,1)} collective-permute-done((bf16[4,192,384]{2,1,0:T(8,128)(2,1)S(1)}, bf16[4,192,384]{2,1,0:T(8,128)(2,1)}, u32[]{:S(2)}, u32[]{:S(2)}) %collective-permute-start.67) | collective-permute-done | bytes 589856 | tf_op jit(solution)/shard_map/ppermute | solution.py:630
  500.4 7.7 %shard_map.228 = (f32[192,3072]{1,0:T(8,128)}, f32[192,3072]{1,0:T(8,128)}, f32[768,768]{1,0:T(8,128)}) custom-call(s32[5]{0:T(128)} %stack.176.info_ref, bf16[4,192,384]{2,1,0:T(8,128)(2,1)} %copy-done.28, bf16[4,192,384]{2,1,0:T(8,128)(2,1)} %copy-done.45, bf16[4,192,384]{2,1,0:T(8,128)(2,1)} %copy-done.30, bf16[4,192,384]{2,1,0:T(8,128)(2,1)} %copy-done.46, ...), custom_call_target="tpu_custom_call" | custom-call | flops 1 | bytes 1 | tf_op jit(solution)/shard_map/pallas_call | solution.py:1096
  510.4 3.0 collective-permute-done.71
  514.5 2.5 collective-permute-done.69.refs_1_
  517.0 3.2 collective-permute-done.72.refs_3_
  520.9 3.7 shard_map.229
  (351 shorter events, 111.8 us)
Async XLA Ops:
  0.6 22.9 %collective-permute-start.1 = (bf16[192,2304]{1,0:T(8,128)(2,1)}, bf16[192,2304]{1,0:T(8,128)(2,1)S(1)}, u32[]{:S(2)}, u32[]{:S(2)}) collective-permute-start(bf16[192,2304]{1,0:T(8,128)(2,1)} %refs_0_.7), channel_id=1, source_target_pairs={{0,2},{1,3},{2,0},{3,1},{4,6},{5,7},{6,4},{7,5},{8,10},{9,11},{10,... | collective-permute-start | bytes 2654216 | tf_op jit(solution)/shard_map/ppermute | solution.py:630
  3.6 27.3 %collective-permute-start = (bf16[192,2304]{1,0:T(8,128)(2,1)}, bf16[192,2304]{1,0:T(8,128)(2,1)S(1)}, u32[]{:S(2)}, u32[]{:S(2)}) collective-permute-start(bf16[192,2304]{1,0:T(8,128)(2,1)} %refs_0_.7), channel_id=1, source_target_pairs={{0,1},{1,0},{2,3},{3,2},{4,5},{5,4},{6,7},{7,6},{8,9},{9,8},{10,11... | collective-permute-start | bytes 2654216 | tf_op jit(solution)/shard_map/ppermute | solution.py:630
  24.6 42.1 %collective-permute-start.5 = (bf16[96,768]{1,0:T(8,128)(2,1)S(1)}, bf16[96,768]{1,0:T(8,128)(2,1)}, u32[]{:S(2)}, u32[]{:S(2)}) collective-permute-start(bf16[96,768]{1,0:T(8,128)(2,1)S(1)} %constant_dynamic-slice_fusion.1), channel_id=1, source_target_pairs={{0,2},{1,3},{2,0},{3,1},{4,6},{5,7},{6,4},{7,5},{8,10},{9,11},{10,... | collective-permute-start | bytes 442376 | tf_op jit(solution)/shard_map/ppermute | solution.py:630
  26.4 10.6 %collective-permute-start.2 = (bf16[192,2304]{1,0:T(8,128)(2,1)S(1)}, bf16[192,2304]{1,0:T(8,128)(2,1)S(1)}, u32[]{:S(2)}, u32[]{:S(2)}) collective-permute-start(bf16[192,2304]{1,0:T(8,128)(2,1)S(1)} %collective-permute-done.1.refs_2_), channel_id=1, source_target_pairs={{0,1},{1,0},{2,3},{3,2},{4,5},{5,4},{6,7},{7,6},{8,9},{9,8},{10,11... | collective-permute-start | bytes 2654216 | tf_op jit(solution)/shard_map/ppermute | solution.py:630
  27.2 24.6 %collective-permute-start.3 = (bf16[96,3072]{1,0:T(8,128)(2,1)}, bf16[96,3072]{1,0:T(8,128)(2,1)S(1)}, u32[]{:S(2)}, u32[]{:S(2)}) collective-permute-start(bf16[96,3072]{1,0:T(8,128)(2,1)} %constant_dynamic-slice_fusion.3), channel_id=1, source_target_pairs={{0,2},{1,3},{2,0},{3,1},{4,6},{5,7},{6,4},{7,5},{8,10},{9,11},{10,... | collective-permute-start | bytes 1769480 | tf_op jit(solution)/shard_map/ppermute | solution.py:630
  28.4 44.5 %collective-permute-start.4 = (bf16[96,3072]{1,0:T(8,128)(2,1)}, bf16[96,3072]{1,0:T(8,128)(2,1)}, u32[]{:S(2)}, u32[]{:S(2)}) collective-permute-start(bf16[96,3072]{1,0:T(8,128)(2,1)} %constant_dynamic-slice_fusion.2), channel_id=1, source_target_pairs={{0,2},{1,3},{2,0},{3,1},{4,6},{5,7},{6,4},{7,5},{8,10},{9,11},{10,... | collective-permute-start | bytes 1769480 | tf_op jit(solution)/shard_map/ppermute | solution.py:630
  31.0 43.8 %collective-permute-start.13 = (bf16[384,768]{1,0:T(8,128)(2,1)}, bf16[384,768]{1,0:T(8,128)(2,1)}, u32[]{:S(2)}, u32[]{:S(2)}) collective-permute-start(bf16[384,768]{1,0:T(8,128)(2,1)} %constant_dynamic-slice_fusion), channel_id=1, source_target_pairs={{0,2},{1,3},{2,0},{3,1},{4,6},{5,7},{6,4},{7,5},{8,10},{9,11},{10,... | collective-permute-start | bytes 1769480 | tf_op jit(solution)/shard_map/ppermute | solution.py:630
  66.7 6.1 %collective-permute-start.10 = (bf16[96,768]{1,0:T(8,128)(2,1)}, bf16[96,768]{1,0:T(8,128)(2,1)S(1)}, u32[]{:S(2)}, u32[]{:S(2)}) collective-permute-start(bf16[96,768]{1,0:T(8,128)(2,1)} %collective-permute-done.5.refs_8_.refs_2_), channel_id=1, source_target_pairs={{0,4},{4,0},{8,12},{12,8},{16,20},{20,16},{24,28},{28,24},{1,5},{5... | collective-permute-start | bytes 442376 | tf_op jit(solution)/shard_map/ppermute | solution.py:630
  66.8 26.6 %collective-permute-start.9 = (bf16[192,768]{1,0:T(8,128)(2,1)}, bf16[192,768]{1,0:T(8,128)(2,1)S(1)}, u32[]{:S(2)}, u32[]{:S(2)}) collective-permute-start(bf16[192,768]{1,0:T(8,128)(2,1)} %refs_0_.5), channel_id=1, source_target_pairs={{0,1},{1,0},{2,3},{3,2},{4,5},{5,4},{6,7},{7,6},{8,9},{9,8},{10,11... | collective-permute-start | bytes 884744 | tf_op jit(solution)/shard_map/ppermute | solution.py:630
  68.0 24.7 %collective-permute-start.11 = (bf16[96,768]{1,0:T(8,128)(2,1)}, bf16[96,768]{1,0:T(8,128)(2,1)}, u32[]{:S(2)}, u32[]{:S(2)}) collective-permute-start(bf16[96,768]{1,0:T(8,128)(2,1)} %collective-permute-done.5.refs_8_.refs_2_), channel_id=1, source_target_pairs={{0,1},{1,0},{2,3},{3,2},{4,5},{5,4},{6,7},{7,6},{8,9},{9,8},{10,11... | collective-permute-start | bytes 442376 | tf_op jit(solution)/shard_map/ppermute | solution.py:630
  72.8 21.8 %collective-permute-start.12 = (bf16[96,768]{1,0:T(8,128)(2,1)S(1)}, bf16[96,768]{1,0:T(8,128)(2,1)}, u32[]{:S(2)}, u32[]{:S(2)}) collective-permute-start(bf16[96,768]{1,0:T(8,128)(2,1)S(1)} %collective-permute-done.10.refs_3_), channel_id=1, source_target_pairs={{0,1},{1,0},{2,3},{3,2},{4,5},{5,4},{6,7},{7,6},{8,9},{9,8},{10,11... | collective-permute-start | bytes 442376 | tf_op jit(solution)/shard_map/ppermute | solution.py:630
  78.3 16.9 %collective-permute-start.16 = (bf16[96,3072]{1,0:T(8,128)(2,1)}, bf16[96,3072]{1,0:T(8,128)(2,1)}, u32[]{:S(2)}, u32[]{:S(2)}) collective-permute-start(bf16[96,3072]{1,0:T(8,128)(2,1)} %copy-done.14), channel_id=1, source_target_pairs={{0,1},{1,0},{2,3},{3,2},{4,5},{5,4},{6,7},{7,6},{8,9},{9,8},{10,11... | collective-permute-start | bytes 1769480 | tf_op jit(solution)/shard_map/ppermute | solution.py:630
  78.3 17.7 %collective-permute-start.15 = (bf16[96,3072]{1,0:T(8,128)(2,1)}, bf16[96,3072]{1,0:T(8,128)(2,1)}, u32[]{:S(2)}, u32[]{:S(2)}) collective-permute-start(bf16[96,3072]{1,0:T(8,128)(2,1)} %copy-done.14), channel_id=1, source_target_pairs={{0,4},{4,0},{8,12},{12,8},{16,20},{20,16},{24,28},{28,24},{1,5},{5... | collective-permute-start | bytes 1769480 | tf_op jit(solution)/shard_map/ppermute | solution.py:630
  93.3 16.4 %collective-permute-start.19 = (bf16[96,3072]{1,0:T(8,128)(2,1)}, bf16[96,3072]{1,0:T(8,128)(2,1)S(1)}, u32[]{:S(2)}, u32[]{:S(2)}) collective-permute-start(bf16[96,3072]{1,0:T(8,128)(2,1)} %collective-permute-done.4.refs_7_.refs_8_), channel_id=1, source_target_pairs={{0,4},{4,0},{8,12},{12,8},{16,20},{20,16},{24,28},{28,24},{1,5},{5... | collective-permute-start | bytes 1769480 | tf_op jit(solution)/shard_map/ppermute | solution.py:630
  94.6 15.1 %collective-permute-start.24 = (bf16[384,768]{1,0:T(8,128)(2,1)}, bf16[384,768]{1,0:T(8,128)(2,1)S(1)}, u32[]{:S(2)}, u32[]{:S(2)}) collective-permute-start(bf16[384,768]{1,0:T(8,128)(2,1)} %collective-permute-done.13.refs_6_.refs_14_), channel_id=1, source_target_pairs={{0,1},{1,0},{2,3},{3,2},{4,5},{5,4},{6,7},{7,6},{8,9},{9,8},{10,11... | collective-permute-start | bytes 1769480 | tf_op jit(solution)/shard_map/ppermute | solution.py:630
  95.3 26.3 %collective-permute-start.23 = (bf16[384,768]{1,0:T(8,128)(2,1)}, bf16[384,768]{1,0:T(8,128)(2,1)}, u32[]{:S(2)}, u32[]{:S(2)}) collective-permute-start(bf16[384,768]{1,0:T(8,128)(2,1)} %collective-permute-done.13.refs_6_.refs_14_), channel_id=1, source_target_pairs={{0,4},{4,0},{8,12},{12,8},{16,20},{20,16},{24,28},{28,24},{1,5},{5... | collective-permute-start | bytes 1769480 | tf_op jit(solution)/shard_map/ppermute | solution.py:630
  96.0 25.6 %collective-permute-start.17 = (bf16[96,3072]{1,0:T(8,128)(2,1)}, bf16[96,3072]{1,0:T(8,128)(2,1)}, u32[]{:S(2)}, u32[]{:S(2)}) collective-permute-start(bf16[96,3072]{1,0:T(8,128)(2,1)} %collective-permute-done.15.refs_3_), channel_id=1, source_target_pairs={{0,1},{1,0},{2,3},{3,2},{4,5},{5,4},{6,7},{7,6},{8,9},{9,8},{10,11... | collective-permute-start | bytes 1769480 | tf_op jit(solution)/shard_map/ppermute | solution.py:630
  96.3 36.4 %collective-permute-start.22 = (bf16[768,768]{1,0:T(8,128)(2,1)S(1)}, bf16[768,768]{1,0:T(8,128)(2,1)}, u32[]{:S(2)}, u32[]{:S(2)}) collective-permute-start(bf16[768,768]{1,0:T(8,128)(2,1)S(1)} %copy-done.13), channel_id=1, source_target_pairs={{0,1},{1,0},{2,3},{3,2},{4,5},{5,4},{6,7},{7,6},{8,9},{9,8},{10,11... | collective-permute-start | bytes 3538952 | tf_op jit(solution)/shard_map/ppermute | solution.py:630
  109.7 23.0 %collective-permute-start.18 = (bf16[192,3072]{1,0:T(8,128)(2,1)S(1)}, bf16[192,3072]{1,0:T(8,128)(2,1)}, u32[]{:S(2)}, u32[]{:S(2)}) collective-permute-start(bf16[192,3072]{1,0:T(8,128)(2,1)S(1)} %copy-done.11), channel_id=1, source_target_pairs={{0,1},{1,0},{2,3},{3,2},{4,5},{5,4},{6,7},{7,6},{8,9},{9,8},{10,11... | collective-permute-start | bytes 3538952 | tf_op jit(solution)/shard_map/ppermute | solution.py:630
  109.8 23.0 %collective-permute-start.14 = (bf16[192,3072]{1,0:T(8,128)(2,1)S(1)}, bf16[192,3072]{1,0:T(8,128)(2,1)}, u32[]{:S(2)}, u32[]{:S(2)}) collective-permute-start(bf16[192,3072]{1,0:T(8,128)(2,1)S(1)} %copy-done.9), channel_id=1, source_target_pairs={{0,1},{1,0},{2,3},{3,2},{4,5},{5,4},{6,7},{7,6},{8,9},{9,8},{10,11... | collective-permute-start | bytes 3538952 | tf_op jit(solution)/shard_map/ppermute | solution.py:630
  121.6 11.1 %collective-permute-start.21 = (bf16[96,3072]{1,0:T(8,128)(2,1)}, bf16[96,3072]{1,0:T(8,128)(2,1)}, u32[]{:S(2)}, u32[]{:S(2)}) collective-permute-start(bf16[96,3072]{1,0:T(8,128)(2,1)} %copy-done.41), channel_id=1, source_target_pairs={{0,1},{1,0},{2,3},{3,2},{4,5},{5,4},{6,7},{7,6},{8,9},{9,8},{10,11... | collective-permute-start | bytes 1769480 | tf_op jit(solution)/shard_map/ppermute | solution.py:630
  121.6 11.1 %collective-permute-start.25 = (bf16[384,768]{1,0:T(8,128)(2,1)}, bf16[384,768]{1,0:T(8,128)(2,1)}, u32[]{:S(2)}, u32[]{:S(2)}) collective-permute-start(bf16[384,768]{1,0:T(8,128)(2,1)} %collective-permute-done.23.refs_15_), channel_id=1, source_target_pairs={{0,1},{1,0},{2,3},{3,2},{4,5},{5,4},{6,7},{7,6},{8,9},{9,8},{10,11... | collective-permute-start | bytes 1769480 | tf_op jit(solution)/shard_map/ppermute | solution.py:630
  173.0 8.8 %collective-permute-start.32 = (bf16[8,8,896]{2,1,0:T(8,128)(2,1)S(1)}, bf16[8,8,896]{2,1,0:T(8,128)(2,1)S(1)}, u32[]{:S(2)}, u32[]{:S(2)}) collective-permute-start(bf16[8,8,896]{2,1,0:T(8,128)(2,1)S(1)} %constant_dynamic-update-slice_fusion), channel_id=1, source_target_pairs={{0,24},{4,28},{8,16},{12,20},{16,8},{20,12},{24,0},{28,4},{1,25},{... | collective-permute-start | bytes 344072 | tf_op jit(solution)/shard_map/ppermute | solution.py:630
  177.8 8.7 %collective-permute-start.31 = (bf16[8,8,896]{2,1,0:T(8,128)(2,1)S(1)}, bf16[8,8,896]{2,1,0:T(8,128)(2,1)S(1)}, u32[]{:S(2)}, u32[]{:S(2)}) collective-permute-start(bf16[8,8,896]{2,1,0:T(8,128)(2,1)S(1)} %constant_dynamic-update-slice_fusion), channel_id=1, source_target_pairs={{0,16},{4,20},{8,24},{12,28},{16,0},{20,4},{24,8},{28,12},{1,17},{... | collective-permute-start | bytes 344072 | tf_op jit(solution)/shard_map/ppermute | solution.py:630
  177.8 8.7 %collective-permute-start.30 = (bf16[8,8,896]{2,1,0:T(8,128)(2,1)S(1)}, bf16[8,8,896]{2,1,0:T(8,128)(2,1)S(1)}, u32[]{:S(2)}, u32[]{:S(2)}) collective-permute-start(bf16[8,8,896]{2,1,0:T(8,128)(2,1)S(1)} %constant_dynamic-update-slice_fusion), channel_id=1, source_target_pairs={{0,8},{4,12},{8,0},{12,4},{16,24},{20,28},{24,16},{28,20},{1,9},{5... | collective-permute-start | bytes 344072 | tf_op jit(solution)/shard_map/ppermute | solution.py:630
  216.8 22.5 %collective-permute-start.33 = (bf16[2,2,4,192,384]{4,3,2,1,0:T(8,128)(2,1)}, bf16[2,2,4,192,384]{4,3,2,1,0:T(8,128)(2,1)S(1)}, u32[]{:S(2)}, u32[]{:S(2)}) collective-permute-start(bf16[2,2,4,192,384]{4,3,2,1,0:T(8,128)(2,1)} %get-tuple-element.154), channel_id=1, source_target_pairs={{0,1},{1,0},{2,3},{3,2},{4,5},{5,4},{6,7},{7,6},{8,9},{9,8},{10,11... | collective-permute-start | bytes 7077896 | tf_op jit(solution)/shard_map/ppermute | solution.py:630
  235.9 32.7 %collective-permute-start.34 = (bf16[2,2,4,192,384]{4,3,2,1,0:T(8,128)(2,1)}, bf16[2,2,4,192,384]{4,3,2,1,0:T(8,128)(2,1)}, u32[]{:S(2)}, u32[]{:S(2)}) collective-permute-start(bf16[2,2,4,192,384]{4,3,2,1,0:T(8,128)(2,1)} %get-tuple-element.160), channel_id=1, source_target_pairs={{0,1},{1,0},{2,3},{3,2},{4,5},{5,4},{6,7},{7,6},{8,9},{9,8},{10,11... | collective-permute-start | bytes 7077896 | tf_op jit(solution)/shard_map/ppermute | solution.py:630
  262.7 38.7 %collective-permute-start.35 = (bf16[2,2,4,192,384]{4,3,2,1,0:T(8,128)(2,1)}, bf16[2,2,4,192,384]{4,3,2,1,0:T(8,128)(2,1)}, u32[]{:S(2)}, u32[]{:S(2)}) collective-permute-start(bf16[2,2,4,192,384]{4,3,2,1,0:T(8,128)(2,1)} %get-tuple-element.166), channel_id=1, source_target_pairs={{0,1},{1,0},{2,3},{3,2},{4,5},{5,4},{6,7},{7,6},{8,9},{9,8},{10,11... | collective-permute-start | bytes 7077896 | tf_op jit(solution)/shard_map/ppermute | solution.py:630
  262.8 29.3 %collective-permute-start.36 = (bf16[2,2,2,192,384]{4,3,1,2,0:T(8,128)(2,1)}, bf16[2,2,2,192,384]{4,3,1,2,0:T(8,128)(2,1)}, u32[]{:S(2)}, u32[]{:S(2)}) collective-permute-start(bf16[2,2,2,192,384]{4,3,1,2,0:T(8,128)(2,1)} %fusion.1), channel_id=1, source_target_pairs={{0,2},{1,3},{2,0},{3,1},{4,6},{5,7},{6,4},{7,5},{8,10},{9,11},{10,... | collective-permute-start | bytes 3538952 | tf_op jit(solution)/shard_map/ppermute | solution.py:630
  271.3 57.5 %collective-permute-start.39 = (bf16[2,2,2,192,384]{4,3,2,1,0:T(8,128)(2,1)S(1)}, bf16[2,2,2,192,384]{4,3,2,1,0:T(8,128)(2,1)}, u32[]{:S(2)}, u32[]{:S(2)}) collective-permute-start(bf16[2,2,2,192,384]{4,3,2,1,0:T(8,128)(2,1)S(1)} %fusion.3.refs_0_), channel_id=1, source_target_pairs={{0,4},{4,0},{8,12},{12,8},{16,20},{20,16},{24,28},{28,24},{1,5},{5... | collective-permute-start | bytes 3538952 | tf_op jit(solution)/shard_map/ppermute | solution.py:630
  294.2 30.5 %collective-permute-start.37 = (bf16[2,2,192,384]{3,2,1,0:T(8,128)(2,1)}, bf16[2,2,192,384]{3,2,1,0:T(8,128)(2,1)}, u32[]{:S(2)}, u32[]{:S(2)}) collective-permute-start(bf16[2,2,192,384]{3,2,1,0:T(8,128)(2,1)} %fusion.8.refs_15_), channel_id=1, source_target_pairs={{0,8},{4,12},{8,0},{12,4},{16,24},{20,28},{24,16},{28,20},{1,9},{5... | collective-permute-start | bytes 1769480 | tf_op jit(solution)/shard_map/ppermute | solution.py:630
  304.1 42.5 %collective-permute-start.40 = (bf16[2,2,2,192,384]{4,3,2,1,0:T(8,128)(2,1)}, bf16[2,2,2,192,384]{4,3,2,1,0:T(8,128)(2,1)}, u32[]{:S(2)}, u32[]{:S(2)}) collective-permute-start(bf16[2,2,2,192,384]{4,3,2,1,0:T(8,128)(2,1)} %fusion.refs_14_), channel_id=1, source_target_pairs={{0,2},{1,3},{2,0},{3,1},{4,6},{5,7},{6,4},{7,5},{8,10},{9,11},{10,... | collective-permute-start | bytes 3538952 | tf_op jit(solution)/shard_map/ppermute | solution.py:630
  328.8 14.4 %collective-permute-start.38 = (bf16[2,192,384]{2,1,0:T(8,128)(2,1)}, bf16[2,192,384]{2,1,0:T(8,128)(2,1)S(1)}, u32[]{:S(2)}, u32[]{:S(2)}) collective-permute-start(bf16[2,192,384]{2,1,0:T(8,128)(2,1)} %fusion.10.refs_0_), channel_id=1, source_target_pairs={{0,4},{4,0},{8,12},{12,8},{16,20},{20,16},{24,28},{28,24},{1,5},{5... | collective-permute-start | bytes 884744 | tf_op jit(solution)/shard_map/ppermute | solution.py:630
  332.4 39.7 %collective-permute-start.43 = (bf16[2,2,192,384]{3,2,1,0:T(8,128)(2,1)S(1)}, bf16[2,2,192,384]{3,2,1,0:T(8,128)(2,1)}, u32[]{:S(2)}, u32[]{:S(2)}) collective-permute-start(bf16[2,2,192,384]{3,2,1,0:T(8,128)(2,1)S(1)} %fusion.6.refs_1_), channel_id=1, source_target_pairs={{0,2},{1,3},{2,0},{3,1},{4,6},{5,7},{6,4},{7,5},{8,10},{9,11},{10,... | collective-permute-start | bytes 1769480 | tf_op jit(solution)/shard_map/ppermute | solution.py:630
  341.2 32.8 %collective-permute-start.41 = (bf16[2,2,4,112,384]{4,3,2,1,0:T(8,128)(2,1)}, bf16[2,2,4,112,384]{4,3,2,1,0:T(8,128)(2,1)}, u32[]{:S(2)}, u32[]{:S(2)}) collective-permute-start(bf16[2,2,4,112,384]{4,3,2,1,0:T(8,128)(2,1)} %get-tuple-element.187), channel_id=1, source_target_pairs={{0,1},{1,0},{2,3},{3,2},{4,5},{5,4},{6,7},{7,6},{8,9},{9,8},{10,11... | collective-permute-start | bytes 4128776 | tf_op jit(solution)/shard_map/ppermute | solution.py:630
  344.5 24.1 %collective-permute-start.42 = (bf16[192,384]{1,0:T(8,128)(2,1)S(1)}, bf16[192,384]{1,0:T(8,128)(2,1)}, u32[]{:S(2)}, u32[]{:S(2)}) collective-permute-start(bf16[192,384]{1,0:T(8,128)(2,1)S(1)} %fusion.25.refs_14_), channel_id=1, source_target_pairs={{0,16},{4,20},{8,24},{12,28},{16,0},{20,4},{24,8},{28,12},{1,17},{... | collective-permute-start | bytes 442376 | tf_op jit(solution)/shard_map/ppermute | solution.py:630
  348.1 28.1 %collective-permute-start.44 = (bf16[2,2,192,384]{3,2,1,0:T(8,128)(2,1)S(1)}, bf16[2,2,192,384]{3,2,1,0:T(8,128)(2,1)}, u32[]{:S(2)}, u32[]{:S(2)}) collective-permute-start(bf16[2,2,192,384]{3,2,1,0:T(8,128)(2,1)S(1)} %fusion.5.refs_15_), channel_id=1, source_target_pairs={{0,4},{4,0},{8,12},{12,8},{16,20},{20,16},{24,28},{28,24},{1,5},{5... | collective-permute-start | bytes 1769480 | tf_op jit(solution)/shard_map/ppermute | solution.py:630
  386.6 24.0 %collective-permute-start.45 = (bf16[2,2,4,96,384]{4,3,2,1,0:T(8,128)(2,1)}, bf16[2,2,4,96,384]{4,3,2,1,0:T(8,128)(2,1)S(1)}, u32[]{:S(2)}, u32[]{:S(2)}) collective-permute-start(bf16[2,2,4,96,384]{4,3,2,1,0:T(8,128)(2,1)} %get-tuple-element.193), channel_id=1, source_target_pairs={{0,1},{1,0},{2,3},{3,2},{4,5},{5,4},{6,7},{7,6},{8,9},{9,8},{10,11... | collective-permute-start | bytes 3538952 | tf_op jit(solution)/shard_map/ppermute | solution.py:630
  387.6 13.2 %collective-permute-start.47 = (bf16[2,192,384]{2,1,0:T(8,128)(2,1)}, bf16[2,192,384]{2,1,0:T(8,128)(2,1)S(1)}, u32[]{:S(2)}, u32[]{:S(2)}) collective-permute-start(bf16[2,192,384]{2,1,0:T(8,128)(2,1)} %fusion.15.refs_2_), channel_id=1, source_target_pairs={{0,8},{4,12},{8,0},{12,4},{16,24},{20,28},{24,16},{28,20},{1,9},{5... | collective-permute-start | bytes 884744 | tf_op jit(solution)/shard_map/ppermute | solution.py:630
  388.4 12.5 %collective-permute-start.46 = (bf16[1,192,384]{2,1,0:T(8,128)(2,1)S(1)}, bf16[1,192,384]{2,1,0:T(8,128)(2,1)S(1)}, u32[]{:S(2)}, u32[]{:S(2)}) collective-permute-start(bf16[1,192,384]{2,1,0:T(8,128)(2,1)S(1)} %copy-done.31), channel_id=1, source_target_pairs={{0,16},{4,20},{8,24},{12,28},{16,0},{20,4},{24,8},{28,12},{1,17},{... | collective-permute-start | bytes 442376 | tf_op jit(solution)/shard_map/ppermute | solution.py:630
  391.2 36.4 %collective-permute-start.49 = (bf16[2,2,2,112,384]{4,3,2,1,0:T(8,128)(2,1)S(1)}, bf16[2,2,2,112,384]{4,3,2,1,0:T(8,128)(2,1)}, u32[]{:S(2)}, u32[]{:S(2)}) collective-permute-start(bf16[2,2,2,112,384]{4,3,2,1,0:T(8,128)(2,1)S(1)} %copy-done.7), channel_id=1, source_target_pairs={{0,2},{1,3},{2,0},{3,1},{4,6},{5,7},{6,4},{7,5},{8,10},{9,11},{10,... | collective-permute-start | bytes 2064392 | tf_op jit(solution)/shard_map/ppermute | solution.py:630
  394.1 14.4 %collective-permute-start.48 = (bf16[2,192,384]{2,1,0:T(8,128)(2,1)S(1)}, bf16[2,192,384]{2,1,0:T(8,128)(2,1)S(1)}, u32[]{:S(2)}, u32[]{:S(2)}) collective-permute-start(bf16[2,192,384]{2,1,0:T(8,128)(2,1)S(1)} %copy-done.33), channel_id=1, source_target_pairs={{0,8},{4,12},{8,0},{12,4},{16,24},{20,28},{24,16},{28,20},{1,9},{5... | collective-permute-start | bytes 884744 | tf_op jit(solution)/shard_map/ppermute | solution.py:630
  402.7 22.1 %collective-permute-start.52 = (bf16[192,384]{1,0:T(8,128)(2,1)}, bf16[192,384]{1,0:T(8,128)(2,1)}, u32[]{:S(2)}, u32[]{:S(2)}) collective-permute-start(bf16[192,384]{1,0:T(8,128)(2,1)} %fusion.22), channel_id=1, source_target_pairs={{0,16},{4,20},{8,24},{12,28},{16,0},{20,4},{24,8},{28,12},{1,17},{... | collective-permute-start | bytes 442376 | tf_op jit(solution)/shard_map/ppermute | solution.py:630
  405.0 26.7 %collective-permute-start.51 = (bf16[2,192,384]{2,1,0:T(8,128)(2,1)}, bf16[2,192,384]{2,1,0:T(8,128)(2,1)}, u32[]{:S(2)}, u32[]{:S(2)}) collective-permute-start(bf16[2,192,384]{2,1,0:T(8,128)(2,1)} %pad_maximum_fusion.7), channel_id=1, source_target_pairs={{0,4},{4,0},{8,12},{12,8},{16,20},{20,16},{24,28},{28,24},{1,5},{5... | collective-permute-start | bytes 884744 | tf_op jit(solution)/shard_map/ppermute | solution.py:630
  410.4 14.5 %collective-permute-start.53 = (bf16[192,384]{1,0:T(8,128)(2,1)}, bf16[192,384]{1,0:T(8,128)(2,1)}, u32[]{:S(2)}, u32[]{:S(2)}) collective-permute-start(bf16[192,384]{1,0:T(8,128)(2,1)} %fusion.21), channel_id=1, source_target_pairs={{0,16},{4,20},{8,24},{12,28},{16,0},{20,4},{24,8},{28,12},{1,17},{... | collective-permute-start | bytes 442376 | tf_op jit(solution)/shard_map/ppermute | solution.py:630
  411.7 37.8 %collective-permute-start.55 = (bf16[2,2,2,96,384]{4,3,2,1,0:T(8,128)(2,1)S(1)}, bf16[2,2,2,96,384]{4,3,2,1,0:T(8,128)(2,1)}, u32[]{:S(2)}, u32[]{:S(2)}) collective-permute-start(bf16[2,2,2,96,384]{4,3,2,1,0:T(8,128)(2,1)S(1)} %fusion.4.refs_4_), channel_id=1, source_target_pairs={{0,2},{1,3},{2,0},{3,1},{4,6},{5,7},{6,4},{7,5},{8,10},{9,11},{10,... | collective-permute-start | bytes 1769480 | tf_op jit(solution)/shard_map/ppermute | solution.py:630
  427.6 15.5 %collective-permute-start.56 = (bf16[1,192,384]{2,1,0:T(8,128)(2,1)S(1)}, bf16[1,192,384]{2,1,0:T(8,128)(2,1)S(1)}, u32[]{:S(2)}, u32[]{:S(2)}) collective-permute-start(bf16[1,192,384]{2,1,0:T(8,128)(2,1)S(1)} %fusion.32), channel_id=1, source_target_pairs={{0,16},{4,20},{8,24},{12,28},{16,0},{20,4},{24,8},{28,12},{1,17},{... | collective-permute-start | bytes 442376 | tf_op jit(solution)/shard_map/ppermute | solution.py:630
  430.4 12.7 %collective-permute-start.57 = (bf16[1,192,384]{2,1,0:T(8,128)(2,1)S(1)}, bf16[1,192,384]{2,1,0:T(8,128)(2,1)S(1)}, u32[]{:S(2)}, u32[]{:S(2)}) collective-permute-start(bf16[1,192,384]{2,1,0:T(8,128)(2,1)S(1)} %fusion.33), channel_id=1, source_target_pairs={{0,16},{4,20},{8,24},{12,28},{16,0},{20,4},{24,8},{28,12},{1,17},{... | collective-permute-start | bytes 442376 | tf_op jit(solution)/shard_map/ppermute | solution.py:630
  431.8 16.0 %collective-permute-start.50 = (bf16[2,2,112,384]{3,2,1,0:T(8,128)(2,1)S(1)}, bf16[2,2,112,384]{3,2,1,0:T(8,128)(2,1)S(1)}, u32[]{:S(2)}, u32[]{:S(2)}) collective-permute-start(bf16[2,2,112,384]{3,2,1,0:T(8,128)(2,1)S(1)} %fusion.13), channel_id=1, source_target_pairs={{0,8},{4,12},{8,0},{12,4},{16,24},{20,28},{24,16},{28,20},{1,9},{5... | collective-permute-start | bytes 1032200 | tf_op jit(solution)/shard_map/ppermute | solution.py:630
  435.0 55.7 %collective-permute-start.65 = (bf16[4,192,384]{2,1,0:T(8,128)(2,1)S(1)}, bf16[4,192,384]{2,1,0:T(8,128)(2,1)S(1)}, u32[]{:S(2)}, u32[]{:S(2)}) collective-permute-start(bf16[4,192,384]{2,1,0:T(8,128)(2,1)S(1)} %pad_maximum_fusion.refs_0_), channel_id=1, source_target_pairs={{0,8},{4,12},{8,0},{12,4},{16,24},{20,28},{24,16},{28,20},{1,9},{5... | collective-permute-start | bytes 1769480 | tf_op jit(solution)/shard_map/ppermute | solution.py:630
  443.1 23.6 %collective-permute-start.61 = (bf16[2,192,384]{2,1,0:T(8,128)(2,1)S(1)}, bf16[2,192,384]{2,1,0:T(8,128)(2,1)S(1)}, u32[]{:S(2)}, u32[]{:S(2)}) collective-permute-start(bf16[2,192,384]{2,1,0:T(8,128)(2,1)S(1)} %pad_maximum_fusion.9), channel_id=1, source_target_pairs={{0,8},{4,12},{8,0},{12,4},{16,24},{20,28},{24,16},{28,20},{1,9},{5... | collective-permute-start | bytes 884744 | tf_op jit(solution)/shard_map/ppermute | solution.py:630
  443.2 27.5 %collective-permute-start.60 = (bf16[2,192,384]{2,1,0:T(8,128)(2,1)S(1)}, bf16[2,192,384]{2,1,0:T(8,128)(2,1)S(1)}, u32[]{:S(2)}, u32[]{:S(2)}) collective-permute-start(bf16[2,192,384]{2,1,0:T(8,128)(2,1)S(1)} %pad_maximum_fusion.8), channel_id=1, source_target_pairs={{0,8},{4,12},{8,0},{12,4},{16,24},{20,28},{24,16},{28,20},{1,9},{5... | collective-permute-start | bytes 884744 | tf_op jit(solution)/shard_map/ppermute | solution.py:630
  448.8 22.0 %collective-permute-start.54 = (bf16[2,112,384]{2,1,0:T(8,128)(2,1)S(1)}, bf16[2,112,384]{2,1,0:T(8,128)(2,1)S(1)}, u32[]{:S(2)}, u32[]{:S(2)}) collective-permute-start(bf16[2,112,384]{2,1,0:T(8,128)(2,1)S(1)} %fusion.14), channel_id=1, source_target_pairs={{0,4},{4,0},{8,12},{12,8},{16,20},{20,16},{24,28},{28,24},{1,5},{5... | collective-permute-start | bytes 516104 | tf_op jit(solution)/shard_map/ppermute | solution.py:630
  450.6 25.2 %collective-permute-start.59 = (bf16[2,2,96,384]{3,2,1,0:T(8,128)(2,1)S(1)}, bf16[2,2,96,384]{3,2,1,0:T(8,128)(2,1)S(1)}, u32[]{:S(2)}, u32[]{:S(2)}) collective-permute-start(bf16[2,2,96,384]{3,2,1,0:T(8,128)(2,1)S(1)} %fusion.9), channel_id=1, source_target_pairs={{0,4},{4,0},{8,12},{12,8},{16,20},{20,16},{24,28},{28,24},{1,5},{5... | collective-permute-start | bytes 884744 | tf_op jit(solution)/shard_map/ppermute | solution.py:630
  472.1 5.6 %collective-permute-start.58 = (bf16[112,384]{1,0:T(8,128)(2,1)S(1)}, bf16[112,384]{1,0:T(8,128)(2,1)S(1)}, u32[]{:S(2)}, u32[]{:S(2)}) collective-permute-start(bf16[112,384]{1,0:T(8,128)(2,1)S(1)} %fusion.26), channel_id=1, source_target_pairs={{0,16},{4,20},{8,24},{12,28},{16,0},{20,4},{24,8},{28,12},{1,17},{... | collective-permute-start | bytes 258056 | tf_op jit(solution)/shard_map/ppermute | solution.py:630
  472.7 18.1 %collective-permute-start.66 = (bf16[4,192,384]{2,1,0:T(8,128)(2,1)S(1)}, bf16[4,192,384]{2,1,0:T(8,128)(2,1)S(1)}, u32[]{:S(2)}, u32[]{:S(2)}) collective-permute-start(bf16[4,192,384]{2,1,0:T(8,128)(2,1)S(1)} %pad_maximum_fusion.1.refs_2_), channel_id=1, source_target_pairs={{0,4},{4,0},{8,12},{12,8},{16,20},{20,16},{24,28},{28,24},{1,5},{5... | collective-permute-start | bytes 1769480 | tf_op jit(solution)/shard_map/ppermute | solution.py:630
  473.3 27.1 %collective-permute-start.67 = (bf16[4,192,384]{2,1,0:T(8,128)(2,1)S(1)}, bf16[4,192,384]{2,1,0:T(8,128)(2,1)}, u32[]{:S(2)}, u32[]{:S(2)}) collective-permute-start(bf16[4,192,384]{2,1,0:T(8,128)(2,1)S(1)} %pad_maximum_fusion.2.refs_4_), channel_id=1, source_target_pairs={{0,4},{4,0},{8,12},{12,8},{16,20},{20,16},{24,28},{28,24},{1,5},{5... | collective-permute-start | bytes 1769480 | tf_op jit(solution)/shard_map/ppermute | solution.py:630
  475.9 5.8 %collective-permute-start.63 = (bf16[2,96,384]{2,1,0:T(8,128)(2,1)S(1)}, bf16[2,96,384]{2,1,0:T(8,128)(2,1)S(1)}, u32[]{:S(2)}, u32[]{:S(2)}) collective-permute-start(bf16[2,96,384]{2,1,0:T(8,128)(2,1)S(1)} %fusion.30), channel_id=1, source_target_pairs={{0,8},{4,12},{8,0},{12,4},{16,24},{20,28},{24,16},{28,20},{1,9},{5... | collective-permute-start | bytes 442376 | tf_op jit(solution)/shard_map/ppermute | solution.py:630
  478.7 6.7 %collective-permute-start.62 = (bf16[1,112,384]{2,1,0:T(8,128)(2,1)S(1)}, bf16[1,112,384]{2,1,0:T(8,128)(2,1)S(1)}, u32[]{:S(2)}, u32[]{:S(2)}) collective-permute-start(bf16[1,112,384]{2,1,0:T(8,128)(2,1)S(1)} %fusion.37), channel_id=1, source_target_pairs={{0,16},{4,20},{8,24},{12,28},{16,0},{20,4},{24,8},{28,12},{1,17},{... | collective-permute-start | bytes 258056 | tf_op jit(solution)/shard_map/ppermute | solution.py:630
  481.8 6.9 %collective-permute-start.68 = (bf16[96,384]{1,0:T(8,128)(2,1)S(1)}, bf16[96,384]{1,0:T(8,128)(2,1)S(1)}, u32[]{:S(2)}, u32[]{:S(2)}) collective-permute-start(bf16[96,384]{1,0:T(8,128)(2,1)S(1)} %fusion.36), channel_id=1, source_target_pairs={{0,16},{4,20},{8,24},{12,28},{16,0},{20,4},{24,8},{28,12},{1,17},{... | collective-permute-start | bytes 221192 | tf_op jit(solution)/shard_map/ppermute | solution.py:630
  488.8 19.4 %collective-permute-start.70 = (bf16[1,96,384]{2,1,0:T(8,128)(2,1)S(1)}, bf16[1,96,384]{2,1,0:T(8,128)(2,1)S(1)}, u32[]{:S(2)}, u32[]{:S(2)}) collective-permute-start(bf16[1,96,384]{2,1,0:T(8,128)(2,1)S(1)} %fusion.38), channel_id=1, source_target_pairs={{0,16},{4,20},{8,24},{12,28},{16,0},{20,4},{24,8},{28,12},{1,17},{... | collective-permute-start | bytes 221192 | tf_op jit(solution)/shard_map/ppermute | solution.py:630
  490.3 19.0 %collective-permute-start.64 = (bf16[2,112,384]{2,1,0:T(8,128)(2,1)S(1)}, bf16[2,112,384]{2,1,0:T(8,128)(2,1)S(1)}, u32[]{:S(2)}, u32[]{:S(2)}) collective-permute-start(bf16[2,112,384]{2,1,0:T(8,128)(2,1)S(1)} %pad_maximum_fusion.11), channel_id=1, source_target_pairs={{0,4},{4,0},{8,12},{12,8},{16,20},{20,16},{24,28},{28,24},{1,5},{5... | collective-permute-start | bytes 516104 | tf_op jit(solution)/shard_map/ppermute | solution.py:630
  509.4 7.7 %collective-permute-start.69 = (bf16[4,112,384]{2,1,0:T(8,128)(2,1)S(1)}, bf16[4,112,384]{2,1,0:T(8,128)(2,1)S(1)}, u32[]{:S(2)}, u32[]{:S(2)}) collective-permute-start(bf16[4,112,384]{2,1,0:T(8,128)(2,1)S(1)} %pad_maximum_fusion.6.refs_0_), channel_id=1, source_target_pairs={{0,8},{4,12},{8,0},{12,4},{16,24},{20,28},{24,16},{28,20},{1,9},{5... | collective-permute-start | bytes 1032200 | tf_op jit(solution)/shard_map/ppermute | solution.py:630
  513.4 6.8 %collective-permute-start.72 = (bf16[4,96,384]{2,1,0:T(8,128)(2,1)S(1)}, bf16[4,96,384]{2,1,0:T(8,128)(2,1)S(1)}, u32[]{:S(2)}, u32[]{:S(2)}) collective-permute-start(bf16[4,96,384]{2,1,0:T(8,128)(2,1)S(1)} %pad_maximum_fusion.10.refs_2_), channel_id=1, source_target_pairs={{0,4},{4,0},{8,12},{12,8},{16,20},{20,16},{24,28},{28,24},{1,5},{5... | collective-permute-start | bytes 884744 | tf_op jit(solution)/shard_map/ppermute | solution.py:630
  (75 other events, 730.8 us)

commit v2 on v1

--- a/solution.py
+++ b/solution.py
@@ -95,7 +95,7 @@
 
 def qkv_kernel(rows_ref, x_ref, cos_ref, sin_ref, *refs):
     pieces = refs[:4]
-    out_ref, xt_ref, weight, sems = refs[4:]
+    out_ref, xt_ref, weight, sems = refs[5:]
     step = pl.program_id(0)
     width = x_ref.shape[1]
 
@@ -222,8 +222,9 @@
 
 
 def mixer_kernel(rows_ref, att0_ref, att1_ref, x_ref, vec_ref, *refs):
-    pieces = refs[:6]
-    xhat_ref, inv_ref, low_ref, lowt_ref, full_ref, weight, sems, out_sem = refs[7:]
+    xhat_ref, inv_ref, low_ref, lowt_ref, full_ref, weight, sems, out_sem = refs[8:]
+    width = weight.shape[1]
+    pieces = list(refs[:2]) + [piece.at[:, pl.ds(piece.shape[1] - width, width)] for piece in refs[2:6]]
     step = pl.program_id(0)
     out_copy = pltpu.make_async_copy(weight, full_ref, out_sem)
 
@@ -409,46 +410,53 @@
     lowt_ref[...] = low.T
 
 
+BIT = dict(y=0, z0=1, z1=2)
+
+
+def part_index(order, x, away):
+    at = 0
+    for axis in order:
+        if axis == "z":
+            at = at * 4 + (away >> 1)
+        else:
+            at = at * 2 + (x if axis == "x" else (away >> BIT[axis]) & 1)
+    return at
+
+
+def strips(source, to, sems, first, groups, g, shards, by_rows=False):
+    copies = []
+    for k, shard in enumerate(shards):
+        at = (shard * groups + g) * BLOCK
+        here = pl.ds(at if isinstance(at, int) else pl.multiple_of(at, BLOCK), BLOCK)
+        there = pl.ds(k * BLOCK, BLOCK)
+        if by_rows:
+            copies.append(pltpu.make_async_copy(source.at[here], to.at[there], sems.at[first + k]))
+        else:
+            copies.append(pltpu.make_async_copy(source.at[:, here], to.at[:, there], sems.at[first + k]))
+    return copies
+
+
 def ffn_back_kernel(
-    g, groups, info_ref, prod_any, up_fac_any, gate_fac_any, low_any, lowt_any, hidt_any, wu_any, wg_any, wd_any, hid_any,
-    *refs,
+    g, order, groups, info_ref, prod_any, up_fac_any, gate_fac_any, low_any, lowt_any, hidt_any, wd_any, *refs
 ):
-    out_any, keep_any, send_any = refs[-18:-15]
-    prod, up_fac, gate_fac, low, lowt, hidt, wu, wg, wd, hid, keep, send, total, sems, out_sems = refs[-15:]
+    dup_any, dgate_any, keep_any, send_any = refs[-16:-12]
+    prod, up_fac, gate_fac, low, lowt, hidt, wd, dups, keep, send, sems, out_sems = refs[-12:]
     own = info_ref[4]
-    rows = keep.shape[3]
+    rows = keep.shape[1]
     targets = [(keep, 0), (send, 0), (keep, 1), (send, 1)]
-
-    def strip(index):
-        if isinstance(index, int):
-            return pl.ds((index * groups + g) * BLOCK, BLOCK)
-        return pl.ds(pl.multiple_of((index * groups + g) * BLOCK, BLOCK), BLOCK)
-
-    def blocks(source, to, first, relative=False, by_rows=False):
-        copies = []
-        for k in range(4):
-            here, there = strip(info_ref[k] if relative else k), pl.ds(k * BLOCK, BLOCK)
-            if by_rows:
-                copy = pltpu.make_async_copy(source.at[here], to.at[there], sems.at[first + k])
-            else:
-                copy = pltpu.make_async_copy(source.at[:, here], to.at[:, there], sems.at[first + k])
-            copies.append(copy)
-        return copies
 
     def one(source, to, first):
         return [pltpu.make_async_copy(source, to, sems.at[first])]
 
+    plain = range(4)
     loads = dict(
         low=one(low_any, low, 0),
-        wd=blocks(wd_any, wd, 4, by_rows=True),
-        up_fac=blocks(up_fac_any, up_fac, 8),
+        wd=strips(wd_any, wd, sems, 4, groups, g, plain, by_rows=True),
+        up_fac=strips(up_fac_any, up_fac, sems, 8, groups, g, plain),
         hidt=one(hidt_any, hidt, 1),
-        gate_fac=blocks(gate_fac_any, gate_fac, 12),
+        gate_fac=strips(gate_fac_any, gate_fac, sems, 12, groups, g, plain),
         lowt=one(lowt_any, lowt, 2),
-        prod=blocks(prod_any, prod, 16, relative=True),
-        wu=blocks(wu_any, wu, 20),
-        wg=blocks(wg_any, wg, 24),
-        hid=one(hid_any, hid, 3),
+        prod=strips(prod_any, prod, sems, 16, groups, g, [info_ref[k] for k in range(4)]),
     )
     for copies in loads.values():
         for copy in copies:
@@ -461,22 +469,30 @@
 
     def store(rel, tile, value):
         ref, across = targets[rel]
-        away = (tile // 3) ^ own
-        ref[across, away & 1, away >> 1, :, tile % 3 * LANE : (tile % 3 + 1) * LANE] = value.astype(bf16)
+        at = part_index(order, across, (tile // 3) ^ own)
+        ref[at, :, tile % 3 * LANE : (tile % 3 + 1) * LANE] = value.astype(bf16)
 
     def store_columns(kind, value):
         for rel in range(4):
             for t in range(8):
                 store(rel, kind * 8 + t, value[rel * rows : (rel + 1) * rows, t * LANE : (t + 1) * LANE])
 
+    outs = [
+        pltpu.make_async_copy(dups.at[0], dup_any, out_sems.at[0]),
+        pltpu.make_async_copy(dups.at[1], dgate_any, out_sems.at[1]),
+        pltpu.make_async_copy(send, send_any, out_sems.at[2]),
+        pltpu.make_async_copy(keep, keep_any, out_sems.at[3]),
+    ]
     arrive("low", "wd", "up_fac")
     dprod = dot(low[...], wd[...], 1, 1)
-    dup = (dprod * up_fac[...].astype(f32)).astype(bf16)
+    dups[0] = (dprod * up_fac[...].astype(f32)).astype(bf16)
     arrive("gate_fac")
-    dgate = (dprod * gate_fac[...].astype(f32)).astype(bf16)
+    dups[1] = (dprod * gate_fac[...].astype(f32)).astype(bf16)
+    outs[0].start()
+    outs[1].start()
     arrive("hidt")
-    store_columns(0, dot(hidt[...], dup, 1, 0))
-    store_columns(1, dot(hidt[...], dgate, 1, 0))
+    store_columns(0, dot(hidt[...], dups[0], 1, 0))
+    store_columns(1, dot(hidt[...], dups[1], 1, 0))
     arrive("lowt", "prod")
     down = dot(lowt[...], prod[...], 1, 0)
     for rel in range(4):
@@ -484,22 +500,55 @@
             for t in range(2):
                 at = rel * BLOCK + t * LANE
                 store(rel, 16 + 2 * k + t, down[k * rows : (k + 1) * rows, at : at + LANE])
-    outs = [
-        pltpu.make_async_copy(send, send_any, out_sems.at[0]),
-        pltpu.make_async_copy(keep, keep_any, out_sems.at[1]),
-        pltpu.make_async_copy(total, out_any, out_sems.at[2]),
-    ]
-    outs[0].start()
-    outs[1].start()
-    arrive("wu", "wg", "hid")
-    total[...] = hid[...] + dot(dup, wu[...], 1, 1) + dot(dgate, wg[...], 1, 1)
     outs[2].start()
+    outs[3].start()
     for copy in outs:
         copy.wait()
 
 
-def mixer_back_kernel(info_ref, grad_ref, xhat_ref, inv_ref, vec_ref, att0_ref, att1_ref, w_ref, heads_ref, *refs):
-    sum_ref, low_ref, datt_ref, dl_ref, attt_ref, small_ref = refs[-6:]
+def ffn_input_back_kernel(groups, wu_any, wg_any, hid_any, *refs):
+    dups = refs[: 2 * groups]
+    out_any = refs[-7]
+    dup, wu, wg, total, sems, out_sem = refs[-6:]
+    plain = range(4)
+
+    def loads(g):
+        copies = [
+            pltpu.make_async_copy(dups[2 * g + which], dup.at[2 * g + which], sems.at[g * 10 + which])
+            for which in range(2)
+        ]
+        copies += strips(wu_any, wu.at[g], sems, g * 10 + 2, groups, g, plain)
+        copies += strips(wg_any, wg.at[g], sems, g * 10 + 6, groups, g, plain)
+        return copies
+
+    base = pltpu.make_async_copy(hid_any, total, sems.at[groups * 10])
+    for g in range(groups):
+        for copy in loads(g):
+            copy.start()
+        if g == 0:
+            base.start()
+
+    def work(g, _):
+        for k in range(groups):
+
+            @pl.when(g == k)
+            def _(k=k):
+                for copy in loads(k):
+                    copy.wait()
+                if k == 0:
+                    base.wait()
+
+        total[...] += dot(dup[2 * g], wu[g], 1, 1) + dot(dup[2 * g + 1], wg[g], 1, 1)
+        return 0
+
+    lax.fori_loop(0, groups, work, 0)
+    out = pltpu.make_async_copy(total, out_any, out_sem)
+    out.start()
+    out.wait()
+
+
+def mixer_back_kernel(info_ref, grad_ref, xhat_ref, inv_ref, vec_ref, att0_ref, att1_ref, w_ref, heads_ref, two_ref, *refs):
+    sum_ref, low_ref, datt_ref, dl_ref, attt_ref, small_ref, sums = refs[-7:]
     step = pl.program_id(0)
     grad, xhat = grad_ref[...], xhat_ref[...]
     out = norm_back(grad * vec_ref[0:1], xhat, inv_ref[:, 0:1])
@@ -521,16 +570,26 @@
     @pl.when(step == 0)
     def _():
         small_ref[...] = jnp.zeros_like(small_ref)
-
-    small_ref[0:1] += jnp.sum(grad * xhat, axis=0, keepdims=True)
-    small_ref[1:2] += jnp.sum(grad, axis=0, keepdims=True)
-
-
-def qkv_back_kernel(extra, info_ref, xt_ref, attt_ref, gq_ref, gk_ref, gv_ref, gb_ref, small_ref, *refs):
+        sums[...] = jnp.zeros_like(sums)
+
+    sums[0:1] += jnp.sum(grad * xhat, axis=0, keepdims=True)
+    sums[1:2] += jnp.sum(grad, axis=0, keepdims=True)
+
+    @pl.when(step == pl.num_programs(0) - 1)
+    def _():
+        width = sums.shape[1] // 4
+        for y, ref in enumerate((sums, two_ref)):
+            for shard in range(4):
+                cols = slice(shard * width, (shard + 1) * width)
+                small_ref[shard, y, 0:1, 0:width] = ref[0:1, cols]
+                small_ref[shard, y, 0:1, width : 2 * width] = ref[1:2, cols]
+
+
+def qkv_back_kernel(extra, order, info_ref, xt_ref, attt_ref, gq_ref, gk_ref, gv_ref, gb_ref, small_ref, *refs):
     keep_ref, send_ref = refs[-2:]
     step = pl.program_id(0)
-    half = keep_ref.shape[3] - extra
-    own_y = info_ref[4] & 1
+    half = keep_ref.shape[1] - extra
+    own = info_ref[4]
     targets = [(keep_ref, 0), (send_ref, 0), (keep_ref, 1), (send_ref, 1)]
 
     def run(left_ref, right_ref):
@@ -538,25 +597,24 @@
         for rel, (ref, across) in enumerate(targets):
             for y in range(2):
                 at = (2 * rel + y) * half
-                ref[across, y ^ own_y, 0, 0:half, :] = value[at : at + half]
+                to = part_index(order, across, (2 * step + y) ^ own)
+                ref[to, 0:half, :] = value[at : at + half]
                 if extra:
-                    ref[across, y ^ own_y, 0, half:, :] = small_ref[info_ref[rel], y].astype(bf16)
+                    ref[to, half:, :] = small_ref[info_ref[rel], y].astype(bf16)
 
     for which, right_ref in enumerate((gq_ref, gk_ref, gv_ref, gb_ref)):
         pl.when(step == which)(functools.partial(run, xt_ref if which < 3 else attt_ref, right_ref))
 
 
-BIT = dict(y=0, z0=1, z1=2)
-
-
 def copy_part(order, own, part, pair, write):
     away = part ^ own
-    one, two, three = [(away >> BIT[axis]) & 1 for axis in order if axis != "x"]
+    one, *rest = [axis for axis in order if axis != "x"]
+    at = part_index(rest, 0, away)
     for which in range(2):
 
-        @pl.when(one == which)
+        @pl.when((away >> BIT[one]) & 1 == which)
         def _(which=which):
-            write(pair[which][two * 2 + three].astype(f32))
+            write(pair[which][at].astype(f32))
 
 
 def ffn_out_kernel(orders, info_ref, *refs):
@@ -628,6 +686,41 @@
 
 def xor_permute(value, axis, size, bits):
     return lax.ppermute(value, axis, [(i, i ^ bits) for i in range(size)])
+
+
+def sums_kernel(plan, *refs):
+    outs = refs[len(refs) - len(plan) :]
+    for out_ref, pieces in zip(outs, plan, strict=True):
+        for offset, terms in pieces:
+            total = refs[terms[0]][...].astype(f32)
+            for term in terms[1:]:
+                total += refs[term][...].astype(f32)
+            out_ref[offset : offset + total.shape[0]] = total.astype(bf16)
+
+
+def sums_of(wanted, after):
+    inputs, specs, plan, shapes = [], [], [], []
+    for pieces in wanted:
+        offset, steps = 0, []
+        for terms in pieces:
+            indices = []
+            for array, first, count in terms:
+                indices.append(len(inputs))
+                inputs.append(array)
+                at = first // count
+                specs.append(pl.BlockSpec((count,) + array.shape[1:], lambda i, at=at: (at, 0, 0)))
+            steps.append((offset, indices))
+            offset += terms[0][2]
+        plan.append(steps)
+        shapes.append((offset,) + pieces[0][0][0].shape[1:])
+    return pl.pallas_call(
+        functools.partial(drop_last, functools.partial(sums_kernel, plan), len(after), len(inputs)),
+        grid=(1,),
+        in_specs=specs + [ANY] * len(after),
+        out_specs=[pl.BlockSpec(dims, lambda i: (0, 0, 0)) for dims in shapes],
+        out_shape=[shape(dims, bf16) for dims in shapes],
+        **params(),
+    )(*inputs, *after)
 
 
 def drop_last(kernel, count, inputs, *refs):
@@ -680,21 +773,23 @@
     def tie(value, *others):
         return lax.optimization_barrier((value,) + others)[0]
 
-    def halves_across(own):
+    def own_half(own):
         rows = own.shape[0]
-        return xor_permute(lax.dynamic_slice_in_dim(own, y_bit * (rows // 2), rows // 2, 0), "fsdp", nf, 2)
-
-    def gather_rest(own, mine, *others):
-        mine = tie(mine, *others)
+        return lax.dynamic_slice_in_dim(own, y_bit * (rows // 2), rows // 2, 0)
+
+    def gather_rest(own, mine, before):
+        mine = tie(mine, before)
         other = xor_permute(mine, "batch", nb, 1)
         return (
             own,
-            xor_permute(tie(own, *others), "fsdp", nf, 1),
+            xor_permute(tie(own, before), "fsdp", nf, 1),
             mine,
             other,
             xor_permute(mine, "fsdp", nf, 1),
-            xor_permute(other, "fsdp", nf, 1),
         )
+
+    def gather_last(pieces, during):
+        return pieces + (xor_permute(tie(pieces[3], during), "fsdp", nf, 1),)
 
     def piece_rows(rows, share):
         half = rows // 2
@@ -705,19 +800,6 @@
         down = [y * (FF // nf // 2), (1 - y) * (FF // nf // 2)]
         return jnp.stack(starts + [f] + down).astype(jnp.int32)
 
-    rows = combined_projection_matrix.shape[0]
-    beyond = xor_permute(combined_projection_matrix, "fsdp", nf, 2)
-    beside = xor_permute(combined_projection_matrix, "fsdp", nf, 1)
-    far = xor_permute(beyond, "fsdp", nf, 1)
-    qkv_pieces = (combined_projection_matrix, beside, beyond, far)
-    later = lax.optimization_barrier(
-        (beyond, mixer_projection_matrix, widening_matrix, gating_matrix, narrowing_matrix)
-    )[1:]
-    up_half, out_half, gate_half, down_half = [halves_across(later[k]) for k in (1, 0, 2, 3)]
-    vectors = jnp.stack(
-        [mixer_scaling_factor, mixer_scaling_offset, perceptron_scaling_factor, perceptron_scaling_offset]
-    )
-
     marks = (segment[:, None] == jnp.arange(SEGS, dtype=jnp.int32)[None, :]).astype(jnp.int32)
     counts = jnp.sum(marks, axis=0)
     ends = jnp.cumsum(counts)
@@ -725,11 +807,10 @@
     start_of = jnp.sum(marks * firsts[None, :], axis=1)
     end_of = jnp.sum(marks * ends[None, :], axis=1)
     positions = jnp.arange(T, dtype=jnp.int32) - start_of
-    inverse = 1000.0 ** (-(jnp.arange(HD // 2, dtype=f32) * 2.0) / HD)
+    lane = jnp.arange(LANE)
+    inverse = 1000.0 ** (-((lane % (HD // 2)).astype(f32) * 2.0) / HD)
     angles = positions.astype(f32)[:, None] * inverse[None, :]
-    cosine, sine = jnp.cos(angles), jnp.sin(angles)
-    cosine = jnp.concatenate([cosine] * 4, axis=1)
-    sine = jnp.concatenate([-sine, sine, -sine, sine], axis=1)
+    cosine, sine = jnp.cos(angles), jnp.where((lane % HD < HD // 2)[None, :], -1.0, 1.0) * jnp.sin(angles)
     same = segment[:, None] == jnp.arange(LANE, dtype=jnp.int32)[None, :]
     mask_q = same.astype(bf16)
     mask_k = jnp.where(same | (jnp.arange(LANE)[None, :] >= SEGS), 0.0, NEG).astype(bf16)
@@ -737,6 +818,26 @@
     lo = (start_of.reshape(nblk, BLOCK)[:, 0] // LANE).astype(jnp.int32)
     hi = ((end_of.reshape(nblk, BLOCK)[:, -1] + LANE - 1) // LANE).astype(jnp.int32)
     spans = hi - lo
+    rows = combined_projection_matrix.shape[0]
+    beyond = xor_permute(combined_projection_matrix, "fsdp", nf, 2)
+    beside = xor_permute(combined_projection_matrix, "fsdp", nf, 1)
+    both = jnp.concatenate([own_half(widening_matrix), own_half(mixer_projection_matrix)], axis=1)
+    halves = [both, own_half(gating_matrix), own_half(narrowing_matrix)]
+    vectors = jnp.stack(
+        [mixer_scaling_factor, mixer_scaling_offset, perceptron_scaling_factor, perceptron_scaling_offset]
+    )
+    vectors = gather_relative(vectors, "fsdp", nf)
+    beyond = tie(beyond, mask_q, mask_k, cosine, vectors, *halves)
+    far = xor_permute(beyond, "fsdp", nf, 1)
+    qkv_pieces = (combined_projection_matrix, beside, beyond, far)
+    up_half, gate_half, down_half = [
+        xor_permute(tie(half, cosine, mask_q, mask_k), "fsdp", nf, 2) for half in halves
+    ]
+
+    heads = (
+        (jnp.arange(PAIRS * 8)[:, None] // 8 * 2 + jnp.arange(PAIRS * 8)[:, None] % 8 == jnp.arange(D)[None, :] // HD)
+        & (jnp.arange(PAIRS * 8)[:, None] % 8 < 2)
+    ).astype(bf16)
     count_rows = jnp.broadcast_to(counts.astype(f32)[:, None], (SEGS, LANE))
 
     def rowblk(width, rows=BLOCK):
@@ -751,15 +852,15 @@
         grid_spec=pltpu.PrefetchScalarGridSpec(
             num_scalar_prefetch=1,
             grid=(3,),
-            in_specs=[whole((T, D)), whole((T, LANE)), whole((T, LANE))] + [ANY] * 4,
+            in_specs=[whole((T, D)), whole((T, LANE)), whole((T, LANE))] + [ANY] * 5,
             out_specs=[pl.BlockSpec((T, D), lambda i, *_: (0, i)), whole((D, T))],
             scratch_shapes=[pltpu.VMEM((D, 3 * D), bf16), pltpu.SemaphoreType.DMA((4,))],
         ),
         out_shape=[shape((T, 3 * D), bf16), shape((D, T), bf16)],
         **params(),
-    )(whole_rows, x, cosine, sine, *qkv_pieces)
-
-    vectors = absolute(gather_relative(tie(vectors, qkv), "fsdp", nf), f, 2)
+    )(whole_rows, x, cosine, sine, *qkv_pieces, vectors)
+
+    vectors = absolute(vectors, f, 2)
     vectors = vectors.transpose(1, 0, 2).reshape(4, D).astype(f32)
 
     def attend(h, *after):
@@ -787,9 +888,12 @@
 
     up_pieces = gather_rest(widening_matrix, up_half, qkv)
     attended0, lse0 = attend(0, up_pieces[2])
-    out_pieces = gather_rest(mixer_projection_matrix, out_half, attended0)
+    up_pieces = gather_last(up_pieces, attended0)
+    out_beside = xor_permute(tie(mixer_projection_matrix, qkv), "fsdp", nf, 1)
+    out_pieces = (mixer_projection_matrix, out_beside) + up_pieces[2:]
     gate_pieces = gather_rest(gating_matrix, gate_half, attended0)
-    attended1, lse1 = attend(1, gate_pieces[2], out_pieces[2])
+    attended1, lse1 = attend(1, gate_pieces[2], up_pieces[3])
+    gate_pieces = gather_last(gate_pieces, attended1)
     down_pieces = gather_rest(narrowing_matrix, down_half, attended1)
 
     shared_rows = piece_rows(R, True)
@@ -798,15 +902,16 @@
         grid_spec=pltpu.PrefetchScalarGridSpec(
             num_scalar_prefetch=1,
             grid=(nblk,),
-            in_specs=[rowblk(PART), rowblk(PART), rowblk(D), whole((4, D))] + [ANY] * 7,
+            in_specs=[rowblk(PART), rowblk(PART), rowblk(D), whole((4, D))] + [ANY] * 8,
             out_specs=[rowblk(D), rowblk(LANE), rowblk(D), colblk(D), ANY],
             scratch_shapes=[pltpu.VMEM((D, D), bf16), pltpu.SemaphoreType.DMA((6,)), pltpu.SemaphoreType.DMA],
         ),
         out_shape=[shape((T, D), f32), shape((T, LANE), f32), shape((T, D), bf16), shape((D, T), bf16), shape((D, D), bf16)],
         **params(),
-    )(shared_rows, attended0, attended1, x, vectors, *out_pieces, down_pieces[2])
+    )(shared_rows, attended0, attended1, x, vectors, *out_pieces, down_pieces[2], gate_pieces[3])
 
     W = FF // nf
+    down_pieces = gather_last(down_pieces, low1)
     up_fac, gate_fac, prod, xhat2, inv2, pool, embed, full_up, full_gate, full_down = pl.pallas_call(
         ffn_kernel,
         grid_spec=pltpu.PrefetchScalarGridSpec(
@@ -838,12 +943,13 @@
     target = jnp.concatenate([matching_passages[0], jnp.zeros((SEGS - QSEG,), jnp.int32)])
     digits = jnp.pad(jnp.stack([target >> 5, target & 31], axis=1), ((0, 0), (0, LANE - 2))).astype(bf16)
     sent = jnp.concatenate([embed, digits], axis=1)
-    everyone = gather_relative(sent, "fsdp", nf)
     if nb == 8:
-        everyone = jnp.concatenate([everyone, xor_permute(everyone, "batch", nb, 1)])
-        everyone = jnp.stack([everyone] + [xor_permute(everyone, "batch", nb, 2 * z) for z in range(1, 4)])
+        everyone = jnp.stack([sent] + [xor_permute(sent, "batch", nb, 2 * z) for z in range(1, 4)])
+        everyone = jnp.stack([everyone, xor_permute(everyone, "fsdp", nf, 2)], axis=1)
+        everyone = jnp.stack([everyone, xor_permute(everyone, "batch", nb, 1)], axis=1)
+        everyone = jnp.stack([everyone, xor_permute(everyone, "fsdp", nf, 1)], axis=3)
     else:
-        everyone = gather_relative(everyone, "batch", nb)
+        everyone = gather_relative(gather_relative(sent, "fsdp", nf), "batch", nb)
     everyone = everyone.reshape(total_rows, D + LANE)
     rank_of = ((jnp.arange(nb)[:, None] ^ b) * nf + (jnp.arange(nf)[None, :] ^ f)).reshape(ranks, 1)
     place_of = jnp.arange(SEGS)[None, :]
@@ -884,82 +990,139 @@
             return xor_permute(value, "fsdp", nf, 2)
         return xor_permute(value, "batch", nb, 1 << BIT[axis])
 
+    def over_batch(total):
+        total = lax.psum(total.astype(f32), "batch").astype(bf16)
+        return [total[:4], total[4:]]
+
     class Reduce:
-        def __init__(self, keep, send, *order):
-            if nb != 8:
-                order = ("x", "y", "z0", "z1")
-            self.order, self.axes, self.stage = order, ["x", "y", "z1", "z0"], 0
-            view = (2, 2, 2, 2) + keep.shape[-2:]
-            self.terms = [keep.reshape(view), xor_permute(send, "fsdp", nf, 1).reshape(view)]
-
-        def step(self, *after):
-            self.stage += 1
-            if nb != 8 and self.stage > 1:
-                if self.stage == 2:
-                    total = lax.psum(sum([term.astype(f32) for term in self.terms]), "batch").astype(bf16)
-                    total = total.swapaxes(1, 2)
-                    self.parts = [total[k].reshape((4,) + total.shape[-2:]) for k in range(2)]
-                    self.out = self.parts[0]
-                return
-            self.terms[-1] = tie(self.terms[-1], *after)
-            if self.stage <= 4:
-                axis = self.order[self.stage - 1]
-                at = self.axes.index(axis)
-                self.axes.pop(at)
-                self.out = add(*[lax.index_in_dim(term, 1, at, keepdims=False) for term in self.terms])
-                self.terms = [lax.index_in_dim(term, 0, at, keepdims=False) for term in self.terms]
-                self.terms.append(across(self.out, axis))
-                return
-            axis = [axis for axis in self.order if axis != "x"][7 - self.stage]
-            if self.stage == 5:
-                self.out = add(*self.terms)[None]
+        def __init__(self, order, keep, send):
+            self.order, self.left, self.stage = order, 16, 0
+            self.terms = [[[0, keep]], [[0, xor_permute(send, "fsdp", nf, 1)]]]
+            self.arriving, self.pending = [], []
+
+        def pick(self, low, high):
+            found = []
+            for term in self.terms:
+                for start, array in term:
+                    if array is not None and start <= low and high <= start + array.shape[0]:
+                        found.append((array, low - start, high - low))
+                        break
+            return found
+
+        def wanted(self, which):
+            if which == "back":
+                rest = [axis for axis in self.order if axis != "x"]
+                self.pending.append((rest[6 - self.stage], None))
+                self.stage += 1
+                return [self.pick(0, 1)] if self.stage == 5 else [[(part, 0, part.shape[0])] for part in self.parts]
+            half = self.left // 2
+            middle = half + half // 2
+            low, high = dict(all=(half, self.left), far=(middle, self.left), near=(half, middle))[which]
+            sums = [self.pick(low, high)]
+            arrival = [low - half, None]
+            self.pending.append((self.order[self.stage], arrival))
+            self.arriving.append(arrival)
+            if which != "far":
+                self.terms.append(self.arriving)
+                self.arriving, self.left, self.stage = [], half, self.stage + 1
+            return sums
+
+        def go(self, out):
+            axis, arrival = self.pending.pop(0)
+            got = across(out, axis)
+            if arrival is None:
+                self.parts = [out, got]
             else:
-                self.out = jnp.concatenate(self.terms, axis=0)
-            self.terms = [self.out, across(self.out, axis)]
-            self.parts = self.terms
+                arrival[1] = got
+            return got
+
+    orders = [
+        ("x", "z0", "y", "z1"),
+        ("y", "x", "z0", "z1"),
+        ("x", "y", "z0", "z1"),
+        ("x", "z0", "y", "z1"),
+        ("x", "y", "z0", "z1"),
+    ]
+    if nb != 8:
+        orders = [("x", "y", "z0", "z1")] * 5
+
+    def plain_sum(pieces, after):
+        made = []
+        for terms in pieces:
+            arrays = [tie(array, *after) if after else array for array, _, _ in terms[-1:]]
+            arrays = [array for array, _, _ in terms[:-1]] + arrays
+            made.append(add(*[array[first : first + count] for array, (_, first, count) in zip(arrays, terms, strict=True)]))
+        return made[0] if len(made) == 1 else jnp.concatenate(made, axis=0)
+
+    def slot(after, *sends, apart=False):
+        if nb != 8:
+            sends = [
+                (group, which)
+                for k, (group, which) in enumerate(sends)
+                if group.stage == 0 and not any(other is group and kind != "far" for other, kind in sends[:k])
+            ]
+        if not sends:
+            return [], []
+        wanted = [group.wanted(which) for group, which in sends]
+        made = [plain_sum(pieces, after) for pieces in wanted] if apart else sums_of(wanted, after)
+        gots = [group.go(out) for (group, _), out in zip(sends, made, strict=True)]
+        for group, _ in sends:
+            if nb != 8 and group.stage == 1 and not hasattr(group, "parts"):
+                total = sum([array[first : first + count].astype(f32) for array, first, count in group.pick(0, 8)])
+                group.parts = over_batch(total)
+        return list(made), gots
 
     own_part = b if nb == 8 else 0
     info = jnp.stack([f, f ^ 1, f ^ 2, f ^ 3, own_part + 0 * f]).astype(jnp.int32)
     groups = W // BLOCK
 
-    def ffn_back(g, grad_hidden, *after):
-        wide = nf * BLOCK
-        parts = (2, 2, 4, R, PART)
+    wide = nf * BLOCK
+
+    def ffn_back(g, *after):
+        parts = (16, R, PART)
         return pl.pallas_call(
-            functools.partial(ffn_back_kernel, g, groups),
+            functools.partial(ffn_back_kernel, g, orders[g], groups),
             grid_spec=pltpu.PrefetchScalarGridSpec(
                 num_scalar_prefetch=1,
                 grid=(1,),
-                in_specs=[ANY] * (10 + len(after)),
-                out_specs=[ANY] * 3,
+                in_specs=[ANY] * (7 + len(after)),
+                out_specs=[ANY] * 4,
                 scratch_shapes=[pltpu.VMEM((T, wide), bf16)] * 3
                 + [pltpu.VMEM((T, D), bf16), pltpu.VMEM((D, T), bf16), pltpu.VMEM((D, T), bf16)]
-                + [pltpu.VMEM((D, wide), bf16)] * 2
-                + [pltpu.VMEM((wide, D), bf16), pltpu.VMEM((T, D), f32)]
+                + [pltpu.VMEM((wide, D), bf16), pltpu.VMEM((2, T, wide), bf16)]
                 + [pltpu.VMEM(parts, bf16)] * 2
-                + [pltpu.VMEM((T, D), f32), pltpu.SemaphoreType.DMA((28,)), pltpu.SemaphoreType.DMA((3,))],
+                + [pltpu.SemaphoreType.DMA((20,)), pltpu.SemaphoreType.DMA((4,))],
             ),
-            out_shape=[shape((T, D), f32)] + [shape(parts, bf16)] * 2,
+            out_shape=[shape((T, wide), bf16)] * 2 + [shape(parts, bf16)] * 2,
             **params(),
-        )(
-            info, prod, up_fac, gate_fac, grad_low, grad_low_turned, low1_turned, full_up, full_gate, full_down,
-            grad_hidden, *after,
-        )
-
-    grad_hidden, keep, send = ffn_back(0, sum_two)
-    r0 = Reduce(keep, send, "x", "z0", "y", "z1")
-    grad_hidden, keep, send = ffn_back(1, grad_hidden)
-    r1 = Reduce(keep, send, "y", "x", "z0", "z1")
-    r0.step(grad_hidden)
-    grad_hidden, keep, send = ffn_back(2, grad_hidden, r0.out)
-    r2 = Reduce(keep, send, "x", "y", "z0", "z1")
-    r1.step(grad_hidden)
-
-    heads = (
-        (jnp.arange(PAIRS * 8)[:, None] // 8 * 2 + jnp.arange(PAIRS * 8)[:, None] % 8 == jnp.arange(D)[None, :] // HD)
-        & (jnp.arange(PAIRS * 8)[:, None] % 8 < 2)
-    ).astype(bf16)
-    sum_one, grad_branch, grad_att, delta, att_turned, small_one = pl.pallas_call(
+        )(info, prod, up_fac, gate_fac, grad_low, grad_low_turned, low1_turned, full_down, *after)
+
+    dup0, dgate0, keep, send = ffn_back(0)
+    r0 = Reduce(orders[0], keep, send)
+    dup1, dgate1, keep, send = ffn_back(1, send)
+    r1 = Reduce(orders[1], keep, send)
+    outs, gots = slot([dup1], (r0, "far"))
+    dup2, dgate2, keep, send = ffn_back(2, send, *outs)
+    r2 = Reduce(orders[2], keep, tie(send, *gots))
+    outs, gots = slot([dup2] + gots, (r0, "near"), (r0, "all"), (r1, "far"))
+    grad_hidden = pl.pallas_call(
+        functools.partial(ffn_input_back_kernel, groups),
+        in_specs=[ANY] * (3 + 2 * groups + len(outs)),
+        out_specs=ANY,
+        scratch_shapes=[
+            pltpu.VMEM((2 * groups, T, wide), bf16),
+            pltpu.VMEM((groups, D, wide), bf16),
+            pltpu.VMEM((groups, D, wide), bf16),
+            pltpu.VMEM((T, D), f32),
+            pltpu.SemaphoreType.DMA((groups * 10 + 1,)),
+            pltpu.SemaphoreType.DMA,
+        ],
+        out_shape=shape((T, D), f32),
+        **params(),
+    )(full_up, full_gate, sum_two, dup0, dgate0, dup1, dgate1, dup2, dgate2, *outs)
+    outs, gots = slot([grad_hidden] + gots, (r1, "near"), (r2, "far"))
+
+    sum_one, grad_branch, grad_att, delta, att_turned, small = pl.pallas_call(
         mixer_back_kernel,
         grid_spec=pltpu.PrefetchScalarGridSpec(
             num_scalar_prefetch=1,
@@ -973,16 +1136,18 @@
                 rowblk(PART),
                 whole((D, D)),
                 whole((PAIRS * 8, D)),
-                ANY,
-            ],
+                whole((8, D)),
+            ]
+            + [ANY] * len(outs),
             out_specs=[
                 rowblk(D),
                 rowblk(D),
                 rowblk(D),
                 pl.BlockSpec((PAIRS, 8, BLOCK), lambda i, *_: (0, 0, i)),
                 colblk(D),
-                whole((8, D)),
+                whole((nf, 2, SMALL, PART)),
             ],
+            scratch_shapes=[pltpu.VMEM((8, D), f32)],
         ),
         out_shape=[
             shape((T, D), f32),
@@ -990,12 +1155,11 @@
             shape((T, D), bf16),
             shape((PAIRS, 8, T), f32),
             shape((D, T), bf16),
-            shape((8, D), f32),
+            shape((nf, 2, SMALL, PART), f32),
         ],
         **params(),
-    )(info, grad_hidden, xhat1, inv1, vectors, attended0, attended1, full_out, heads, r1.out)
-    r2.step(grad_branch)
-    r0.step(grad_branch)
+    )(info, grad_hidden, xhat1, inv1, vectors, attended0, attended1, full_out, heads, small_two, *outs)
+    outs, gots = slot([grad_branch] + gots, (r0, "all"), (r1, "all"))
 
     def attend_back(h, *after):
         def cols(part, rows=None):
@@ -1030,15 +1194,10 @@
             **params(),
         )(lo, spans, qkv, qkv, qkv, grad_att, (lse0, lse1)[h], delta, mask_q, mask_k, cosine, sine, cosine, sine, *after)
 
-    small = jnp.stack([small_one[0], small_one[1], small_two[0], small_two[1]]).reshape(4, nf, R)
-    small = small.transpose(1, 0, 2).reshape(nf, 2, 1, 2 * R)
-    small = jnp.pad(small, ((0, 0), (0, 0), (0, SMALL - 1), (0, 0)))
-
     def qkv_back(h, grads, extra, *after):
-        dims = (2, 2, 4, R // 2 + extra, PART)
-        parts = pl.BlockSpec(dims[:2] + (1,) + dims[3:], lambda c, info: (0, 0, c ^ (info[4] >> 1), 0, 0))
+        dims = (16, R // 2 + extra, PART)
         return pl.pallas_call(
-            functools.partial(qkv_back_kernel, extra),
+            functools.partial(qkv_back_kernel, extra, orders[3 + h]),
             grid_spec=pltpu.PrefetchScalarGridSpec(
                 num_scalar_prefetch=1,
                 grid=(4,),
@@ -1046,53 +1205,48 @@
                 + [whole((T, PART))] * 3
                 + [pl.BlockSpec((T, PART), lambda c, *_: (0, h)), whole((nf, 2, SMALL, PART))]
                 + [ANY] * len(after),
-                out_specs=[parts, parts],
+                out_specs=[whole(dims)] * 2,
             ),
             out_shape=[shape(dims, bf16)] * 2,
             **params(),
         )(info, x_turned, att_turned, *grads, grad_branch, small, *after)
 
-    grads0 = attend_back(0, r2.out, r0.out)
-    r0.step(grads0[0])
-    r1.step(grads0[0])
-    keep, send = qkv_back(0, grads0, SMALL, r0.out, r1.out)
-    r3 = Reduce(keep, send, "x", "z0", "y", "z1")
-    r0.step(keep)
-    r2.step(keep)
-    grads1 = attend_back(1, r0.out, r2.out)
-    r3.step(grads1[0])
-    r0.step(grads1[0])
-    r1.step(grads1[0])
-    r2.step(grads1[0])
-    keep, send = qkv_back(1, grads1, 0, r3.out, r0.out, r1.out, r2.out)
-    r4 = Reduce(keep, send, "x", "y", "z0", "z1")
-    r0.step(keep)
-    r1.step(keep)
-    r2.step(keep)
-    r4.step(r0.out, r1.out, r2.out)
+    grads0 = attend_back(0, *outs)
+    outs, gots = slot([grads0[0]] + gots, (r2, "near"), (r2, "far"), (r0, "all"), (r1, "all"))
+    keep, send = qkv_back(0, grads0, SMALL, *outs)
+    r3 = Reduce(orders[3], keep, tie(send, *gots))
+    outs, gots = slot([keep] + gots, (r0, "back"), (r1, "all"), (r2, "near"), (r2, "all"), (r3, "all"))
+    grads1 = attend_back(1, *outs)
+    outs, gots = slot([grads1[0]] + gots, (r0, "back"), (r1, "back"), (r2, "all"), (r3, "all"))
+    keep, send = qkv_back(1, grads1, 0, *outs)
+    r4 = Reduce(orders[4], keep, tie(send, *gots))
+    outs, gots = slot([keep] + gots, (r0, "back"), (r1, "back"), (r2, "back"), (r3, "all"))
+    more = slot([], (r4, "all"), apart=True)
+    outs = outs + more[0]
 
     grad_input = pl.pallas_call(
         input_back_kernel,
         grid_spec=pltpu.PrefetchScalarGridSpec(
             num_scalar_prefetch=1,
             grid=(nblk,),
-            in_specs=[rowblk(PART)] * 6 + [rowblk(D)] + [ANY] * 5,
+            in_specs=[rowblk(PART)] * 6 + [rowblk(D)] + [ANY] * (4 + len(outs)),
             out_specs=rowblk(D),
             scratch_shapes=[pltpu.VMEM((D, 3 * D), bf16), pltpu.SemaphoreType.DMA((4,))],
         ),
         out_shape=shape((T, D), f32),
         **params(),
-    )(whole_rows, *grads0, *grads1, sum_one, *qkv_pieces, r4.out)
-
-    def together(groups, *after):
-        for group in groups:
-            group.step(*after)
-        return [group.out for group in groups]
-
-    last = together([r3, r0, r1, r2], grad_input)
-    last = together([r4, r3, r1, r2], *last)
-    last = together([r4, r3, r1, r2], *last)
-    last = together([r4, r3], *last)
+    )(whole_rows, *grads0, *grads1, sum_one, *qkv_pieces, *outs)
+
+    outs, _ = slot([grad_input], (r4, "all"), apart=True)
+    slot(outs, (r1, "back"), (r2, "back"), (r3, "all"), apart=True)
+    outs, _ = slot([], (r4, "all"), apart=True)
+    slot(outs, (r2, "back"), (r3, "back"), apart=True)
+    outs, _ = slot([], (r4, "all"), apart=True)
+    slot(outs, (r3, "back"), apart=True)
+    outs, _ = slot([], (r4, "back"), apart=True)
+    slot(outs, (r3, "back"), apart=True)
+    slot([], (r4, "back"), apart=True)
+    slot([], (r4, "back"), apart=True)
     sum_up, sum_gate, sum_down = pl.pallas_call(
         functools.partial(ffn_out_kernel, (r0.order, r1.order, r2.order)),
         grid_spec=pltpu.PrefetchScalarGridSpec(
@@ -1104,9 +1258,6 @@
         out_shape=[shape((R, FF), f32), shape((R, FF), f32), shape((W, D), f32)],
         **params(),
     )(info, *r0.parts, *r1.parts, *r2.parts)
-    last = together([r4, r3], *last)
-    last = together([r4, r3], sum_up, *last)
-    last = together([r4], *last)
     sum_qkv, sum_out, sum_small = pl.pallas_call(
         functools.partial(qkv_out_kernel, (r3.order, r4.order)),
         grid_spec=pltpu.PrefetchScalarGridSpec(

time: 534 us -> 454 us (0.85)
  waiting for transfers between devices: 115 us -> 77 us
  other arithmetic: 56.1 us -> 18.9 us
  Pallas kernels: 237 us -> 261 us
  local copies, waits for them, and re-layouts: 48.2 us -> 28.4 us
  starting transfers between devices: 67.7 us -> 58.9 us
    ppermute x73 -> x72, waiting for transfers between devices: 115 us -> 77 us  [xor_permute(): return lax.ppermute(value, axis, [(i, i ^ bits) for i in range(size)])]
    pallas_call x5 -> x14, Pallas kernels: 74 us -> 98.2 us  [the longest x3 39.1 us: ffn_back(): pl.pallas_call(functools.partial(ffn_back_kernel, g, orders[g], groups),...]
    convert_element_type x17 -> x7, other arithmetic: 23.5 us -> 3.68 us  [add(): return sum([term.astype(f32) for term in terms]).astype(bf16)]
    squeeze x9 -> x0, local copies, waits for them, and re-layouts: 11.9 us -> none  [step(): lax.index_in_dim(term, 0, at, keepdims=False)]
    slice x8 -> x0, local copies, waits for them, and re-layouts: 11.5 us -> none  [the longest x4 7.68 us: step(): lax.index_in_dim(term, 0, at, keepdims=False)]
    ppermute x73 -> x72, starting transfers between devices: 67.7 us -> 58.9 us  [xor_permute(): return lax.ppermute(value, axis, [(i, i ^ bits) for i in range(size)])]
    unnamed x135 -> x133, local copies, waits for them, and re-layouts: 5.78 us -> 12.1 us
    broadcast_in_dim x5 -> x0, other arithmetic: 6 us -> none  [step(): self.out = add(*self.terms)[None]]
  transfers between devices with their start and end apart: 73 -> 72, of which waited for: 25 -> 24; matrix products, arithmetic and copies ran while one was open for 18% -> 7% of each run, Pallas kernels for 31% -> 42%
where the time goes in v2:
time: 454 us; the launch traced here: 447 us
  Pallas kernels  261 us (57%)
  waiting for transfers between devices  77 us (17%)
  starting transfers between devices  58.9 us (13%)
  local copies, waits for them, and re-layouts  28.4 us (6%)
  other arithmetic  18.9 us (4%)
    ppermute x72, waiting for transfers between devices, xor_permute(): return lax.ppermute(value, axis, [(i, i ^ bits) for i in range(size)])  77 us
    ppermute x72, starting transfers between devices, xor_permute(): return lax.ppermute(value, axis, [(i, i ^ bits) for i in range(size)])  58.9 us
    pallas_call x3, Pallas kernels, ffn_back(): pl.pallas_call(functools.partial(ffn_back_kernel, g, orders[g], groups),...  39.1 us
    pallas_call x2, Pallas kernels, attend_back(): pl.pallas_call(kernel, grid_spec=pltpu.PrefetchScalarGridSpec(num_scalar_...  37.4 us
    pallas_call x1, Pallas kernels, per_device(): pl.pallas_call(ffn_kernel, grid_spec=pltpu.PrefetchScalarGridSpec(num_sca...  30.4 us
    pallas_call x2, Pallas kernels, attend(): pl.pallas_call(functools.partial(drop_last, attend_kernel, len(after), 7)...  28 us
    pallas_call x8, Pallas kernels, sums_of(): pl.pallas_call(functools.partial(drop_last, functools.partial(sums_kernel...  24.6 us
    pallas_call x2, Pallas kernels, qkv_back(): pl.pallas_call(functools.partial(qkv_back_kernel, extra, orders[3 + h]),...  18 us
  transfers between devices with their start and end apart: 72, of which 24 were waited for; matrix products, arithmetic and copies ran while one was open for 7% of the time, Pallas kernels for 42%

profile of v2, /device:TPU:0, one launch (start us, length us, event | category | flops | bytes accessed | tf_op | source)
XLA Modules:
  0.0 446.9 jit_solution(6928169800442012733)
XLA Ops:
  1.2 2.6 collective-permute-start.1
  7.0 1.8 collective-permute-start.3
  11.7 1.6 select_convert_fusion.refs_6_.refs_9_
  13.3 1.6 constant_dynamic-slice_fusion.2
  14.9 2.1 constant_dynamic-slice_fusion.1
  17.9 3.8 fusion
  25.7 1.8 collective-permute-start.6
  29.4 13.9 %shard_map.212 = (bf16[1024,2304]{1,0:T(8,128)(2,1)}, bf16[768,1024]{1,0:T(8,128)(2,1)}) custom-call(s32[7]{0:T(128)} %stack.156.rows_ref, bf16[1024,768]{1,0:T(8,128)(2,1)} %bitcast.62, f32[1024,128]{1,0:T(8,128)} %get-tuple-element.258.cos_ref.refs_10_.refs_12_, f32[1024,128]{1,0:T(8,128)} %get-tuple-element.257.sin_ref.refs_11_.refs_13_, ...), custom_call_target="tpu_custom_call" | custom-call | flops 1 | bytes 1 | tf_op jit(solution)/shard_map/pallas_call | solution.py:850
  43.3 1.5 collective-permute-done.6.refs_7_.refs_2_
  44.8 1.8 collective-permute-start.8
  49.4 14.0 %shard_map.213 = (bf16[1024,384]{1,0:T(8,128)(2,1)}, f32[3,8,1024]{2,1,0:T(8,128)}) custom-call(s32[4]{0:T(128)} %get-tuple-element.244.refs_0_, s32[4]{0:T(128)} %get-tuple-element.243.refs_1_, bf16[1024,2304]{1,0:T(8,128)(2,1)} %get-tuple-element.127.refs_2_.refs_3_.refs_4_, bf16[1024,2304]{1,0:T(8,128)(2,1)} %get-tuple-element.127.refs_2_.refs_3_.refs_4_, ...), custom_call_target="tpu_custom_call" | custom-call | flops 1 | bytes 1 | tf_op jit(solution)/shard_map/pallas_call | solution.py:870
  64.8 9.3 %collective-permute-done.12.refs_6_.refs_14_ = bf16[384,768]{1,0:T(8,128)(2,1)} collective-permute-done((bf16[384,768]{1,0:T(8,128)(2,1)}, bf16[384,768]{1,0:T(8,128)(2,1)}, u32[]{:S(2)}, u32[]{:S(2)}) %collective-permute-start.12) | collective-permute-done | bytes 589856 | tf_op jit(solution)/shard_map/ppermute | solution.py:688
  74.7 14.0 %shard_map.214 = (bf16[1024,384]{1,0:T(8,128)(2,1)}, f32[3,8,1024]{2,1,0:T(8,128)}) custom-call(s32[4]{0:T(128)} %get-tuple-element.244.refs_0_, s32[4]{0:T(128)} %get-tuple-element.243.refs_1_, bf16[1024,2304]{1,0:T(8,128)(2,1)} %get-tuple-element.127.refs_2_.refs_3_.refs_4_, bf16[1024,2304]{1,0:T(8,128)(2,1)} %get-tuple-element.127.refs_2_.refs_3_.refs_4_, ...), custom_call_target="tpu_custom_call" | custom-call | flops 1 | bytes 1 | tf_op jit(solution)/shard_map/pallas_call | solution.py:870
  91.3 9.1 %shard_map.215 = (f32[1024,768]{1,0:T(8,128)}, f32[1024,128]{1,0:T(8,128)}, bf16[1024,768]{1,0:T(8,128)(2,1)}, bf16[768,1024]{1,0:T(8,128)(2,1)}, bf16[768,768]{1,0:T(8,128)(2,1)}) custom-call(s32[9]{0:T(128)} %stack.153.rows_ref, bf16[1024,384]{1,0:T(8,128)(2,1)} %get-tuple-element.130.att0_ref, bf16[1024,384]{1,0:T(8,128)(2,1)} %get-tuple-element.133.att1_ref, ...), custom_call_target="tpu_custom_call" | custom-call | flops 1 | bytes 1 | tf_op jit(solution)/shard_map/pallas_call | solution.py:900
  100.4 5.4 %collective-permute-done.19.refs_15_ = bf16[384,768]{1,0:T(8,128)(2,1)S(1)} collective-permute-done((bf16[384,768]{1,0:T(8,128)(2,1)}, bf16[384,768]{1,0:T(8,128)(2,1)S(1)}, u32[]{:S(2)}, u32[]{:S(2)}) %collective-permute-start.19) | collective-permute-done | bytes 589856 | tf_op jit(solution)/shard_map/ppermute | solution.py:688
  107.1 2.6 collective-permute-done.17.refs_11_
  110.9 30.4 %shard_map.216 = (bf16[1024,3072]{1,0:T(8,128)(2,1)}, bf16[1024,3072]{1,0:T(8,128)(2,1)}, bf16[1024,3072]{1,0:T(8,128)(2,1)}, f32[1024,768]{1,0:T(8,128)}, f32[1...) custom-call(s32[9]{0:T(128)} %stack.153.rows_ref, ...), custom_call_target="tpu_custom_call" | custom-call | flops 1 | bytes 1 | tf_op jit(solution)/shard_map/pallas_call | solution.py:915
  142.0 3.5 collective-permute-start.24
  147.5 2.6 collective-permute-done.23
  151.5 2.9 collective-permute-done.25
  155.1 4.2 collective-permute-done.26
  162.4 3.1 shard_map.217
  165.5 6.9 %shard_map.218 = (f32[1024,768]{1,0:T(8,128)}, bf16[1024,768]{1,0:T(8,128)(2,1)}, bf16[768,1024]{1,0:T(8,128)(2,1)}) custom-call(bf16[1024,128]{1,0:T(8,128)(2,1)} %fusion.2.refs_5_.mq_ref.refs_8_, f32[128,768]{1,0:T(8,128)} %get-tuple-element.150.rows_ref, f32[1024,768]{1,0:T(8,128)} %get-tuple-element.151.xhat_ref, ...), custom_call_target="tpu_custom_call" | custom-call | flops 1 | bytes 1 | tf_op jit(solution)/shard_map/pallas_call | solution.py:976
  172.5 12.9 %shard_map.219 = (bf16[1024,1024]{1,0:T(8,128)(2,1)}, bf16[1024,1024]{1,0:T(8,128)(2,1)}, bf16[16,192,384]{2,1,0:T(8,128)(2,1)}, bf16[16,192,384]{2,1,0:T(8,128)(2,1)}) custom-call(s32[5]{0:T(128)} %stack.188.info_ref, bf16[1024,3072]{1,0:T(8,128)(2,1)} %get-tuple-element.154.prod_any, bf16[1024,3072]{1,0:T(8,128)(2,1)} %get-tuple-element.155.up_fac_any, ...), custom_call_target="tpu_custom_call" | custom-call | flops 1 | bytes 1 | tf_op jit(solution)/shard_map/pallas_call | solution.py:1083
  186.0 12.9 %shard_map.220 = (bf16[1024,1024]{1,0:T(8,128)(2,1)}, bf16[1024,1024]{1,0:T(8,128)(2,1)}, bf16[16,192,384]{2,1,0:T(8,128)(2,1)}, bf16[16,192,384]{2,1,0:T(8,128)(2,1)}) custom-call(s32[5]{0:T(128)} %stack.188.info_ref, bf16[1024,3072]{1,0:T(8,128)(2,1)} %get-tuple-element.154.prod_any, bf16[1024,3072]{1,0:T(8,128)(2,1)} %get-tuple-element.155.up_fac_any, ...), custom_call_target="tpu_custom_call" | custom-call | flops 1 | bytes 1 | tf_op jit(solution)/shard_map/pallas_call | solution.py:1083
  200.4 2.2 shard_map.221.refs_1_
  203.9 13.3 %shard_map.222 = (bf16[1024,1024]{1,0:T(8,128)(2,1)}, bf16[1024,1024]{1,0:T(8,128)(2,1)}, bf16[16,192,384]{2,1,0:T(8,128)(2,1)}, bf16[16,192,384]{2,1,0:T(8,128)(2,1)}) custom-call(s32[5]{0:T(128)} %stack.188.info_ref, bf16[1024,3072]{1,0:T(8,128)(2,1)} %get-tuple-element.154.prod_any, bf16[1024,3072]{1,0:T(8,128)(2,1)} %get-tuple-element.155.up_fac_any, ...), custom_call_target="tpu_custom_call" | custom-call | flops 1 | bytes 1 | tf_op jit(solution)/shard_map/pallas_call | solution.py:1083
  219.3 3.6 shard_map.223
  224.8 16.5 %shard_map.224.refs_4_.grad_ref = f32[1024,768]{1,0:T(8,128)} custom-call(bf16[768,3072]{1,0:T(8,128)(2,1)} %get-tuple-element.148.wu_any, bf16[768,3072]{1,0:T(8,128)(2,1)} %get-tuple-element.149.wg_any, f32[1024,768]{1,0:T(8,128)} %get-tuple-element.153.hid_any, bf16[1024,1024]{1,0:T(8,128)(2,1)} %get-tuple-element.161.refs_0_, ...), custom_call_target="tpu_custom_call" | custom-call | flops 1 | bytes 1 | tf_op jit(solution)/shard_map/pallas_call | solution.py:1108
  243.3 2.8 shard_map.225
  246.1 1.7 collective-permute-start.35
  249.1 11.2 %shard_map.226 = (f32[1024,768]{1,0:T(8,128)}, bf16[1024,768]{1,0:T(8,128)(2,1)}, bf16[1024,768]{1,0:T(8,128)(2,1)}, f32[6,8,1024]{2,1,0:T(8,128)}, bf16[768,102...) custom-call(s32[5]{0:T(128)} %stack.188.info_ref, f32[1024,768]{1,0:T(8,128)} %shard_map.224.refs_4_.grad_ref, ...), custom_call_target="tpu_custom_call" | custom-call | flops 1 | bytes 1 | tf_op jit(solution)/shard_map/pallas_call | solution.py:1125
  262.7 3.0 shard_map.227
  266.9 18.9 %shard_map.228 = (bf16[1024,384]{1,0:T(8,128)(2,1)}, bf16[1024,384]{1,0:T(8,128)(2,1)}, bf16[1024,384]{1,0:T(8,128)(2,1)}) custom-call(s32[4]{0:T(128)} %get-tuple-element.244.refs_0_, s32[4]{0:T(128)} %get-tuple-element.243.refs_1_, bf16[1024,2304]{1,0:T(8,128)(2,1)} %get-tuple-element.127.refs_2_.refs_3_.refs_4_, ...), custom_call_target="tpu_custom_call" | custom-call | flops 1 | bytes 1 | tf_op jit(solution)/shard_map/pallas_call | solution.py:1170
  286.8 3.3 shard_map.229
  290.1 2.3 collective-permute-start.41
  293.1 3.6 collective-permute-start.39
  296.7 9.0 %shard_map.230 = (bf16[16,112,384]{2,1,0:T(8,128)(2,1)}, bf16[16,112,384]{2,1,0:T(8,128)(2,1)}) custom-call(s32[5]{0:T(128)} %stack.188.info_ref, bf16[768,1024]{1,0:T(8,128)(2,1)} %get-tuple-element.196.xt_ref, bf16[768,1024]{1,0:T(8,128)(2,1)} %get-tuple-element.197.attt_ref, bf16[1024,384]{1,0:T(8,128)(2,1)} %get-tuple-element.188.refs_14_.gq_ref.gq0, ...), custom_call_target="tpu_custom_call" | custom-call | flops 1 | bytes 1 | tf_op jit(solution)/shard_map/pallas_call | solution.py:1199
  305.9 3.3 collective-permute-done.43.refs_19_.refs_14_.refs_11_
  310.3 4.0 shard_map.231
  314.3 1.8 collective-permute-start.48
  317.2 2.5 collective-permute-start.45
  319.8 18.5 %shard_map.232 = (bf16[1024,384]{1,0:T(8,128)(2,1)}, bf16[1024,384]{1,0:T(8,128)(2,1)}, bf16[1024,384]{1,0:T(8,128)(2,1)}) custom-call(s32[4]{0:T(128)} %get-tuple-element.244.refs_0_, s32[4]{0:T(128)} %get-tuple-element.243.refs_1_, bf16[1024,2304]{1,0:T(8,128)(2,1)} %get-tuple-element.127.refs_2_.refs_3_.refs_4_, ...), custom_call_target="tpu_custom_call" | custom-call | flops 1 | bytes 1 | tf_op jit(solution)/shard_map/pallas_call | solution.py:1170
  339.5 3.0 shard_map.233
  342.4 1.7 collective-permute-start.52
  344.2 2.6 collective-permute-start.50
  347.1 8.9 %shard_map.234 = (bf16[16,96,384]{2,1,0:T(8,128)(2,1)}, bf16[16,96,384]{2,1,0:T(8,128)(2,1)}) custom-call(s32[5]{0:T(128)} %stack.188.info_ref, bf16[768,1024]{1,0:T(8,128)(2,1)} %get-tuple-element.196.xt_ref, bf16[768,1024]{1,0:T(8,128)(2,1)} %get-tuple-element.197.attt_ref, bf16[1024,384]{1,0:T(8,128)(2,1)} %get-tuple-element.207.refs_16_.gq_ref.gq1, ...), custom_call_target="tpu_custom_call" | custom-call | flops 1 | bytes 1 | tf_op jit(solution)/shard_map/pallas_call | solution.py:1199
  356.0 2.1 collective-permute-done.50.refs_3_.refs_16_
  358.1 2.1 collective-permute-done.51.refs_9_.refs_17_
  360.3 3.0 collective-permute-done.53
  366.0 2.8 shard_map.235
  369.4 2.0 collective-permute-start.67
  371.6 11.5 %shard_map.236 = f32[1024,768]{1,0:T(8,128)} custom-call(s32[7]{0:T(128)} %stack.156.rows_ref, bf16[1024,384]{1,0:T(8,128)(2,1)} %get-tuple-element.188.refs_14_.gq_ref.gq0, bf16[1024,384]{1,0:T(8,128)(2,1)} %get-tuple-element.189.gk_ref.gk0, bf16[1024,384]{1,0:T(8,128)(2,1)} %get-tuple-element.190.gv_ref.gv0, ...), custom_call_target="tpu_custom_call" | custom-call | flops 1 | bytes 1 | tf_op jit(solution)/shard_map/pallas_call | solution.py:1227
  385.9 3.0 collective-permute-start.56
  388.9 6.9 %collective-permute-done.67 = bf16[2,192,384]{2,1,0:T(8,128)(2,1)} collective-permute-done((bf16[2,192,384]{2,1,0:T(8,128)(2,1)}, bf16[2,192,384]{2,1,0:T(8,128)(2,1)}, u32[]{:S(2)}, u32[]{:S(2)}) %collective-permute-start.67) | collective-permute-done | bytes 294944 | tf_op jit(solution)/shard_map/ppermute | solution.py:688
  396.8 1.7 collective-permute-start.68
  399.6 2.1 collective-permute-start.58
  402.9 7.3 %collective-permute-done.70 = bf16[2,192,384]{2,1,0:T(8,128)(2,1)S(1)} collective-permute-done((bf16[2,192,384]{2,1,0:T(8,128)(2,1)S(1)}, bf16[2,192,384]{2,1,0:T(8,128)(2,1)S(1)}, u32[]{:S(2)}, u32[]{:S(2)}) %collective-permute-start.70) | collective-permute-done | bytes 294944 | tf_op jit(solution)/shard_map/ppermute | solution.py:688
  412.0 6.7 %collective-permute-done.60 = bf16[1,96,384]{2,1,0:T(8,128)(2,1)S(1)} collective-permute-done((bf16[1,96,384]{2,1,0:T(8,128)(2,1)S(1)}, bf16[1,96,384]{2,1,0:T(8,128)(2,1)S(1)}, u32[]{:S(2)}, u32[]{:S(2)}) %collective-permute-start.60) | collective-permute-done | bytes 73760 | tf_op jit(solution)/shard_map/ppermute | solution.py:688
  419.5 4.5 %collective-permute-done.63 = bf16[1,96,384]{2,1,0:T(8,128)(2,1)S(1)} collective-permute-done((bf16[1,96,384]{2,1,0:T(8,128)(2,1)S(1)}, bf16[1,96,384]{2,1,0:T(8,128)(2,1)S(1)}, u32[]{:S(2)}, u32[]{:S(2)}) %collective-permute-start.63) | collective-permute-done | bytes 73760 | tf_op jit(solution)/shard_map/ppermute | solution.py:688
  424.1 3.0 collective-permute-done.61
  427.2 3.6 collective-permute-done.64
  432.4 7.7 %shard_map.238 = (f32[192,3072]{1,0:T(8,128)}, f32[192,3072]{1,0:T(8,128)}, f32[768,768]{1,0:T(8,128)}) custom-call(s32[5]{0:T(128)} %stack.188.info_ref, bf16[4,192,384]{2,1,0:T(8,128)(2,1)} %get-tuple-element.216.refs_4_.refs_0_, bf16[4,192,384]{2,1,0:T(8,128)(2,1)} %collective-permute-done.66.refs_1_, bf16[4,192,384]{2,1,0:T(8,128)(2,1)} %copy-done.28, ...), custom_call_target="tpu_custom_call" | custom-call | flops 1 | bytes 1 | tf_op jit(solution)/shard_map/pallas_call | solution.py:1250
  441.6 3.6 shard_map.237
  (312 shorter events, 66.7 us)
Async XLA Ops:
  0.7 27.5 %collective-permute-start = (bf16[192,2304]{1,0:T(8,128)(2,1)}, bf16[192,2304]{1,0:T(8,128)(2,1)S(1)}, u32[]{:S(2)}, u32[]{:S(2)}) collective-permute-start(bf16[192,2304]{1,0:T(8,128)(2,1)} %refs_0_.7), channel_id=1, source_target_pairs={{0,1},{1,0},{2,3},{3,2},{4,5},{5,4},{6,7},{7,6},{8,9},{9,8},{10,11... | collective-permute-start | bytes 2654216 | tf_op jit(solution)/shard_map/ppermute | solution.py:688
  1.2 24.5 %collective-permute-start.1 = (bf16[192,2304]{1,0:T(8,128)(2,1)}, bf16[192,2304]{1,0:T(8,128)(2,1)S(1)}, u32[]{:S(2)}, u32[]{:S(2)}) collective-permute-start(bf16[192,2304]{1,0:T(8,128)(2,1)} %refs_0_.7), channel_id=1, source_target_pairs={{0,2},{1,3},{2,0},{3,1},{4,6},{5,7},{6,4},{7,5},{8,10},{9,11},{10,... | collective-permute-start | bytes 2654216 | tf_op jit(solution)/shard_map/ppermute | solution.py:688
  7.0 17.1 %collective-permute-start.4 = (bf16[4,192]{1,0:T(4,128)(2,1)}, bf16[4,192]{1,0:T(4,128)(2,1)}, u32[]{:S(2)}, u32[]{:S(2)}) collective-permute-start(bf16[4,192]{1,0:T(4,128)(2,1)} %pad_maximum_fusion.8), channel_id=1, source_target_pairs={{0,3},{1,2},{2,1},{3,0},{4,7},{5,6},{6,5},{7,4},{8,11},{9,10},{10,... | collective-permute-start | bytes 4616 | tf_op jit(solution)/shard_map/ppermute | solution.py:688
  7.0 17.4 %collective-permute-start.3 = (bf16[4,192]{1,0:T(4,128)(2,1)}, bf16[4,192]{1,0:T(4,128)(2,1)}, u32[]{:S(2)}, u32[]{:S(2)}) collective-permute-start(bf16[4,192]{1,0:T(4,128)(2,1)} %pad_maximum_fusion.8), channel_id=1, source_target_pairs={{0,2},{1,3},{2,0},{3,1},{4,6},{5,7},{6,4},{7,5},{8,10},{9,11},{10,... | collective-permute-start | bytes 4616 | tf_op jit(solution)/shard_map/ppermute | solution.py:688
  8.8 15.6 %collective-permute-start.2 = (bf16[4,192]{1,0:T(4,128)(2,1)}, bf16[4,192]{1,0:T(4,128)(2,1)}, u32[]{:S(2)}, u32[]{:S(2)}) collective-permute-start(bf16[4,192]{1,0:T(4,128)(2,1)} %pad_maximum_fusion.8), channel_id=1, source_target_pairs={{0,1},{1,0},{2,3},{3,2},{4,5},{5,4},{6,7},{7,6},{8,9},{9,8},{10,11... | collective-permute-start | bytes 4616 | tf_op jit(solution)/shard_map/ppermute | solution.py:688
  25.7 19.1 %collective-permute-start.6 = (bf16[96,3840]{1,0:T(8,128)(2,1)}, bf16[96,3840]{1,0:T(8,128)(2,1)S(1)}, u32[]{:S(2)}, u32[]{:S(2)}) collective-permute-start(bf16[96,3840]{1,0:T(8,128)(2,1)} %pad_maximum_fusion), channel_id=1, source_target_pairs={{0,2},{1,3},{2,0},{3,1},{4,6},{5,7},{6,4},{7,5},{8,10},{9,11},{10,... | collective-permute-start | bytes 2211848 | tf_op jit(solution)/shard_map/ppermute | solution.py:688
  44.8 18.6 %collective-permute-start.8 = (bf16[96,3840]{1,0:T(8,128)(2,1)S(1)}, bf16[96,3840]{1,0:T(8,128)(2,1)S(1)}, u32[]{:S(2)}, u32[]{:S(2)}) collective-permute-start(bf16[96,3840]{1,0:T(8,128)(2,1)S(1)} %collective-permute-done.6.refs_7_.refs_2_), channel_id=1, source_target_pairs={{0,4},{4,0},{8,12},{12,8},{16,20},{20,16},{24,28},{28,24},{1,5},{5... | collective-permute-start | bytes 2211848 | tf_op jit(solution)/shard_map/ppermute | solution.py:688
  46.6 17.8 %collective-permute-start.7 = (bf16[96,3072]{1,0:T(8,128)(2,1)}, bf16[96,3072]{1,0:T(8,128)(2,1)}, u32[]{:S(2)}, u32[]{:S(2)}) collective-permute-start(bf16[96,3072]{1,0:T(8,128)(2,1)} %get-tuple-element.131), channel_id=1, source_target_pairs={{0,2},{1,3},{2,0},{3,1},{4,6},{5,7},{6,4},{7,5},{8,10},{9,11},{10,... | collective-permute-start | bytes 1769480 | tf_op jit(solution)/shard_map/ppermute | solution.py:688
  48.1 26.1 %collective-permute-start.12 = (bf16[384,768]{1,0:T(8,128)(2,1)}, bf16[384,768]{1,0:T(8,128)(2,1)}, u32[]{:S(2)}, u32[]{:S(2)}) collective-permute-start(bf16[384,768]{1,0:T(8,128)(2,1)} %constant_dynamic-slice_fusion), channel_id=1, source_target_pairs={{0,2},{1,3},{2,0},{3,1},{4,6},{5,7},{6,4},{7,5},{8,10},{9,11},{10,... | collective-permute-start | bytes 1769480 | tf_op jit(solution)/shard_map/ppermute | solution.py:688
  49.4 40.4 %collective-permute-start.10 = (bf16[96,3840]{1,0:T(8,128)(2,1)S(1)}, bf16[96,3840]{1,0:T(8,128)(2,1)S(1)}, u32[]{:S(2)}, u32[]{:S(2)}) collective-permute-start(bf16[96,3840]{1,0:T(8,128)(2,1)S(1)} %collective-permute-done.6.refs_7_.refs_2_), channel_id=1, source_target_pairs={{0,1},{1,0},{2,3},{3,2},{4,5},{5,4},{6,7},{7,6},{8,9},{9,8},{10,11... | collective-permute-start | bytes 2211848 | tf_op jit(solution)/shard_map/ppermute | solution.py:688
  63.4 26.8 %collective-permute-start.11 = (bf16[96,3840]{1,0:T(8,128)(2,1)S(1)}, bf16[96,3840]{1,0:T(8,128)(2,1)S(1)}, u32[]{:S(2)}, u32[]{:S(2)}) collective-permute-start(bf16[96,3840]{1,0:T(8,128)(2,1)S(1)} %collective-permute-done.8.refs_8_.refs_3_), channel_id=1, source_target_pairs={{0,1},{1,0},{2,3},{3,2},{4,5},{5,4},{6,7},{7,6},{8,9},{9,8},{10,11... | collective-permute-start | bytes 2211848 | tf_op jit(solution)/shard_map/ppermute | solution.py:688
  64.3 25.4 %collective-permute-start.13 = (bf16[96,3072]{1,0:T(8,128)(2,1)}, bf16[96,3072]{1,0:T(8,128)(2,1)}, u32[]{:S(2)}, u32[]{:S(2)}) collective-permute-start(bf16[96,3072]{1,0:T(8,128)(2,1)} %collective-permute-done.7.refs_7_.refs_8_), channel_id=1, source_target_pairs={{0,4},{4,0},{8,12},{12,8},{16,20},{20,16},{24,28},{28,24},{1,5},{5... | collective-permute-start | bytes 1769480 | tf_op jit(solution)/shard_map/ppermute | solution.py:688
  64.7 41.6 %collective-permute-start.14 = (bf16[192,3072]{1,0:T(8,128)(2,1)}, bf16[192,3072]{1,0:T(8,128)(2,1)}, u32[]{:S(2)}, u32[]{:S(2)}) collective-permute-start(bf16[192,3072]{1,0:T(8,128)(2,1)} %refs_0_.6), channel_id=1, source_target_pairs={{0,1},{1,0},{2,3},{3,2},{4,5},{5,4},{6,7},{7,6},{8,9},{9,8},{10,11... | collective-permute-start | bytes 3538952 | tf_op jit(solution)/shard_map/ppermute | solution.py:688
  74.1 14.6 %collective-permute-start.9 = (bf16[192,768]{1,0:T(8,128)(2,1)S(1)}, bf16[192,768]{1,0:T(8,128)(2,1)S(1)}, u32[]{:S(2)}, u32[]{:S(2)}) collective-permute-start(bf16[192,768]{1,0:T(8,128)(2,1)S(1)} %copy-done.35), channel_id=1, source_target_pairs={{0,1},{1,0},{2,3},{3,2},{4,5},{5,4},{6,7},{7,6},{8,9},{9,8},{10,11... | collective-permute-start | bytes 884744 | tf_op jit(solution)/shard_map/ppermute | solution.py:688
  88.8 17.0 %collective-permute-start.16 = (bf16[96,3072]{1,0:T(8,128)(2,1)}, bf16[96,3072]{1,0:T(8,128)(2,1)}, u32[]{:S(2)}, u32[]{:S(2)}) collective-permute-start(bf16[96,3072]{1,0:T(8,128)(2,1)} %collective-permute-done.7.refs_7_.refs_8_), channel_id=1, source_target_pairs={{0,1},{1,0},{2,3},{3,2},{4,5},{5,4},{6,7},{7,6},{8,9},{9,8},{10,11... | collective-permute-start | bytes 1769480 | tf_op jit(solution)/shard_map/ppermute | solution.py:688
  89.7 17.4 %collective-permute-start.15 = (bf16[192,3072]{1,0:T(8,128)(2,1)}, bf16[192,3072]{1,0:T(8,128)(2,1)}, u32[]{:S(2)}, u32[]{:S(2)}) collective-permute-start(bf16[192,3072]{1,0:T(8,128)(2,1)} %refs_6_.1), channel_id=1, source_target_pairs={{0,1},{1,0},{2,3},{3,2},{4,5},{5,4},{6,7},{7,6},{8,9},{9,8},{10,11... | collective-permute-start | bytes 3538952 | tf_op jit(solution)/shard_map/ppermute | solution.py:688
  89.8 19.9 %collective-permute-start.18 = (bf16[768,768]{1,0:T(8,128)(2,1)}, bf16[768,768]{1,0:T(8,128)(2,1)}, u32[]{:S(2)}, u32[]{:S(2)}) collective-permute-start(bf16[768,768]{1,0:T(8,128)(2,1)} %refs_12_.1), channel_id=1, source_target_pairs={{0,1},{1,0},{2,3},{3,2},{4,5},{5,4},{6,7},{7,6},{8,9},{9,8},{10,11... | collective-permute-start | bytes 3538952 | tf_op jit(solution)/shard_map/ppermute | solution.py:688
  90.2 15.5 %collective-permute-start.19 = (bf16[384,768]{1,0:T(8,128)(2,1)}, bf16[384,768]{1,0:T(8,128)(2,1)S(1)}, u32[]{:S(2)}, u32[]{:S(2)}) collective-permute-start(bf16[384,768]{1,0:T(8,128)(2,1)} %collective-permute-done.12.refs_6_.refs_14_), channel_id=1, source_target_pairs={{0,4},{4,0},{8,12},{12,8},{16,20},{20,16},{24,28},{28,24},{1,5},{5... | collective-permute-start | bytes 1769480 | tf_op jit(solution)/shard_map/ppermute | solution.py:688
  142.0 5.5 %collective-permute-start.24 = (bf16[8,896]{1,0:T(8,128)(2,1)S(1)}, bf16[8,896]{1,0:T(8,128)(2,1)S(1)}, u32[]{:S(2)}, u32[]{:S(2)}) collective-permute-start(bf16[8,896]{1,0:T(8,128)(2,1)S(1)} %get-tuple-element.256), channel_id=1, source_target_pairs={{0,24},{4,28},{8,16},{12,20},{16,8},{20,12},{24,0},{28,4},{1,25},{... | collective-permute-start | bytes 43016 | tf_op jit(solution)/shard_map/ppermute | solution.py:688
  145.5 4.6 %collective-permute-start.23 = (bf16[8,896]{1,0:T(8,128)(2,1)S(1)}, bf16[8,896]{1,0:T(8,128)(2,1)S(1)}, u32[]{:S(2)}, u32[]{:S(2)}) collective-permute-start(bf16[8,896]{1,0:T(8,128)(2,1)S(1)} %get-tuple-element.256), channel_id=1, source_target_pairs={{0,16},{4,20},{8,24},{12,28},{16,0},{20,4},{24,8},{28,12},{1,17},{... | collective-permute-start | bytes 43016 | tf_op jit(solution)/shard_map/ppermute | solution.py:688
  145.5 4.6 %collective-permute-start.22 = (bf16[8,896]{1,0:T(8,128)(2,1)S(1)}, bf16[8,896]{1,0:T(8,128)(2,1)S(1)}, u32[]{:S(2)}, u32[]{:S(2)}) collective-permute-start(bf16[8,896]{1,0:T(8,128)(2,1)S(1)} %get-tuple-element.256), channel_id=1, source_target_pairs={{0,8},{4,12},{8,0},{12,4},{16,24},{20,28},{24,16},{28,20},{1,9},{5... | collective-permute-start | bytes 43016 | tf_op jit(solution)/shard_map/ppermute | solution.py:688
  154.4 4.9 %collective-permute-start.26 = (bf16[4,2,8,896]{3,2,0,1:T(8,128)(2,1)S(1)}, bf16[4,2,8,896]{3,2,0,1:T(8,128)(2,1)S(1)}, u32[]{:S(2)}, u32[]{:S(2)}) collective-permute-start(bf16[4,2,8,896]{3,2,0,1:T(8,128)(2,1)S(1)} %get-tuple-element.248), channel_id=1, source_target_pairs={{0,4},{4,0},{8,12},{12,8},{16,20},{20,16},{24,28},{28,24},{1,5},{5... | collective-permute-start | bytes 344072 | tf_op jit(solution)/shard_map/ppermute | solution.py:688
  185.4 13.6 %collective-permute-start.28 = (bf16[16,192,384]{2,1,0:T(8,128)(2,1)}, bf16[16,192,384]{2,1,0:T(8,128)(2,1)S(1)}, u32[]{:S(2)}, u32[]{:S(2)}) collective-permute-start(bf16[16,192,384]{2,1,0:T(8,128)(2,1)} %get-tuple-element.163.refs_0_), channel_id=1, source_target_pairs={{0,1},{1,0},{2,3},{3,2},{4,5},{5,4},{6,7},{7,6},{8,9},{9,8},{10,11... | collective-permute-start | bytes 7077896 | tf_op jit(solution)/shard_map/ppermute | solution.py:688
  198.9 19.6 %collective-permute-start.30 = (bf16[16,192,384]{2,1,0:T(8,128)(2,1)}, bf16[16,192,384]{2,1,0:T(8,128)(2,1)}, u32[]{:S(2)}, u32[]{:S(2)}) collective-permute-start(bf16[16,192,384]{2,1,0:T(8,128)(2,1)} %get-tuple-element.166.refs_0_), channel_id=1, source_target_pairs={{0,1},{1,0},{2,3},{3,2},{4,5},{5,4},{6,7},{7,6},{8,9},{9,8},{10,11... | collective-permute-start | bytes 7077896 | tf_op jit(solution)/shard_map/ppermute | solution.py:688
  202.6 15.9 %collective-permute-start.29 = (bf16[4,192,384]{2,1,0:T(8,128)(2,1)}, bf16[4,192,384]{2,1,0:T(8,128)(2,1)S(1)}, u32[]{:S(2)}, u32[]{:S(2)}) collective-permute-start(bf16[4,192,384]{2,1,0:T(8,128)(2,1)} %shard_map.221.refs_1_), channel_id=1, source_target_pairs={{0,2},{1,3},{2,0},{3,1},{4,6},{5,7},{6,4},{7,5},{8,10},{9,11},{10,... | collective-permute-start | bytes 1769480 | tf_op jit(solution)/shard_map/ppermute | solution.py:688
  218.5 22.8 %collective-permute-start.31 = (bf16[16,192,384]{2,1,0:T(8,128)(2,1)}, bf16[16,192,384]{2,1,0:T(8,128)(2,1)S(1)}, u32[]{:S(2)}, u32[]{:S(2)}) collective-permute-start(bf16[16,192,384]{2,1,0:T(8,128)(2,1)} %get-tuple-element.179), channel_id=1, source_target_pairs={{0,1},{1,0},{2,3},{3,2},{4,5},{5,4},{6,7},{7,6},{8,9},{9,8},{10,11... | collective-permute-start | bytes 7077896 | tf_op jit(solution)/shard_map/ppermute | solution.py:688
  222.9 18.3 %collective-permute-start.32 = (bf16[4,192,384]{2,1,0:T(8,128)(2,1)}, bf16[4,192,384]{2,1,0:T(8,128)(2,1)S(1)}, u32[]{:S(2)}, u32[]{:S(2)}) collective-permute-start(bf16[4,192,384]{2,1,0:T(8,128)(2,1)} %get-tuple-element.171.refs_6_), channel_id=1, source_target_pairs={{0,2},{1,3},{2,0},{3,1},{4,6},{5,7},{6,4},{7,5},{8,10},{9,11},{10,... | collective-permute-start | bytes 1769480 | tf_op jit(solution)/shard_map/ppermute | solution.py:688
  224.2 17.1 %collective-permute-start.33 = (bf16[4,192,384]{2,1,0:T(8,128)(2,1)}, bf16[4,192,384]{2,1,0:T(8,128)(2,1)S(1)}, u32[]{:S(2)}, u32[]{:S(2)}) collective-permute-start(bf16[4,192,384]{2,1,0:T(8,128)(2,1)} %get-tuple-element.172.refs_7_), channel_id=1, source_target_pairs={{0,8},{4,12},{8,0},{12,4},{16,24},{20,28},{24,16},{28,20},{1,9},{5... | collective-permute-start | bytes 1769480 | tf_op jit(solution)/shard_map/ppermute | solution.py:688
  224.5 16.8 %collective-permute-start.34 = (bf16[4,192,384]{2,1,0:T(8,128)(2,1)}, bf16[4,192,384]{2,1,0:T(8,128)(2,1)S(1)}, u32[]{:S(2)}, u32[]{:S(2)}) collective-permute-start(bf16[4,192,384]{2,1,0:T(8,128)(2,1)} %get-tuple-element.173.refs_8_), channel_id=1, source_target_pairs={{0,4},{4,0},{8,12},{12,8},{16,20},{20,16},{24,28},{28,24},{1,5},{5... | collective-permute-start | bytes 1769480 | tf_op jit(solution)/shard_map/ppermute | solution.py:688
  246.1 14.5 %collective-permute-start.35 = (bf16[4,192,384]{2,1,0:T(8,128)(2,1)}, bf16[4,192,384]{2,1,0:T(8,128)(2,1)S(1)}, u32[]{:S(2)}, u32[]{:S(2)}) collective-permute-start(bf16[4,192,384]{2,1,0:T(8,128)(2,1)} %get-tuple-element.180.refs_0_), channel_id=1, source_target_pairs={{0,4},{4,0},{8,12},{12,8},{16,20},{20,16},{24,28},{28,24},{1,5},{5... | collective-permute-start | bytes 1769480 | tf_op jit(solution)/shard_map/ppermute | solution.py:688
  247.9 14.1 %collective-permute-start.36 = (bf16[4,192,384]{2,1,0:T(8,128)(2,1)}, bf16[4,192,384]{2,1,0:T(8,128)(2,1)S(1)}, u32[]{:S(2)}, u32[]{:S(2)}) collective-permute-start(bf16[4,192,384]{2,1,0:T(8,128)(2,1)} %get-tuple-element.181.refs_1_), channel_id=1, source_target_pairs={{0,2},{1,3},{2,0},{3,1},{4,6},{5,7},{6,4},{7,5},{8,10},{9,11},{10,... | collective-permute-start | bytes 1769480 | tf_op jit(solution)/shard_map/ppermute | solution.py:688
  265.7 20.2 %collective-permute-start.38 = (bf16[4,192,384]{2,1,0:T(8,128)(2,1)}, bf16[4,192,384]{2,1,0:T(8,128)(2,1)S(1)}, u32[]{:S(2)}, u32[]{:S(2)}) collective-permute-start(bf16[4,192,384]{2,1,0:T(8,128)(2,1)} %get-tuple-element.187.refs_15_), channel_id=1, source_target_pairs={{0,2},{1,3},{2,0},{3,1},{4,6},{5,7},{6,4},{7,5},{8,10},{9,11},{10,... | collective-permute-start | bytes 1769480 | tf_op jit(solution)/shard_map/ppermute | solution.py:688
  266.4 19.4 %collective-permute-start.37 = (bf16[2,192,384]{2,1,0:T(8,128)(2,1)}, bf16[2,192,384]{2,1,0:T(8,128)(2,1)S(1)}, u32[]{:S(2)}, u32[]{:S(2)}) collective-permute-start(bf16[2,192,384]{2,1,0:T(8,128)(2,1)} %get-tuple-element.186.refs_14_), channel_id=1, source_target_pairs={{0,4},{4,0},{8,12},{12,8},{16,20},{20,16},{24,28},{28,24},{1,5},{5... | collective-permute-start | bytes 884744 | tf_op jit(solution)/shard_map/ppermute | solution.py:688
  290.1 15.7 %collective-permute-start.41 = (bf16[4,192,384]{2,1,0:T(8,128)(2,1)}, bf16[4,192,384]{2,1,0:T(8,128)(2,1)S(1)}, u32[]{:S(2)}, u32[]{:S(2)}) collective-permute-start(bf16[4,192,384]{2,1,0:T(8,128)(2,1)} %get-tuple-element.194.refs_0_), channel_id=1, source_target_pairs={{0,2},{1,3},{2,0},{3,1},{4,6},{5,7},{6,4},{7,5},{8,10},{9,11},{10,... | collective-permute-start | bytes 1769480 | tf_op jit(solution)/shard_map/ppermute | solution.py:688
  292.4 13.3 %collective-permute-start.40 = (bf16[2,192,384]{2,1,0:T(8,128)(2,1)}, bf16[2,192,384]{2,1,0:T(8,128)(2,1)S(1)}, u32[]{:S(2)}, u32[]{:S(2)}) collective-permute-start(bf16[2,192,384]{2,1,0:T(8,128)(2,1)} %get-tuple-element.193.refs_3_), channel_id=1, source_target_pairs={{0,8},{4,12},{8,0},{12,4},{16,24},{20,28},{24,16},{28,20},{1,9},{5... | collective-permute-start | bytes 884744 | tf_op jit(solution)/shard_map/ppermute | solution.py:688
  293.1 12.6 %collective-permute-start.42 = (bf16[2,192,384]{2,1,0:T(8,128)(2,1)}, bf16[2,192,384]{2,1,0:T(8,128)(2,1)S(1)}, u32[]{:S(2)}, u32[]{:S(2)}) collective-permute-start(bf16[2,192,384]{2,1,0:T(8,128)(2,1)} %get-tuple-element.195.refs_1_), channel_id=1, source_target_pairs={{0,4},{4,0},{8,12},{12,8},{16,20},{20,16},{24,28},{28,24},{1,5},{5... | collective-permute-start | bytes 884744 | tf_op jit(solution)/shard_map/ppermute | solution.py:688
  293.1 12.6 %collective-permute-start.39 = (bf16[1,192,384]{2,1,0:T(8,128)(2,1)}, bf16[1,192,384]{2,1,0:T(8,128)(2,1)S(1)}, u32[]{:S(2)}, u32[]{:S(2)}) collective-permute-start(bf16[1,192,384]{2,1,0:T(8,128)(2,1)} %get-tuple-element.192.refs_2_), channel_id=1, source_target_pairs={{0,16},{4,20},{8,24},{12,28},{16,0},{20,4},{24,8},{28,12},{1,17},{... | collective-permute-start | bytes 442376 | tf_op jit(solution)/shard_map/ppermute | solution.py:688
  314.3 24.1 %collective-permute-start.48 = (bf16[8,112,384]{2,1,0:T(8,128)(2,1)}, bf16[8,112,384]{2,1,0:T(8,128)(2,1)S(1)}, u32[]{:S(2)}, u32[]{:S(2)}) collective-permute-start(bf16[8,112,384]{2,1,0:T(8,128)(2,1)} %get-tuple-element.206.refs_18_), channel_id=1, source_target_pairs={{0,2},{1,3},{2,0},{3,1},{4,6},{5,7},{6,4},{7,5},{8,10},{9,11},{10,... | collective-permute-start | bytes 2064392 | tf_op jit(solution)/shard_map/ppermute | solution.py:688
  316.1 22.3 %collective-permute-start.46 = (bf16[2,192,384]{2,1,0:T(8,128)(2,1)}, bf16[2,192,384]{2,1,0:T(8,128)(2,1)S(1)}, u32[]{:S(2)}, u32[]{:S(2)}) collective-permute-start(bf16[2,192,384]{2,1,0:T(8,128)(2,1)} %get-tuple-element.204.refs_16_), channel_id=1, source_target_pairs={{0,4},{4,0},{8,12},{12,8},{16,20},{20,16},{24,28},{28,24},{1,5},{5... | collective-permute-start | bytes 884744 | tf_op jit(solution)/shard_map/ppermute | solution.py:688
  316.6 21.8 %collective-permute-start.47 = (bf16[2,192,384]{2,1,0:T(8,128)(2,1)}, bf16[2,192,384]{2,1,0:T(8,128)(2,1)S(1)}, u32[]{:S(2)}, u32[]{:S(2)}) collective-permute-start(bf16[2,192,384]{2,1,0:T(8,128)(2,1)} %get-tuple-element.205.refs_17_), channel_id=1, source_target_pairs={{0,8},{4,12},{8,0},{12,4},{16,24},{20,28},{24,16},{28,20},{1,9},{5... | collective-permute-start | bytes 884744 | tf_op jit(solution)/shard_map/ppermute | solution.py:688
  316.8 21.5 %collective-permute-start.44 = (bf16[1,192,384]{2,1,0:T(8,128)(2,1)}, bf16[1,192,384]{2,1,0:T(8,128)(2,1)S(1)}, u32[]{:S(2)}, u32[]{:S(2)}) collective-permute-start(bf16[1,192,384]{2,1,0:T(8,128)(2,1)} %get-tuple-element.202.refs_14_.refs_0_), channel_id=1, source_target_pairs={{0,16},{4,20},{8,24},{12,28},{16,0},{20,4},{24,8},{28,12},{1,17},{... | collective-permute-start | bytes 442376 | tf_op jit(solution)/shard_map/ppermute | solution.py:688
  317.2 21.1 %collective-permute-start.45 = (bf16[1,192,384]{2,1,0:T(8,128)(2,1)}, bf16[1,192,384]{2,1,0:T(8,128)(2,1)S(1)}, u32[]{:S(2)}, u32[]{:S(2)}) collective-permute-start(bf16[1,192,384]{2,1,0:T(8,128)(2,1)} %get-tuple-element.203.refs_15_), channel_id=1, source_target_pairs={{0,16},{4,20},{8,24},{12,28},{16,0},{20,4},{24,8},{28,12},{1,17},{... | collective-permute-start | bytes 442376 | tf_op jit(solution)/shard_map/ppermute | solution.py:688
  342.4 17.8 %collective-permute-start.52 = (bf16[4,112,384]{2,1,0:T(8,128)(2,1)}, bf16[4,112,384]{2,1,0:T(8,128)(2,1)S(1)}, u32[]{:S(2)}, u32[]{:S(2)}) collective-permute-start(bf16[4,112,384]{2,1,0:T(8,128)(2,1)} %get-tuple-element.214.refs_3_), channel_id=1, source_target_pairs={{0,8},{4,12},{8,0},{12,4},{16,24},{20,28},{24,16},{28,20},{1,9},{5... | collective-permute-start | bytes 1032200 | tf_op jit(solution)/shard_map/ppermute | solution.py:688
  344.2 16.0 %collective-permute-start.49 = (bf16[2,192,384]{2,1,0:T(8,128)(2,1)}, bf16[2,192,384]{2,1,0:T(8,128)(2,1)S(1)}, u32[]{:S(2)}, u32[]{:S(2)}) collective-permute-start(bf16[2,192,384]{2,1,0:T(8,128)(2,1)} %get-tuple-element.211.refs_0_), channel_id=1, source_target_pairs={{0,4},{4,0},{8,12},{12,8},{16,20},{20,16},{24,28},{28,24},{1,5},{5... | collective-permute-start | bytes 884744 | tf_op jit(solution)/shard_map/ppermute | solution.py:688
  344.2 13.9 %collective-permute-start.50 = (bf16[1,192,384]{2,1,0:T(8,128)(2,1)}, bf16[1,192,384]{2,1,0:T(8,128)(2,1)S(1)}, u32[]{:S(2)}, u32[]{:S(2)}) collective-permute-start(bf16[1,192,384]{2,1,0:T(8,128)(2,1)} %get-tuple-element.212.refs_1_.refs_2_), channel_id=1, source_target_pairs={{0,16},{4,20},{8,24},{12,28},{16,0},{20,4},{24,8},{28,12},{1,17},{... | collective-permute-start | bytes 442376 | tf_op jit(solution)/shard_map/ppermute | solution.py:688
  346.7 13.5 %collective-permute-start.51 = (bf16[1,192,384]{2,1,0:T(8,128)(2,1)}, bf16[1,192,384]{2,1,0:T(8,128)(2,1)S(1)}, u32[]{:S(2)}, u32[]{:S(2)}) collective-permute-start(bf16[1,192,384]{2,1,0:T(8,128)(2,1)} %get-tuple-element.213.refs_2_), channel_id=1, source_target_pairs={{0,16},{4,20},{8,24},{12,28},{16,0},{20,4},{24,8},{28,12},{1,17},{... | collective-permute-start | bytes 442376 | tf_op jit(solution)/shard_map/ppermute | solution.py:688
  364.6 18.6 %collective-permute-start.55 = (bf16[8,96,384]{2,1,0:T(8,128)(2,1)S(1)}, bf16[8,96,384]{2,1,0:T(8,128)(2,1)S(1)}, u32[]{:S(2)}, u32[]{:S(2)}) collective-permute-start(bf16[8,96,384]{2,1,0:T(8,128)(2,1)S(1)} %add_convert_fusion.refs_8_), channel_id=1, source_target_pairs={{0,2},{1,3},{2,0},{3,1},{4,6},{5,7},{6,4},{7,5},{8,10},{9,11},{10,... | collective-permute-start | bytes 1769480 | tf_op jit(solution)/shard_map/ppermute | solution.py:688
  368.8 15.9 %collective-permute-start.54 = (bf16[2,112,384]{2,1,0:T(8,128)(2,1)}, bf16[2,112,384]{2,1,0:T(8,128)(2,1)}, u32[]{:S(2)}, u32[]{:S(2)}) collective-permute-start(bf16[2,112,384]{2,1,0:T(8,128)(2,1)} %get-tuple-element.219.refs_7_), channel_id=1, source_target_pairs={{0,4},{4,0},{8,12},{12,8},{16,20},{20,16},{24,28},{28,24},{1,5},{5... | collective-permute-start | bytes 516104 | tf_op jit(solution)/shard_map/ppermute | solution.py:688
  369.4 62.2 %collective-permute-start.66 = (bf16[4,192,384]{2,1,0:T(8,128)(2,1)}, bf16[4,192,384]{2,1,0:T(8,128)(2,1)}, u32[]{:S(2)}, u32[]{:S(2)}) collective-permute-start(bf16[4,192,384]{2,1,0:T(8,128)(2,1)} %get-tuple-element.216.refs_4_.refs_0_), channel_id=1, source_target_pairs={{0,8},{4,12},{8,0},{12,4},{16,24},{20,28},{24,16},{28,20},{1,9},{5... | collective-permute-start | bytes 1769480 | tf_op jit(solution)/shard_map/ppermute | solution.py:688
  369.4 26.3 %collective-permute-start.67 = (bf16[2,192,384]{2,1,0:T(8,128)(2,1)}, bf16[2,192,384]{2,1,0:T(8,128)(2,1)}, u32[]{:S(2)}, u32[]{:S(2)}) collective-permute-start(bf16[2,192,384]{2,1,0:T(8,128)(2,1)} %get-tuple-element.231.refs_5_), channel_id=1, source_target_pairs={{0,8},{4,12},{8,0},{12,4},{16,24},{20,28},{24,16},{28,20},{1,9},{5... | collective-permute-start | bytes 884744 | tf_op jit(solution)/shard_map/ppermute | solution.py:688
  371.4 27.0 %collective-permute-start.69 = (bf16[1,192,384]{2,1,0:T(8,128)(2,1)}, bf16[1,192,384]{2,1,0:T(8,128)(2,1)}, u32[]{:S(2)}, u32[]{:S(2)}) collective-permute-start(bf16[1,192,384]{2,1,0:T(8,128)(2,1)} %get-tuple-element.233.refs_6_), channel_id=1, source_target_pairs={{0,16},{4,20},{8,24},{12,28},{16,0},{20,4},{24,8},{28,12},{1,17},{... | collective-permute-start | bytes 442376 | tf_op jit(solution)/shard_map/ppermute | solution.py:688
  383.3 16.2 %collective-permute-start.57 = (bf16[4,96,384]{2,1,0:T(8,128)(2,1)S(1)}, bf16[4,96,384]{2,1,0:T(8,128)(2,1)S(1)}, u32[]{:S(2)}, u32[]{:S(2)}) collective-permute-start(bf16[4,96,384]{2,1,0:T(8,128)(2,1)S(1)} %add_convert_fusion.1), channel_id=1, source_target_pairs={{0,4},{4,0},{8,12},{12,8},{16,20},{20,16},{24,28},{28,24},{1,5},{5... | collective-permute-start | bytes 884744 | tf_op jit(solution)/shard_map/ppermute | solution.py:688
  385.9 15.8 %collective-permute-start.56 = (bf16[1,112,384]{2,1,0:T(8,128)(2,1)S(1)}, bf16[1,112,384]{2,1,0:T(8,128)(2,1)S(1)}, u32[]{:S(2)}, u32[]{:S(2)}) collective-permute-start(bf16[1,112,384]{2,1,0:T(8,128)(2,1)S(1)} %add_convert_fusion.4), channel_id=1, source_target_pairs={{0,16},{4,20},{8,24},{12,28},{16,0},{20,4},{24,8},{28,12},{1,17},{... | collective-permute-start | bytes 258056 | tf_op jit(solution)/shard_map/ppermute | solution.py:688
  396.8 34.8 %collective-permute-start.68 = (bf16[4,192,384]{2,1,0:T(8,128)(2,1)S(1)}, bf16[4,192,384]{2,1,0:T(8,128)(2,1)S(1)}, u32[]{:S(2)}, u32[]{:S(2)}) collective-permute-start(bf16[4,192,384]{2,1,0:T(8,128)(2,1)S(1)} %constant_dynamic-update-slice_fusion.4.refs_2_), channel_id=1, source_target_pairs={{0,4},{4,0},{8,12},{12,8},{16,20},{20,16},{24,28},{28,24},{1,5},{5... | collective-permute-start | bytes 1769480 | tf_op jit(solution)/shard_map/ppermute | solution.py:688
  399.4 10.8 %collective-permute-start.70 = (bf16[2,192,384]{2,1,0:T(8,128)(2,1)S(1)}, bf16[2,192,384]{2,1,0:T(8,128)(2,1)S(1)}, u32[]{:S(2)}, u32[]{:S(2)}) collective-permute-start(bf16[2,192,384]{2,1,0:T(8,128)(2,1)S(1)} %constant_dynamic-update-slice_fusion.6), channel_id=1, source_target_pairs={{0,8},{4,12},{8,0},{12,4},{16,24},{20,28},{24,16},{28,20},{1,9},{5... | collective-permute-start | bytes 884744 | tf_op jit(solution)/shard_map/ppermute | solution.py:688
  399.6 12.2 %collective-permute-start.58 = (bf16[2,96,384]{2,1,0:T(8,128)(2,1)S(1)}, bf16[2,96,384]{2,1,0:T(8,128)(2,1)S(1)}, u32[]{:S(2)}, u32[]{:S(2)}) collective-permute-start(bf16[2,96,384]{2,1,0:T(8,128)(2,1)S(1)} %add_convert_fusion.2), channel_id=1, source_target_pairs={{0,8},{4,12},{8,0},{12,4},{16,24},{20,28},{24,16},{28,20},{1,9},{5... | collective-permute-start | bytes 442376 | tf_op jit(solution)/shard_map/ppermute | solution.py:688
  402.8 9.2 %collective-permute-start.59 = (bf16[1,112,384]{2,1,0:T(8,128)(2,1)S(1)}, bf16[1,112,384]{2,1,0:T(8,128)(2,1)S(1)}, u32[]{:S(2)}, u32[]{:S(2)}) collective-permute-start(bf16[1,112,384]{2,1,0:T(8,128)(2,1)S(1)} %add_convert_fusion.3), channel_id=1, source_target_pairs={{0,16},{4,20},{8,24},{12,28},{16,0},{20,4},{24,8},{28,12},{1,17},{... | collective-permute-start | bytes 258056 | tf_op jit(solution)/shard_map/ppermute | solution.py:688
  410.3 22.1 %collective-permute-start.71 = (bf16[4,192,384]{2,1,0:T(8,128)(2,1)S(1)}, bf16[4,192,384]{2,1,0:T(8,128)(2,1)}, u32[]{:S(2)}, u32[]{:S(2)}) collective-permute-start(bf16[4,192,384]{2,1,0:T(8,128)(2,1)S(1)} %constant_dynamic-update-slice_fusion.8.refs_4_), channel_id=1, source_target_pairs={{0,4},{4,0},{8,12},{12,8},{16,20},{20,16},{24,28},{28,24},{1,5},{5... | collective-permute-start | bytes 1769480 | tf_op jit(solution)/shard_map/ppermute | solution.py:688
  411.9 6.8 %collective-permute-start.60 = (bf16[1,96,384]{2,1,0:T(8,128)(2,1)S(1)}, bf16[1,96,384]{2,1,0:T(8,128)(2,1)S(1)}, u32[]{:S(2)}, u32[]{:S(2)}) collective-permute-start(bf16[1,96,384]{2,1,0:T(8,128)(2,1)S(1)} %add_convert_fusion.6), channel_id=1, source_target_pairs={{0,16},{4,20},{8,24},{12,28},{16,0},{20,4},{24,8},{28,12},{1,17},{... | collective-permute-start | bytes 221192 | tf_op jit(solution)/shard_map/ppermute | solution.py:688
  418.7 5.3 %collective-permute-start.63 = (bf16[1,96,384]{2,1,0:T(8,128)(2,1)S(1)}, bf16[1,96,384]{2,1,0:T(8,128)(2,1)S(1)}, u32[]{:S(2)}, u32[]{:S(2)}) collective-permute-start(bf16[1,96,384]{2,1,0:T(8,128)(2,1)S(1)} %add_convert_fusion.5), channel_id=1, source_target_pairs={{0,16},{4,20},{8,24},{12,28},{16,0},{20,4},{24,8},{28,12},{1,17},{... | collective-permute-start | bytes 221192 | tf_op jit(solution)/shard_map/ppermute | solution.py:688
  418.8 8.3 %collective-permute-start.61 = (bf16[2,112,384]{2,1,0:T(8,128)(2,1)S(1)}, bf16[2,112,384]{2,1,0:T(8,128)(2,1)S(1)}, u32[]{:S(2)}, u32[]{:S(2)}) collective-permute-start(bf16[2,112,384]{2,1,0:T(8,128)(2,1)S(1)} %constant_dynamic-update-slice_fusion), channel_id=1, source_target_pairs={{0,4},{4,0},{8,12},{12,8},{16,20},{20,16},{24,28},{28,24},{1,5},{5... | collective-permute-start | bytes 516104 | tf_op jit(solution)/shard_map/ppermute | solution.py:688
  424.0 6.8 %collective-permute-start.64 = (bf16[2,96,384]{2,1,0:T(8,128)(2,1)S(1)}, bf16[2,96,384]{2,1,0:T(8,128)(2,1)S(1)}, u32[]{:S(2)}, u32[]{:S(2)}) collective-permute-start(bf16[2,96,384]{2,1,0:T(8,128)(2,1)S(1)} %pad_maximum_fusion.4), channel_id=1, source_target_pairs={{0,8},{4,12},{8,0},{12,4},{16,24},{20,28},{24,16},{28,20},{1,9},{5... | collective-permute-start | bytes 442376 | tf_op jit(solution)/shard_map/ppermute | solution.py:688
  427.2 13.0 %collective-permute-start.62 = (bf16[4,112,384]{2,1,0:T(8,128)(2,1)S(1)}, bf16[4,112,384]{2,1,0:T(8,128)(2,1)S(1)}, u32[]{:S(2)}, u32[]{:S(2)}) collective-permute-start(bf16[4,112,384]{2,1,0:T(8,128)(2,1)S(1)} %constant_dynamic-update-slice_fusion.2.refs_0_), channel_id=1, source_target_pairs={{0,8},{4,12},{8,0},{12,4},{16,24},{20,28},{24,16},{28,20},{1,9},{5... | collective-permute-start | bytes 1032200 | tf_op jit(solution)/shard_map/ppermute | solution.py:688
  430.8 9.3 %collective-permute-start.65 = (bf16[4,96,384]{2,1,0:T(8,128)(2,1)S(1)}, bf16[4,96,384]{2,1,0:T(8,128)(2,1)S(1)}, u32[]{:S(2)}, u32[]{:S(2)}) collective-permute-start(bf16[4,96,384]{2,1,0:T(8,128)(2,1)S(1)} %pad_maximum_fusion.2.refs_2_), channel_id=1, source_target_pairs={{0,4},{4,0},{8,12},{12,8},{16,20},{20,16},{24,28},{28,24},{1,5},{5... | collective-permute-start | bytes 884744 | tf_op jit(solution)/shard_map/ppermute | solution.py:688
  (72 other events, 378.5 us)

commit v3 on v2

--- a/solution.py
+++ b/solution.py
@@ -54,7 +54,7 @@
 
 
 def whole(dims):
-    return pl.BlockSpec(dims, lambda *_: (0,) * len(dims))
+    return pl.BlockSpec(dims, lambda *_: (0,) * len(dims), pipeline_mode=pl.Buffered(1))
 
 
 def swap_halves(tile):
@@ -95,7 +95,7 @@
 
 def qkv_kernel(rows_ref, x_ref, cos_ref, sin_ref, *refs):
     pieces = refs[:4]
-    out_ref, xt_ref, weight, sems = refs[5:]
+    out_ref, xt_ref, weight, sems = refs[-4:]
     step = pl.program_id(0)
     width = x_ref.shape[1]
 
@@ -104,7 +104,7 @@
         copies = piece_copies(lambda k: rows_ref[k], pieces, weight, sems)
         for copy in copies:
             copy.start()
-        store_turned(xt_ref, x_ref[...], rows_ref[6])
+        store_turned(xt_ref, x_ref[...], rows_ref[4])
         for copy in copies:
             copy.wait()
 
@@ -222,9 +222,9 @@
 
 
 def mixer_kernel(rows_ref, att0_ref, att1_ref, x_ref, vec_ref, *refs):
-    xhat_ref, inv_ref, low_ref, lowt_ref, full_ref, weight, sems, out_sem = refs[8:]
+    xhat_ref, inv_ref, low_ref, lowt_ref, full_ref, weight, sems, out_sem = refs[-8:]
     width = weight.shape[1]
-    pieces = list(refs[:2]) + [piece.at[:, pl.ds(piece.shape[1] - width, width)] for piece in refs[2:6]]
+    pieces = list(refs[:2]) + [piece.at[:, pl.ds(piece.shape[1] - width, width)] for piece in refs[2:4]]
     step = pl.program_id(0)
     out_copy = pltpu.make_async_copy(weight, full_ref, out_sem)
 
@@ -243,7 +243,7 @@
     xhat_ref[...] = xhat
     inv_ref[...] = jnp.broadcast_to(inv, inv_ref.shape)
     low_ref[...] = low
-    store_turned(lowt_ref, low, rows_ref[6])
+    store_turned(lowt_ref, low, rows_ref[4])
 
     @pl.when(step == pl.num_programs(0) - 1)
     def _():
@@ -251,12 +251,12 @@
 
 
 def ffn_kernel(rows_ref, low_ref, xhat_ref, vec_ref, mark_ref, cnt_ref, *refs):
-    up_pieces, gate_pieces, down_pieces = refs[0:6], refs[6:12], refs[12:18]
-    up_fac_ref, gate_fac_ref, prod_ref, xhat2_ref, inv2_ref, pool_ref, emb_ref = refs[18:25]
-    full_up, full_gate, full_down = refs[25:28]
-    w_up, w_gate, w_down, sems, down_sems, out_sems, pooled, total = refs[28:]
+    up_pieces, gate_pieces, down_pieces = refs[0:4], refs[4:8], refs[8:12]
+    up_fac_ref, gate_fac_ref, prod_ref, xhat2_ref, inv2_ref, pool_ref, emb_ref = refs[12:19]
+    full_up, full_gate, full_down = refs[19:22]
+    w_up, w_gate, w_down, sems, down_sems, out_sems, pooled, total = refs[22:]
     step = pl.program_id(0)
-    own = rows_ref[6]
+    own = rows_ref[4]
     tokens, width = low_ref.shape
     wide = prod_ref.shape[1]
     steps = 4
@@ -268,14 +268,9 @@
             for k, piece in enumerate(pieces):
                 rows = pl.ds(pl.multiple_of(rows_ref[k], 32), piece.shape[0])
                 copies.append(
-                    pltpu.make_async_copy(piece.at[:, cols], scratch.at[rel, rows], sems.at[rel * 12 + which * 6 + k])
+                    pltpu.make_async_copy(piece.at[:, cols], scratch.at[rel, rows], sems.at[rel * 8 + which * 4 + k])
                 )
-        for k in ((0,), (1,), (2, 3), (4, 5))[rel]:
-            piece = down_pieces[k]
-            start = 0 if k < 2 else pl.multiple_of(rows_ref[7 + (k & 1)], 32)
-            copies.append(
-                pltpu.make_async_copy(piece, w_down.at[rel, pl.ds(start, piece.shape[0])], down_sems.at[k])
-            )
+        copies.append(pltpu.make_async_copy(down_pieces[rel], w_down.at[rel], down_sems.at[rel]))
         return copies
 
     def out_copies(rel):
@@ -688,6 +683,28 @@
     return lax.ppermute(value, axis, [(i, i ^ bits) for i in range(size)])
 
 
+def join_kernel(first_ref, one_ref, two_ref, *refs):
+    out_ref = refs[-1]
+    rows = one_ref.shape[0]
+    for ref, at in ((one_ref, first_ref[0]), (two_ref, 1 - first_ref[0])):
+        out_ref[pl.ds(pl.multiple_of(at * rows, 32), rows), :] = ref[...]
+
+
+def join(first, one, two, *after):
+    dims = (2 * one.shape[0], one.shape[1])
+    return pl.pallas_call(
+        join_kernel,
+        grid_spec=pltpu.PrefetchScalarGridSpec(
+            num_scalar_prefetch=1,
+            grid=(1,),
+            in_specs=[whole(one.shape), whole(two.shape)] + [ANY] * len(after),
+            out_specs=whole(dims),
+        ),
+        out_shape=shape(dims, one.dtype),
+        **params(8),
+    )(first, one, two, *after)
+
+
 def sums_kernel(plan, *refs):
     outs = refs[len(refs) - len(plan) :]
     for out_ref, pieces in zip(outs, plan, strict=True):
@@ -719,7 +736,7 @@
         in_specs=specs + [ANY] * len(after),
         out_specs=[pl.BlockSpec(dims, lambda i: (0, 0, 0)) for dims in shapes],
         out_shape=[shape(dims, bf16) for dims in shapes],
-        **params(),
+        **params(16),
     )(*inputs, *after)
 
 
@@ -777,28 +794,9 @@
         rows = own.shape[0]
         return lax.dynamic_slice_in_dim(own, y_bit * (rows // 2), rows // 2, 0)
 
-    def gather_rest(own, mine, before):
-        mine = tie(mine, before)
-        other = xor_permute(mine, "batch", nb, 1)
-        return (
-            own,
-            xor_permute(tie(own, before), "fsdp", nf, 1),
-            mine,
-            other,
-            xor_permute(mine, "fsdp", nf, 1),
-        )
-
-    def gather_last(pieces, during):
-        return pieces + (xor_permute(tie(pieces[3], during), "fsdp", nf, 1),)
-
-    def piece_rows(rows, share):
-        half = rows // 2
-        y = y_bit if share else 0 * y_bit
-        two, three = (f ^ 2) * rows, (f ^ 3) * rows
-        halves = [y * half, (1 - y) * half]
-        starts = [f * rows, (f ^ 1) * rows, two + halves[0], two + halves[1], three + halves[0], three + halves[1]]
-        down = [y * (FF // nf // 2), (1 - y) * (FF // nf // 2)]
-        return jnp.stack(starts + [f] + down).astype(jnp.int32)
+    def gather_far(own, beside, mine, other, *after):
+        pair = join(y_bit.reshape(1), mine, other, *after)
+        return (own, beside, pair, xor_permute(pair, "fsdp", nf, 1))
 
     marks = (segment[:, None] == jnp.arange(SEGS, dtype=jnp.int32)[None, :]).astype(jnp.int32)
     counts = jnp.sum(marks, axis=0)
@@ -830,9 +828,11 @@
     beyond = tie(beyond, mask_q, mask_k, cosine, vectors, *halves)
     far = xor_permute(beyond, "fsdp", nf, 1)
     qkv_pieces = (combined_projection_matrix, beside, beyond, far)
-    up_half, gate_half, down_half = [
-        xor_permute(tie(half, cosine, mask_q, mask_k), "fsdp", nf, 2) for half in halves
+    beside_all = [
+        xor_permute(weight, "fsdp", nf, 1)
+        for weight in (mixer_projection_matrix, widening_matrix, gating_matrix, narrowing_matrix)
     ]
+    up_half = xor_permute(tie(halves[0], cosine, mask_q, mask_k), "fsdp", nf, 2)
 
     heads = (
         (jnp.arange(PAIRS * 8)[:, None] // 8 * 2 + jnp.arange(PAIRS * 8)[:, None] % 8 == jnp.arange(D)[None, :] // HD)
@@ -846,19 +846,19 @@
     def colblk(height, cols=BLOCK):
         return pl.BlockSpec((height, cols), lambda i, *_: (0, i))
 
-    whole_rows = jnp.stack([f * R, (f ^ 1) * R, (f ^ 2) * R, (f ^ 3) * R, f, f, f]).astype(jnp.int32)
+    whole_rows = jnp.stack([f * R, (f ^ 1) * R, (f ^ 2) * R, (f ^ 3) * R, f]).astype(jnp.int32)
     qkv, x_turned = pl.pallas_call(
         qkv_kernel,
         grid_spec=pltpu.PrefetchScalarGridSpec(
             num_scalar_prefetch=1,
             grid=(3,),
-            in_specs=[whole((T, D)), whole((T, LANE)), whole((T, LANE))] + [ANY] * 5,
+            in_specs=[whole((T, D)), whole((T, LANE)), whole((T, LANE))] + [ANY] * 9,
             out_specs=[pl.BlockSpec((T, D), lambda i, *_: (0, i)), whole((D, T))],
             scratch_shapes=[pltpu.VMEM((D, 3 * D), bf16), pltpu.SemaphoreType.DMA((4,))],
         ),
         out_shape=[shape((T, 3 * D), bf16), shape((D, T), bf16)],
-        **params(),
-    )(whole_rows, x, cosine, sine, *qkv_pieces, vectors)
+        **params(22),
+    )(whole_rows, x, cosine, sine, *qkv_pieces, vectors, *beside_all)
 
     vectors = absolute(vectors, f, 2)
     vectors = vectors.transpose(1, 0, 2).reshape(4, D).astype(f32)
@@ -883,50 +883,54 @@
                 out_specs=[rowblk(PART), pl.BlockSpec((PAIRS // 2, 8, BLOCK), lambda i, *_: (0, 0, i))],
             ),
             out_shape=[shape((T, PART), bf16), shape((PAIRS // 2, 8, T), f32)],
-            **params(),
+            **params(14),
         )(lo, spans, qkv, qkv, qkv, mask_q, mask_k, *after)
 
-    up_pieces = gather_rest(widening_matrix, up_half, qkv)
-    attended0, lse0 = attend(0, up_pieces[2])
-    up_pieces = gather_last(up_pieces, attended0)
-    out_beside = xor_permute(tie(mixer_projection_matrix, qkv), "fsdp", nf, 1)
-    out_pieces = (mixer_projection_matrix, out_beside) + up_pieces[2:]
-    gate_pieces = gather_rest(gating_matrix, gate_half, attended0)
-    attended1, lse1 = attend(1, gate_pieces[2], up_pieces[3])
-    gate_pieces = gather_last(gate_pieces, attended1)
-    down_pieces = gather_rest(narrowing_matrix, down_half, attended1)
-
-    shared_rows = piece_rows(R, True)
+    def onward(half, *before):
+        half = tie(half, *before)
+        return half, xor_permute(half, "batch", nb, 1)
+
+    gate_half = xor_permute(tie(halves[1], qkv, up_half), "fsdp", nf, 2)
+    up_half, up_other = onward(up_half, qkv)
+    attended0, lse0 = attend(0, up_half)
+    down_half = xor_permute(tie(halves[2], attended0, gate_half, up_other), "fsdp", nf, 2)
+    gate_half, gate_other = onward(gate_half, attended0, up_other)
+    up_pieces = gather_far(widening_matrix, beside_all[1], up_half, up_other, attended0, gate_half)
+    attended1, lse1 = attend(1, gate_half, up_pieces[2])
+    down_half, down_other = onward(down_half, attended1, gate_other)
+    gate_pieces = gather_far(gating_matrix, beside_all[2], gate_half, gate_other, attended1, down_half)
+    out_pieces = (mixer_projection_matrix, beside_all[0]) + up_pieces[2:]
+
     xhat1, inv1, low1, low1_turned, full_out = pl.pallas_call(
         mixer_kernel,
         grid_spec=pltpu.PrefetchScalarGridSpec(
             num_scalar_prefetch=1,
             grid=(nblk,),
-            in_specs=[rowblk(PART), rowblk(PART), rowblk(D), whole((4, D))] + [ANY] * 8,
+            in_specs=[rowblk(PART), rowblk(PART), rowblk(D), whole((4, D))] + [ANY] * 6,
             out_specs=[rowblk(D), rowblk(LANE), rowblk(D), colblk(D), ANY],
-            scratch_shapes=[pltpu.VMEM((D, D), bf16), pltpu.SemaphoreType.DMA((6,)), pltpu.SemaphoreType.DMA],
+            scratch_shapes=[pltpu.VMEM((D, D), bf16), pltpu.SemaphoreType.DMA((4,)), pltpu.SemaphoreType.DMA],
         ),
         out_shape=[shape((T, D), f32), shape((T, LANE), f32), shape((T, D), bf16), shape((D, T), bf16), shape((D, D), bf16)],
-        **params(),
-    )(shared_rows, attended0, attended1, x, vectors, *out_pieces, down_pieces[2], gate_pieces[3])
+        **params(14),
+    )(whole_rows, attended0, attended1, x, vectors, *out_pieces, down_half, gate_pieces[2])
 
     W = FF // nf
-    down_pieces = gather_last(down_pieces, low1)
+    down_pieces = gather_far(narrowing_matrix, beside_all[3], down_half, down_other, low1)
     up_fac, gate_fac, prod, xhat2, inv2, pool, embed, full_up, full_gate, full_down = pl.pallas_call(
         ffn_kernel,
         grid_spec=pltpu.PrefetchScalarGridSpec(
             num_scalar_prefetch=1,
             grid=(nf,),
-            in_specs=[whole((T, D)), whole((T, D)), whole((4, D)), whole((16, T)), whole((SEGS, LANE))] + [ANY] * 18,
-            out_specs=[pl.BlockSpec((T, W), lambda i, rows: (0, rows[6] ^ i))] * 3
+            in_specs=[whole((T, D)), whole((T, D)), whole((4, D)), whole((16, T)), whole((SEGS, LANE))] + [ANY] * 12,
+            out_specs=[pl.BlockSpec((T, W), lambda i, rows: (0, rows[4] ^ i))] * 3
             + [whole((T, D)), whole((T, LANE)), whole((2 * SEGS, D)), whole((SEGS, D))]
             + [ANY] * 3,
             scratch_shapes=[
                 pltpu.VMEM((nf, D, W), bf16),
                 pltpu.VMEM((nf, D, W), bf16),
                 pltpu.VMEM((nf, W, D), bf16),
-                pltpu.SemaphoreType.DMA((nf * 12,)),
-                pltpu.SemaphoreType.DMA((6,)),
+                pltpu.SemaphoreType.DMA((nf * 8,)),
+                pltpu.SemaphoreType.DMA((nf,)),
                 pltpu.SemaphoreType.DMA((nf * 3,)),
                 pltpu.VMEM((16, D), f32),
                 pltpu.VMEM((T, D), f32),
@@ -935,8 +939,8 @@
         out_shape=[shape((T, FF), bf16)] * 3
         + [shape((T, D), f32), shape((T, LANE), f32), shape((2 * SEGS, D), f32), shape((SEGS, D), bf16)]
         + [shape((D, FF), bf16), shape((D, FF), bf16), shape((FF, D), bf16)],
-        **params(),
-    )(shared_rows, low1, xhat1, vectors, mark_rows, count_rows, *up_pieces, *gate_pieces, *down_pieces)
+        **params(46),
+    )(whole_rows, low1, xhat1, vectors, mark_rows, count_rows, *up_pieces, *gate_pieces, *down_pieces)
 
     ranks = nb * nf
     total_rows = ranks * SEGS
@@ -969,7 +973,7 @@
         out_specs=[whole((SEGS, LANE)), whole((LANE, D)), whole((8, D))],
         out_shape=[shape((SEGS, LANE), f32), shape((LANE, D), f32), shape((8, D), f32)],
         scratch_shapes=[pltpu.VMEM((SEGS, D), f32)],
-        **params(),
+        **params(8),
     )(softness_scale.reshape(1), everyone, everyone, doc_ids, pool, count_rows)
     query_loss = loss_rows[:QSEG, 0].reshape(1, QSEG)
 
@@ -979,7 +983,7 @@
         in_specs=[rowblk(LANE), whole((LANE, D)), rowblk(D), rowblk(LANE), whole((4, D))],
         out_specs=[rowblk(D), rowblk(D), colblk(D)],
         out_shape=[shape((T, D), f32), shape((T, D), bf16), shape((D, T), bf16)],
-        **params(),
+        **params(12),
     )(mask_q, grad_rows, xhat2, inv2, vectors)
 
     def add(*terms):
@@ -1094,7 +1098,7 @@
                 + [pltpu.SemaphoreType.DMA((20,)), pltpu.SemaphoreType.DMA((4,))],
             ),
             out_shape=[shape((T, wide), bf16)] * 2 + [shape(parts, bf16)] * 2,
-            **params(),
+            **params(38),
         )(info, prod, up_fac, gate_fac, grad_low, grad_low_turned, low1_turned, full_down, *after)
 
     dup0, dgate0, keep, send = ffn_back(0)
@@ -1118,7 +1122,7 @@
             pltpu.SemaphoreType.DMA,
         ],
         out_shape=shape((T, D), f32),
-        **params(),
+        **params(36),
     )(full_up, full_gate, sum_two, dup0, dgate0, dup1, dgate1, dup2, dgate2, *outs)
     outs, gots = slot([grad_hidden] + gots, (r1, "near"), (r2, "far"))
 
@@ -1157,7 +1161,7 @@
             shape((D, T), bf16),
             shape((nf, 2, SMALL, PART), f32),
         ],
-        **params(),
+        **params(16),
     )(info, grad_hidden, xhat1, inv1, vectors, attended0, attended1, full_out, heads, small_two, *outs)
     outs, gots = slot([grad_branch] + gots, (r0, "all"), (r1, "all"))
 
@@ -1191,7 +1195,7 @@
                 scratch_shapes=[pltpu.VMEM((PART, T), f32)],
             ),
             out_shape=[shape((T, PART), bf16)] * 3,
-            **params(),
+            **params(16),
         )(lo, spans, qkv, qkv, qkv, grad_att, (lse0, lse1)[h], delta, mask_q, mask_k, cosine, sine, cosine, sine, *after)
 
     def qkv_back(h, grads, extra, *after):
@@ -1208,7 +1212,7 @@
                 out_specs=[whole(dims)] * 2,
             ),
             out_shape=[shape(dims, bf16)] * 2,
-            **params(),
+            **params(18),
         )(info, x_turned, att_turned, *grads, grad_branch, small, *after)
 
     grads0 = attend_back(0, *outs)
@@ -1234,7 +1238,7 @@
             scratch_shapes=[pltpu.VMEM((D, 3 * D), bf16), pltpu.SemaphoreType.DMA((4,))],
         ),
         out_shape=shape((T, D), f32),
-        **params(),
+        **params(16),
     )(whole_rows, *grads0, *grads1, sum_one, *qkv_pieces, *outs)
 
     outs, _ = slot([grad_input], (r4, "all"), apart=True)
@@ -1256,7 +1260,7 @@
             out_specs=[whole((R, FF)), whole((R, FF)), whole((W, D))],
         ),
         out_shape=[shape((R, FF), f32), shape((R, FF), f32), shape((W, D), f32)],
-        **params(),
+        **params(26),
     )(info, *r0.parts, *r1.parts, *r2.parts)
     sum_qkv, sum_out, sum_small = pl.pallas_call(
         functools.partial(qkv_out_kernel, (r3.order, r4.order)),
@@ -1267,7 +1271,7 @@
             out_specs=[whole((R, 3 * D)), whole((R, D)), whole((16, PART))],
         ),
         out_shape=[shape((R, 3 * D), f32), shape((R, D), f32), shape((16, PART), f32)],
-        **params(),
+        **params(16),
     )(info, *r3.parts, *r4.parts)
     return (
         query_loss,

time: 454 us -> 410 us (0.903)
  Pallas kernels: 261 us -> 201 us
  local copies, waits for them, and re-layouts: 28.4 us -> 48.3 us
  waiting for transfers between devices: 77 us -> 90.4 us
  other arithmetic: 18.9 us -> 7.07 us
    unnamed x133 -> x177, local copies, waits for them, and re-layouts: 12.1 us -> 37.6 us
    pallas_call x8, Pallas kernels: 24.6 us -> 5.53 us  [sums_of(): pl.pallas_call(functools.partial(drop_last, functools.partial(sums_kernel...]
    ppermute x72 -> x69, waiting for transfers between devices: 77 us -> 90.4 us  [xor_permute(): return lax.ppermute(value, axis, [(i, i ^ bits) for i in range(size)])]
    pallas_call x2, Pallas kernels: 18 us -> 9.28 us  [qkv_back(): pl.pallas_call(functools.partial(qkv_back_kernel, extra, orders[3 + h]),...]
    pallas_call x2, Pallas kernels: 37.4 us -> 31.2 us  [attend_back(): pl.pallas_call(kernel, grid_spec=pltpu.PrefetchScalarGridSpec(num_scalar_...]
    pallas_call x0 -> x3, Pallas kernels: none -> 6.15 us  [join(): pl.pallas_call(join_kernel, grid_spec=pltpu.PrefetchScalarGridSpec(num_sc...]
    pallas_call x2, Pallas kernels: 28 us -> 23.2 us  [attend(): pl.pallas_call(functools.partial(drop_last, attend_kernel, len(after), 7)...]
    ppermute x72 -> x69, starting transfers between devices: 58.9 us -> 56.2 us  [xor_permute(): return lax.ppermute(value, axis, [(i, i ^ bits) for i in range(size)])]
  transfers between devices with their start and end apart: 72 -> 69, of which waited for: 24 -> 32; matrix products, arithmetic and copies ran while one was open for 7% -> 4% of each run, Pallas kernels for 42% -> 36%
where the time goes in v3:
time: 410 us; the launch traced here: 406 us
  Pallas kernels  201 us (49%)
  waiting for transfers between devices  90.4 us (22%)
  starting transfers between devices  56.2 us (14%)
  local copies, waits for them, and re-layouts  48.3 us (12%)
  other arithmetic  7.07 us (2%)
    ppermute x69, waiting for transfers between devices, xor_permute(): return lax.ppermute(value, axis, [(i, i ^ bits) for i in range(size)])  90.4 us
    ppermute x69, starting transfers between devices, xor_permute(): return lax.ppermute(value, axis, [(i, i ^ bits) for i in range(size)])  56.2 us
    unnamed x177, local copies, waits for them, and re-layouts  37.6 us
    pallas_call x3, Pallas kernels, ffn_back(): pl.pallas_call(functools.partial(ffn_back_kernel, g, orders[g], groups),...  37 us
    pallas_call x2, Pallas kernels, attend_back(): pl.pallas_call(kernel, grid_spec=pltpu.PrefetchScalarGridSpec(num_scalar_...  31.2 us
    pallas_call x1, Pallas kernels, per_device(): pl.pallas_call(ffn_kernel, grid_spec=pltpu.PrefetchScalarGridSpec(num_sca...  29.2 us
    pallas_call x2, Pallas kernels, attend(): pl.pallas_call(functools.partial(drop_last, attend_kernel, len(after), 7)...  23.2 us
    pallas_call x1, Pallas kernels, per_device(): pl.pallas_call(functools.partial(ffn_input_back_kernel, groups), in_specs...  14.1 us
  transfers between devices with their start and end apart: 69, of which 32 were waited for; matrix products, arithmetic and copies ran while one was open for 4% of the time, Pallas kernels for 36%

profile of v3, /device:TPU:0, one launch (start us, length us, event | category | flops | bytes accessed | tf_op | source)
XLA Modules:
  0.0 405.7 jit_solution(16603071468546690268)
XLA Ops:
  1.2 2.6 collective-permute-start.1
  6.5 1.7 collective-permute-start.3
  14.1 2.0 constant_dynamic-slice_fusion
  16.0 1.9 constant_dynamic-slice_fusion.1
  18.0 1.9 fusion
  19.9 4.1 %collective-permute-done.4 = bf16[4,192]{1,0:T(4,128)(2,1)S(1)} collective-permute-done((bf16[4,192]{1,0:T(4,128)(2,1)S(1)}, bf16[4,192]{1,0:T(4,128)(2,1)S(1)}, u32[]{:S(2)}, u32[]{:S(2)}) %collective-permute-start.4) | collective-permute-done | bytes 1568 | tf_op jit(solution)/shard_map/ppermute | solution.py:683
  26.0 1.8 collective-permute-start.10
  34.9 11.0 %shard_map.212 = (bf16[1024,2304]{1,0:T(8,128)(2,1)S(1)}, bf16[768,1024]{1,0:T(8,128)(2,1)S(1)}) custom-call(s32[5]{0:T(128)S(1)} %stack.123.rows_ref, bf16[1024,768]{1,0:T(8,128)(2,1)S(1)} %bitcast.59, f32[1024,128]{1,0:T(8,128)S(1)} %get-tuple-element.244.cos_ref.refs_10_.refs_12_, f32[1024,128]{1,0:T(8,128)S(1)} %get-tuple-element.243.sin_ref.refs_11_.refs_13_, ...), custom_call_target="tpu_custom_call" | custom-call | flops 1 | bytes 1 | tf_op jit(solution)/shard_map/pallas_call | solution.py:850
  45.9 2.2 copy-done
  49.3 1.8 collective-permute-start.12
  52.8 2.3 copy-done.1
  55.1 11.7 %shard_map.213 = (bf16[1024,384]{1,0:T(8,128)(2,1)S(1)}, f32[3,8,1024]{2,1,0:T(8,128)S(1)}) custom-call(s32[4]{0:T(128)S(1)} %get-tuple-element.230.refs_0_, s32[4]{0:T(128)S(1)} %get-tuple-element.229.refs_1_, bf16[1024,2304]{1,0:T(8,128)(2,1)S(1)} %copy-done.1, bf16[1024,2304]{1,0:T(8,128)(2,1)S(1)} %copy-done.1, bf16[1024,2304]{1,0:T(8,128)(2,1)S(1)} %copy-done.1, ...), custom_call_target="tpu_custom_call" | custom-call | flops 1 | bytes 1 | tf_op jit(solution)/shard_map/pallas_call | solution.py:870
  71.6 1.8 collective-permute-start.14
  74.9 2.3 copy-done.2
  77.2 11.5 %shard_map.215 = (bf16[1024,384]{1,0:T(8,128)(2,1)S(1)}, f32[3,8,1024]{2,1,0:T(8,128)S(1)}) custom-call(s32[4]{0:T(128)S(1)} %get-tuple-element.230.refs_0_, s32[4]{0:T(128)S(1)} %get-tuple-element.229.refs_1_, bf16[1024,2304]{1,0:T(8,128)(2,1)S(1)} %copy-done.2, bf16[1024,2304]{1,0:T(8,128)(2,1)S(1)} %copy-done.2, bf16[1024,2304]{1,0:T(8,128)(2,1)S(1)} %copy-done.2, ...), custom_call_target="tpu_custom_call" | custom-call | flops 1 | bytes 1 | tf_op jit(solution)/shard_map/pallas_call | solution.py:870
  91.9 2.5 shard_map.216.refs_5_.refs_6_
  94.4 6.0 %shard_map.217 = (f32[1024,768]{1,0:T(8,128)S(1)}, f32[1024,128]{1,0:T(8,128)S(1)}, bf16[1024,768]{1,0:T(8,128)(2,1)S(1)}, bf16[768,1024]{1,0:T(8,128)(2,1)S(1)}, bf16[768,768]{1,0:T(8,128)(2,1)S(1)}) custom-call(s32[5]{0:T(128)S(1)} %stack.123.rows_ref, bf16[1024,384]{1,0:T(8,128)(2,1)S(1)} %copy-done.25, bf16[1024,384]{1,0:T(8,128)(2,1)S(1)} %copy-done.29, ...), custom_call_target="tpu_custom_call" | custom-call | flops 1 | bytes 1 | tf_op jit(solution)/shard_map/pallas_call | solution.py:904
  103.1 2.0 collective-permute-done.17.two_ref
  105.1 2.4 shard_map.218.refs_10_
  107.8 3.0 collective-permute-done.18.refs_11_
  110.9 29.2 %shard_map.219 = (bf16[1024,3072]{1,0:T(8,128)(2,1)}, bf16[1024,3072]{1,0:T(8,128)(2,1)}, bf16[1024,3072]{1,0:T(8,128)(2,1)}, f32[1024,768]{1,0:T(8,128)}, f32[1...) custom-call(s32[5]{0:T(128)S(1)} %stack.123.rows_ref, ...), custom_call_target="tpu_custom_call" | custom-call | flops 1 | bytes 1 | tf_op jit(solution)/shard_map/pallas_call | solution.py:919
  140.9 4.0 collective-permute-start.21
  146.6 2.9 collective-permute-done.20
  149.6 4.2 %collective-permute-done.22 = bf16[4,8,896]{2,1,0:T(8,128)(2,1)S(1)} collective-permute-done((bf16[4,8,896]{2,1,0:T(8,128)(2,1)S(1)}, bf16[4,8,896]{2,1,0:T(8,128)(2,1)S(1)}, u32[]{:S(2)}, u32[]{:S(2)}) %collective-permute-start.22) | collective-permute-done | bytes 57376 | tf_op jit(solution)/shard_map/ppermute | solution.py:683
  154.2 4.4 %collective-permute-done.23 = bf16[4,2,8,896]{3,2,0,1:T(8,128)(2,1)S(1)} collective-permute-done((bf16[4,2,8,896]{3,2,0,1:T(8,128)(2,1)S(1)}, bf16[4,2,8,896]{3,2,0,1:T(8,128)(2,1)S(1)}, u32[]{:S(2)}, u32[]{:S(2)}) %collective-permute-start.23) | collective-permute-done | bytes 114720 | tf_op jit(solution)/shard_map/ppermute | solution.py:683
  161.7 1.9 copy-done.55
  163.5 3.2 shard_map.221
  166.8 12.6 %shard_map.222 = (bf16[1024,1024]{1,0:T(8,128)(2,1)S(1)}, bf16[1024,1024]{1,0:T(8,128)(2,1)S(1)}, bf16[16,192,384]{2,1,0:T(8,128)(2,1)S(1)}, bf16[16,192,384]{2,1,0:T(8,128)(2,1)}) custom-call(s32[5]{0:T(128)S(1)} %stack.155.info_ref, bf16[1024,3072]{1,0:T(8,128)(2,1)} %get-tuple-element.140.prod_any, bf16[1024,3072]{1,0:T(8,128)(2,1)} %get-tuple-element.141.up_fac_any, ...), custom_call_target="tpu_custom_call" | custom-call | flops 1 | bytes 1 | tf_op jit(solution)/shard_map/pallas_call | solution.py:1087
  182.2 12.0 %shard_map.223 = (bf16[1024,1024]{1,0:T(8,128)(2,1)S(1)}, bf16[1024,1024]{1,0:T(8,128)(2,1)S(1)}, bf16[16,192,384]{2,1,0:T(8,128)(2,1)S(1)}, bf16[16,192,384]{2,1,0:T(8,128)(2,1)}) custom-call(s32[5]{0:T(128)S(1)} %stack.155.info_ref, bf16[1024,3072]{1,0:T(8,128)(2,1)} %get-tuple-element.140.prod_any, bf16[1024,3072]{1,0:T(8,128)(2,1)} %get-tuple-element.141.up_fac_any, ...), custom_call_target="tpu_custom_call" | custom-call | flops 1 | bytes 1 | tf_op jit(solution)/shard_map/pallas_call | solution.py:1087
  196.9 12.4 %shard_map.225 = (bf16[1024,1024]{1,0:T(8,128)(2,1)S(1)}, bf16[1024,1024]{1,0:T(8,128)(2,1)S(1)}, bf16[16,192,384]{2,1,0:T(8,128)(2,1)S(1)}, bf16[16,192,384]{2,1,0:T(8,128)(2,1)}) custom-call(s32[5]{0:T(128)S(1)} %stack.155.info_ref, bf16[1024,3072]{1,0:T(8,128)(2,1)} %get-tuple-element.140.prod_any, bf16[1024,3072]{1,0:T(8,128)(2,1)} %get-tuple-element.141.up_fac_any, ...), custom_call_target="tpu_custom_call" | custom-call | flops 1 | bytes 1 | tf_op jit(solution)/shard_map/pallas_call | solution.py:1087
  210.7 1.7 collective-permute-done.26.refs_4_.refs_8_
  223.3 14.1 %shard_map.227.refs_4_.grad_ref = f32[1024,768]{1,0:T(8,128)S(1)} custom-call(bf16[768,3072]{1,0:T(8,128)(2,1)} %get-tuple-element.134.wu_any, bf16[768,3072]{1,0:T(8,128)(2,1)} %get-tuple-element.135.wg_any, f32[1024,768]{1,0:T(8,128)} %copy-done.54, bf16[1024,1024]{1,0:T(8,128)(2,1)S(1)} %copy-done.59, bf16[1024,1024]{1,0:T(8,128)(2,1)S(1)} %copy-done.61, ...), custom_call_target="tpu_custom_call" | custom-call | flops 1 | bytes 1 | tf_op jit(solution)/shard_map/pallas_call | solution.py:1112
  240.3 6.8 %shard_map.229 = (f32[1024,768]{1,0:T(8,128)S(1)}, bf16[1024,768]{1,0:T(8,128)(2,1)S(1)}, bf16[1024,768]{1,0:T(8,128)(2,1)S(1)}, f32[6,8,1024]{2,1,0:T(8,128)S(1...) custom-call(s32[5]{0:T(128)S(1)} %stack.155.info_ref, f32[1024,768]{1,0:T(8,128)S(1)} %shard_map.227.refs_4_.grad_ref, ...), custom_call_target="tpu_custom_call" | custom-call | flops 1 | bytes 1 | tf_op jit(solution)/shard_map/pallas_call | solution.py:1129
  248.3 5.3 %collective-permute-done.32.refs_8_.refs_12_.refs_4_ = bf16[4,192,384]{2,1,0:T(8,128)(2,1)S(1)} collective-permute-done((bf16[4,192,384]{2,1,0:T(8,128)(2,1)S(1)}, bf16[4,192,384]{2,1,0:T(8,128)(2,1)S(1)}, u32[]{:S(2)}, u32[]{:S(2)}) %collective-permute-start.32) | collective-permute-done | bytes 589856 | tf_op jit(solution)/shard_map/ppermute | solution.py:683
  253.7 1.8 shard_map.230
  257.6 15.4 %shard_map.231 = (bf16[1024,384]{1,0:T(8,128)(2,1)S(1)}, bf16[1024,384]{1,0:T(8,128)(2,1)S(1)}, bf16[1024,384]{1,0:T(8,128)(2,1)S(1)}) custom-call(s32[4]{0:T(128)S(1)} %get-tuple-element.230.refs_0_, s32[4]{0:T(128)S(1)} %get-tuple-element.229.refs_1_, bf16[1024,2304]{1,0:T(8,128)(2,1)S(1)} %bitcast.58, bf16[1024,2304]{1,0:T(8,128)(2,1)S(1)} %bitcast.58, ...), custom_call_target="tpu_custom_call" | custom-call | flops 1 | bytes 1 | tf_op jit(solution)/shard_map/pallas_call | solution.py:1174
  273.5 2.8 collective-permute-start.38
  277.0 2.3 collective-permute-start.36
  279.3 4.6 %shard_map.233 = (bf16[16,112,384]{2,1,0:T(8,128)(2,1)S(1)}, bf16[16,112,384]{2,1,0:T(8,128)(2,1)S(1)}) custom-call(s32[5]{0:T(128)S(1)} %stack.155.info_ref, bf16[768,1024]{1,0:T(8,128)(2,1)S(1)} %copy-done.34, bf16[768,1024]{1,0:T(8,128)(2,1)S(1)} %copy-done.36, bf16[1024,384]{1,0:T(8,128)(2,1)S(1)} %get-tuple-element.174.refs_14_.gq_ref.gq0, ...), custom_call_target="tpu_custom_call" | custom-call | flops 1 | bytes 1 | tf_op jit(solution)/shard_map/pallas_call | solution.py:1203
  284.0 2.0 collective-permute-done.37.refs_10_.refs_24_.refs_6_
  285.9 1.8 collective-permute-done.38.refs_16_.refs_21_.refs_10_.refs_6_
  287.7 3.1 collective-permute-done.40.refs_19_.refs_14_.refs_11_
  291.5 1.7 collective-permute-start.45
  293.2 1.9 collective-permute-start.43
  296.3 1.7 collective-permute-start.42
  298.0 15.8 %shard_map.235 = (bf16[1024,384]{1,0:T(8,128)(2,1)S(1)}, bf16[1024,384]{1,0:T(8,128)(2,1)S(1)}, bf16[1024,384]{1,0:T(8,128)(2,1)S(1)}) custom-call(s32[4]{0:T(128)S(1)} %get-tuple-element.230.refs_0_, s32[4]{0:T(128)S(1)} %get-tuple-element.229.refs_1_, bf16[1024,2304]{1,0:T(8,128)(2,1)S(1)} %bitcast.58, bf16[1024,2304]{1,0:T(8,128)(2,1)S(1)} %bitcast.58, ...), custom_call_target="tpu_custom_call" | custom-call | flops 1 | bytes 1 | tf_op jit(solution)/shard_map/pallas_call | solution.py:1174
  314.3 2.1 collective-permute-start.49
  317.7 2.9 collective-permute-start.47
  320.6 4.6 %shard_map.237 = (bf16[16,96,384]{2,1,0:T(8,128)(2,1)S(1)}, bf16[16,96,384]{2,1,0:T(8,128)(2,1)S(1)}) custom-call(s32[5]{0:T(128)S(1)} %stack.155.info_ref, bf16[768,1024]{1,0:T(8,128)(2,1)S(1)} %copy-done.34, bf16[768,1024]{1,0:T(8,128)(2,1)S(1)} %copy-done.36, bf16[1024,384]{1,0:T(8,128)(2,1)S(1)} %get-tuple-element.193.refs_16_.gq_ref.gq1, ...), custom_call_target="tpu_custom_call" | custom-call | flops 1 | bytes 1 | tf_op jit(solution)/shard_map/pallas_call | solution.py:1203
  325.3 2.1 collective-permute-done.47.refs_3_.refs_16_
  327.3 5.4 %collective-permute-done.48.refs_9_.refs_17_ = bf16[1,192,384]{2,1,0:T(8,128)(2,1)S(1)} collective-permute-done((bf16[1,192,384]{2,1,0:T(8,128)(2,1)S(1)}, bf16[1,192,384]{2,1,0:T(8,128)(2,1)S(1)}, u32[]{:S(2)}, u32[]{:S(2)}) %collective-permute-start.48) | collective-permute-done | bytes 147488 | tf_op jit(solution)/shard_map/ppermute | solution.py:683
  332.7 2.8 collective-permute-done.50
  340.3 9.1 %shard_map.239 = f32[1024,768]{1,0:T(8,128)} custom-call(s32[5]{0:T(128)S(1)} %stack.123.rows_ref, bf16[1024,384]{1,0:T(8,128)(2,1)S(1)} %get-tuple-element.174.refs_14_.gq_ref.gq0, bf16[1024,384]{1,0:T(8,128)(2,1)S(1)} %copy-done.49, bf16[1024,384]{1,0:T(8,128)(2,1)S(1)} %copy-done.51, bf16[1024,384]{1,0:T(8,128)(2,1)S(1)} %get-tuple-element.193.refs_16_.gq_ref.gq1, ...), custom_call_target="tpu_custom_call" | custom-call | flops 1 | bytes 1 | tf_op jit(solution)/shard_map/pallas_call | solution.py:1231
  349.3 1.9 collective-permute-done.52
  352.8 10.2 %collective-permute-done.64 = bf16[2,192,384]{2,1,0:T(8,128)(2,1)S(1)} collective-permute-done((bf16[2,192,384]{2,1,0:T(8,128)(2,1)S(1)}, bf16[2,192,384]{2,1,0:T(8,128)(2,1)S(1)}, u32[]{:S(2)}, u32[]{:S(2)}) %collective-permute-start.64) | collective-permute-done | bytes 294944 | tf_op jit(solution)/shard_map/ppermute | solution.py:683
  363.0 1.7 collective-permute-start.65
  365.0 2.1 collective-permute-start.55
  367.7 8.2 %collective-permute-done.67 = bf16[2,192,384]{2,1,0:T(8,128)(2,1)S(1)} collective-permute-done((bf16[2,192,384]{2,1,0:T(8,128)(2,1)S(1)}, bf16[2,192,384]{2,1,0:T(8,128)(2,1)S(1)}, u32[]{:S(2)}, u32[]{:S(2)}) %collective-permute-start.67) | collective-permute-done | bytes 294944 | tf_op jit(solution)/shard_map/ppermute | solution.py:683
  377.7 6.3 %collective-permute-done.57 = bf16[1,96,384]{2,1,0:T(8,128)(2,1)S(1)} collective-permute-done((bf16[1,96,384]{2,1,0:T(8,128)(2,1)S(1)}, bf16[1,96,384]{2,1,0:T(8,128)(2,1)S(1)}, u32[]{:S(2)}, u32[]{:S(2)}) %collective-permute-start.57) | collective-permute-done | bytes 73760 | tf_op jit(solution)/shard_map/ppermute | solution.py:683
  385.2 4.5 %collective-permute-done.60 = bf16[1,96,384]{2,1,0:T(8,128)(2,1)S(1)} collective-permute-done((bf16[1,96,384]{2,1,0:T(8,128)(2,1)S(1)}, bf16[1,96,384]{2,1,0:T(8,128)(2,1)S(1)}, u32[]{:S(2)}, u32[]{:S(2)}) %collective-permute-start.60) | collective-permute-done | bytes 73760 | tf_op jit(solution)/shard_map/ppermute | solution.py:683
  389.7 3.8 collective-permute-done.58
  393.7 2.1 collective-permute-done.61
  396.7 5.7 %shard_map.241 = (f32[192,3072]{1,0:T(8,128)}, f32[192,3072]{1,0:T(8,128)}, f32[768,768]{1,0:T(8,128)}) custom-call(s32[5]{0:T(128)S(1)} %stack.155.info_ref, bf16[4,192,384]{2,1,0:T(8,128)(2,1)S(1)} %get-tuple-element.202.refs_4_.refs_0_, bf16[4,192,384]{2,1,0:T(8,128)(2,1)S(1)} %collective-permute-done.63.refs_1_, ...), custom_call_target="tpu_custom_call" | custom-call | flops 1 | bytes 1 | tf_op jit(solution)/shard_map/pallas_call | solution.py:1254
  402.6 2.3 shard_map.240
  (354 shorter events, 79.1 us)
Async XLA Ops:
  0.6 25.4 %collective-permute-start = (bf16[192,2304]{1,0:T(8,128)(2,1)}, bf16[192,2304]{1,0:T(8,128)(2,1)}, u32[]{:S(2)}, u32[]{:S(2)}) collective-permute-start(bf16[192,2304]{1,0:T(8,128)(2,1)} %refs_0_.7), channel_id=1, source_target_pairs={{0,1},{1,0},{2,3},{3,2},{4,5},{5,4},{6,7},{7,6},{8,9},{9,8},{10,11... | collective-permute-start | bytes 2654216 | tf_op jit(solution)/shard_map/ppermute | solution.py:683
  1.2 23.8 %collective-permute-start.1 = (bf16[192,2304]{1,0:T(8,128)(2,1)}, bf16[192,2304]{1,0:T(8,128)(2,1)}, u32[]{:S(2)}, u32[]{:S(2)}) collective-permute-start(bf16[192,2304]{1,0:T(8,128)(2,1)} %refs_0_.7), channel_id=1, source_target_pairs={{0,2},{1,3},{2,0},{3,1},{4,6},{5,7},{6,4},{7,5},{8,10},{9,11},{10,... | collective-permute-start | bytes 2654216 | tf_op jit(solution)/shard_map/ppermute | solution.py:683
  6.4 17.6 %collective-permute-start.4 = (bf16[4,192]{1,0:T(4,128)(2,1)S(1)}, bf16[4,192]{1,0:T(4,128)(2,1)S(1)}, u32[]{:S(2)}, u32[]{:S(2)}) collective-permute-start(bf16[4,192]{1,0:T(4,128)(2,1)S(1)} %pad_maximum_fusion.8), channel_id=1, source_target_pairs={{0,3},{1,2},{2,1},{3,0},{4,7},{5,6},{6,5},{7,4},{8,11},{9,10},{10,... | collective-permute-start | bytes 4616 | tf_op jit(solution)/shard_map/ppermute | solution.py:683
  6.5 18.0 %collective-permute-start.3 = (bf16[4,192]{1,0:T(4,128)(2,1)S(1)}, bf16[4,192]{1,0:T(4,128)(2,1)S(1)}, u32[]{:S(2)}, u32[]{:S(2)}) collective-permute-start(bf16[4,192]{1,0:T(4,128)(2,1)S(1)} %pad_maximum_fusion.8), channel_id=1, source_target_pairs={{0,2},{1,3},{2,0},{3,1},{4,6},{5,7},{6,4},{7,5},{8,10},{9,11},{10,... | collective-permute-start | bytes 4616 | tf_op jit(solution)/shard_map/ppermute | solution.py:683
  8.2 16.3 %collective-permute-start.2 = (bf16[4,192]{1,0:T(4,128)(2,1)S(1)}, bf16[4,192]{1,0:T(4,128)(2,1)S(1)}, u32[]{:S(2)}, u32[]{:S(2)}) collective-permute-start(bf16[4,192]{1,0:T(4,128)(2,1)S(1)} %pad_maximum_fusion.8), channel_id=1, source_target_pairs={{0,1},{1,0},{2,3},{3,2},{4,5},{5,4},{6,7},{7,6},{8,9},{9,8},{10,11... | collective-permute-start | bytes 4616 | tf_op jit(solution)/shard_map/ppermute | solution.py:683
  24.4 4.0 collective-permute-start.7
  24.5 4.8 %collective-permute-start.8 = (bf16[192,3072]{1,0:T(8,128)(2,1)}, bf16[192,3072]{1,0:T(8,128)(2,1)}, u32[]{:S(2)}, u32[]{:S(2)}) collective-permute-start(bf16[192,3072]{1,0:T(8,128)(2,1)} %refs_4_.1), channel_id=1, source_target_pairs={{0,1},{1,0},{2,3},{3,2},{4,5},{5,4},{6,7},{7,6},{8,9},{9,8},{10,11... | collective-permute-start | bytes 3538952 | tf_op jit(solution)/shard_map/ppermute | solution.py:683
  25.0 6.1 %collective-permute-start.9 = (bf16[768,768]{1,0:T(8,128)(2,1)}, bf16[768,768]{1,0:T(8,128)(2,1)}, u32[]{:S(2)}, u32[]{:S(2)}) collective-permute-start(bf16[768,768]{1,0:T(8,128)(2,1)} %refs_8_.1), channel_id=1, source_target_pairs={{0,1},{1,0},{2,3},{3,2},{4,5},{5,4},{6,7},{7,6},{8,9},{9,8},{10,11... | collective-permute-start | bytes 3538952 | tf_op jit(solution)/shard_map/ppermute | solution.py:683
  25.7 6.7 %collective-permute-start.5 = (bf16[192,2304]{1,0:T(8,128)(2,1)}, bf16[192,2304]{1,0:T(8,128)(2,1)}, u32[]{:S(2)}, u32[]{:S(2)}) collective-permute-start(bf16[192,2304]{1,0:T(8,128)(2,1)} %collective-permute-done.1.refs_2_), channel_id=1, source_target_pairs={{0,1},{1,0},{2,3},{3,2},{4,5},{5,4},{6,7},{7,6},{8,9},{9,8},{10,11... | collective-permute-start | bytes 2654216 | tf_op jit(solution)/shard_map/ppermute | solution.py:683
  26.0 23.2 %collective-permute-start.10 = (bf16[96,3840]{1,0:T(8,128)(2,1)}, bf16[96,3840]{1,0:T(8,128)(2,1)}, u32[]{:S(2)}, u32[]{:S(2)}) collective-permute-start(bf16[96,3840]{1,0:T(8,128)(2,1)} %pad_maximum_fusion), channel_id=1, source_target_pairs={{0,2},{1,3},{2,0},{3,1},{4,6},{5,7},{6,4},{7,5},{8,10},{9,11},{10,... | collective-permute-start | bytes 2211848 | tf_op jit(solution)/shard_map/ppermute | solution.py:683
  49.3 19.0 %collective-permute-start.12 = (bf16[96,3840]{1,0:T(8,128)(2,1)}, bf16[96,3840]{1,0:T(8,128)(2,1)S(1)}, u32[]{:S(2)}, u32[]{:S(2)}) collective-permute-start(bf16[96,3840]{1,0:T(8,128)(2,1)} %collective-permute-done.10.refs_7_.one_ref), channel_id=1, source_target_pairs={{0,4},{4,0},{8,12},{12,8},{16,20},{20,16},{24,28},{28,24},{1,5},{5... | collective-permute-start | bytes 2211848 | tf_op jit(solution)/shard_map/ppermute | solution.py:683
  51.1 16.4 %collective-permute-start.11 = (bf16[96,3072]{1,0:T(8,128)(2,1)}, bf16[96,3072]{1,0:T(8,128)(2,1)}, u32[]{:S(2)}, u32[]{:S(2)}) collective-permute-start(bf16[96,3072]{1,0:T(8,128)(2,1)} %constant_dynamic-slice_fusion.1), channel_id=1, source_target_pairs={{0,2},{1,3},{2,0},{3,1},{4,6},{5,7},{6,4},{7,5},{8,10},{9,11},{10,... | collective-permute-start | bytes 1769480 | tf_op jit(solution)/shard_map/ppermute | solution.py:683
  71.5 22.9 %collective-permute-start.13 = (bf16[192,3840]{1,0:T(8,128)(2,1)S(1)}, bf16[192,3840]{1,0:T(8,128)(2,1)}, u32[]{:S(2)}, u32[]{:S(2)}) collective-permute-start(bf16[192,3840]{1,0:T(8,128)(2,1)S(1)} %shard_map.214.refs_8_.refs_2_), channel_id=1, source_target_pairs={{0,1},{1,0},{2,3},{3,2},{4,5},{5,4},{6,7},{7,6},{8,9},{9,8},{10,11... | collective-permute-start | bytes 4423688 | tf_op jit(solution)/shard_map/ppermute | solution.py:683
  71.6 18.0 %collective-permute-start.14 = (bf16[384,768]{1,0:T(8,128)(2,1)}, bf16[384,768]{1,0:T(8,128)(2,1)}, u32[]{:S(2)}, u32[]{:S(2)}) collective-permute-start(bf16[384,768]{1,0:T(8,128)(2,1)} %constant_dynamic-slice_fusion), channel_id=1, source_target_pairs={{0,2},{1,3},{2,0},{3,1},{4,6},{5,7},{6,4},{7,5},{8,10},{9,11},{10,... | collective-permute-start | bytes 1769480 | tf_op jit(solution)/shard_map/ppermute | solution.py:683
  73.3 16.3 %collective-permute-start.15 = (bf16[96,3072]{1,0:T(8,128)(2,1)}, bf16[96,3072]{1,0:T(8,128)(2,1)}, u32[]{:S(2)}, u32[]{:S(2)}) collective-permute-start(bf16[96,3072]{1,0:T(8,128)(2,1)} %collective-permute-done.11.refs_1_.refs_7_.one_ref), channel_id=1, source_target_pairs={{0,4},{4,0},{8,12},{12,8},{16,20},{20,16},{24,28},{28,24},{1,5},{5... | collective-permute-start | bytes 1769480 | tf_op jit(solution)/shard_map/ppermute | solution.py:683
  89.6 15.5 %collective-permute-start.17 = (bf16[384,768]{1,0:T(8,128)(2,1)}, bf16[384,768]{1,0:T(8,128)(2,1)}, u32[]{:S(2)}, u32[]{:S(2)}) collective-permute-start(bf16[384,768]{1,0:T(8,128)(2,1)} %collective-permute-done.14.refs_1_.refs_4_.one_ref), channel_id=1, source_target_pairs={{0,4},{4,0},{8,12},{12,8},{16,20},{20,16},{24,28},{28,24},{1,5},{5... | collective-permute-start | bytes 1769480 | tf_op jit(solution)/shard_map/ppermute | solution.py:683
  94.3 13.4 %collective-permute-start.16 = (bf16[192,3072]{1,0:T(8,128)(2,1)}, bf16[192,3072]{1,0:T(8,128)(2,1)}, u32[]{:S(2)}, u32[]{:S(2)}) collective-permute-start(bf16[192,3072]{1,0:T(8,128)(2,1)} %shard_map.216.refs_5_.refs_6_), channel_id=1, source_target_pairs={{0,1},{1,0},{2,3},{3,2},{4,5},{5,4},{6,7},{7,6},{8,9},{9,8},{10,11... | collective-permute-start | bytes 3538952 | tf_op jit(solution)/shard_map/ppermute | solution.py:683
  140.9 5.7 %collective-permute-start.21 = (bf16[8,896]{1,0:T(8,128)(2,1)S(1)}, bf16[8,896]{1,0:T(8,128)(2,1)S(1)}, u32[]{:S(2)}, u32[]{:S(2)}) collective-permute-start(bf16[8,896]{1,0:T(8,128)(2,1)S(1)} %get-tuple-element.242), channel_id=1, source_target_pairs={{0,24},{4,28},{8,16},{12,20},{16,8},{20,12},{24,0},{28,4},{1,25},{... | collective-permute-start | bytes 43016 | tf_op jit(solution)/shard_map/ppermute | solution.py:683
  144.9 4.6 %collective-permute-start.20 = (bf16[8,896]{1,0:T(8,128)(2,1)S(1)}, bf16[8,896]{1,0:T(8,128)(2,1)S(1)}, u32[]{:S(2)}, u32[]{:S(2)}) collective-permute-start(bf16[8,896]{1,0:T(8,128)(2,1)S(1)} %get-tuple-element.242), channel_id=1, source_target_pairs={{0,16},{4,20},{8,24},{12,28},{16,0},{20,4},{24,8},{28,12},{1,17},{... | collective-permute-start | bytes 43016 | tf_op jit(solution)/shard_map/ppermute | solution.py:683
  144.9 4.6 %collective-permute-start.19 = (bf16[8,896]{1,0:T(8,128)(2,1)S(1)}, bf16[8,896]{1,0:T(8,128)(2,1)S(1)}, u32[]{:S(2)}, u32[]{:S(2)}) collective-permute-start(bf16[8,896]{1,0:T(8,128)(2,1)S(1)} %get-tuple-element.242), channel_id=1, source_target_pairs={{0,8},{4,12},{8,0},{12,4},{16,24},{20,28},{24,16},{28,20},{1,9},{5... | collective-permute-start | bytes 43016 | tf_op jit(solution)/shard_map/ppermute | solution.py:683
  149.5 4.2 %collective-permute-start.22 = (bf16[4,8,896]{2,1,0:T(8,128)(2,1)S(1)}, bf16[4,8,896]{2,1,0:T(8,128)(2,1)S(1)}, u32[]{:S(2)}, u32[]{:S(2)}) collective-permute-start(bf16[4,8,896]{2,1,0:T(8,128)(2,1)S(1)} %get-tuple-element.236), channel_id=1, source_target_pairs={{0,2},{1,3},{2,0},{3,1},{4,6},{5,7},{6,4},{7,5},{8,10},{9,11},{10,... | collective-permute-start | bytes 172040 | tf_op jit(solution)/shard_map/ppermute | solution.py:683
  153.8 4.9 %collective-permute-start.23 = (bf16[4,2,8,896]{3,2,0,1:T(8,128)(2,1)S(1)}, bf16[4,2,8,896]{3,2,0,1:T(8,128)(2,1)S(1)}, u32[]{:S(2)}, u32[]{:S(2)}) collective-permute-start(bf16[4,2,8,896]{3,2,0,1:T(8,128)(2,1)S(1)} %get-tuple-element.234), channel_id=1, source_target_pairs={{0,4},{4,0},{8,12},{12,8},{16,20},{20,16},{24,28},{28,24},{1,5},{5... | collective-permute-start | bytes 344072 | tf_op jit(solution)/shard_map/ppermute | solution.py:683
  182.0 12.6 %collective-permute-start.25 = (bf16[16,192,384]{2,1,0:T(8,128)(2,1)}, bf16[16,192,384]{2,1,0:T(8,128)(2,1)S(1)}, u32[]{:S(2)}, u32[]{:S(2)}) collective-permute-start(bf16[16,192,384]{2,1,0:T(8,128)(2,1)} %get-tuple-element.149.refs_0_), channel_id=1, source_target_pairs={{0,1},{1,0},{2,3},{3,2},{4,5},{5,4},{6,7},{7,6},{8,9},{9,8},{10,11... | collective-permute-start | bytes 7077896 | tf_op jit(solution)/shard_map/ppermute | solution.py:683
  194.2 19.1 %collective-permute-start.27 = (bf16[16,192,384]{2,1,0:T(8,128)(2,1)}, bf16[16,192,384]{2,1,0:T(8,128)(2,1)S(1)}, u32[]{:S(2)}, u32[]{:S(2)}) collective-permute-start(bf16[16,192,384]{2,1,0:T(8,128)(2,1)} %get-tuple-element.152.refs_0_), channel_id=1, source_target_pairs={{0,1},{1,0},{2,3},{3,2},{4,5},{5,4},{6,7},{7,6},{8,9},{9,8},{10,11... | collective-permute-start | bytes 7077896 | tf_op jit(solution)/shard_map/ppermute | solution.py:683
  196.8 15.6 %collective-permute-start.26 = (bf16[4,192,384]{2,1,0:T(8,128)(2,1)S(1)}, bf16[4,192,384]{2,1,0:T(8,128)(2,1)S(1)}, u32[]{:S(2)}, u32[]{:S(2)}) collective-permute-start(bf16[4,192,384]{2,1,0:T(8,128)(2,1)S(1)} %shard_map.224.refs_1_), channel_id=1, source_target_pairs={{0,2},{1,3},{2,0},{3,1},{4,6},{5,7},{6,4},{7,5},{8,10},{9,11},{10,... | collective-permute-start | bytes 1769480 | tf_op jit(solution)/shard_map/ppermute | solution.py:683
  213.2 24.2 %collective-permute-start.28 = (bf16[16,192,384]{2,1,0:T(8,128)(2,1)}, bf16[16,192,384]{2,1,0:T(8,128)(2,1)S(1)}, u32[]{:S(2)}, u32[]{:S(2)}) collective-permute-start(bf16[16,192,384]{2,1,0:T(8,128)(2,1)} %get-tuple-element.165), channel_id=1, source_target_pairs={{0,1},{1,0},{2,3},{3,2},{4,5},{5,4},{6,7},{7,6},{8,9},{9,8},{10,11... | collective-permute-start | bytes 7077896 | tf_op jit(solution)/shard_map/ppermute | solution.py:683
  217.4 20.0 %collective-permute-start.29 = (bf16[4,192,384]{2,1,0:T(8,128)(2,1)}, bf16[4,192,384]{2,1,0:T(8,128)(2,1)S(1)}, u32[]{:S(2)}, u32[]{:S(2)}) collective-permute-start(bf16[4,192,384]{2,1,0:T(8,128)(2,1)} %get-tuple-element.157.refs_6_), channel_id=1, source_target_pairs={{0,2},{1,3},{2,0},{3,1},{4,6},{5,7},{6,4},{7,5},{8,10},{9,11},{10,... | collective-permute-start | bytes 1769480 | tf_op jit(solution)/shard_map/ppermute | solution.py:683
  217.8 19.6 %collective-permute-start.30 = (bf16[4,192,384]{2,1,0:T(8,128)(2,1)}, bf16[4,192,384]{2,1,0:T(8,128)(2,1)S(1)}, u32[]{:S(2)}, u32[]{:S(2)}) collective-permute-start(bf16[4,192,384]{2,1,0:T(8,128)(2,1)} %get-tuple-element.158.refs_7_), channel_id=1, source_target_pairs={{0,8},{4,12},{8,0},{12,4},{16,24},{20,28},{24,16},{28,20},{1,9},{5... | collective-permute-start | bytes 1769480 | tf_op jit(solution)/shard_map/ppermute | solution.py:683
  217.8 19.6 %collective-permute-start.31 = (bf16[4,192,384]{2,1,0:T(8,128)(2,1)}, bf16[4,192,384]{2,1,0:T(8,128)(2,1)}, u32[]{:S(2)}, u32[]{:S(2)}) collective-permute-start(bf16[4,192,384]{2,1,0:T(8,128)(2,1)} %get-tuple-element.159.refs_8_), channel_id=1, source_target_pairs={{0,4},{4,0},{8,12},{12,8},{16,20},{20,16},{24,28},{28,24},{1,5},{5... | collective-permute-start | bytes 1769480 | tf_op jit(solution)/shard_map/ppermute | solution.py:683
  237.8 15.8 %collective-permute-start.32 = (bf16[4,192,384]{2,1,0:T(8,128)(2,1)S(1)}, bf16[4,192,384]{2,1,0:T(8,128)(2,1)S(1)}, u32[]{:S(2)}, u32[]{:S(2)}) collective-permute-start(bf16[4,192,384]{2,1,0:T(8,128)(2,1)S(1)} %get-tuple-element.166.refs_0_), channel_id=1, source_target_pairs={{0,4},{4,0},{8,12},{12,8},{16,20},{20,16},{24,28},{28,24},{1,5},{5... | collective-permute-start | bytes 1769480 | tf_op jit(solution)/shard_map/ppermute | solution.py:683
  238.2 15.5 %collective-permute-start.33 = (bf16[4,192,384]{2,1,0:T(8,128)(2,1)S(1)}, bf16[4,192,384]{2,1,0:T(8,128)(2,1)S(1)}, u32[]{:S(2)}, u32[]{:S(2)}) collective-permute-start(bf16[4,192,384]{2,1,0:T(8,128)(2,1)S(1)} %get-tuple-element.167.refs_1_), channel_id=1, source_target_pairs={{0,2},{1,3},{2,0},{3,1},{4,6},{5,7},{6,4},{7,5},{8,10},{9,11},{10,... | collective-permute-start | bytes 1769480 | tf_op jit(solution)/shard_map/ppermute | solution.py:683
  255.6 17.4 %collective-permute-start.35 = (bf16[4,192,384]{2,1,0:T(8,128)(2,1)S(1)}, bf16[4,192,384]{2,1,0:T(8,128)(2,1)S(1)}, u32[]{:S(2)}, u32[]{:S(2)}) collective-permute-start(bf16[4,192,384]{2,1,0:T(8,128)(2,1)S(1)} %get-tuple-element.173.refs_15_), channel_id=1, source_target_pairs={{0,2},{1,3},{2,0},{3,1},{4,6},{5,7},{6,4},{7,5},{8,10},{9,11},{10,... | collective-permute-start | bytes 1769480 | tf_op jit(solution)/shard_map/ppermute | solution.py:683
  256.0 17.0 %collective-permute-start.34 = (bf16[2,192,384]{2,1,0:T(8,128)(2,1)S(1)}, bf16[2,192,384]{2,1,0:T(8,128)(2,1)S(1)}, u32[]{:S(2)}, u32[]{:S(2)}) collective-permute-start(bf16[2,192,384]{2,1,0:T(8,128)(2,1)S(1)} %get-tuple-element.172.refs_14_), channel_id=1, source_target_pairs={{0,4},{4,0},{8,12},{12,8},{16,20},{20,16},{24,28},{28,24},{1,5},{5... | collective-permute-start | bytes 884744 | tf_op jit(solution)/shard_map/ppermute | solution.py:683
  273.5 14.2 %collective-permute-start.38 = (bf16[4,192,384]{2,1,0:T(8,128)(2,1)S(1)}, bf16[4,192,384]{2,1,0:T(8,128)(2,1)S(1)}, u32[]{:S(2)}, u32[]{:S(2)}) collective-permute-start(bf16[4,192,384]{2,1,0:T(8,128)(2,1)S(1)} %get-tuple-element.180.refs_0_), channel_id=1, source_target_pairs={{0,2},{1,3},{2,0},{3,1},{4,6},{5,7},{6,4},{7,5},{8,10},{9,11},{10,... | collective-permute-start | bytes 1769480 | tf_op jit(solution)/shard_map/ppermute | solution.py:683
  276.3 9.6 %collective-permute-start.37 = (bf16[2,192,384]{2,1,0:T(8,128)(2,1)S(1)}, bf16[2,192,384]{2,1,0:T(8,128)(2,1)S(1)}, u32[]{:S(2)}, u32[]{:S(2)}) collective-permute-start(bf16[2,192,384]{2,1,0:T(8,128)(2,1)S(1)} %get-tuple-element.179.refs_3_), channel_id=1, source_target_pairs={{0,8},{4,12},{8,0},{12,4},{16,24},{20,28},{24,16},{28,20},{1,9},{5... | collective-permute-start | bytes 884744 | tf_op jit(solution)/shard_map/ppermute | solution.py:683
  276.3 9.6 %collective-permute-start.39 = (bf16[2,192,384]{2,1,0:T(8,128)(2,1)S(1)}, bf16[2,192,384]{2,1,0:T(8,128)(2,1)S(1)}, u32[]{:S(2)}, u32[]{:S(2)}) collective-permute-start(bf16[2,192,384]{2,1,0:T(8,128)(2,1)S(1)} %get-tuple-element.181.refs_1_), channel_id=1, source_target_pairs={{0,4},{4,0},{8,12},{12,8},{16,20},{20,16},{24,28},{28,24},{1,5},{5... | collective-permute-start | bytes 884744 | tf_op jit(solution)/shard_map/ppermute | solution.py:683
  277.0 7.0 %collective-permute-start.36 = (bf16[1,192,384]{2,1,0:T(8,128)(2,1)S(1)}, bf16[1,192,384]{2,1,0:T(8,128)(2,1)S(1)}, u32[]{:S(2)}, u32[]{:S(2)}) collective-permute-start(bf16[1,192,384]{2,1,0:T(8,128)(2,1)S(1)} %get-tuple-element.178.refs_2_), channel_id=1, source_target_pairs={{0,16},{4,20},{8,24},{12,28},{16,0},{20,4},{24,8},{28,12},{1,17},{... | collective-permute-start | bytes 442376 | tf_op jit(solution)/shard_map/ppermute | solution.py:683
  291.5 22.4 %collective-permute-start.45 = (bf16[8,112,384]{2,1,0:T(8,128)(2,1)S(1)}, bf16[8,112,384]{2,1,0:T(8,128)(2,1)S(1)}, u32[]{:S(2)}, u32[]{:S(2)}) collective-permute-start(bf16[8,112,384]{2,1,0:T(8,128)(2,1)S(1)} %get-tuple-element.192.refs_18_), channel_id=1, source_target_pairs={{0,2},{1,3},{2,0},{3,1},{4,6},{5,7},{6,4},{7,5},{8,10},{9,11},{10,... | collective-permute-start | bytes 2064392 | tf_op jit(solution)/shard_map/ppermute | solution.py:683
  293.2 20.6 %collective-permute-start.43 = (bf16[2,192,384]{2,1,0:T(8,128)(2,1)S(1)}, bf16[2,192,384]{2,1,0:T(8,128)(2,1)S(1)}, u32[]{:S(2)}, u32[]{:S(2)}) collective-permute-start(bf16[2,192,384]{2,1,0:T(8,128)(2,1)S(1)} %get-tuple-element.190.refs_16_), channel_id=1, source_target_pairs={{0,4},{4,0},{8,12},{12,8},{16,20},{20,16},{24,28},{28,24},{1,5},{5... | collective-permute-start | bytes 884744 | tf_op jit(solution)/shard_map/ppermute | solution.py:683
  295.1 18.7 %collective-permute-start.44 = (bf16[2,192,384]{2,1,0:T(8,128)(2,1)S(1)}, bf16[2,192,384]{2,1,0:T(8,128)(2,1)S(1)}, u32[]{:S(2)}, u32[]{:S(2)}) collective-permute-start(bf16[2,192,384]{2,1,0:T(8,128)(2,1)S(1)} %get-tuple-element.191.refs_17_), channel_id=1, source_target_pairs={{0,8},{4,12},{8,0},{12,4},{16,24},{20,28},{24,16},{28,20},{1,9},{5... | collective-permute-start | bytes 884744 | tf_op jit(solution)/shard_map/ppermute | solution.py:683
  295.1 18.7 %collective-permute-start.41 = (bf16[1,192,384]{2,1,0:T(8,128)(2,1)S(1)}, bf16[1,192,384]{2,1,0:T(8,128)(2,1)S(1)}, u32[]{:S(2)}, u32[]{:S(2)}) collective-permute-start(bf16[1,192,384]{2,1,0:T(8,128)(2,1)S(1)} %get-tuple-element.188.refs_14_.refs_0_), channel_id=1, source_target_pairs={{0,16},{4,20},{8,24},{12,28},{16,0},{20,4},{24,8},{28,12},{1,17},{... | collective-permute-start | bytes 442376 | tf_op jit(solution)/shard_map/ppermute | solution.py:683
  296.3 17.5 %collective-permute-start.42 = (bf16[1,192,384]{2,1,0:T(8,128)(2,1)S(1)}, bf16[1,192,384]{2,1,0:T(8,128)(2,1)S(1)}, u32[]{:S(2)}, u32[]{:S(2)}) collective-permute-start(bf16[1,192,384]{2,1,0:T(8,128)(2,1)S(1)} %get-tuple-element.189.refs_15_), channel_id=1, source_target_pairs={{0,16},{4,20},{8,24},{12,28},{16,0},{20,4},{24,8},{28,12},{1,17},{... | collective-permute-start | bytes 442376 | tf_op jit(solution)/shard_map/ppermute | solution.py:683
  314.3 18.5 %collective-permute-start.49 = (bf16[4,112,384]{2,1,0:T(8,128)(2,1)S(1)}, bf16[4,112,384]{2,1,0:T(8,128)(2,1)S(1)}, u32[]{:S(2)}, u32[]{:S(2)}) collective-permute-start(bf16[4,112,384]{2,1,0:T(8,128)(2,1)S(1)} %get-tuple-element.200.refs_3_), channel_id=1, source_target_pairs={{0,8},{4,12},{8,0},{12,4},{16,24},{20,28},{24,16},{28,20},{1,9},{5... | collective-permute-start | bytes 1032200 | tf_op jit(solution)/shard_map/ppermute | solution.py:683
  316.4 16.4 %collective-permute-start.46 = (bf16[2,192,384]{2,1,0:T(8,128)(2,1)S(1)}, bf16[2,192,384]{2,1,0:T(8,128)(2,1)S(1)}, u32[]{:S(2)}, u32[]{:S(2)}) collective-permute-start(bf16[2,192,384]{2,1,0:T(8,128)(2,1)S(1)} %get-tuple-element.197.refs_0_), channel_id=1, source_target_pairs={{0,4},{4,0},{8,12},{12,8},{16,20},{20,16},{24,28},{28,24},{1,5},{5... | collective-permute-start | bytes 884744 | tf_op jit(solution)/shard_map/ppermute | solution.py:683
  317.7 9.7 %collective-permute-start.47 = (bf16[1,192,384]{2,1,0:T(8,128)(2,1)S(1)}, bf16[1,192,384]{2,1,0:T(8,128)(2,1)S(1)}, u32[]{:S(2)}, u32[]{:S(2)}) collective-permute-start(bf16[1,192,384]{2,1,0:T(8,128)(2,1)S(1)} %get-tuple-element.198.refs_1_.refs_2_), channel_id=1, source_target_pairs={{0,16},{4,20},{8,24},{12,28},{16,0},{20,4},{24,8},{28,12},{1,17},{... | collective-permute-start | bytes 442376 | tf_op jit(solution)/shard_map/ppermute | solution.py:683
  320.6 12.1 %collective-permute-start.48 = (bf16[1,192,384]{2,1,0:T(8,128)(2,1)S(1)}, bf16[1,192,384]{2,1,0:T(8,128)(2,1)S(1)}, u32[]{:S(2)}, u32[]{:S(2)}) collective-permute-start(bf16[1,192,384]{2,1,0:T(8,128)(2,1)S(1)} %get-tuple-element.199.refs_2_), channel_id=1, source_target_pairs={{0,16},{4,20},{8,24},{12,28},{16,0},{20,4},{24,8},{28,12},{1,17},{... | collective-permute-start | bytes 442376 | tf_op jit(solution)/shard_map/ppermute | solution.py:683
  335.8 15.4 %collective-permute-start.52 = (bf16[8,96,384]{2,1,0:T(8,128)(2,1)S(1)}, bf16[8,96,384]{2,1,0:T(8,128)(2,1)S(1)}, u32[]{:S(2)}, u32[]{:S(2)}) collective-permute-start(bf16[8,96,384]{2,1,0:T(8,128)(2,1)S(1)} %add_convert_fusion.refs_8_), channel_id=1, source_target_pairs={{0,2},{1,3},{2,0},{3,1},{4,6},{5,7},{6,4},{7,5},{8,10},{9,11},{10,... | collective-permute-start | bytes 1769480 | tf_op jit(solution)/shard_map/ppermute | solution.py:683
  336.2 15.2 %collective-permute-start.51 = (bf16[2,112,384]{2,1,0:T(8,128)(2,1)S(1)}, bf16[2,112,384]{2,1,0:T(8,128)(2,1)S(1)}, u32[]{:S(2)}, u32[]{:S(2)}) collective-permute-start(bf16[2,112,384]{2,1,0:T(8,128)(2,1)S(1)} %get-tuple-element.205.refs_7_), channel_id=1, source_target_pairs={{0,4},{4,0},{8,12},{12,8},{16,20},{20,16},{24,28},{28,24},{1,5},{5... | collective-permute-start | bytes 516104 | tf_op jit(solution)/shard_map/ppermute | solution.py:683
  336.9 59.8 %collective-permute-start.63 = (bf16[4,192,384]{2,1,0:T(8,128)(2,1)S(1)}, bf16[4,192,384]{2,1,0:T(8,128)(2,1)S(1)}, u32[]{:S(2)}, u32[]{:S(2)}) collective-permute-start(bf16[4,192,384]{2,1,0:T(8,128)(2,1)S(1)} %get-tuple-element.202.refs_4_.refs_0_), channel_id=1, source_target_pairs={{0,8},{4,12},{8,0},{12,4},{16,24},{20,28},{24,16},{28,20},{1,9},{5... | collective-permute-start | bytes 1769480 | tf_op jit(solution)/shard_map/ppermute | solution.py:683
  337.4 25.6 %collective-permute-start.64 = (bf16[2,192,384]{2,1,0:T(8,128)(2,1)S(1)}, bf16[2,192,384]{2,1,0:T(8,128)(2,1)S(1)}, u32[]{:S(2)}, u32[]{:S(2)}) collective-permute-start(bf16[2,192,384]{2,1,0:T(8,128)(2,1)S(1)} %get-tuple-element.217.refs_5_), channel_id=1, source_target_pairs={{0,8},{4,12},{8,0},{12,4},{16,24},{20,28},{24,16},{28,20},{1,9},{5... | collective-permute-start | bytes 884744 | tf_op jit(solution)/shard_map/ppermute | solution.py:683
  338.9 25.9 %collective-permute-start.66 = (bf16[1,192,384]{2,1,0:T(8,128)(2,1)S(1)}, bf16[1,192,384]{2,1,0:T(8,128)(2,1)S(1)}, u32[]{:S(2)}, u32[]{:S(2)}) collective-permute-start(bf16[1,192,384]{2,1,0:T(8,128)(2,1)S(1)} %get-tuple-element.219.refs_6_), channel_id=1, source_target_pairs={{0,16},{4,20},{8,24},{12,28},{16,0},{20,4},{24,8},{28,12},{1,17},{... | collective-permute-start | bytes 442376 | tf_op jit(solution)/shard_map/ppermute | solution.py:683
  351.3 13.6 %collective-permute-start.54 = (bf16[4,96,384]{2,1,0:T(8,128)(2,1)S(1)}, bf16[4,96,384]{2,1,0:T(8,128)(2,1)S(1)}, u32[]{:S(2)}, u32[]{:S(2)}) collective-permute-start(bf16[4,96,384]{2,1,0:T(8,128)(2,1)S(1)} %add_convert_fusion.1), channel_id=1, source_target_pairs={{0,4},{4,0},{8,12},{12,8},{16,20},{20,16},{24,28},{28,24},{1,5},{5... | collective-permute-start | bytes 884744 | tf_op jit(solution)/shard_map/ppermute | solution.py:683
  351.5 15.6 %collective-permute-start.53 = (bf16[1,112,384]{2,1,0:T(8,128)(2,1)S(1)}, bf16[1,112,384]{2,1,0:T(8,128)(2,1)S(1)}, u32[]{:S(2)}, u32[]{:S(2)}) collective-permute-start(bf16[1,112,384]{2,1,0:T(8,128)(2,1)S(1)} %add_convert_fusion.4), channel_id=1, source_target_pairs={{0,16},{4,20},{8,24},{12,28},{16,0},{20,4},{24,8},{28,12},{1,17},{... | collective-permute-start | bytes 258056 | tf_op jit(solution)/shard_map/ppermute | solution.py:683
  363.0 33.7 %collective-permute-start.65 = (bf16[4,192,384]{2,1,0:T(8,128)(2,1)S(1)}, bf16[4,192,384]{2,1,0:T(8,128)(2,1)S(1)}, u32[]{:S(2)}, u32[]{:S(2)}) collective-permute-start(bf16[4,192,384]{2,1,0:T(8,128)(2,1)S(1)} %constant_dynamic-update-slice_fusion.4.refs_2_), channel_id=1, source_target_pairs={{0,4},{4,0},{8,12},{12,8},{16,20},{20,16},{24,28},{28,24},{1,5},{5... | collective-permute-start | bytes 1769480 | tf_op jit(solution)/shard_map/ppermute | solution.py:683
  364.8 11.1 %collective-permute-start.67 = (bf16[2,192,384]{2,1,0:T(8,128)(2,1)S(1)}, bf16[2,192,384]{2,1,0:T(8,128)(2,1)S(1)}, u32[]{:S(2)}, u32[]{:S(2)}) collective-permute-start(bf16[2,192,384]{2,1,0:T(8,128)(2,1)S(1)} %constant_dynamic-update-slice_fusion.6), channel_id=1, source_target_pairs={{0,8},{4,12},{8,0},{12,4},{16,24},{20,28},{24,16},{28,20},{1,9},{5... | collective-permute-start | bytes 884744 | tf_op jit(solution)/shard_map/ppermute | solution.py:683
  365.0 12.5 %collective-permute-start.55 = (bf16[2,96,384]{2,1,0:T(8,128)(2,1)S(1)}, bf16[2,96,384]{2,1,0:T(8,128)(2,1)S(1)}, u32[]{:S(2)}, u32[]{:S(2)}) collective-permute-start(bf16[2,96,384]{2,1,0:T(8,128)(2,1)S(1)} %add_convert_fusion.2), channel_id=1, source_target_pairs={{0,8},{4,12},{8,0},{12,4},{16,24},{20,28},{24,16},{28,20},{1,9},{5... | collective-permute-start | bytes 442376 | tf_op jit(solution)/shard_map/ppermute | solution.py:683
  367.2 10.5 %collective-permute-start.56 = (bf16[1,112,384]{2,1,0:T(8,128)(2,1)S(1)}, bf16[1,112,384]{2,1,0:T(8,128)(2,1)S(1)}, u32[]{:S(2)}, u32[]{:S(2)}) collective-permute-start(bf16[1,112,384]{2,1,0:T(8,128)(2,1)S(1)} %add_convert_fusion.3), channel_id=1, source_target_pairs={{0,16},{4,20},{8,24},{12,28},{16,0},{20,4},{24,8},{28,12},{1,17},{... | collective-permute-start | bytes 258056 | tf_op jit(solution)/shard_map/ppermute | solution.py:683
  376.0 20.7 %collective-permute-start.68 = (bf16[4,192,384]{2,1,0:T(8,128)(2,1)S(1)}, bf16[4,192,384]{2,1,0:T(8,128)(2,1)S(1)}, u32[]{:S(2)}, u32[]{:S(2)}) collective-permute-start(bf16[4,192,384]{2,1,0:T(8,128)(2,1)S(1)} %constant_dynamic-update-slice_fusion.8.refs_4_), channel_id=1, source_target_pairs={{0,4},{4,0},{8,12},{12,8},{16,20},{20,16},{24,28},{28,24},{1,5},{5... | collective-permute-start | bytes 1769480 | tf_op jit(solution)/shard_map/ppermute | solution.py:683
  377.6 6.4 %collective-permute-start.57 = (bf16[1,96,384]{2,1,0:T(8,128)(2,1)S(1)}, bf16[1,96,384]{2,1,0:T(8,128)(2,1)S(1)}, u32[]{:S(2)}, u32[]{:S(2)}) collective-permute-start(bf16[1,96,384]{2,1,0:T(8,128)(2,1)S(1)} %add_convert_fusion.6), channel_id=1, source_target_pairs={{0,16},{4,20},{8,24},{12,28},{16,0},{20,4},{24,8},{28,12},{1,17},{... | collective-permute-start | bytes 221192 | tf_op jit(solution)/shard_map/ppermute | solution.py:683
  384.0 5.6 %collective-permute-start.60 = (bf16[1,96,384]{2,1,0:T(8,128)(2,1)S(1)}, bf16[1,96,384]{2,1,0:T(8,128)(2,1)S(1)}, u32[]{:S(2)}, u32[]{:S(2)}) collective-permute-start(bf16[1,96,384]{2,1,0:T(8,128)(2,1)S(1)} %add_convert_fusion.5), channel_id=1, source_target_pairs={{0,16},{4,20},{8,24},{12,28},{16,0},{20,4},{24,8},{28,12},{1,17},{... | collective-permute-start | bytes 221192 | tf_op jit(solution)/shard_map/ppermute | solution.py:683
  384.1 9.4 %collective-permute-start.58 = (bf16[2,112,384]{2,1,0:T(8,128)(2,1)S(1)}, bf16[2,112,384]{2,1,0:T(8,128)(2,1)S(1)}, u32[]{:S(2)}, u32[]{:S(2)}) collective-permute-start(bf16[2,112,384]{2,1,0:T(8,128)(2,1)S(1)} %constant_dynamic-update-slice_fusion), channel_id=1, source_target_pairs={{0,4},{4,0},{8,12},{12,8},{16,20},{20,16},{24,28},{28,24},{1,5},{5... | collective-permute-start | bytes 516104 | tf_op jit(solution)/shard_map/ppermute | solution.py:683
  389.6 6.2 %collective-permute-start.61 = (bf16[2,96,384]{2,1,0:T(8,128)(2,1)S(1)}, bf16[2,96,384]{2,1,0:T(8,128)(2,1)S(1)}, u32[]{:S(2)}, u32[]{:S(2)}) collective-permute-start(bf16[2,96,384]{2,1,0:T(8,128)(2,1)S(1)} %pad_maximum_fusion.4), channel_id=1, source_target_pairs={{0,8},{4,12},{8,0},{12,4},{16,24},{20,28},{24,16},{28,20},{1,9},{5... | collective-permute-start | bytes 442376 | tf_op jit(solution)/shard_map/ppermute | solution.py:683
  393.6 8.8 %collective-permute-start.59 = (bf16[4,112,384]{2,1,0:T(8,128)(2,1)S(1)}, bf16[4,112,384]{2,1,0:T(8,128)(2,1)S(1)}, u32[]{:S(2)}, u32[]{:S(2)}) collective-permute-start(bf16[4,112,384]{2,1,0:T(8,128)(2,1)S(1)} %constant_dynamic-update-slice_fusion.2.refs_0_), channel_id=1, source_target_pairs={{0,8},{4,12},{8,0},{12,4},{16,24},{20,28},{24,16},{28,20},{1,9},{5... | collective-permute-start | bytes 1032200 | tf_op jit(solution)/shard_map/ppermute | solution.py:683
  395.8 6.8 %collective-permute-start.62 = (bf16[4,96,384]{2,1,0:T(8,128)(2,1)S(1)}, bf16[4,96,384]{2,1,0:T(8,128)(2,1)S(1)}, u32[]{:S(2)}, u32[]{:S(2)}) collective-permute-start(bf16[4,96,384]{2,1,0:T(8,128)(2,1)S(1)} %pad_maximum_fusion.2.refs_2_), channel_id=1, source_target_pairs={{0,4},{4,0},{8,12},{12,8},{16,20},{20,16},{24,28},{28,24},{1,5},{5... | collective-permute-start | bytes 884744 | tf_op jit(solution)/shard_map/ppermute | solution.py:683
  (91 other events, 672.3 us)

commit v4 on v3

--- a/solution.py
+++ b/solution.py
@@ -852,13 +852,13 @@
         grid_spec=pltpu.PrefetchScalarGridSpec(
             num_scalar_prefetch=1,
             grid=(3,),
-            in_specs=[whole((T, D)), whole((T, LANE)), whole((T, LANE))] + [ANY] * 9,
+            in_specs=[whole((T, D)), whole((T, LANE)), whole((T, LANE))] + [ANY] * 5,
             out_specs=[pl.BlockSpec((T, D), lambda i, *_: (0, i)), whole((D, T))],
             scratch_shapes=[pltpu.VMEM((D, 3 * D), bf16), pltpu.SemaphoreType.DMA((4,))],
         ),
         out_shape=[shape((T, 3 * D), bf16), shape((D, T), bf16)],
-        **params(22),
-    )(whole_rows, x, cosine, sine, *qkv_pieces, vectors, *beside_all)
+        **params(60),
+    )(whole_rows, x, cosine, sine, *qkv_pieces, vectors)
 
     vectors = absolute(vectors, f, 2)
     vectors = vectors.transpose(1, 0, 2).reshape(4, D).astype(f32)
@@ -1124,7 +1124,7 @@
         out_shape=shape((T, D), f32),
         **params(36),
     )(full_up, full_gate, sum_two, dup0, dgate0, dup1, dgate1, dup2, dgate2, *outs)
-    outs, gots = slot([grad_hidden] + gots, (r1, "near"), (r2, "far"))
+    outs, gots = slot([grad_hidden] + gots, (r0, "all"), (r1, "near"), (r1, "all"), (r2, "far"))
 
     sum_one, grad_branch, grad_att, delta, att_turned, small = pl.pallas_call(
         mixer_back_kernel,
@@ -1163,8 +1163,6 @@
         ],
         **params(16),
     )(info, grad_hidden, xhat1, inv1, vectors, attended0, attended1, full_out, heads, small_two, *outs)
-    outs, gots = slot([grad_branch] + gots, (r0, "all"), (r1, "all"))
-
     def attend_back(h, *after):
         def cols(part, rows=None):
             at = 2 * part + h
@@ -1215,7 +1213,7 @@
             **params(18),
         )(info, x_turned, att_turned, *grads, grad_branch, small, *after)
 
-    grads0 = attend_back(0, *outs)
+    grads0 = attend_back(0)
     outs, gots = slot([grads0[0]] + gots, (r2, "near"), (r2, "far"), (r0, "all"), (r1, "all"))
     keep, send = qkv_back(0, grads0, SMALL, *outs)
     r3 = Reduce(orders[3], keep, tie(send, *gots))

time: 410 us -> 399 us (0.973)
  waiting for transfers between devices: 90.4 us -> 77.6 us
  local copies, waits for them, and re-layouts: 48.3 us -> 41 us
    ppermute x69, waiting for transfers between devices: 90.4 us -> 77.6 us  [xor_permute(): return lax.ppermute(value, axis, [(i, i ^ bits) for i in range(size)])]
    unnamed x177, local copies, waits for them, and re-layouts: 37.6 us -> 28.9 us
  transfers between devices with their start and end apart: 69 -> 69, of which waited for: 32 -> 29; matrix products, arithmetic and copies ran while one was open for 4% -> 5% of each run, Pallas kernels for 36% -> 39%
where the time goes in v4:
time: 399 us; the launch traced here: 393 us
  Pallas kernels  204 us (51%)
  waiting for transfers between devices  77.6 us (19%)
  starting transfers between devices  57.5 us (14%)
  local copies, waits for them, and re-layouts  41 us (10%)
  other arithmetic  9.87 us (2%)
    ppermute x69, waiting for transfers between devices, xor_permute(): return lax.ppermute(value, axis, [(i, i ^ bits) for i in range(size)])  77.6 us
    ppermute x69, starting transfers between devices, xor_permute(): return lax.ppermute(value, axis, [(i, i ^ bits) for i in range(size)])  57.5 us
    pallas_call x3, Pallas kernels, ffn_back(): pl.pallas_call(functools.partial(ffn_back_kernel, g, orders[g], groups),...  36.4 us
    pallas_call x2, Pallas kernels, attend_back(): pl.pallas_call(kernel, grid_spec=pltpu.PrefetchScalarGridSpec(num_scalar_...  33 us
    pallas_call x1, Pallas kernels, per_device(): pl.pallas_call(ffn_kernel, grid_spec=pltpu.PrefetchScalarGridSpec(num_sca...  29.7 us
    unnamed x177, local copies, waits for them, and re-layouts  28.9 us
    pallas_call x2, Pallas kernels, attend(): pl.pallas_call(functools.partial(drop_last, attend_kernel, len(after), 7)...  24.6 us
    pallas_call x1, Pallas kernels, per_device(): pl.pallas_call(functools.partial(ffn_input_back_kernel, groups), in_specs...  14.1 us
  transfers between devices with their start and end apart: 69, of which 29 were waited for; matrix products, arithmetic and copies ran while one was open for 5% of the time, Pallas kernels for 39%

profile of v4, /device:TPU:0, one launch (start us, length us, event | category | flops | bytes accessed | tf_op | source)
XLA Modules:
  0.0 393.3 jit_solution(4736577514795106087)
XLA Ops:
  1.2 2.6 collective-permute-start.1
  6.5 1.7 collective-permute-start.3
  12.1 1.9 constant_dynamic-slice_fusion.3
  14.0 1.9 constant_dynamic-slice_fusion.1
  15.9 1.9 constant_dynamic-slice_fusion
  17.8 3.0 fusion
  21.1 2.0 pad_maximum_fusion
  25.0 1.8 collective-permute-start.6
  28.3 13.9 %shard_map.212 = (bf16[1024,2304]{1,0:T(8,128)(2,1)}, bf16[768,1024]{1,0:T(8,128)(2,1)}) custom-call(s32[5]{0:T(128)} %stack.123.rows_ref, bf16[1024,768]{1,0:T(8,128)(2,1)} %bitcast.59, f32[1024,128]{1,0:T(8,128)} %get-tuple-element.244.cos_ref.refs_10_.refs_12_, f32[1024,128]{1,0:T(8,128)} %get-tuple-element.243.sin_ref.refs_11_.refs_13_, ...), custom_call_target="tpu_custom_call" | custom-call | flops 1 | bytes 1 | tf_op jit(solution)/shard_map/pallas_call | solution.py:850
  42.2 1.9 collective-permute-done.6.refs_7_.one_ref
  44.1 1.8 collective-permute-start.8
  47.6 2.3 copy-done
  49.9 12.2 %shard_map.213 = (bf16[1024,384]{1,0:T(8,128)(2,1)S(1)}, f32[3,8,1024]{2,1,0:T(8,128)S(1)}) custom-call(s32[4]{0:T(128)S(1)} %get-tuple-element.230.refs_0_, s32[4]{0:T(128)S(1)} %get-tuple-element.229.refs_1_, bf16[1024,2304]{1,0:T(8,128)(2,1)S(1)} %copy-done, bf16[1024,2304]{1,0:T(8,128)(2,1)S(1)} %copy-done, bf16[1024,2304]{1,0:T(8,128)(2,1)S(1)} %copy-done, ...), custom_call_target="tpu_custom_call" | custom-call | flops 1 | bytes 1 | tf_op jit(solution)/shard_map/pallas_call | solution.py:870
  63.8 1.8 collective-permute-start.11
  67.6 2.3 copy-done.1
  69.9 12.4 %shard_map.215 = (bf16[1024,384]{1,0:T(8,128)(2,1)S(1)}, f32[3,8,1024]{2,1,0:T(8,128)S(1)}) custom-call(s32[4]{0:T(128)S(1)} %get-tuple-element.230.refs_0_, s32[4]{0:T(128)S(1)} %get-tuple-element.229.refs_1_, bf16[1024,2304]{1,0:T(8,128)(2,1)S(1)} %copy-done.1, bf16[1024,2304]{1,0:T(8,128)(2,1)S(1)} %copy-done.1, bf16[1024,2304]{1,0:T(8,128)(2,1)S(1)} %copy-done.1, ...), custom_call_target="tpu_custom_call" | custom-call | flops 1 | bytes 1 | tf_op jit(solution)/shard_map/pallas_call | solution.py:870
  83.1 2.5 shard_map.216.refs_5_.refs_6_
  87.3 5.9 %shard_map.217 = (f32[1024,768]{1,0:T(8,128)S(1)}, f32[1024,128]{1,0:T(8,128)S(1)}, bf16[1024,768]{1,0:T(8,128)(2,1)S(1)}, bf16[768,1024]{1,0:T(8,128)(2,1)S(1)}, bf16[768,768]{1,0:T(8,128)(2,1)S(1)}) custom-call(s32[5]{0:T(128)S(1)} %copy-done.77, bf16[1024,384]{1,0:T(8,128)(2,1)S(1)} %copy-done.24, bf16[1024,384]{1,0:T(8,128)(2,1)S(1)} %copy-done.27, ...), custom_call_target="tpu_custom_call" | custom-call | flops 1 | bytes 1 | tf_op jit(solution)/shard_map/pallas_call | solution.py:904
  93.3 1.7 copy-done.15
  96.0 2.5 collective-permute-done.17.two_ref
  100.2 2.8 collective-permute-done.18.refs_11_
  103.0 29.7 %shard_map.219 = (bf16[1024,3072]{1,0:T(8,128)(2,1)}, bf16[1024,3072]{1,0:T(8,128)(2,1)}, bf16[1024,3072]{1,0:T(8,128)(2,1)}, f32[1024,768]{1,0:T(8,128)}, f32[1...) custom-call(s32[5]{0:T(128)S(1)} %copy-done.77, ...), custom_call_target="tpu_custom_call" | custom-call | flops 1 | bytes 1 | tf_op jit(solution)/shard_map/pallas_call | solution.py:919
  133.5 3.2 collective-permute-start.21
  139.0 2.3 collective-permute-done.20
  142.1 3.5 collective-permute-done.22
  146.7 3.8 collective-permute-done.23
  153.4 1.9 copy-done.54
  155.3 3.2 shard_map.221
  158.6 12.4 %shard_map.222 = (bf16[1024,1024]{1,0:T(8,128)(2,1)S(1)}, bf16[1024,1024]{1,0:T(8,128)(2,1)S(1)}, bf16[16,192,384]{2,1,0:T(8,128)(2,1)S(1)}, bf16[16,192,384]{2,1,0:T(8,128)(2,1)}) custom-call(s32[5]{0:T(128)S(1)} %stack.155.info_ref, bf16[1024,3072]{1,0:T(8,128)(2,1)} %get-tuple-element.140.prod_any, bf16[1024,3072]{1,0:T(8,128)(2,1)} %get-tuple-element.141.up_fac_any, ...), custom_call_target="tpu_custom_call" | custom-call | flops 1 | bytes 1 | tf_op jit(solution)/shard_map/pallas_call | solution.py:1087
  173.8 12.0 %shard_map.223 = (bf16[1024,1024]{1,0:T(8,128)(2,1)S(1)}, bf16[1024,1024]{1,0:T(8,128)(2,1)S(1)}, bf16[16,192,384]{2,1,0:T(8,128)(2,1)S(1)}, bf16[16,192,384]{2,1,0:T(8,128)(2,1)}) custom-call(s32[5]{0:T(128)S(1)} %stack.155.info_ref, bf16[1024,3072]{1,0:T(8,128)(2,1)} %get-tuple-element.140.prod_any, bf16[1024,3072]{1,0:T(8,128)(2,1)} %get-tuple-element.141.up_fac_any, ...), custom_call_target="tpu_custom_call" | custom-call | flops 1 | bytes 1 | tf_op jit(solution)/shard_map/pallas_call | solution.py:1087
  189.1 12.0 %shard_map.225 = (bf16[1024,1024]{1,0:T(8,128)(2,1)S(1)}, bf16[1024,1024]{1,0:T(8,128)(2,1)S(1)}, bf16[16,192,384]{2,1,0:T(8,128)(2,1)S(1)}, bf16[16,192,384]{2,1,0:T(8,128)(2,1)}) custom-call(s32[5]{0:T(128)S(1)} %stack.155.info_ref, bf16[1024,3072]{1,0:T(8,128)(2,1)} %get-tuple-element.140.prod_any, bf16[1024,3072]{1,0:T(8,128)(2,1)} %get-tuple-element.141.up_fac_any, ...), custom_call_target="tpu_custom_call" | custom-call | flops 1 | bytes 1 | tf_op jit(solution)/shard_map/pallas_call | solution.py:1087
  201.2 2.9 collective-permute-done.26.refs_4_.refs_8_
  204.0 1.7 copy-done.7
  213.0 14.1 %shard_map.227.refs_11_.grad_ref = f32[1024,768]{1,0:T(8,128)S(1)} custom-call(bf16[768,3072]{1,0:T(8,128)(2,1)} %get-tuple-element.134.wu_any, bf16[768,3072]{1,0:T(8,128)(2,1)} %get-tuple-element.135.wg_any, f32[1024,768]{1,0:T(8,128)} %copy-done.53, bf16[1024,1024]{1,0:T(8,128)(2,1)S(1)} %copy-done.58, bf16[1024,1024]{1,0:T(8,128)(2,1)S(1)} %copy-done.60, ...), custom_call_target="tpu_custom_call" | custom-call | flops 1 | bytes 1 | tf_op jit(solution)/shard_map/pallas_call | solution.py:1112
  227.2 1.9 copy-done.4
  229.1 1.7 copy-done.8
  235.8 6.9 %shard_map.229 = (f32[1024,768]{1,0:T(8,128)S(1)}, bf16[1024,768]{1,0:T(8,128)(2,1)S(1)}, bf16[1024,768]{1,0:T(8,128)(2,1)S(1)}, f32[6,8,1024]{2,1,0:T(8,128)S(1...) custom-call(s32[5]{0:T(128)S(1)} %stack.155.info_ref, f32[1024,768]{1,0:T(8,128)S(1)} %shard_map.227.refs_11_.grad_ref, ...), custom_call_target="tpu_custom_call" | custom-call | flops 1 | bytes 1 | tf_op jit(solution)/shard_map/pallas_call | solution.py:1129
  242.7 1.7 copy-done.51
  244.4 16.3 %shard_map.230 = (bf16[1024,384]{1,0:T(8,128)(2,1)S(1)}, bf16[1024,384]{1,0:T(8,128)(2,1)S(1)}, bf16[1024,384]{1,0:T(8,128)(2,1)S(1)}) custom-call(s32[4]{0:T(128)S(1)} %get-tuple-element.230.refs_0_, s32[4]{0:T(128)S(1)} %get-tuple-element.229.refs_1_, bf16[1024,2304]{1,0:T(8,128)(2,1)S(1)} %bitcast.58, bf16[1024,2304]{1,0:T(8,128)(2,1)S(1)} %bitcast.58, ...), custom_call_target="tpu_custom_call" | custom-call | flops 1 | bytes 1 | tf_op jit(solution)/shard_map/pallas_call | solution.py:1172
  263.2 2.1 collective-permute-start.39
  266.4 4.7 %shard_map.232 = (bf16[16,112,384]{2,1,0:T(8,128)(2,1)S(1)}, bf16[16,112,384]{2,1,0:T(8,128)(2,1)S(1)}) custom-call(s32[5]{0:T(128)S(1)} %stack.155.info_ref, bf16[768,1024]{1,0:T(8,128)(2,1)S(1)} %copy-done.32, bf16[768,1024]{1,0:T(8,128)(2,1)S(1)} %copy-done.34, bf16[1024,384]{1,0:T(8,128)(2,1)S(1)} %get-tuple-element.173.refs_14_.gq_ref.gq0, ...), custom_call_target="tpu_custom_call" | custom-call | flops 1 | bytes 1 | tf_op jit(solution)/shard_map/pallas_call | solution.py:1201
  271.5 1.9 collective-permute-done.37.refs_10_.refs_24_.refs_6_
  273.4 3.2 collective-permute-done.38.refs_16_.refs_21_.refs_10_.refs_6_
  276.5 3.1 collective-permute-done.40.refs_19_.refs_14_.refs_11_
  283.0 2.0 collective-permute-start.41
  285.9 16.7 %shard_map.234 = (bf16[1024,384]{1,0:T(8,128)(2,1)S(1)}, bf16[1024,384]{1,0:T(8,128)(2,1)S(1)}, bf16[1024,384]{1,0:T(8,128)(2,1)S(1)}) custom-call(s32[4]{0:T(128)S(1)} %get-tuple-element.230.refs_0_, s32[4]{0:T(128)S(1)} %get-tuple-element.229.refs_1_, bf16[1024,2304]{1,0:T(8,128)(2,1)S(1)} %bitcast.58, bf16[1024,2304]{1,0:T(8,128)(2,1)S(1)} %bitcast.58, ...), custom_call_target="tpu_custom_call" | custom-call | flops 1 | bytes 1 | tf_op jit(solution)/shard_map/pallas_call | solution.py:1172
  303.2 1.7 collective-permute-start.46
  304.9 2.4 collective-permute-start.47
  307.8 4.6 %shard_map.236 = (bf16[16,96,384]{2,1,0:T(8,128)(2,1)S(1)}, bf16[16,96,384]{2,1,0:T(8,128)(2,1)S(1)}) custom-call(s32[5]{0:T(128)S(1)} %stack.155.info_ref, bf16[768,1024]{1,0:T(8,128)(2,1)S(1)} %copy-done.32, bf16[768,1024]{1,0:T(8,128)(2,1)S(1)} %copy-done.34, bf16[1024,384]{1,0:T(8,128)(2,1)S(1)} %get-tuple-element.193.refs_16_.gq_ref.gq1, ...), custom_call_target="tpu_custom_call" | custom-call | flops 1 | bytes 1 | tf_op jit(solution)/shard_map/pallas_call | solution.py:1201
  312.5 2.0 collective-permute-done.47.refs_3_.refs_16_
  314.4 4.4 %collective-permute-done.48.refs_9_.refs_17_ = bf16[1,192,384]{2,1,0:T(8,128)(2,1)S(1)} collective-permute-done((bf16[1,192,384]{2,1,0:T(8,128)(2,1)S(1)}, bf16[1,192,384]{2,1,0:T(8,128)(2,1)S(1)}, u32[]{:S(2)}, u32[]{:S(2)}) %collective-permute-start.48) | collective-permute-done | bytes 147488 | tf_op jit(solution)/shard_map/ppermute | solution.py:683
  318.9 2.8 collective-permute-done.50
  321.9 2.3 collective-permute-start.52
  328.2 8.9 %shard_map.238 = f32[1024,768]{1,0:T(8,128)} custom-call(s32[5]{0:T(128)S(1)} %copy-done.78, bf16[1024,384]{1,0:T(8,128)(2,1)S(1)} %get-tuple-element.173.refs_14_.gq_ref.gq0, bf16[1024,384]{1,0:T(8,128)(2,1)S(1)} %copy-done.48, bf16[1024,384]{1,0:T(8,128)(2,1)S(1)} %copy-done.50, bf16[1024,384]{1,0:T(8,128)(2,1)S(1)} %get-tuple-element.193.refs_16_.gq_ref.gq1, ...), custom_call_target="tpu_custom_call" | custom-call | flops 1 | bytes 1 | tf_op jit(solution)/shard_map/pallas_call | solution.py:1229
  339.1 1.7 collective-permute-start.53
  340.9 10.2 %collective-permute-done.64 = bf16[2,192,384]{2,1,0:T(8,128)(2,1)S(1)} collective-permute-done((bf16[2,192,384]{2,1,0:T(8,128)(2,1)S(1)}, bf16[2,192,384]{2,1,0:T(8,128)(2,1)S(1)}, u32[]{:S(2)}, u32[]{:S(2)}) %collective-permute-start.64) | collective-permute-done | bytes 294944 | tf_op jit(solution)/shard_map/ppermute | solution.py:683
  351.2 1.7 collective-permute-start.65
  353.1 2.1 collective-permute-start.55
  355.6 8.1 %collective-permute-done.67 = bf16[2,192,384]{2,1,0:T(8,128)(2,1)S(1)} collective-permute-done((bf16[2,192,384]{2,1,0:T(8,128)(2,1)S(1)}, bf16[2,192,384]{2,1,0:T(8,128)(2,1)S(1)}, u32[]{:S(2)}, u32[]{:S(2)}) %collective-permute-start.67) | collective-permute-done | bytes 294944 | tf_op jit(solution)/shard_map/ppermute | solution.py:683
  365.5 6.6 %collective-permute-done.57 = bf16[1,96,384]{2,1,0:T(8,128)(2,1)S(1)} collective-permute-done((bf16[1,96,384]{2,1,0:T(8,128)(2,1)S(1)}, bf16[1,96,384]{2,1,0:T(8,128)(2,1)S(1)}, u32[]{:S(2)}, u32[]{:S(2)}) %collective-permute-start.57) | collective-permute-done | bytes 73760 | tf_op jit(solution)/shard_map/ppermute | solution.py:683
  372.7 4.9 %collective-permute-done.60 = bf16[1,96,384]{2,1,0:T(8,128)(2,1)S(1)} collective-permute-done((bf16[1,96,384]{2,1,0:T(8,128)(2,1)S(1)}, bf16[1,96,384]{2,1,0:T(8,128)(2,1)S(1)}, u32[]{:S(2)}, u32[]{:S(2)}) %collective-permute-start.60) | collective-permute-done | bytes 73760 | tf_op jit(solution)/shard_map/ppermute | solution.py:683
  377.7 4.1 %collective-permute-done.58 = bf16[2,112,384]{2,1,0:T(8,128)(2,1)S(1)} collective-permute-done((bf16[2,112,384]{2,1,0:T(8,128)(2,1)S(1)}, bf16[2,112,384]{2,1,0:T(8,128)(2,1)S(1)}, u32[]{:S(2)}, u32[]{:S(2)}) %collective-permute-start.58) | collective-permute-done | bytes 172064 | tf_op jit(solution)/shard_map/ppermute | solution.py:683
  384.0 5.7 %shard_map.240 = (f32[192,3072]{1,0:T(8,128)}, f32[192,3072]{1,0:T(8,128)}, f32[768,768]{1,0:T(8,128)}) custom-call(s32[5]{0:T(128)S(1)} %stack.155.info_ref, bf16[4,192,384]{2,1,0:T(8,128)(2,1)S(1)} %get-tuple-element.202.refs_4_.refs_0_, bf16[4,192,384]{2,1,0:T(8,128)(2,1)S(1)} %collective-permute-done.63.refs_1_, ...), custom_call_target="tpu_custom_call" | custom-call | flops 1 | bytes 1 | tf_op jit(solution)/shard_map/pallas_call | solution.py:1252
  390.2 2.3 shard_map.239
  (353 shorter events, 68.3 us)
Async XLA Ops:
  0.6 26.7 %collective-permute-start = (bf16[192,2304]{1,0:T(8,128)(2,1)}, bf16[192,2304]{1,0:T(8,128)(2,1)S(1)}, u32[]{:S(2)}, u32[]{:S(2)}) collective-permute-start(bf16[192,2304]{1,0:T(8,128)(2,1)} %refs_0_.7), channel_id=1, source_target_pairs={{0,1},{1,0},{2,3},{3,2},{4,5},{5,4},{6,7},{7,6},{8,9},{9,8},{10,11... | collective-permute-start | bytes 2654216 | tf_op jit(solution)/shard_map/ppermute | solution.py:683
  1.2 23.7 %collective-permute-start.1 = (bf16[192,2304]{1,0:T(8,128)(2,1)}, bf16[192,2304]{1,0:T(8,128)(2,1)S(1)}, u32[]{:S(2)}, u32[]{:S(2)}) collective-permute-start(bf16[192,2304]{1,0:T(8,128)(2,1)} %refs_0_.7), channel_id=1, source_target_pairs={{0,2},{1,3},{2,0},{3,1},{4,6},{5,7},{6,4},{7,5},{8,10},{9,11},{10,... | collective-permute-start | bytes 2654216 | tf_op jit(solution)/shard_map/ppermute | solution.py:683
  6.4 17.6 %collective-permute-start.4 = (bf16[4,192]{1,0:T(4,128)(2,1)S(1)}, bf16[4,192]{1,0:T(4,128)(2,1)S(1)}, u32[]{:S(2)}, u32[]{:S(2)}) collective-permute-start(bf16[4,192]{1,0:T(4,128)(2,1)S(1)} %pad_maximum_fusion.8), channel_id=1, source_target_pairs={{0,3},{1,2},{2,1},{3,0},{4,7},{5,6},{6,5},{7,4},{8,11},{9,10},{10,... | collective-permute-start | bytes 4616 | tf_op jit(solution)/shard_map/ppermute | solution.py:683
  6.5 17.8 %collective-permute-start.3 = (bf16[4,192]{1,0:T(4,128)(2,1)S(1)}, bf16[4,192]{1,0:T(4,128)(2,1)S(1)}, u32[]{:S(2)}, u32[]{:S(2)}) collective-permute-start(bf16[4,192]{1,0:T(4,128)(2,1)S(1)} %pad_maximum_fusion.8), channel_id=1, source_target_pairs={{0,2},{1,3},{2,0},{3,1},{4,6},{5,7},{6,4},{7,5},{8,10},{9,11},{10,... | collective-permute-start | bytes 4616 | tf_op jit(solution)/shard_map/ppermute | solution.py:683
  8.2 16.0 %collective-permute-start.2 = (bf16[4,192]{1,0:T(4,128)(2,1)S(1)}, bf16[4,192]{1,0:T(4,128)(2,1)S(1)}, u32[]{:S(2)}, u32[]{:S(2)}) collective-permute-start(bf16[4,192]{1,0:T(4,128)(2,1)S(1)} %pad_maximum_fusion.8), channel_id=1, source_target_pairs={{0,1},{1,0},{2,3},{3,2},{4,5},{5,4},{6,7},{7,6},{8,9},{9,8},{10,11... | collective-permute-start | bytes 4616 | tf_op jit(solution)/shard_map/ppermute | solution.py:683
  25.0 19.2 %collective-permute-start.6 = (bf16[96,3840]{1,0:T(8,128)(2,1)}, bf16[96,3840]{1,0:T(8,128)(2,1)}, u32[]{:S(2)}, u32[]{:S(2)}) collective-permute-start(bf16[96,3840]{1,0:T(8,128)(2,1)} %pad_maximum_fusion), channel_id=1, source_target_pairs={{0,2},{1,3},{2,0},{3,1},{4,6},{5,7},{6,4},{7,5},{8,10},{9,11},{10,... | collective-permute-start | bytes 2211848 | tf_op jit(solution)/shard_map/ppermute | solution.py:683
  44.1 18.3 %collective-permute-start.8 = (bf16[96,3840]{1,0:T(8,128)(2,1)}, bf16[96,3840]{1,0:T(8,128)(2,1)S(1)}, u32[]{:S(2)}, u32[]{:S(2)}) collective-permute-start(bf16[96,3840]{1,0:T(8,128)(2,1)} %collective-permute-done.6.refs_7_.one_ref), channel_id=1, source_target_pairs={{0,4},{4,0},{8,12},{12,8},{16,20},{20,16},{24,28},{28,24},{1,5},{5... | collective-permute-start | bytes 2211848 | tf_op jit(solution)/shard_map/ppermute | solution.py:683
  45.9 16.2 %collective-permute-start.7 = (bf16[96,3072]{1,0:T(8,128)(2,1)}, bf16[96,3072]{1,0:T(8,128)(2,1)}, u32[]{:S(2)}, u32[]{:S(2)}) collective-permute-start(bf16[96,3072]{1,0:T(8,128)(2,1)} %constant_dynamic-slice_fusion.1), channel_id=1, source_target_pairs={{0,2},{1,3},{2,0},{3,1},{4,6},{5,7},{6,4},{7,5},{8,10},{9,11},{10,... | collective-permute-start | bytes 1769480 | tf_op jit(solution)/shard_map/ppermute | solution.py:683
  63.7 22.0 %collective-permute-start.10 = (bf16[192,3840]{1,0:T(8,128)(2,1)S(1)}, bf16[192,3840]{1,0:T(8,128)(2,1)}, u32[]{:S(2)}, u32[]{:S(2)}) collective-permute-start(bf16[192,3840]{1,0:T(8,128)(2,1)S(1)} %shard_map.214.refs_8_.refs_2_), channel_id=1, source_target_pairs={{0,1},{1,0},{2,3},{3,2},{4,5},{5,4},{6,7},{7,6},{8,9},{9,8},{10,11... | collective-permute-start | bytes 4423688 | tf_op jit(solution)/shard_map/ppermute | solution.py:683
  63.8 18.6 %collective-permute-start.11 = (bf16[384,768]{1,0:T(8,128)(2,1)}, bf16[384,768]{1,0:T(8,128)(2,1)}, u32[]{:S(2)}, u32[]{:S(2)}) collective-permute-start(bf16[384,768]{1,0:T(8,128)(2,1)} %constant_dynamic-slice_fusion), channel_id=1, source_target_pairs={{0,2},{1,3},{2,0},{3,1},{4,6},{5,7},{6,4},{7,5},{8,10},{9,11},{10,... | collective-permute-start | bytes 1769480 | tf_op jit(solution)/shard_map/ppermute | solution.py:683
  65.6 16.9 %collective-permute-start.12 = (bf16[96,3072]{1,0:T(8,128)(2,1)}, bf16[96,3072]{1,0:T(8,128)(2,1)}, u32[]{:S(2)}, u32[]{:S(2)}) collective-permute-start(bf16[96,3072]{1,0:T(8,128)(2,1)} %collective-permute-done.7.refs_1_.refs_7_.one_ref), channel_id=1, source_target_pairs={{0,4},{4,0},{8,12},{12,8},{16,20},{20,16},{24,28},{28,24},{1,5},{5... | collective-permute-start | bytes 1769480 | tf_op jit(solution)/shard_map/ppermute | solution.py:683
  67.1 18.5 %collective-permute-start.9 = (bf16[192,768]{1,0:T(8,128)(2,1)S(1)}, bf16[192,768]{1,0:T(8,128)(2,1)}, u32[]{:S(2)}, u32[]{:S(2)}) collective-permute-start(bf16[192,768]{1,0:T(8,128)(2,1)S(1)} %copy-done.67), channel_id=1, source_target_pairs={{0,1},{1,0},{2,3},{3,2},{4,5},{5,4},{6,7},{7,6},{8,9},{9,8},{10,11... | collective-permute-start | bytes 884744 | tf_op jit(solution)/shard_map/ppermute | solution.py:683
  67.1 33.0 %collective-permute-start.13 = (bf16[192,3072]{1,0:T(8,128)(2,1)}, bf16[192,3072]{1,0:T(8,128)(2,1)}, u32[]{:S(2)}, u32[]{:S(2)}) collective-permute-start(bf16[192,3072]{1,0:T(8,128)(2,1)} %refs_0_.6), channel_id=1, source_target_pairs={{0,1},{1,0},{2,3},{3,2},{4,5},{5,4},{6,7},{7,6},{8,9},{9,8},{10,11... | collective-permute-start | bytes 3538952 | tf_op jit(solution)/shard_map/ppermute | solution.py:683
  82.4 17.8 %collective-permute-start.14 = (bf16[192,3072]{1,0:T(8,128)(2,1)}, bf16[192,3072]{1,0:T(8,128)(2,1)}, u32[]{:S(2)}, u32[]{:S(2)}) collective-permute-start(bf16[192,3072]{1,0:T(8,128)(2,1)} %refs_4_.1), channel_id=1, source_target_pairs={{0,1},{1,0},{2,3},{3,2},{4,5},{5,4},{6,7},{7,6},{8,9},{9,8},{10,11... | collective-permute-start | bytes 3538952 | tf_op jit(solution)/shard_map/ppermute | solution.py:683
  82.5 16.1 %collective-permute-start.17 = (bf16[384,768]{1,0:T(8,128)(2,1)}, bf16[384,768]{1,0:T(8,128)(2,1)}, u32[]{:S(2)}, u32[]{:S(2)}) collective-permute-start(bf16[384,768]{1,0:T(8,128)(2,1)} %collective-permute-done.11.refs_1_.refs_4_.one_ref), channel_id=1, source_target_pairs={{0,4},{4,0},{8,12},{12,8},{16,20},{20,16},{24,28},{28,24},{1,5},{5... | collective-permute-start | bytes 1769480 | tf_op jit(solution)/shard_map/ppermute | solution.py:683
  85.6 14.5 %collective-permute-start.16 = (bf16[768,768]{1,0:T(8,128)(2,1)}, bf16[768,768]{1,0:T(8,128)(2,1)}, u32[]{:S(2)}, u32[]{:S(2)}) collective-permute-start(bf16[768,768]{1,0:T(8,128)(2,1)} %refs_8_.1), channel_id=1, source_target_pairs={{0,1},{1,0},{2,3},{3,2},{4,5},{5,4},{6,7},{7,6},{8,9},{9,8},{10,11... | collective-permute-start | bytes 3538952 | tf_op jit(solution)/shard_map/ppermute | solution.py:683
  85.7 14.5 %collective-permute-start.15 = (bf16[192,3072]{1,0:T(8,128)(2,1)}, bf16[192,3072]{1,0:T(8,128)(2,1)}, u32[]{:S(2)}, u32[]{:S(2)}) collective-permute-start(bf16[192,3072]{1,0:T(8,128)(2,1)} %shard_map.216.refs_5_.refs_6_), channel_id=1, source_target_pairs={{0,1},{1,0},{2,3},{3,2},{4,5},{5,4},{6,7},{7,6},{8,9},{9,8},{10,11... | collective-permute-start | bytes 3538952 | tf_op jit(solution)/shard_map/ppermute | solution.py:683
  133.5 5.5 %collective-permute-start.21 = (bf16[8,896]{1,0:T(8,128)(2,1)S(1)}, bf16[8,896]{1,0:T(8,128)(2,1)S(1)}, u32[]{:S(2)}, u32[]{:S(2)}) collective-permute-start(bf16[8,896]{1,0:T(8,128)(2,1)S(1)} %get-tuple-element.242), channel_id=1, source_target_pairs={{0,24},{4,28},{8,16},{12,20},{16,8},{20,12},{24,0},{28,4},{1,25},{... | collective-permute-start | bytes 43016 | tf_op jit(solution)/shard_map/ppermute | solution.py:683
  136.7 4.6 %collective-permute-start.20 = (bf16[8,896]{1,0:T(8,128)(2,1)S(1)}, bf16[8,896]{1,0:T(8,128)(2,1)S(1)}, u32[]{:S(2)}, u32[]{:S(2)}) collective-permute-start(bf16[8,896]{1,0:T(8,128)(2,1)S(1)} %get-tuple-element.242), channel_id=1, source_target_pairs={{0,16},{4,20},{8,24},{12,28},{16,0},{20,4},{24,8},{28,12},{1,17},{... | collective-permute-start | bytes 43016 | tf_op jit(solution)/shard_map/ppermute | solution.py:683
  136.7 4.6 %collective-permute-start.19 = (bf16[8,896]{1,0:T(8,128)(2,1)S(1)}, bf16[8,896]{1,0:T(8,128)(2,1)S(1)}, u32[]{:S(2)}, u32[]{:S(2)}) collective-permute-start(bf16[8,896]{1,0:T(8,128)(2,1)S(1)} %get-tuple-element.242), channel_id=1, source_target_pairs={{0,8},{4,12},{8,0},{12,4},{16,24},{20,28},{24,16},{28,20},{1,9},{5... | collective-permute-start | bytes 43016 | tf_op jit(solution)/shard_map/ppermute | solution.py:683
  141.3 4.2 %collective-permute-start.22 = (bf16[4,8,896]{2,1,0:T(8,128)(2,1)S(1)}, bf16[4,8,896]{2,1,0:T(8,128)(2,1)S(1)}, u32[]{:S(2)}, u32[]{:S(2)}) collective-permute-start(bf16[4,8,896]{2,1,0:T(8,128)(2,1)S(1)} %get-tuple-element.236), channel_id=1, source_target_pairs={{0,2},{1,3},{2,0},{3,1},{4,6},{5,7},{6,4},{7,5},{8,10},{9,11},{10,... | collective-permute-start | bytes 172040 | tf_op jit(solution)/shard_map/ppermute | solution.py:683
  145.6 4.9 %collective-permute-start.23 = (bf16[4,2,8,896]{3,2,0,1:T(8,128)(2,1)S(1)}, bf16[4,2,8,896]{3,2,0,1:T(8,128)(2,1)S(1)}, u32[]{:S(2)}, u32[]{:S(2)}) collective-permute-start(bf16[4,2,8,896]{3,2,0,1:T(8,128)(2,1)S(1)} %get-tuple-element.234), channel_id=1, source_target_pairs={{0,4},{4,0},{8,12},{12,8},{16,20},{20,16},{24,28},{28,24},{1,5},{5... | collective-permute-start | bytes 344072 | tf_op jit(solution)/shard_map/ppermute | solution.py:683
  173.6 12.6 %collective-permute-start.25 = (bf16[16,192,384]{2,1,0:T(8,128)(2,1)}, bf16[16,192,384]{2,1,0:T(8,128)(2,1)S(1)}, u32[]{:S(2)}, u32[]{:S(2)}) collective-permute-start(bf16[16,192,384]{2,1,0:T(8,128)(2,1)} %get-tuple-element.149.refs_0_), channel_id=1, source_target_pairs={{0,1},{1,0},{2,3},{3,2},{4,5},{5,4},{6,7},{7,6},{8,9},{9,8},{10,11... | collective-permute-start | bytes 7077896 | tf_op jit(solution)/shard_map/ppermute | solution.py:683
  185.7 18.3 %collective-permute-start.27 = (bf16[16,192,384]{2,1,0:T(8,128)(2,1)}, bf16[16,192,384]{2,1,0:T(8,128)(2,1)S(1)}, u32[]{:S(2)}, u32[]{:S(2)}) collective-permute-start(bf16[16,192,384]{2,1,0:T(8,128)(2,1)} %get-tuple-element.152.refs_0_), channel_id=1, source_target_pairs={{0,1},{1,0},{2,3},{3,2},{4,5},{5,4},{6,7},{7,6},{8,9},{9,8},{10,11... | collective-permute-start | bytes 7077896 | tf_op jit(solution)/shard_map/ppermute | solution.py:683
  188.4 15.6 %collective-permute-start.26 = (bf16[4,192,384]{2,1,0:T(8,128)(2,1)S(1)}, bf16[4,192,384]{2,1,0:T(8,128)(2,1)S(1)}, u32[]{:S(2)}, u32[]{:S(2)}) collective-permute-start(bf16[4,192,384]{2,1,0:T(8,128)(2,1)S(1)} %shard_map.224.refs_1_), channel_id=1, source_target_pairs={{0,2},{1,3},{2,0},{3,1},{4,6},{5,7},{6,4},{7,5},{8,10},{9,11},{10,... | collective-permute-start | bytes 1769480 | tf_op jit(solution)/shard_map/ppermute | solution.py:683
  204.0 23.2 %collective-permute-start.31 = (bf16[16,192,384]{2,1,0:T(8,128)(2,1)}, bf16[16,192,384]{2,1,0:T(8,128)(2,1)S(1)}, u32[]{:S(2)}, u32[]{:S(2)}) collective-permute-start(bf16[16,192,384]{2,1,0:T(8,128)(2,1)} %get-tuple-element.165), channel_id=1, source_target_pairs={{0,1},{1,0},{2,3},{3,2},{4,5},{5,4},{6,7},{7,6},{8,9},{9,8},{10,11... | collective-permute-start | bytes 7077896 | tf_op jit(solution)/shard_map/ppermute | solution.py:683
  207.2 20.0 %collective-permute-start.28 = (bf16[4,192,384]{2,1,0:T(8,128)(2,1)}, bf16[4,192,384]{2,1,0:T(8,128)(2,1)S(1)}, u32[]{:S(2)}, u32[]{:S(2)}) collective-permute-start(bf16[4,192,384]{2,1,0:T(8,128)(2,1)} %get-tuple-element.157.refs_6_), channel_id=1, source_target_pairs={{0,2},{1,3},{2,0},{3,1},{4,6},{5,7},{6,4},{7,5},{8,10},{9,11},{10,... | collective-permute-start | bytes 1769480 | tf_op jit(solution)/shard_map/ppermute | solution.py:683
  207.8 19.3 %collective-permute-start.29 = (bf16[4,192,384]{2,1,0:T(8,128)(2,1)}, bf16[4,192,384]{2,1,0:T(8,128)(2,1)S(1)}, u32[]{:S(2)}, u32[]{:S(2)}) collective-permute-start(bf16[4,192,384]{2,1,0:T(8,128)(2,1)} %get-tuple-element.158.refs_7_), channel_id=1, source_target_pairs={{0,8},{4,12},{8,0},{12,4},{16,24},{20,28},{24,16},{28,20},{1,9},{5... | collective-permute-start | bytes 1769480 | tf_op jit(solution)/shard_map/ppermute | solution.py:683
  207.8 19.3 %collective-permute-start.30 = (bf16[4,192,384]{2,1,0:T(8,128)(2,1)}, bf16[4,192,384]{2,1,0:T(8,128)(2,1)S(1)}, u32[]{:S(2)}, u32[]{:S(2)}) collective-permute-start(bf16[4,192,384]{2,1,0:T(8,128)(2,1)} %get-tuple-element.159.refs_8_), channel_id=1, source_target_pairs={{0,4},{4,0},{8,12},{12,8},{16,20},{20,16},{24,28},{28,24},{1,5},{5... | collective-permute-start | bytes 1769480 | tf_op jit(solution)/shard_map/ppermute | solution.py:683
  231.4 29.4 %collective-permute-start.33 = (bf16[4,192,384]{2,1,0:T(8,128)(2,1)S(1)}, bf16[4,192,384]{2,1,0:T(8,128)(2,1)S(1)}, u32[]{:S(2)}, u32[]{:S(2)}) collective-permute-start(bf16[4,192,384]{2,1,0:T(8,128)(2,1)S(1)} %get-tuple-element.169.refs_3_), channel_id=1, source_target_pairs={{0,2},{1,3},{2,0},{3,1},{4,6},{5,7},{6,4},{7,5},{8,10},{9,11},{10,... | collective-permute-start | bytes 1769480 | tf_op jit(solution)/shard_map/ppermute | solution.py:683
  232.2 28.7 %collective-permute-start.34 = (bf16[4,192,384]{2,1,0:T(8,128)(2,1)S(1)}, bf16[4,192,384]{2,1,0:T(8,128)(2,1)S(1)}, u32[]{:S(2)}, u32[]{:S(2)}) collective-permute-start(bf16[4,192,384]{2,1,0:T(8,128)(2,1)S(1)} %get-tuple-element.167.refs_1_), channel_id=1, source_target_pairs={{0,4},{4,0},{8,12},{12,8},{16,20},{20,16},{24,28},{28,24},{1,5},{5... | collective-permute-start | bytes 1769480 | tf_op jit(solution)/shard_map/ppermute | solution.py:683
  233.2 27.6 %collective-permute-start.35 = (bf16[4,192,384]{2,1,0:T(8,128)(2,1)S(1)}, bf16[4,192,384]{2,1,0:T(8,128)(2,1)S(1)}, u32[]{:S(2)}, u32[]{:S(2)}) collective-permute-start(bf16[4,192,384]{2,1,0:T(8,128)(2,1)S(1)} %get-tuple-element.168.refs_2_), channel_id=1, source_target_pairs={{0,2},{1,3},{2,0},{3,1},{4,6},{5,7},{6,4},{7,5},{8,10},{9,11},{10,... | collective-permute-start | bytes 1769480 | tf_op jit(solution)/shard_map/ppermute | solution.py:683
  234.5 26.3 %collective-permute-start.32 = (bf16[2,192,384]{2,1,0:T(8,128)(2,1)S(1)}, bf16[2,192,384]{2,1,0:T(8,128)(2,1)S(1)}, u32[]{:S(2)}, u32[]{:S(2)}) collective-permute-start(bf16[2,192,384]{2,1,0:T(8,128)(2,1)S(1)} %get-tuple-element.166.refs_0_), channel_id=1, source_target_pairs={{0,4},{4,0},{8,12},{12,8},{16,20},{20,16},{24,28},{28,24},{1,5},{5... | collective-permute-start | bytes 884744 | tf_op jit(solution)/shard_map/ppermute | solution.py:683
  261.9 14.7 %collective-permute-start.38 = (bf16[4,192,384]{2,1,0:T(8,128)(2,1)S(1)}, bf16[4,192,384]{2,1,0:T(8,128)(2,1)S(1)}, u32[]{:S(2)}, u32[]{:S(2)}) collective-permute-start(bf16[4,192,384]{2,1,0:T(8,128)(2,1)S(1)} %get-tuple-element.179.refs_0_), channel_id=1, source_target_pairs={{0,2},{1,3},{2,0},{3,1},{4,6},{5,7},{6,4},{7,5},{8,10},{9,11},{10,... | collective-permute-start | bytes 1769480 | tf_op jit(solution)/shard_map/ppermute | solution.py:683
  261.9 11.5 %collective-permute-start.37 = (bf16[2,192,384]{2,1,0:T(8,128)(2,1)S(1)}, bf16[2,192,384]{2,1,0:T(8,128)(2,1)S(1)}, u32[]{:S(2)}, u32[]{:S(2)}) collective-permute-start(bf16[2,192,384]{2,1,0:T(8,128)(2,1)S(1)} %get-tuple-element.178.refs_3_), channel_id=1, source_target_pairs={{0,8},{4,12},{8,0},{12,4},{16,24},{20,28},{24,16},{28,20},{1,9},{5... | collective-permute-start | bytes 884744 | tf_op jit(solution)/shard_map/ppermute | solution.py:683
  263.2 10.2 %collective-permute-start.39 = (bf16[2,192,384]{2,1,0:T(8,128)(2,1)S(1)}, bf16[2,192,384]{2,1,0:T(8,128)(2,1)S(1)}, u32[]{:S(2)}, u32[]{:S(2)}) collective-permute-start(bf16[2,192,384]{2,1,0:T(8,128)(2,1)S(1)} %get-tuple-element.180.refs_1_), channel_id=1, source_target_pairs={{0,4},{4,0},{8,12},{12,8},{16,20},{20,16},{24,28},{28,24},{1,5},{5... | collective-permute-start | bytes 884744 | tf_op jit(solution)/shard_map/ppermute | solution.py:683
  265.3 6.1 %collective-permute-start.36 = (bf16[1,192,384]{2,1,0:T(8,128)(2,1)S(1)}, bf16[1,192,384]{2,1,0:T(8,128)(2,1)S(1)}, u32[]{:S(2)}, u32[]{:S(2)}) collective-permute-start(bf16[1,192,384]{2,1,0:T(8,128)(2,1)S(1)} %get-tuple-element.177.refs_2_), channel_id=1, source_target_pairs={{0,16},{4,20},{8,24},{12,28},{16,0},{20,4},{24,8},{28,12},{1,17},{... | collective-permute-start | bytes 442376 | tf_op jit(solution)/shard_map/ppermute | solution.py:683
  280.3 22.4 %collective-permute-start.45 = (bf16[8,112,384]{2,1,0:T(8,128)(2,1)S(1)}, bf16[8,112,384]{2,1,0:T(8,128)(2,1)S(1)}, u32[]{:S(2)}, u32[]{:S(2)}) collective-permute-start(bf16[8,112,384]{2,1,0:T(8,128)(2,1)S(1)} %get-tuple-element.192.refs_18_), channel_id=1, source_target_pairs={{0,2},{1,3},{2,0},{3,1},{4,6},{5,7},{6,4},{7,5},{8,10},{9,11},{10,... | collective-permute-start | bytes 2064392 | tf_op jit(solution)/shard_map/ppermute | solution.py:683
  280.7 22.0 %collective-permute-start.43 = (bf16[2,192,384]{2,1,0:T(8,128)(2,1)S(1)}, bf16[2,192,384]{2,1,0:T(8,128)(2,1)S(1)}, u32[]{:S(2)}, u32[]{:S(2)}) collective-permute-start(bf16[2,192,384]{2,1,0:T(8,128)(2,1)S(1)} %get-tuple-element.190.refs_16_), channel_id=1, source_target_pairs={{0,4},{4,0},{8,12},{12,8},{16,20},{20,16},{24,28},{28,24},{1,5},{5... | collective-permute-start | bytes 884744 | tf_op jit(solution)/shard_map/ppermute | solution.py:683
  281.7 21.0 %collective-permute-start.44 = (bf16[2,192,384]{2,1,0:T(8,128)(2,1)S(1)}, bf16[2,192,384]{2,1,0:T(8,128)(2,1)S(1)}, u32[]{:S(2)}, u32[]{:S(2)}) collective-permute-start(bf16[2,192,384]{2,1,0:T(8,128)(2,1)S(1)} %get-tuple-element.191.refs_17_), channel_id=1, source_target_pairs={{0,8},{4,12},{8,0},{12,4},{16,24},{20,28},{24,16},{28,20},{1,9},{5... | collective-permute-start | bytes 884744 | tf_op jit(solution)/shard_map/ppermute | solution.py:683
  283.0 19.7 %collective-permute-start.41 = (bf16[1,192,384]{2,1,0:T(8,128)(2,1)S(1)}, bf16[1,192,384]{2,1,0:T(8,128)(2,1)S(1)}, u32[]{:S(2)}, u32[]{:S(2)}) collective-permute-start(bf16[1,192,384]{2,1,0:T(8,128)(2,1)S(1)} %get-tuple-element.188.refs_14_.refs_0_), channel_id=1, source_target_pairs={{0,16},{4,20},{8,24},{12,28},{16,0},{20,4},{24,8},{28,12},{1,17},{... | collective-permute-start | bytes 442376 | tf_op jit(solution)/shard_map/ppermute | solution.py:683
  285.0 17.6 %collective-permute-start.42 = (bf16[1,192,384]{2,1,0:T(8,128)(2,1)S(1)}, bf16[1,192,384]{2,1,0:T(8,128)(2,1)S(1)}, u32[]{:S(2)}, u32[]{:S(2)}) collective-permute-start(bf16[1,192,384]{2,1,0:T(8,128)(2,1)S(1)} %get-tuple-element.189.refs_15_), channel_id=1, source_target_pairs={{0,16},{4,20},{8,24},{12,28},{16,0},{20,4},{24,8},{28,12},{1,17},{... | collective-permute-start | bytes 442376 | tf_op jit(solution)/shard_map/ppermute | solution.py:683
  303.1 15.8 %collective-permute-start.49 = (bf16[4,112,384]{2,1,0:T(8,128)(2,1)S(1)}, bf16[4,112,384]{2,1,0:T(8,128)(2,1)S(1)}, u32[]{:S(2)}, u32[]{:S(2)}) collective-permute-start(bf16[4,112,384]{2,1,0:T(8,128)(2,1)S(1)} %get-tuple-element.200.refs_3_), channel_id=1, source_target_pairs={{0,8},{4,12},{8,0},{12,4},{16,24},{20,28},{24,16},{28,20},{1,9},{5... | collective-permute-start | bytes 1032200 | tf_op jit(solution)/shard_map/ppermute | solution.py:683
  303.2 15.7 %collective-permute-start.46 = (bf16[2,192,384]{2,1,0:T(8,128)(2,1)S(1)}, bf16[2,192,384]{2,1,0:T(8,128)(2,1)S(1)}, u32[]{:S(2)}, u32[]{:S(2)}) collective-permute-start(bf16[2,192,384]{2,1,0:T(8,128)(2,1)S(1)} %get-tuple-element.197.refs_0_), channel_id=1, source_target_pairs={{0,4},{4,0},{8,12},{12,8},{16,20},{20,16},{24,28},{28,24},{1,5},{5... | collective-permute-start | bytes 884744 | tf_op jit(solution)/shard_map/ppermute | solution.py:683
  304.9 9.5 %collective-permute-start.47 = (bf16[1,192,384]{2,1,0:T(8,128)(2,1)S(1)}, bf16[1,192,384]{2,1,0:T(8,128)(2,1)S(1)}, u32[]{:S(2)}, u32[]{:S(2)}) collective-permute-start(bf16[1,192,384]{2,1,0:T(8,128)(2,1)S(1)} %get-tuple-element.198.refs_1_.refs_2_), channel_id=1, source_target_pairs={{0,16},{4,20},{8,24},{12,28},{16,0},{20,4},{24,8},{28,12},{1,17},{... | collective-permute-start | bytes 442376 | tf_op jit(solution)/shard_map/ppermute | solution.py:683
  307.3 11.5 %collective-permute-start.48 = (bf16[1,192,384]{2,1,0:T(8,128)(2,1)S(1)}, bf16[1,192,384]{2,1,0:T(8,128)(2,1)S(1)}, u32[]{:S(2)}, u32[]{:S(2)}) collective-permute-start(bf16[1,192,384]{2,1,0:T(8,128)(2,1)S(1)} %get-tuple-element.199.refs_2_), channel_id=1, source_target_pairs={{0,16},{4,20},{8,24},{12,28},{16,0},{20,4},{24,8},{28,12},{1,17},{... | collective-permute-start | bytes 442376 | tf_op jit(solution)/shard_map/ppermute | solution.py:683
  321.9 16.0 %collective-permute-start.52 = (bf16[8,96,384]{2,1,0:T(8,128)(2,1)S(1)}, bf16[8,96,384]{2,1,0:T(8,128)(2,1)S(1)}, u32[]{:S(2)}, u32[]{:S(2)}) collective-permute-start(bf16[8,96,384]{2,1,0:T(8,128)(2,1)S(1)} %add_convert_fusion.refs_8_), channel_id=1, source_target_pairs={{0,2},{1,3},{2,0},{3,1},{4,6},{5,7},{6,4},{7,5},{8,10},{9,11},{10,... | collective-permute-start | bytes 1769480 | tf_op jit(solution)/shard_map/ppermute | solution.py:683
  324.5 14.5 %collective-permute-start.51 = (bf16[2,112,384]{2,1,0:T(8,128)(2,1)S(1)}, bf16[2,112,384]{2,1,0:T(8,128)(2,1)S(1)}, u32[]{:S(2)}, u32[]{:S(2)}) collective-permute-start(bf16[2,112,384]{2,1,0:T(8,128)(2,1)S(1)} %get-tuple-element.205.refs_7_), channel_id=1, source_target_pairs={{0,4},{4,0},{8,12},{12,8},{16,20},{20,16},{24,28},{28,24},{1,5},{5... | collective-permute-start | bytes 516104 | tf_op jit(solution)/shard_map/ppermute | solution.py:683
  324.6 59.4 %collective-permute-start.63 = (bf16[4,192,384]{2,1,0:T(8,128)(2,1)S(1)}, bf16[4,192,384]{2,1,0:T(8,128)(2,1)S(1)}, u32[]{:S(2)}, u32[]{:S(2)}) collective-permute-start(bf16[4,192,384]{2,1,0:T(8,128)(2,1)S(1)} %get-tuple-element.202.refs_4_.refs_0_), channel_id=1, source_target_pairs={{0,8},{4,12},{8,0},{12,4},{16,24},{20,28},{24,16},{28,20},{1,9},{5... | collective-permute-start | bytes 1769480 | tf_op jit(solution)/shard_map/ppermute | solution.py:683
  325.5 25.6 %collective-permute-start.64 = (bf16[2,192,384]{2,1,0:T(8,128)(2,1)S(1)}, bf16[2,192,384]{2,1,0:T(8,128)(2,1)S(1)}, u32[]{:S(2)}, u32[]{:S(2)}) collective-permute-start(bf16[2,192,384]{2,1,0:T(8,128)(2,1)S(1)} %get-tuple-element.217.refs_5_), channel_id=1, source_target_pairs={{0,8},{4,12},{8,0},{12,4},{16,24},{20,28},{24,16},{28,20},{1,9},{5... | collective-permute-start | bytes 884744 | tf_op jit(solution)/shard_map/ppermute | solution.py:683
  326.7 26.2 %collective-permute-start.66 = (bf16[1,192,384]{2,1,0:T(8,128)(2,1)S(1)}, bf16[1,192,384]{2,1,0:T(8,128)(2,1)S(1)}, u32[]{:S(2)}, u32[]{:S(2)}) collective-permute-start(bf16[1,192,384]{2,1,0:T(8,128)(2,1)S(1)} %get-tuple-element.219.refs_6_), channel_id=1, source_target_pairs={{0,16},{4,20},{8,24},{12,28},{16,0},{20,4},{24,8},{28,12},{1,17},{... | collective-permute-start | bytes 442376 | tf_op jit(solution)/shard_map/ppermute | solution.py:683
  338.0 15.0 %collective-permute-start.54 = (bf16[4,96,384]{2,1,0:T(8,128)(2,1)S(1)}, bf16[4,96,384]{2,1,0:T(8,128)(2,1)S(1)}, u32[]{:S(2)}, u32[]{:S(2)}) collective-permute-start(bf16[4,96,384]{2,1,0:T(8,128)(2,1)S(1)} %add_convert_fusion.1), channel_id=1, source_target_pairs={{0,4},{4,0},{8,12},{12,8},{16,20},{20,16},{24,28},{28,24},{1,5},{5... | collective-permute-start | bytes 884744 | tf_op jit(solution)/shard_map/ppermute | solution.py:683
  339.1 16.0 %collective-permute-start.53 = (bf16[1,112,384]{2,1,0:T(8,128)(2,1)S(1)}, bf16[1,112,384]{2,1,0:T(8,128)(2,1)S(1)}, u32[]{:S(2)}, u32[]{:S(2)}) collective-permute-start(bf16[1,112,384]{2,1,0:T(8,128)(2,1)S(1)} %add_convert_fusion.4), channel_id=1, source_target_pairs={{0,16},{4,20},{8,24},{12,28},{16,0},{20,4},{24,8},{28,12},{1,17},{... | collective-permute-start | bytes 258056 | tf_op jit(solution)/shard_map/ppermute | solution.py:683
  351.2 32.9 %collective-permute-start.65 = (bf16[4,192,384]{2,1,0:T(8,128)(2,1)S(1)}, bf16[4,192,384]{2,1,0:T(8,128)(2,1)S(1)}, u32[]{:S(2)}, u32[]{:S(2)}) collective-permute-start(bf16[4,192,384]{2,1,0:T(8,128)(2,1)S(1)} %constant_dynamic-update-slice_fusion.4.refs_2_), channel_id=1, source_target_pairs={{0,4},{4,0},{8,12},{12,8},{16,20},{20,16},{24,28},{28,24},{1,5},{5... | collective-permute-start | bytes 1769480 | tf_op jit(solution)/shard_map/ppermute | solution.py:683
  352.9 10.8 %collective-permute-start.67 = (bf16[2,192,384]{2,1,0:T(8,128)(2,1)S(1)}, bf16[2,192,384]{2,1,0:T(8,128)(2,1)S(1)}, u32[]{:S(2)}, u32[]{:S(2)}) collective-permute-start(bf16[2,192,384]{2,1,0:T(8,128)(2,1)S(1)} %constant_dynamic-update-slice_fusion.6), channel_id=1, source_target_pairs={{0,8},{4,12},{8,0},{12,4},{16,24},{20,28},{24,16},{28,20},{1,9},{5... | collective-permute-start | bytes 884744 | tf_op jit(solution)/shard_map/ppermute | solution.py:683
  353.1 12.2 %collective-permute-start.55 = (bf16[2,96,384]{2,1,0:T(8,128)(2,1)S(1)}, bf16[2,96,384]{2,1,0:T(8,128)(2,1)S(1)}, u32[]{:S(2)}, u32[]{:S(2)}) collective-permute-start(bf16[2,96,384]{2,1,0:T(8,128)(2,1)S(1)} %add_convert_fusion.2), channel_id=1, source_target_pairs={{0,8},{4,12},{8,0},{12,4},{16,24},{20,28},{24,16},{28,20},{1,9},{5... | collective-permute-start | bytes 442376 | tf_op jit(solution)/shard_map/ppermute | solution.py:683
  355.3 10.2 %collective-permute-start.56 = (bf16[1,112,384]{2,1,0:T(8,128)(2,1)S(1)}, bf16[1,112,384]{2,1,0:T(8,128)(2,1)S(1)}, u32[]{:S(2)}, u32[]{:S(2)}) collective-permute-start(bf16[1,112,384]{2,1,0:T(8,128)(2,1)S(1)} %add_convert_fusion.3), channel_id=1, source_target_pairs={{0,16},{4,20},{8,24},{12,28},{16,0},{20,4},{24,8},{28,12},{1,17},{... | collective-permute-start | bytes 258056 | tf_op jit(solution)/shard_map/ppermute | solution.py:683
  363.8 20.2 %collective-permute-start.68 = (bf16[4,192,384]{2,1,0:T(8,128)(2,1)S(1)}, bf16[4,192,384]{2,1,0:T(8,128)(2,1)S(1)}, u32[]{:S(2)}, u32[]{:S(2)}) collective-permute-start(bf16[4,192,384]{2,1,0:T(8,128)(2,1)S(1)} %constant_dynamic-update-slice_fusion.8.refs_4_), channel_id=1, source_target_pairs={{0,4},{4,0},{8,12},{12,8},{16,20},{20,16},{24,28},{28,24},{1,5},{5... | collective-permute-start | bytes 1769480 | tf_op jit(solution)/shard_map/ppermute | solution.py:683
  365.4 6.7 %collective-permute-start.57 = (bf16[1,96,384]{2,1,0:T(8,128)(2,1)S(1)}, bf16[1,96,384]{2,1,0:T(8,128)(2,1)S(1)}, u32[]{:S(2)}, u32[]{:S(2)}) collective-permute-start(bf16[1,96,384]{2,1,0:T(8,128)(2,1)S(1)} %add_convert_fusion.6), channel_id=1, source_target_pairs={{0,16},{4,20},{8,24},{12,28},{16,0},{20,4},{24,8},{28,12},{1,17},{... | collective-permute-start | bytes 221192 | tf_op jit(solution)/shard_map/ppermute | solution.py:683
  372.2 5.4 %collective-permute-start.60 = (bf16[1,96,384]{2,1,0:T(8,128)(2,1)S(1)}, bf16[1,96,384]{2,1,0:T(8,128)(2,1)S(1)}, u32[]{:S(2)}, u32[]{:S(2)}) collective-permute-start(bf16[1,96,384]{2,1,0:T(8,128)(2,1)S(1)} %add_convert_fusion.5), channel_id=1, source_target_pairs={{0,16},{4,20},{8,24},{12,28},{16,0},{20,4},{24,8},{28,12},{1,17},{... | collective-permute-start | bytes 221192 | tf_op jit(solution)/shard_map/ppermute | solution.py:683
  372.3 9.5 %collective-permute-start.58 = (bf16[2,112,384]{2,1,0:T(8,128)(2,1)S(1)}, bf16[2,112,384]{2,1,0:T(8,128)(2,1)S(1)}, u32[]{:S(2)}, u32[]{:S(2)}) collective-permute-start(bf16[2,112,384]{2,1,0:T(8,128)(2,1)S(1)} %constant_dynamic-update-slice_fusion), channel_id=1, source_target_pairs={{0,4},{4,0},{8,12},{12,8},{16,20},{20,16},{24,28},{28,24},{1,5},{5... | collective-permute-start | bytes 516104 | tf_op jit(solution)/shard_map/ppermute | solution.py:683
  377.6 5.4 %collective-permute-start.61 = (bf16[2,96,384]{2,1,0:T(8,128)(2,1)S(1)}, bf16[2,96,384]{2,1,0:T(8,128)(2,1)S(1)}, u32[]{:S(2)}, u32[]{:S(2)}) collective-permute-start(bf16[2,96,384]{2,1,0:T(8,128)(2,1)S(1)} %pad_maximum_fusion.4), channel_id=1, source_target_pairs={{0,8},{4,12},{8,0},{12,4},{16,24},{20,28},{24,16},{28,20},{1,9},{5... | collective-permute-start | bytes 442376 | tf_op jit(solution)/shard_map/ppermute | solution.py:683
  381.8 8.4 %collective-permute-start.59 = (bf16[4,112,384]{2,1,0:T(8,128)(2,1)S(1)}, bf16[4,112,384]{2,1,0:T(8,128)(2,1)S(1)}, u32[]{:S(2)}, u32[]{:S(2)}) collective-permute-start(bf16[4,112,384]{2,1,0:T(8,128)(2,1)S(1)} %constant_dynamic-update-slice_fusion.2.refs_0_), channel_id=1, source_target_pairs={{0,8},{4,12},{8,0},{12,4},{16,24},{20,28},{24,16},{28,20},{1,9},{5... | collective-permute-start | bytes 1032200 | tf_op jit(solution)/shard_map/ppermute | solution.py:683
  383.0 7.1 %collective-permute-start.62 = (bf16[4,96,384]{2,1,0:T(8,128)(2,1)S(1)}, bf16[4,96,384]{2,1,0:T(8,128)(2,1)S(1)}, u32[]{:S(2)}, u32[]{:S(2)}) collective-permute-start(bf16[4,96,384]{2,1,0:T(8,128)(2,1)S(1)} %pad_maximum_fusion.2.refs_2_), channel_id=1, source_target_pairs={{0,4},{4,0},{8,12},{12,8},{16,20},{20,16},{24,28},{28,24},{1,5},{5... | collective-permute-start | bytes 884744 | tf_op jit(solution)/shard_map/ppermute | solution.py:683
  (91 other events, 631.7 us)

commit v5 on v4

--- a/solution.py
+++ b/solution.py
@@ -1222,7 +1222,9 @@
     outs, gots = slot([grads1[0]] + gots, (r0, "back"), (r1, "back"), (r2, "all"), (r3, "all"))
     keep, send = qkv_back(1, grads1, 0, *outs)
     r4 = Reduce(orders[4], keep, tie(send, *gots))
-    outs, gots = slot([keep] + gots, (r0, "back"), (r1, "back"), (r2, "back"), (r3, "all"))
+    late = gots
+    outs, gots = slot([keep] + gots, (r1, "back"), (r2, "back"), (r3, "all"))
+    outs += slot(outs, (r0, "back"), apart=True)[0]
     more = slot([], (r4, "all"), apart=True)
     outs = outs + more[0]
 

time: 399 us -> 397 us (level)
  waiting for transfers between devices: 77.6 us -> 72.5 us
    ppermute x69, waiting for transfers between devices: 77.6 us -> 72.5 us  [xor_permute(): return lax.ppermute(value, axis, [(i, i ^ bits) for i in range(size)])]
    unnamed x177 -> x178, local copies, waits for them, and re-layouts: 28.9 us -> 29.1 us
where the time goes in v5:
time: 397 us; the launch traced here: 391 us
  Pallas kernels  204 us (51%)
  waiting for transfers between devices  72.5 us (18%)
  starting transfers between devices  60.4 us (15%)
  local copies, waits for them, and re-layouts  41.2 us (10%)
  other arithmetic  9.87 us (2%)
    ppermute x69, waiting for transfers between devices, xor_permute(): return lax.ppermute(value, axis, [(i, i ^ bits) for i in range(size)])  72.5 us
    ppermute x69, starting transfers between devices, xor_permute(): return lax.ppermute(value, axis, [(i, i ^ bits) for i in range(size)])  60.4 us
    pallas_call x3, Pallas kernels, ffn_back(): pl.pallas_call(functools.partial(ffn_back_kernel, g, orders[g], groups),...  36.4 us
    pallas_call x2, Pallas kernels, attend_back(): pl.pallas_call(kernel, grid_spec=pltpu.PrefetchScalarGridSpec(num_scalar_...  33.1 us
    pallas_call x1, Pallas kernels, per_device(): pl.pallas_call(ffn_kernel, grid_spec=pltpu.PrefetchScalarGridSpec(num_sca...  29.7 us
    unnamed x178, local copies, waits for them, and re-layouts  29.1 us
    pallas_call x2, Pallas kernels, attend(): pl.pallas_call(functools.partial(drop_last, attend_kernel, len(after), 7)...  24.6 us
    pallas_call x1, Pallas kernels, per_device(): pl.pallas_call(functools.partial(ffn_input_back_kernel, groups), in_specs...  14.1 us
  transfers between devices with their start and end apart: 69, of which 29 were waited for; matrix products, arithmetic and copies ran while one was open for 5% of the time, Pallas kernels for 39%

profile of v5, /device:TPU:0, one launch (start us, length us, event | category | flops | bytes accessed | tf_op | source)
XLA Modules:
  0.0 391.3 jit_solution(8260913178162230685)
XLA Ops:
  1.2 2.6 collective-permute-start.1
  6.5 1.7 collective-permute-start.3
  12.1 1.9 constant_dynamic-slice_fusion.3
  14.0 1.9 constant_dynamic-slice_fusion.1
  15.9 1.9 constant_dynamic-slice_fusion
  17.8 3.0 fusion
  21.1 2.0 pad_maximum_fusion
  25.0 1.8 collective-permute-start.6
  28.3 13.9 %shard_map.212 = (bf16[1024,2304]{1,0:T(8,128)(2,1)}, bf16[768,1024]{1,0:T(8,128)(2,1)}) custom-call(s32[5]{0:T(128)} %stack.123.rows_ref, bf16[1024,768]{1,0:T(8,128)(2,1)} %bitcast.59, f32[1024,128]{1,0:T(8,128)} %get-tuple-element.246.cos_ref.refs_10_.refs_12_, f32[1024,128]{1,0:T(8,128)} %get-tuple-element.245.sin_ref.refs_11_.refs_13_, ...), custom_call_target="tpu_custom_call" | custom-call | flops 1 | bytes 1 | tf_op jit(solution)/shard_map/pallas_call | solution.py:850
  42.2 1.9 collective-permute-done.6.refs_7_.one_ref
  44.1 1.8 collective-permute-start.8
  47.6 2.3 copy-done
  49.9 12.2 %shard_map.213 = (bf16[1024,384]{1,0:T(8,128)(2,1)S(1)}, f32[3,8,1024]{2,1,0:T(8,128)S(1)}) custom-call(s32[4]{0:T(128)S(1)} %get-tuple-element.232.refs_0_, s32[4]{0:T(128)S(1)} %get-tuple-element.231.refs_1_, bf16[1024,2304]{1,0:T(8,128)(2,1)S(1)} %copy-done, bf16[1024,2304]{1,0:T(8,128)(2,1)S(1)} %copy-done, bf16[1024,2304]{1,0:T(8,128)(2,1)S(1)} %copy-done, ...), custom_call_target="tpu_custom_call" | custom-call | flops 1 | bytes 1 | tf_op jit(solution)/shard_map/pallas_call | solution.py:870
  63.8 1.8 collective-permute-start.11
  67.6 2.3 copy-done.1
  69.9 12.4 %shard_map.215 = (bf16[1024,384]{1,0:T(8,128)(2,1)S(1)}, f32[3,8,1024]{2,1,0:T(8,128)S(1)}) custom-call(s32[4]{0:T(128)S(1)} %get-tuple-element.232.refs_0_, s32[4]{0:T(128)S(1)} %get-tuple-element.231.refs_1_, bf16[1024,2304]{1,0:T(8,128)(2,1)S(1)} %copy-done.1, bf16[1024,2304]{1,0:T(8,128)(2,1)S(1)} %copy-done.1, bf16[1024,2304]{1,0:T(8,128)(2,1)S(1)} %copy-done.1, ...), custom_call_target="tpu_custom_call" | custom-call | flops 1 | bytes 1 | tf_op jit(solution)/shard_map/pallas_call | solution.py:870
  83.2 2.5 shard_map.216.refs_5_.refs_6_
  87.4 5.9 %shard_map.217 = (f32[1024,768]{1,0:T(8,128)S(1)}, f32[1024,128]{1,0:T(8,128)S(1)}, bf16[1024,768]{1,0:T(8,128)(2,1)S(1)}, bf16[768,1024]{1,0:T(8,128)(2,1)S(1)}, bf16[768,768]{1,0:T(8,128)(2,1)S(1)}) custom-call(s32[5]{0:T(128)S(1)} %copy-done.77, bf16[1024,384]{1,0:T(8,128)(2,1)S(1)} %copy-done.24, bf16[1024,384]{1,0:T(8,128)(2,1)S(1)} %copy-done.27, ...), custom_call_target="tpu_custom_call" | custom-call | flops 1 | bytes 1 | tf_op jit(solution)/shard_map/pallas_call | solution.py:904
  96.1 2.4 collective-permute-done.17.two_ref
  100.2 2.8 collective-permute-done.18.refs_11_
  103.0 29.7 %shard_map.219 = (bf16[1024,3072]{1,0:T(8,128)(2,1)}, bf16[1024,3072]{1,0:T(8,128)(2,1)}, bf16[1024,3072]{1,0:T(8,128)(2,1)}, f32[1024,768]{1,0:T(8,128)}, f32[1...) custom-call(s32[5]{0:T(128)S(1)} %copy-done.77, ...), custom_call_target="tpu_custom_call" | custom-call | flops 1 | bytes 1 | tf_op jit(solution)/shard_map/pallas_call | solution.py:919
  133.5 3.6 collective-permute-start.21
  139.0 2.7 collective-permute-done.20
  142.5 3.5 collective-permute-done.22
  146.5 4.4 %collective-permute-done.23 = bf16[4,2,8,896]{3,2,0,1:T(8,128)(2,1)S(1)} collective-permute-done((bf16[4,2,8,896]{3,2,0,1:T(8,128)(2,1)S(1)}, bf16[4,2,8,896]{3,2,0,1:T(8,128)(2,1)S(1)}, u32[]{:S(2)}, u32[]{:S(2)}) %collective-permute-start.23) | collective-permute-done | bytes 114720 | tf_op jit(solution)/shard_map/ppermute | solution.py:683
  153.8 1.9 copy-done.54
  155.7 3.2 shard_map.221
  159.0 12.4 %shard_map.222 = (bf16[1024,1024]{1,0:T(8,128)(2,1)S(1)}, bf16[1024,1024]{1,0:T(8,128)(2,1)S(1)}, bf16[16,192,384]{2,1,0:T(8,128)(2,1)S(1)}, bf16[16,192,384]{2,1,0:T(8,128)(2,1)}) custom-call(s32[5]{0:T(128)S(1)} %stack.155.info_ref, bf16[1024,3072]{1,0:T(8,128)(2,1)} %get-tuple-element.141.prod_any, bf16[1024,3072]{1,0:T(8,128)(2,1)} %get-tuple-element.142.up_fac_any, ...), custom_call_target="tpu_custom_call" | custom-call | flops 1 | bytes 1 | tf_op jit(solution)/shard_map/pallas_call | solution.py:1087
  174.2 12.0 %shard_map.223 = (bf16[1024,1024]{1,0:T(8,128)(2,1)S(1)}, bf16[1024,1024]{1,0:T(8,128)(2,1)S(1)}, bf16[16,192,384]{2,1,0:T(8,128)(2,1)S(1)}, bf16[16,192,384]{2,1,0:T(8,128)(2,1)}) custom-call(s32[5]{0:T(128)S(1)} %stack.155.info_ref, bf16[1024,3072]{1,0:T(8,128)(2,1)} %get-tuple-element.141.prod_any, bf16[1024,3072]{1,0:T(8,128)(2,1)} %get-tuple-element.142.up_fac_any, ...), custom_call_target="tpu_custom_call" | custom-call | flops 1 | bytes 1 | tf_op jit(solution)/shard_map/pallas_call | solution.py:1087
  189.5 12.0 %shard_map.225 = (bf16[1024,1024]{1,0:T(8,128)(2,1)S(1)}, bf16[1024,1024]{1,0:T(8,128)(2,1)S(1)}, bf16[16,192,384]{2,1,0:T(8,128)(2,1)S(1)}, bf16[16,192,384]{2,1,0:T(8,128)(2,1)}) custom-call(s32[5]{0:T(128)S(1)} %stack.155.info_ref, bf16[1024,3072]{1,0:T(8,128)(2,1)} %get-tuple-element.141.prod_any, bf16[1024,3072]{1,0:T(8,128)(2,1)} %get-tuple-element.142.up_fac_any, ...), custom_call_target="tpu_custom_call" | custom-call | flops 1 | bytes 1 | tf_op jit(solution)/shard_map/pallas_call | solution.py:1087
  201.5 2.9 collective-permute-done.26.refs_4_.refs_8_
  204.5 1.7 copy-done.7
  213.4 14.1 %shard_map.227.refs_11_.grad_ref = f32[1024,768]{1,0:T(8,128)S(1)} custom-call(bf16[768,3072]{1,0:T(8,128)(2,1)} %get-tuple-element.135.wu_any, bf16[768,3072]{1,0:T(8,128)(2,1)} %get-tuple-element.136.wg_any, f32[1024,768]{1,0:T(8,128)} %copy-done.53, bf16[1024,1024]{1,0:T(8,128)(2,1)S(1)} %copy-done.58, bf16[1024,1024]{1,0:T(8,128)(2,1)S(1)} %copy-done.60, ...), custom_call_target="tpu_custom_call" | custom-call | flops 1 | bytes 1 | tf_op jit(solution)/shard_map/pallas_call | solution.py:1112
  227.6 1.9 copy-done.4
  229.5 1.7 copy-done.8
  234.2 1.7 collective-permute-start.32
  236.2 6.9 %shard_map.229 = (f32[1024,768]{1,0:T(8,128)S(1)}, bf16[1024,768]{1,0:T(8,128)(2,1)S(1)}, bf16[1024,768]{1,0:T(8,128)(2,1)S(1)}, f32[6,8,1024]{2,1,0:T(8,128)S(1...) custom-call(s32[5]{0:T(128)S(1)} %stack.155.info_ref, f32[1024,768]{1,0:T(8,128)S(1)} %shard_map.227.refs_11_.grad_ref, ...), custom_call_target="tpu_custom_call" | custom-call | flops 1 | bytes 1 | tf_op jit(solution)/shard_map/pallas_call | solution.py:1129
  244.8 16.3 %shard_map.230 = (bf16[1024,384]{1,0:T(8,128)(2,1)S(1)}, bf16[1024,384]{1,0:T(8,128)(2,1)S(1)}, bf16[1024,384]{1,0:T(8,128)(2,1)S(1)}) custom-call(s32[4]{0:T(128)S(1)} %get-tuple-element.232.refs_0_, s32[4]{0:T(128)S(1)} %get-tuple-element.231.refs_1_, bf16[1024,2304]{1,0:T(8,128)(2,1)S(1)} %bitcast.58, bf16[1024,2304]{1,0:T(8,128)(2,1)S(1)} %bitcast.58, ...), custom_call_target="tpu_custom_call" | custom-call | flops 1 | bytes 1 | tf_op jit(solution)/shard_map/pallas_call | solution.py:1172
  262.3 1.7 collective-permute-start.37
  264.0 1.7 collective-permute-start.39
  265.7 2.0 collective-permute-start.36
  267.8 4.7 %shard_map.232 = (bf16[16,112,384]{2,1,0:T(8,128)(2,1)S(1)}, bf16[16,112,384]{2,1,0:T(8,128)(2,1)S(1)}) custom-call(s32[5]{0:T(128)S(1)} %stack.155.info_ref, bf16[768,1024]{1,0:T(8,128)(2,1)S(1)} %copy-done.32, bf16[768,1024]{1,0:T(8,128)(2,1)S(1)} %copy-done.34, bf16[1024,384]{1,0:T(8,128)(2,1)S(1)} %get-tuple-element.174.refs_14_.gq_ref.gq0, ...), custom_call_target="tpu_custom_call" | custom-call | flops 1 | bytes 1 | tf_op jit(solution)/shard_map/pallas_call | solution.py:1201
  274.1 2.8 collective-permute-done.38.refs_16_.refs_21_.refs_10_.refs_4_
  276.9 3.1 collective-permute-done.40.refs_19_.refs_14_.refs_9_
  281.4 2.0 collective-permute-start.44
  284.3 2.0 collective-permute-start.42
  286.3 16.7 %shard_map.234 = (bf16[1024,384]{1,0:T(8,128)(2,1)S(1)}, bf16[1024,384]{1,0:T(8,128)(2,1)S(1)}, bf16[1024,384]{1,0:T(8,128)(2,1)S(1)}) custom-call(s32[4]{0:T(128)S(1)} %get-tuple-element.232.refs_0_, s32[4]{0:T(128)S(1)} %get-tuple-element.231.refs_1_, bf16[1024,2304]{1,0:T(8,128)(2,1)S(1)} %bitcast.58, bf16[1024,2304]{1,0:T(8,128)(2,1)S(1)} %bitcast.58, ...), custom_call_target="tpu_custom_call" | custom-call | flops 1 | bytes 1 | tf_op jit(solution)/shard_map/pallas_call | solution.py:1172
  306.9 4.6 %shard_map.236 = (bf16[16,96,384]{2,1,0:T(8,128)(2,1)S(1)}, bf16[16,96,384]{2,1,0:T(8,128)(2,1)S(1)}) custom-call(s32[5]{0:T(128)S(1)} %stack.155.info_ref, bf16[768,1024]{1,0:T(8,128)(2,1)S(1)} %copy-done.32, bf16[768,1024]{1,0:T(8,128)(2,1)S(1)} %copy-done.34, bf16[1024,384]{1,0:T(8,128)(2,1)S(1)} %get-tuple-element.194.refs_16_.gq_ref.gq1, ...), custom_call_target="tpu_custom_call" | custom-call | flops 1 | bytes 1 | tf_op jit(solution)/shard_map/pallas_call | solution.py:1201
  311.5 3.4 collective-permute-done.46.refs_1_.refs_14_
  314.9 5.1 %collective-permute-done.47.refs_7_.refs_15_ = bf16[1,192,384]{2,1,0:T(8,128)(2,1)S(1)} collective-permute-done((bf16[1,192,384]{2,1,0:T(8,128)(2,1)S(1)}, bf16[1,192,384]{2,1,0:T(8,128)(2,1)S(1)}, u32[]{:S(2)}, u32[]{:S(2)}) %collective-permute-start.47) | collective-permute-done | bytes 147488 | tf_op jit(solution)/shard_map/ppermute | solution.py:683
  320.0 2.8 collective-permute-done.50
  326.7 1.9 collective-permute-start.63
  328.6 8.9 %shard_map.238 = f32[1024,768]{1,0:T(8,128)} custom-call(s32[5]{0:T(128)S(1)} %copy-done.78, bf16[1024,384]{1,0:T(8,128)(2,1)S(1)} %get-tuple-element.174.refs_14_.gq_ref.gq0, bf16[1024,384]{1,0:T(8,128)(2,1)S(1)} %copy-done.48, bf16[1024,384]{1,0:T(8,128)(2,1)S(1)} %copy-done.50, bf16[1024,384]{1,0:T(8,128)(2,1)S(1)} %get-tuple-element.194.refs_16_.gq_ref.gq1, ...), custom_call_target="tpu_custom_call" | custom-call | flops 1 | bytes 1 | tf_op jit(solution)/shard_map/pallas_call | solution.py:1231
  339.0 2.2 collective-permute-start.53
  343.2 5.4 %collective-permute-done.54 = bf16[4,96,384]{2,1,0:T(8,128)(2,1)S(1)} collective-permute-done((bf16[4,96,384]{2,1,0:T(8,128)(2,1)S(1)}, bf16[4,96,384]{2,1,0:T(8,128)(2,1)S(1)}, u32[]{:S(2)}, u32[]{:S(2)}) %collective-permute-start.54) | collective-permute-done | bytes 294944 | tf_op jit(solution)/shard_map/ppermute | solution.py:683
  350.4 3.4 collective-permute-start.56
  353.8 6.8 %collective-permute-done.67 = bf16[2,192,384]{2,1,0:T(8,128)(2,1)S(1)} collective-permute-done((bf16[2,192,384]{2,1,0:T(8,128)(2,1)S(1)}, bf16[2,192,384]{2,1,0:T(8,128)(2,1)S(1)}, u32[]{:S(2)}, u32[]{:S(2)}) %collective-permute-start.67) | collective-permute-done | bytes 294944 | tf_op jit(solution)/shard_map/ppermute | solution.py:683
  360.7 1.7 collective-permute-start.68
  363.1 5.0 %collective-permute-done.57 = bf16[1,96,384]{2,1,0:T(8,128)(2,1)S(1)} collective-permute-done((bf16[1,96,384]{2,1,0:T(8,128)(2,1)S(1)}, bf16[1,96,384]{2,1,0:T(8,128)(2,1)S(1)}, u32[]{:S(2)}, u32[]{:S(2)}) %collective-permute-start.57) | collective-permute-done | bytes 73760 | tf_op jit(solution)/shard_map/ppermute | solution.py:683
  370.0 3.5 collective-permute-done.60
  373.6 4.0 %collective-permute-done.58 = bf16[2,112,384]{2,1,0:T(8,128)(2,1)S(1)} collective-permute-done((bf16[2,112,384]{2,1,0:T(8,128)(2,1)S(1)}, bf16[2,112,384]{2,1,0:T(8,128)(2,1)S(1)}, u32[]{:S(2)}, u32[]{:S(2)}) %collective-permute-start.58) | collective-permute-done | bytes 172064 | tf_op jit(solution)/shard_map/ppermute | solution.py:683
  377.7 2.4 collective-permute-done.61
  382.4 5.7 %shard_map.240 = (f32[192,3072]{1,0:T(8,128)}, f32[192,3072]{1,0:T(8,128)}, f32[768,768]{1,0:T(8,128)}) custom-call(s32[5]{0:T(128)S(1)} %stack.155.info_ref, bf16[4,192,384]{2,1,0:T(8,128)(2,1)S(1)} %constant_dynamic-update-slice_fusion.refs_7_.refs_0_, bf16[4,192,384]{2,1,0:T(8,128)(2,1)S(1)} %collective-permute-done.63.refs_1_, ...), custom_call_target="tpu_custom_call" | custom-call | flops 1 | bytes 1 | tf_op jit(solution)/shard_map/pallas_call | solution.py:1254
  388.2 2.3 shard_map.239
  (355 shorter events, 71.0 us)
Async XLA Ops:
  0.6 26.7 %collective-permute-start = (bf16[192,2304]{1,0:T(8,128)(2,1)}, bf16[192,2304]{1,0:T(8,128)(2,1)S(1)}, u32[]{:S(2)}, u32[]{:S(2)}) collective-permute-start(bf16[192,2304]{1,0:T(8,128)(2,1)} %refs_0_.7), channel_id=1, source_target_pairs={{0,1},{1,0},{2,3},{3,2},{4,5},{5,4},{6,7},{7,6},{8,9},{9,8},{10,11... | collective-permute-start | bytes 2654216 | tf_op jit(solution)/shard_map/ppermute | solution.py:683
  1.2 23.7 %collective-permute-start.1 = (bf16[192,2304]{1,0:T(8,128)(2,1)}, bf16[192,2304]{1,0:T(8,128)(2,1)S(1)}, u32[]{:S(2)}, u32[]{:S(2)}) collective-permute-start(bf16[192,2304]{1,0:T(8,128)(2,1)} %refs_0_.7), channel_id=1, source_target_pairs={{0,2},{1,3},{2,0},{3,1},{4,6},{5,7},{6,4},{7,5},{8,10},{9,11},{10,... | collective-permute-start | bytes 2654216 | tf_op jit(solution)/shard_map/ppermute | solution.py:683
  6.4 17.6 %collective-permute-start.4 = (bf16[4,192]{1,0:T(4,128)(2,1)S(1)}, bf16[4,192]{1,0:T(4,128)(2,1)S(1)}, u32[]{:S(2)}, u32[]{:S(2)}) collective-permute-start(bf16[4,192]{1,0:T(4,128)(2,1)S(1)} %pad_maximum_fusion.8), channel_id=1, source_target_pairs={{0,3},{1,2},{2,1},{3,0},{4,7},{5,6},{6,5},{7,4},{8,11},{9,10},{10,... | collective-permute-start | bytes 4616 | tf_op jit(solution)/shard_map/ppermute | solution.py:683
  6.5 17.8 %collective-permute-start.3 = (bf16[4,192]{1,0:T(4,128)(2,1)S(1)}, bf16[4,192]{1,0:T(4,128)(2,1)S(1)}, u32[]{:S(2)}, u32[]{:S(2)}) collective-permute-start(bf16[4,192]{1,0:T(4,128)(2,1)S(1)} %pad_maximum_fusion.8), channel_id=1, source_target_pairs={{0,2},{1,3},{2,0},{3,1},{4,6},{5,7},{6,4},{7,5},{8,10},{9,11},{10,... | collective-permute-start | bytes 4616 | tf_op jit(solution)/shard_map/ppermute | solution.py:683
  8.2 16.0 %collective-permute-start.2 = (bf16[4,192]{1,0:T(4,128)(2,1)S(1)}, bf16[4,192]{1,0:T(4,128)(2,1)S(1)}, u32[]{:S(2)}, u32[]{:S(2)}) collective-permute-start(bf16[4,192]{1,0:T(4,128)(2,1)S(1)} %pad_maximum_fusion.8), channel_id=1, source_target_pairs={{0,1},{1,0},{2,3},{3,2},{4,5},{5,4},{6,7},{7,6},{8,9},{9,8},{10,11... | collective-permute-start | bytes 4616 | tf_op jit(solution)/shard_map/ppermute | solution.py:683
  25.0 19.2 %collective-permute-start.6 = (bf16[96,3840]{1,0:T(8,128)(2,1)}, bf16[96,3840]{1,0:T(8,128)(2,1)}, u32[]{:S(2)}, u32[]{:S(2)}) collective-permute-start(bf16[96,3840]{1,0:T(8,128)(2,1)} %pad_maximum_fusion), channel_id=1, source_target_pairs={{0,2},{1,3},{2,0},{3,1},{4,6},{5,7},{6,4},{7,5},{8,10},{9,11},{10,... | collective-permute-start | bytes 2211848 | tf_op jit(solution)/shard_map/ppermute | solution.py:683
  44.1 18.3 %collective-permute-start.8 = (bf16[96,3840]{1,0:T(8,128)(2,1)}, bf16[96,3840]{1,0:T(8,128)(2,1)S(1)}, u32[]{:S(2)}, u32[]{:S(2)}) collective-permute-start(bf16[96,3840]{1,0:T(8,128)(2,1)} %collective-permute-done.6.refs_7_.one_ref), channel_id=1, source_target_pairs={{0,4},{4,0},{8,12},{12,8},{16,20},{20,16},{24,28},{28,24},{1,5},{5... | collective-permute-start | bytes 2211848 | tf_op jit(solution)/shard_map/ppermute | solution.py:683
  45.9 16.2 %collective-permute-start.7 = (bf16[96,3072]{1,0:T(8,128)(2,1)}, bf16[96,3072]{1,0:T(8,128)(2,1)}, u32[]{:S(2)}, u32[]{:S(2)}) collective-permute-start(bf16[96,3072]{1,0:T(8,128)(2,1)} %constant_dynamic-slice_fusion.1), channel_id=1, source_target_pairs={{0,2},{1,3},{2,0},{3,1},{4,6},{5,7},{6,4},{7,5},{8,10},{9,11},{10,... | collective-permute-start | bytes 1769480 | tf_op jit(solution)/shard_map/ppermute | solution.py:683
  63.7 22.2 %collective-permute-start.10 = (bf16[192,3840]{1,0:T(8,128)(2,1)S(1)}, bf16[192,3840]{1,0:T(8,128)(2,1)}, u32[]{:S(2)}, u32[]{:S(2)}) collective-permute-start(bf16[192,3840]{1,0:T(8,128)(2,1)S(1)} %shard_map.214.refs_8_.refs_2_), channel_id=1, source_target_pairs={{0,1},{1,0},{2,3},{3,2},{4,5},{5,4},{6,7},{7,6},{8,9},{9,8},{10,11... | collective-permute-start | bytes 4423688 | tf_op jit(solution)/shard_map/ppermute | solution.py:683
  63.8 18.6 %collective-permute-start.11 = (bf16[384,768]{1,0:T(8,128)(2,1)}, bf16[384,768]{1,0:T(8,128)(2,1)}, u32[]{:S(2)}, u32[]{:S(2)}) collective-permute-start(bf16[384,768]{1,0:T(8,128)(2,1)} %constant_dynamic-slice_fusion), channel_id=1, source_target_pairs={{0,2},{1,3},{2,0},{3,1},{4,6},{5,7},{6,4},{7,5},{8,10},{9,11},{10,... | collective-permute-start | bytes 1769480 | tf_op jit(solution)/shard_map/ppermute | solution.py:683
  65.6 16.9 %collective-permute-start.12 = (bf16[96,3072]{1,0:T(8,128)(2,1)}, bf16[96,3072]{1,0:T(8,128)(2,1)}, u32[]{:S(2)}, u32[]{:S(2)}) collective-permute-start(bf16[96,3072]{1,0:T(8,128)(2,1)} %collective-permute-done.7.refs_1_.refs_7_.one_ref), channel_id=1, source_target_pairs={{0,4},{4,0},{8,12},{12,8},{16,20},{20,16},{24,28},{28,24},{1,5},{5... | collective-permute-start | bytes 1769480 | tf_op jit(solution)/shard_map/ppermute | solution.py:683
  67.1 18.6 %collective-permute-start.9 = (bf16[192,768]{1,0:T(8,128)(2,1)S(1)}, bf16[192,768]{1,0:T(8,128)(2,1)}, u32[]{:S(2)}, u32[]{:S(2)}) collective-permute-start(bf16[192,768]{1,0:T(8,128)(2,1)S(1)} %copy-done.67), channel_id=1, source_target_pairs={{0,1},{1,0},{2,3},{3,2},{4,5},{5,4},{6,7},{7,6},{8,9},{9,8},{10,11... | collective-permute-start | bytes 884744 | tf_op jit(solution)/shard_map/ppermute | solution.py:683
  67.1 33.0 %collective-permute-start.13 = (bf16[192,3072]{1,0:T(8,128)(2,1)}, bf16[192,3072]{1,0:T(8,128)(2,1)}, u32[]{:S(2)}, u32[]{:S(2)}) collective-permute-start(bf16[192,3072]{1,0:T(8,128)(2,1)} %refs_0_.6), channel_id=1, source_target_pairs={{0,1},{1,0},{2,3},{3,2},{4,5},{5,4},{6,7},{7,6},{8,9},{9,8},{10,11... | collective-permute-start | bytes 3538952 | tf_op jit(solution)/shard_map/ppermute | solution.py:683
  82.4 17.8 %collective-permute-start.14 = (bf16[192,3072]{1,0:T(8,128)(2,1)}, bf16[192,3072]{1,0:T(8,128)(2,1)}, u32[]{:S(2)}, u32[]{:S(2)}) collective-permute-start(bf16[192,3072]{1,0:T(8,128)(2,1)} %refs_4_.1), channel_id=1, source_target_pairs={{0,1},{1,0},{2,3},{3,2},{4,5},{5,4},{6,7},{7,6},{8,9},{9,8},{10,11... | collective-permute-start | bytes 3538952 | tf_op jit(solution)/shard_map/ppermute | solution.py:683
  82.5 16.1 %collective-permute-start.17 = (bf16[384,768]{1,0:T(8,128)(2,1)}, bf16[384,768]{1,0:T(8,128)(2,1)}, u32[]{:S(2)}, u32[]{:S(2)}) collective-permute-start(bf16[384,768]{1,0:T(8,128)(2,1)} %collective-permute-done.11.refs_1_.refs_4_.one_ref), channel_id=1, source_target_pairs={{0,4},{4,0},{8,12},{12,8},{16,20},{20,16},{24,28},{28,24},{1,5},{5... | collective-permute-start | bytes 1769480 | tf_op jit(solution)/shard_map/ppermute | solution.py:683
  85.7 14.4 %collective-permute-start.16 = (bf16[768,768]{1,0:T(8,128)(2,1)}, bf16[768,768]{1,0:T(8,128)(2,1)}, u32[]{:S(2)}, u32[]{:S(2)}) collective-permute-start(bf16[768,768]{1,0:T(8,128)(2,1)} %refs_8_.1), channel_id=1, source_target_pairs={{0,1},{1,0},{2,3},{3,2},{4,5},{5,4},{6,7},{7,6},{8,9},{9,8},{10,11... | collective-permute-start | bytes 3538952 | tf_op jit(solution)/shard_map/ppermute | solution.py:683
  85.9 14.2 %collective-permute-start.15 = (bf16[192,3072]{1,0:T(8,128)(2,1)}, bf16[192,3072]{1,0:T(8,128)(2,1)}, u32[]{:S(2)}, u32[]{:S(2)}) collective-permute-start(bf16[192,3072]{1,0:T(8,128)(2,1)} %shard_map.216.refs_5_.refs_6_), channel_id=1, source_target_pairs={{0,1},{1,0},{2,3},{3,2},{4,5},{5,4},{6,7},{7,6},{8,9},{9,8},{10,11... | collective-permute-start | bytes 3538952 | tf_op jit(solution)/shard_map/ppermute | solution.py:683
  133.5 5.5 %collective-permute-start.21 = (bf16[8,896]{1,0:T(8,128)(2,1)S(1)}, bf16[8,896]{1,0:T(8,128)(2,1)S(1)}, u32[]{:S(2)}, u32[]{:S(2)}) collective-permute-start(bf16[8,896]{1,0:T(8,128)(2,1)S(1)} %get-tuple-element.244), channel_id=1, source_target_pairs={{0,24},{4,28},{8,16},{12,20},{16,8},{20,12},{24,0},{28,4},{1,25},{... | collective-permute-start | bytes 43016 | tf_op jit(solution)/shard_map/ppermute | solution.py:683
  137.1 4.6 %collective-permute-start.20 = (bf16[8,896]{1,0:T(8,128)(2,1)S(1)}, bf16[8,896]{1,0:T(8,128)(2,1)S(1)}, u32[]{:S(2)}, u32[]{:S(2)}) collective-permute-start(bf16[8,896]{1,0:T(8,128)(2,1)S(1)} %get-tuple-element.244), channel_id=1, source_target_pairs={{0,16},{4,20},{8,24},{12,28},{16,0},{20,4},{24,8},{28,12},{1,17},{... | collective-permute-start | bytes 43016 | tf_op jit(solution)/shard_map/ppermute | solution.py:683
  137.1 4.6 %collective-permute-start.19 = (bf16[8,896]{1,0:T(8,128)(2,1)S(1)}, bf16[8,896]{1,0:T(8,128)(2,1)S(1)}, u32[]{:S(2)}, u32[]{:S(2)}) collective-permute-start(bf16[8,896]{1,0:T(8,128)(2,1)S(1)} %get-tuple-element.244), channel_id=1, source_target_pairs={{0,8},{4,12},{8,0},{12,4},{16,24},{20,28},{24,16},{28,20},{1,9},{5... | collective-permute-start | bytes 43016 | tf_op jit(solution)/shard_map/ppermute | solution.py:683
  141.7 4.2 %collective-permute-start.22 = (bf16[4,8,896]{2,1,0:T(8,128)(2,1)S(1)}, bf16[4,8,896]{2,1,0:T(8,128)(2,1)S(1)}, u32[]{:S(2)}, u32[]{:S(2)}) collective-permute-start(bf16[4,8,896]{2,1,0:T(8,128)(2,1)S(1)} %get-tuple-element.238), channel_id=1, source_target_pairs={{0,2},{1,3},{2,0},{3,1},{4,6},{5,7},{6,4},{7,5},{8,10},{9,11},{10,... | collective-permute-start | bytes 172040 | tf_op jit(solution)/shard_map/ppermute | solution.py:683
  146.0 4.9 %collective-permute-start.23 = (bf16[4,2,8,896]{3,2,0,1:T(8,128)(2,1)S(1)}, bf16[4,2,8,896]{3,2,0,1:T(8,128)(2,1)S(1)}, u32[]{:S(2)}, u32[]{:S(2)}) collective-permute-start(bf16[4,2,8,896]{3,2,0,1:T(8,128)(2,1)S(1)} %get-tuple-element.236), channel_id=1, source_target_pairs={{0,4},{4,0},{8,12},{12,8},{16,20},{20,16},{24,28},{28,24},{1,5},{5... | collective-permute-start | bytes 344072 | tf_op jit(solution)/shard_map/ppermute | solution.py:683
  174.0 12.6 %collective-permute-start.25 = (bf16[16,192,384]{2,1,0:T(8,128)(2,1)}, bf16[16,192,384]{2,1,0:T(8,128)(2,1)S(1)}, u32[]{:S(2)}, u32[]{:S(2)}) collective-permute-start(bf16[16,192,384]{2,1,0:T(8,128)(2,1)} %get-tuple-element.150.refs_0_), channel_id=1, source_target_pairs={{0,1},{1,0},{2,3},{3,2},{4,5},{5,4},{6,7},{7,6},{8,9},{9,8},{10,11... | collective-permute-start | bytes 7077896 | tf_op jit(solution)/shard_map/ppermute | solution.py:683
  186.2 18.3 %collective-permute-start.27 = (bf16[16,192,384]{2,1,0:T(8,128)(2,1)}, bf16[16,192,384]{2,1,0:T(8,128)(2,1)S(1)}, u32[]{:S(2)}, u32[]{:S(2)}) collective-permute-start(bf16[16,192,384]{2,1,0:T(8,128)(2,1)} %get-tuple-element.153.refs_0_), channel_id=1, source_target_pairs={{0,1},{1,0},{2,3},{3,2},{4,5},{5,4},{6,7},{7,6},{8,9},{9,8},{10,11... | collective-permute-start | bytes 7077896 | tf_op jit(solution)/shard_map/ppermute | solution.py:683
  188.8 15.6 %collective-permute-start.26 = (bf16[4,192,384]{2,1,0:T(8,128)(2,1)S(1)}, bf16[4,192,384]{2,1,0:T(8,128)(2,1)S(1)}, u32[]{:S(2)}, u32[]{:S(2)}) collective-permute-start(bf16[4,192,384]{2,1,0:T(8,128)(2,1)S(1)} %shard_map.224.refs_1_), channel_id=1, source_target_pairs={{0,2},{1,3},{2,0},{3,1},{4,6},{5,7},{6,4},{7,5},{8,10},{9,11},{10,... | collective-permute-start | bytes 1769480 | tf_op jit(solution)/shard_map/ppermute | solution.py:683
  204.4 23.2 %collective-permute-start.31 = (bf16[16,192,384]{2,1,0:T(8,128)(2,1)}, bf16[16,192,384]{2,1,0:T(8,128)(2,1)S(1)}, u32[]{:S(2)}, u32[]{:S(2)}) collective-permute-start(bf16[16,192,384]{2,1,0:T(8,128)(2,1)} %get-tuple-element.166), channel_id=1, source_target_pairs={{0,1},{1,0},{2,3},{3,2},{4,5},{5,4},{6,7},{7,6},{8,9},{9,8},{10,11... | collective-permute-start | bytes 7077896 | tf_op jit(solution)/shard_map/ppermute | solution.py:683
  207.6 20.0 %collective-permute-start.28 = (bf16[4,192,384]{2,1,0:T(8,128)(2,1)}, bf16[4,192,384]{2,1,0:T(8,128)(2,1)S(1)}, u32[]{:S(2)}, u32[]{:S(2)}) collective-permute-start(bf16[4,192,384]{2,1,0:T(8,128)(2,1)} %get-tuple-element.158.refs_6_), channel_id=1, source_target_pairs={{0,2},{1,3},{2,0},{3,1},{4,6},{5,7},{6,4},{7,5},{8,10},{9,11},{10,... | collective-permute-start | bytes 1769480 | tf_op jit(solution)/shard_map/ppermute | solution.py:683
  208.2 19.3 %collective-permute-start.29 = (bf16[4,192,384]{2,1,0:T(8,128)(2,1)}, bf16[4,192,384]{2,1,0:T(8,128)(2,1)S(1)}, u32[]{:S(2)}, u32[]{:S(2)}) collective-permute-start(bf16[4,192,384]{2,1,0:T(8,128)(2,1)} %get-tuple-element.159.refs_7_), channel_id=1, source_target_pairs={{0,8},{4,12},{8,0},{12,4},{16,24},{20,28},{24,16},{28,20},{1,9},{5... | collective-permute-start | bytes 1769480 | tf_op jit(solution)/shard_map/ppermute | solution.py:683
  208.2 19.4 %collective-permute-start.30 = (bf16[4,192,384]{2,1,0:T(8,128)(2,1)}, bf16[4,192,384]{2,1,0:T(8,128)(2,1)S(1)}, u32[]{:S(2)}, u32[]{:S(2)}) collective-permute-start(bf16[4,192,384]{2,1,0:T(8,128)(2,1)} %get-tuple-element.160.refs_8_), channel_id=1, source_target_pairs={{0,4},{4,0},{8,12},{12,8},{16,20},{20,16},{24,28},{28,24},{1,5},{5... | collective-permute-start | bytes 1769480 | tf_op jit(solution)/shard_map/ppermute | solution.py:683
  231.8 29.4 %collective-permute-start.33 = (bf16[4,192,384]{2,1,0:T(8,128)(2,1)S(1)}, bf16[4,192,384]{2,1,0:T(8,128)(2,1)S(1)}, u32[]{:S(2)}, u32[]{:S(2)}) collective-permute-start(bf16[4,192,384]{2,1,0:T(8,128)(2,1)S(1)} %get-tuple-element.170.refs_3_), channel_id=1, source_target_pairs={{0,2},{1,3},{2,0},{3,1},{4,6},{5,7},{6,4},{7,5},{8,10},{9,11},{10,... | collective-permute-start | bytes 1769480 | tf_op jit(solution)/shard_map/ppermute | solution.py:683
  232.6 28.7 %collective-permute-start.34 = (bf16[4,192,384]{2,1,0:T(8,128)(2,1)S(1)}, bf16[4,192,384]{2,1,0:T(8,128)(2,1)S(1)}, u32[]{:S(2)}, u32[]{:S(2)}) collective-permute-start(bf16[4,192,384]{2,1,0:T(8,128)(2,1)S(1)} %get-tuple-element.168.refs_1_), channel_id=1, source_target_pairs={{0,4},{4,0},{8,12},{12,8},{16,20},{20,16},{24,28},{28,24},{1,5},{5... | collective-permute-start | bytes 1769480 | tf_op jit(solution)/shard_map/ppermute | solution.py:683
  233.3 28.0 %collective-permute-start.35 = (bf16[4,192,384]{2,1,0:T(8,128)(2,1)S(1)}, bf16[4,192,384]{2,1,0:T(8,128)(2,1)S(1)}, u32[]{:S(2)}, u32[]{:S(2)}) collective-permute-start(bf16[4,192,384]{2,1,0:T(8,128)(2,1)S(1)} %get-tuple-element.169.refs_2_), channel_id=1, source_target_pairs={{0,2},{1,3},{2,0},{3,1},{4,6},{5,7},{6,4},{7,5},{8,10},{9,11},{10,... | collective-permute-start | bytes 1769480 | tf_op jit(solution)/shard_map/ppermute | solution.py:683
  234.2 27.0 %collective-permute-start.32 = (bf16[2,192,384]{2,1,0:T(8,128)(2,1)S(1)}, bf16[2,192,384]{2,1,0:T(8,128)(2,1)S(1)}, u32[]{:S(2)}, u32[]{:S(2)}) collective-permute-start(bf16[2,192,384]{2,1,0:T(8,128)(2,1)S(1)} %get-tuple-element.167.refs_0_), channel_id=1, source_target_pairs={{0,4},{4,0},{8,12},{12,8},{16,20},{20,16},{24,28},{28,24},{1,5},{5... | collective-permute-start | bytes 884744 | tf_op jit(solution)/shard_map/ppermute | solution.py:683
  262.3 14.6 %collective-permute-start.38 = (bf16[4,192,384]{2,1,0:T(8,128)(2,1)S(1)}, bf16[4,192,384]{2,1,0:T(8,128)(2,1)S(1)}, u32[]{:S(2)}, u32[]{:S(2)}) collective-permute-start(bf16[4,192,384]{2,1,0:T(8,128)(2,1)S(1)} %get-tuple-element.180.refs_0_), channel_id=1, source_target_pairs={{0,2},{1,3},{2,0},{3,1},{4,6},{5,7},{6,4},{7,5},{8,10},{9,11},{10,... | collective-permute-start | bytes 1769480 | tf_op jit(solution)/shard_map/ppermute | solution.py:683
  262.3 11.8 %collective-permute-start.37 = (bf16[2,192,384]{2,1,0:T(8,128)(2,1)S(1)}, bf16[2,192,384]{2,1,0:T(8,128)(2,1)S(1)}, u32[]{:S(2)}, u32[]{:S(2)}) collective-permute-start(bf16[2,192,384]{2,1,0:T(8,128)(2,1)S(1)} %get-tuple-element.179.refs_3_), channel_id=1, source_target_pairs={{0,8},{4,12},{8,0},{12,4},{16,24},{20,28},{24,16},{28,20},{1,9},{5... | collective-permute-start | bytes 884744 | tf_op jit(solution)/shard_map/ppermute | solution.py:683
  264.0 10.1 %collective-permute-start.39 = (bf16[2,192,384]{2,1,0:T(8,128)(2,1)S(1)}, bf16[2,192,384]{2,1,0:T(8,128)(2,1)S(1)}, u32[]{:S(2)}, u32[]{:S(2)}) collective-permute-start(bf16[2,192,384]{2,1,0:T(8,128)(2,1)S(1)} %get-tuple-element.181.refs_1_), channel_id=1, source_target_pairs={{0,4},{4,0},{8,12},{12,8},{16,20},{20,16},{24,28},{28,24},{1,5},{5... | collective-permute-start | bytes 884744 | tf_op jit(solution)/shard_map/ppermute | solution.py:683
  265.7 7.5 %collective-permute-start.36 = (bf16[1,192,384]{2,1,0:T(8,128)(2,1)S(1)}, bf16[1,192,384]{2,1,0:T(8,128)(2,1)S(1)}, u32[]{:S(2)}, u32[]{:S(2)}) collective-permute-start(bf16[1,192,384]{2,1,0:T(8,128)(2,1)S(1)} %get-tuple-element.178.refs_2_), channel_id=1, source_target_pairs={{0,16},{4,20},{8,24},{12,28},{16,0},{20,4},{24,8},{28,12},{1,17},{... | collective-permute-start | bytes 442376 | tf_op jit(solution)/shard_map/ppermute | solution.py:683
  280.7 22.4 %collective-permute-start.45 = (bf16[8,112,384]{2,1,0:T(8,128)(2,1)S(1)}, bf16[8,112,384]{2,1,0:T(8,128)(2,1)S(1)}, u32[]{:S(2)}, u32[]{:S(2)}) collective-permute-start(bf16[8,112,384]{2,1,0:T(8,128)(2,1)S(1)} %get-tuple-element.193.refs_18_), channel_id=1, source_target_pairs={{0,2},{1,3},{2,0},{3,1},{4,6},{5,7},{6,4},{7,5},{8,10},{9,11},{10,... | collective-permute-start | bytes 2064392 | tf_op jit(solution)/shard_map/ppermute | solution.py:683
  281.4 21.7 %collective-permute-start.43 = (bf16[2,192,384]{2,1,0:T(8,128)(2,1)S(1)}, bf16[2,192,384]{2,1,0:T(8,128)(2,1)S(1)}, u32[]{:S(2)}, u32[]{:S(2)}) collective-permute-start(bf16[2,192,384]{2,1,0:T(8,128)(2,1)S(1)} %get-tuple-element.191.refs_16_), channel_id=1, source_target_pairs={{0,4},{4,0},{8,12},{12,8},{16,20},{20,16},{24,28},{28,24},{1,5},{5... | collective-permute-start | bytes 884744 | tf_op jit(solution)/shard_map/ppermute | solution.py:683
  281.4 21.7 %collective-permute-start.44 = (bf16[2,192,384]{2,1,0:T(8,128)(2,1)S(1)}, bf16[2,192,384]{2,1,0:T(8,128)(2,1)S(1)}, u32[]{:S(2)}, u32[]{:S(2)}) collective-permute-start(bf16[2,192,384]{2,1,0:T(8,128)(2,1)S(1)} %get-tuple-element.192.refs_17_), channel_id=1, source_target_pairs={{0,8},{4,12},{8,0},{12,4},{16,24},{20,28},{24,16},{28,20},{1,9},{5... | collective-permute-start | bytes 884744 | tf_op jit(solution)/shard_map/ppermute | solution.py:683
  283.4 19.7 %collective-permute-start.41 = (bf16[1,192,384]{2,1,0:T(8,128)(2,1)S(1)}, bf16[1,192,384]{2,1,0:T(8,128)(2,1)S(1)}, u32[]{:S(2)}, u32[]{:S(2)}) collective-permute-start(bf16[1,192,384]{2,1,0:T(8,128)(2,1)S(1)} %get-tuple-element.189.refs_14_.refs_0_), channel_id=1, source_target_pairs={{0,16},{4,20},{8,24},{12,28},{16,0},{20,4},{24,8},{28,12},{1,17},{... | collective-permute-start | bytes 442376 | tf_op jit(solution)/shard_map/ppermute | solution.py:683
  284.3 18.8 %collective-permute-start.42 = (bf16[1,192,384]{2,1,0:T(8,128)(2,1)S(1)}, bf16[1,192,384]{2,1,0:T(8,128)(2,1)S(1)}, u32[]{:S(2)}, u32[]{:S(2)}) collective-permute-start(bf16[1,192,384]{2,1,0:T(8,128)(2,1)S(1)} %get-tuple-element.190.refs_15_), channel_id=1, source_target_pairs={{0,16},{4,20},{8,24},{12,28},{16,0},{20,4},{24,8},{28,12},{1,17},{... | collective-permute-start | bytes 442376 | tf_op jit(solution)/shard_map/ppermute | solution.py:683
  303.5 16.5 %collective-permute-start.48 = (bf16[4,112,384]{2,1,0:T(8,128)(2,1)S(1)}, bf16[4,112,384]{2,1,0:T(8,128)(2,1)S(1)}, u32[]{:S(2)}, u32[]{:S(2)}) collective-permute-start(bf16[4,112,384]{2,1,0:T(8,128)(2,1)S(1)} %get-tuple-element.200.refs_3_), channel_id=1, source_target_pairs={{0,8},{4,12},{8,0},{12,4},{16,24},{20,28},{24,16},{28,20},{1,9},{5... | collective-permute-start | bytes 1032200 | tf_op jit(solution)/shard_map/ppermute | solution.py:683
  303.6 16.4 %collective-permute-start.49 = (bf16[2,192,384]{2,1,0:T(8,128)(2,1)S(1)}, bf16[2,192,384]{2,1,0:T(8,128)(2,1)S(1)}, u32[]{:S(2)}, u32[]{:S(2)}) collective-permute-start(bf16[2,192,384]{2,1,0:T(8,128)(2,1)S(1)} %get-tuple-element.206.refs_0_), channel_id=1, source_target_pairs={{0,4},{4,0},{8,12},{12,8},{16,20},{20,16},{24,28},{28,24},{1,5},{5... | collective-permute-start | bytes 884744 | tf_op jit(solution)/shard_map/ppermute | solution.py:683
  304.0 10.9 %collective-permute-start.46 = (bf16[1,192,384]{2,1,0:T(8,128)(2,1)S(1)}, bf16[1,192,384]{2,1,0:T(8,128)(2,1)S(1)}, u32[]{:S(2)}, u32[]{:S(2)}) collective-permute-start(bf16[1,192,384]{2,1,0:T(8,128)(2,1)S(1)} %get-tuple-element.198.refs_1_.refs_0_), channel_id=1, source_target_pairs={{0,16},{4,20},{8,24},{12,28},{16,0},{20,4},{24,8},{28,12},{1,17},{... | collective-permute-start | bytes 442376 | tf_op jit(solution)/shard_map/ppermute | solution.py:683
  305.3 14.7 %collective-permute-start.47 = (bf16[1,192,384]{2,1,0:T(8,128)(2,1)S(1)}, bf16[1,192,384]{2,1,0:T(8,128)(2,1)S(1)}, u32[]{:S(2)}, u32[]{:S(2)}) collective-permute-start(bf16[1,192,384]{2,1,0:T(8,128)(2,1)S(1)} %get-tuple-element.199.refs_2_), channel_id=1, source_target_pairs={{0,16},{4,20},{8,24},{12,28},{16,0},{20,4},{24,8},{28,12},{1,17},{... | collective-permute-start | bytes 442376 | tf_op jit(solution)/shard_map/ppermute | solution.py:683
  323.0 15.4 %collective-permute-start.52 = (bf16[8,96,384]{2,1,0:T(8,128)(2,1)S(1)}, bf16[8,96,384]{2,1,0:T(8,128)(2,1)S(1)}, u32[]{:S(2)}, u32[]{:S(2)}) collective-permute-start(bf16[8,96,384]{2,1,0:T(8,128)(2,1)S(1)} %add_convert_fusion.refs_8_), channel_id=1, source_target_pairs={{0,2},{1,3},{2,0},{3,1},{4,6},{5,7},{6,4},{7,5},{8,10},{9,11},{10,... | collective-permute-start | bytes 1769480 | tf_op jit(solution)/shard_map/ppermute | solution.py:683
  324.8 14.2 %collective-permute-start.51 = (bf16[2,112,384]{2,1,0:T(8,128)(2,1)S(1)}, bf16[2,112,384]{2,1,0:T(8,128)(2,1)S(1)}, u32[]{:S(2)}, u32[]{:S(2)}) collective-permute-start(bf16[2,112,384]{2,1,0:T(8,128)(2,1)S(1)} %get-tuple-element.205.refs_6_), channel_id=1, source_target_pairs={{0,4},{4,0},{8,12},{12,8},{16,20},{20,16},{24,28},{28,24},{1,5},{5... | collective-permute-start | bytes 516104 | tf_op jit(solution)/shard_map/ppermute | solution.py:683
  325.2 16.0 %collective-permute-start.64 = (bf16[2,192,384]{2,1,0:T(8,128)(2,1)S(1)}, bf16[2,192,384]{2,1,0:T(8,128)(2,1)S(1)}, u32[]{:S(2)}, u32[]{:S(2)}) collective-permute-start(bf16[2,192,384]{2,1,0:T(8,128)(2,1)S(1)} %get-tuple-element.219.refs_4_), channel_id=1, source_target_pairs={{0,8},{4,12},{8,0},{12,4},{16,24},{20,28},{24,16},{28,20},{1,9},{5... | collective-permute-start | bytes 884744 | tf_op jit(solution)/shard_map/ppermute | solution.py:683
  325.2 16.5 %collective-permute-start.66 = (bf16[1,192,384]{2,1,0:T(8,128)(2,1)S(1)}, bf16[1,192,384]{2,1,0:T(8,128)(2,1)S(1)}, u32[]{:S(2)}, u32[]{:S(2)}) collective-permute-start(bf16[1,192,384]{2,1,0:T(8,128)(2,1)S(1)} %get-tuple-element.221.refs_5_), channel_id=1, source_target_pairs={{0,16},{4,20},{8,24},{12,28},{16,0},{20,4},{24,8},{28,12},{1,17},{... | collective-permute-start | bytes 442376 | tf_op jit(solution)/shard_map/ppermute | solution.py:683
  326.7 55.8 %collective-permute-start.63 = (bf16[4,192,384]{2,1,0:T(8,128)(2,1)S(1)}, bf16[4,192,384]{2,1,0:T(8,128)(2,1)S(1)}, u32[]{:S(2)}, u32[]{:S(2)}) collective-permute-start(bf16[4,192,384]{2,1,0:T(8,128)(2,1)S(1)} %constant_dynamic-update-slice_fusion.refs_7_.refs_0_), channel_id=1, source_target_pairs={{0,8},{4,12},{8,0},{12,4},{16,24},{20,28},{24,16},{28,20},{1,9},{5... | collective-permute-start | bytes 1769480 | tf_op jit(solution)/shard_map/ppermute | solution.py:683
  338.6 10.0 %collective-permute-start.54 = (bf16[4,96,384]{2,1,0:T(8,128)(2,1)S(1)}, bf16[4,96,384]{2,1,0:T(8,128)(2,1)S(1)}, u32[]{:S(2)}, u32[]{:S(2)}) collective-permute-start(bf16[4,96,384]{2,1,0:T(8,128)(2,1)S(1)} %add_convert_fusion.1), channel_id=1, source_target_pairs={{0,4},{4,0},{8,12},{12,8},{16,20},{20,16},{24,28},{28,24},{1,5},{5... | collective-permute-start | bytes 884744 | tf_op jit(solution)/shard_map/ppermute | solution.py:683
  339.0 11.3 %collective-permute-start.53 = (bf16[1,112,384]{2,1,0:T(8,128)(2,1)S(1)}, bf16[1,112,384]{2,1,0:T(8,128)(2,1)S(1)}, u32[]{:S(2)}, u32[]{:S(2)}) collective-permute-start(bf16[1,112,384]{2,1,0:T(8,128)(2,1)S(1)} %add_convert_fusion.4), channel_id=1, source_target_pairs={{0,16},{4,20},{8,24},{12,28},{16,0},{20,4},{24,8},{28,12},{1,17},{... | collective-permute-start | bytes 258056 | tf_op jit(solution)/shard_map/ppermute | solution.py:683
  341.3 41.1 %collective-permute-start.65 = (bf16[4,192,384]{2,1,0:T(8,128)(2,1)S(1)}, bf16[4,192,384]{2,1,0:T(8,128)(2,1)S(1)}, u32[]{:S(2)}, u32[]{:S(2)}) collective-permute-start(bf16[4,192,384]{2,1,0:T(8,128)(2,1)S(1)} %constant_dynamic-update-slice_fusion.6.refs_2_), channel_id=1, source_target_pairs={{0,4},{4,0},{8,12},{12,8},{16,20},{20,16},{24,28},{28,24},{1,5},{5... | collective-permute-start | bytes 1769480 | tf_op jit(solution)/shard_map/ppermute | solution.py:683
  341.8 18.8 %collective-permute-start.67 = (bf16[2,192,384]{2,1,0:T(8,128)(2,1)S(1)}, bf16[2,192,384]{2,1,0:T(8,128)(2,1)S(1)}, u32[]{:S(2)}, u32[]{:S(2)}) collective-permute-start(bf16[2,192,384]{2,1,0:T(8,128)(2,1)S(1)} %constant_dynamic-update-slice_fusion.8), channel_id=1, source_target_pairs={{0,8},{4,12},{8,0},{12,4},{16,24},{20,28},{24,16},{28,20},{1,9},{5... | collective-permute-start | bytes 884744 | tf_op jit(solution)/shard_map/ppermute | solution.py:683
  348.7 14.0 %collective-permute-start.55 = (bf16[2,96,384]{2,1,0:T(8,128)(2,1)S(1)}, bf16[2,96,384]{2,1,0:T(8,128)(2,1)S(1)}, u32[]{:S(2)}, u32[]{:S(2)}) collective-permute-start(bf16[2,96,384]{2,1,0:T(8,128)(2,1)S(1)} %add_convert_fusion.2), channel_id=1, source_target_pairs={{0,8},{4,12},{8,0},{12,4},{16,24},{20,28},{24,16},{28,20},{1,9},{5... | collective-permute-start | bytes 442376 | tf_op jit(solution)/shard_map/ppermute | solution.py:683
  350.4 12.7 %collective-permute-start.56 = (bf16[1,112,384]{2,1,0:T(8,128)(2,1)S(1)}, bf16[1,112,384]{2,1,0:T(8,128)(2,1)S(1)}, u32[]{:S(2)}, u32[]{:S(2)}) collective-permute-start(bf16[1,112,384]{2,1,0:T(8,128)(2,1)S(1)} %add_convert_fusion.3), channel_id=1, source_target_pairs={{0,16},{4,20},{8,24},{12,28},{16,0},{20,4},{24,8},{28,12},{1,17},{... | collective-permute-start | bytes 258056 | tf_op jit(solution)/shard_map/ppermute | solution.py:683
  360.7 21.8 %collective-permute-start.68 = (bf16[4,192,384]{2,1,0:T(8,128)(2,1)S(1)}, bf16[4,192,384]{2,1,0:T(8,128)(2,1)S(1)}, u32[]{:S(2)}, u32[]{:S(2)}) collective-permute-start(bf16[4,192,384]{2,1,0:T(8,128)(2,1)S(1)} %constant_dynamic-update-slice_fusion.10.refs_4_), channel_id=1, source_target_pairs={{0,4},{4,0},{8,12},{12,8},{16,20},{20,16},{24,28},{28,24},{1,5},{5... | collective-permute-start | bytes 1769480 | tf_op jit(solution)/shard_map/ppermute | solution.py:683
  362.7 5.3 %collective-permute-start.57 = (bf16[1,96,384]{2,1,0:T(8,128)(2,1)S(1)}, bf16[1,96,384]{2,1,0:T(8,128)(2,1)S(1)}, u32[]{:S(2)}, u32[]{:S(2)}) collective-permute-start(bf16[1,96,384]{2,1,0:T(8,128)(2,1)S(1)} %add_convert_fusion.6), channel_id=1, source_target_pairs={{0,16},{4,20},{8,24},{12,28},{16,0},{20,4},{24,8},{28,12},{1,17},{... | collective-permute-start | bytes 221192 | tf_op jit(solution)/shard_map/ppermute | solution.py:683
  368.1 5.4 %collective-permute-start.60 = (bf16[1,96,384]{2,1,0:T(8,128)(2,1)S(1)}, bf16[1,96,384]{2,1,0:T(8,128)(2,1)S(1)}, u32[]{:S(2)}, u32[]{:S(2)}) collective-permute-start(bf16[1,96,384]{2,1,0:T(8,128)(2,1)S(1)} %add_convert_fusion.5), channel_id=1, source_target_pairs={{0,16},{4,20},{8,24},{12,28},{16,0},{20,4},{24,8},{28,12},{1,17},{... | collective-permute-start | bytes 221192 | tf_op jit(solution)/shard_map/ppermute | solution.py:683
  368.5 9.1 %collective-permute-start.58 = (bf16[2,112,384]{2,1,0:T(8,128)(2,1)S(1)}, bf16[2,112,384]{2,1,0:T(8,128)(2,1)S(1)}, u32[]{:S(2)}, u32[]{:S(2)}) collective-permute-start(bf16[2,112,384]{2,1,0:T(8,128)(2,1)S(1)} %constant_dynamic-update-slice_fusion.2), channel_id=1, source_target_pairs={{0,4},{4,0},{8,12},{12,8},{16,20},{20,16},{24,28},{28,24},{1,5},{5... | collective-permute-start | bytes 516104 | tf_op jit(solution)/shard_map/ppermute | solution.py:683
  373.5 6.6 %collective-permute-start.61 = (bf16[2,96,384]{2,1,0:T(8,128)(2,1)S(1)}, bf16[2,96,384]{2,1,0:T(8,128)(2,1)S(1)}, u32[]{:S(2)}, u32[]{:S(2)}) collective-permute-start(bf16[2,96,384]{2,1,0:T(8,128)(2,1)S(1)} %pad_maximum_fusion.4), channel_id=1, source_target_pairs={{0,8},{4,12},{8,0},{12,4},{16,24},{20,28},{24,16},{28,20},{1,9},{5... | collective-permute-start | bytes 442376 | tf_op jit(solution)/shard_map/ppermute | solution.py:683
  377.6 10.5 %collective-permute-start.59 = (bf16[4,112,384]{2,1,0:T(8,128)(2,1)S(1)}, bf16[4,112,384]{2,1,0:T(8,128)(2,1)S(1)}, u32[]{:S(2)}, u32[]{:S(2)}) collective-permute-start(bf16[4,112,384]{2,1,0:T(8,128)(2,1)S(1)} %constant_dynamic-update-slice_fusion.4.refs_0_), channel_id=1, source_target_pairs={{0,8},{4,12},{8,0},{12,4},{16,24},{20,28},{24,16},{28,20},{1,9},{5... | collective-permute-start | bytes 1032200 | tf_op jit(solution)/shard_map/ppermute | solution.py:683
  380.2 8.0 %collective-permute-start.62 = (bf16[4,96,384]{2,1,0:T(8,128)(2,1)S(1)}, bf16[4,96,384]{2,1,0:T(8,128)(2,1)S(1)}, u32[]{:S(2)}, u32[]{:S(2)}) collective-permute-start(bf16[4,96,384]{2,1,0:T(8,128)(2,1)S(1)} %pad_maximum_fusion.2.refs_2_), channel_id=1, source_target_pairs={{0,4},{4,0},{8,12},{12,8},{16,20},{20,16},{24,28},{28,24},{1,5},{5... | collective-permute-start | bytes 884744 | tf_op jit(solution)/shard_map/ppermute | solution.py:683
  (91 other events, 623.9 us)
